TPU v7x, 32 devices: a whole 2x2x4 slice. The times are simulated.
32 devices in a mesh: gx: 4 (over y, core), gy: 8 (over z, x).
Axes of the slice: x: 2, y: 2, z: 4, core: 2. Of those that a mesh axis runs over, the one named last changes fastest.
Arguments:
- right_side: float32 [128, 128, 256], P('gx', 'gy'), may hold values from -8 to 8
- coefficient: float32 [128, 128, 256], P('gx', 'gy'), may hold values from 0.1 to 10
Outputs:
- solution_field: float32 [128, 128, 256], P('gx', 'gy')
- residual: float32 [128, 128, 256], P('gx', 'gy')
All inputs are finite; a program needn't handle non-finite values.
Results may differ from a plain program's by a relative error of at most 0.0003.
Values sent between devices are 32-bit elements; how exact they have to be, the bound alone decides.
No kernel may reach another device: no remote copies, remote signals or barrier semaphores. Data moves between devices by JAX's collectives and lax.ppermute only.
A program may use at most 128 MiB of HBM per device.

v0:
```python
from functools import partial

import jax
import jax.numpy as jnp
from jax import lax
from jax.sharding import PartitionSpec as P

LEVELS = 5
PRE = 2
POST = 2
BOTTOM = 8


SMOOTH_LO = 0.5
SMOOTH_HI = 2.0
COARSE_LO = 0.05
COARSE_HI = 2.0


def with_halo(value, sides, width):
    for axis, dim in sides:
        size, length = (lax.axis_size(axis), value.shape[dim])
        up = [(i, (i + 1) % size) for i in range(size - 1)]
        down = [(j, i) for i, j in up]
        last = lax.slice_in_dim(value, length - width, length, axis=dim)
        leading = lax.slice_in_dim(value, 0, width, axis=dim)
        before = lax.ppermute(last, axis, up)
        after = lax.ppermute(leading, axis, down)
        value = jnp.concatenate([before, value, after], axis=dim)
    return value


def harmonic(own, other):
    return 2.0 * own * other / (own + other)


def face_weights(conduct, padded):
    lower_x = jnp.where(padded[:-2, 1:-1, :] > 0.0, padded[:-2, 1:-1, :], conduct)
    upper_x = jnp.where(padded[2:, 1:-1, :] > 0.0, padded[2:, 1:-1, :], conduct)
    lower_y = jnp.where(padded[1:-1, :-2, :] > 0.0, padded[1:-1, :-2, :], conduct)
    upper_y = jnp.where(padded[1:-1, 2:, :] > 0.0, padded[1:-1, 2:, :], conduct)
    edged = jnp.pad(conduct, ((0, 0), (0, 0), (1, 1)), mode="edge")
    lower_z = edged[:, :, :-2]
    upper_z = edged[:, :, 2:]
    faces = [
        harmonic(conduct, other) for other in (lower_x, upper_x, lower_y, upper_y, lower_z, upper_z)
    ]
    total = faces[0] + faces[1] + faces[2] + faces[3] + faces[4] + faces[5]
    return tuple(faces) + (total,)


def stencil(field, padded, weights, scale):
    zpad = jnp.pad(field, ((0, 0), (0, 0), (1, 1)))
    beside = weights[0] * padded[:-2, 1:-1, :] + weights[1] * padded[2:, 1:-1, :]
    beside = beside + weights[2] * padded[1:-1, :-2, :] + weights[3] * padded[1:-1, 2:, :]
    beside = beside + weights[4] * zpad[:, :, :-2] + weights[5] * zpad[:, :, 2:]
    return scale * (weights[6] * field - beside)


def pad_plane(field):
    return jnp.pad(field, ((1, 1), (1, 1), (0, 0)))


def whole_operate(field, weights, scale):
    return stencil(field, pad_plane(field), weights, scale)


def local_operate(field, weights, scale):
    padded = with_halo(field, (("gx", 0), ("gy", 1)), 1)
    return stencil(field, padded, weights, scale)


def chebyshev(source, start, sweeps, low_end, high_end, operate, inverse):
    theta_val = (high_end + low_end) / 2.0
    half_width = (high_end - low_end) / 2.0
    sigma_val = theta_val / half_width
    rho_now = 1.0 / sigma_val
    if start is None:
        update = inverse * source / theta_val
        iterate = update
    else:
        update = inverse * (source - operate(start)) / theta_val
        iterate = start + update
    for sweep_index in range(sweeps - 1):
        rho_next = 1.0 / (2.0 * sigma_val - rho_now)
        update = rho_next * rho_now * update + 2.0 * rho_next / half_width * inverse * (
            source - operate(iterate)
        )
        iterate = iterate + update
        rho_now = rho_next
    return iterate


def restrict(field):
    size_x, size_y, size_z = field.shape
    return jnp.mean(field.reshape(size_x // 2, 2, size_y // 2, 2, size_z // 2, 2), axis=(1, 3, 5))


def prolong(field):
    size_x, size_y, size_z = field.shape
    grown = jnp.broadcast_to(field[:, None, :, None, :, None], (size_x, 2, size_y, 2, size_z, 2))
    return grown.reshape(2 * size_x, 2 * size_y, 2 * size_z)


def cycle(level_index, source, conduct):
    weights = face_weights(conduct, pad_plane(conduct))
    scale = 0.25**level_index
    inverse = 1.0 / (scale * weights[6])
    operate = partial(whole_operate, weights=weights, scale=scale)
    return chebyshev(source, None, BOTTOM, COARSE_LO, COARSE_HI, operate, inverse)


def collect(source, conduct):
    row_parts = (
        lax.all_gather(source, "gy", axis=1, tiled=True),
        lax.all_gather(conduct, "gy", axis=1, tiled=True),
    )
    whole_parts = (
        lax.all_gather(row_parts[0], "gx", axis=0, tiled=True),
        lax.all_gather(row_parts[1], "gx", axis=0, tiled=True),
    )
    return (whole_parts[0], whole_parts[1])


def own_block(whole, shape):
    start_x = lax.axis_index("gx") * shape[0]
    start_y = lax.axis_index("gy") * shape[1]
    return lax.dynamic_slice(whole, (start_x, start_y, jnp.zeros((), jnp.int32)), shape)


def per_device(right_side, coefficient):
    joined = LEVELS - 1
    conducts = [coefficient]
    for level_index in range(1, joined + 1):
        conducts.append(restrict(conducts[-1]))
    operators = []
    inverses = []
    for level_index in range(joined):
        padded = with_halo(conducts[level_index], (("gx", 0), ("gy", 1)), 1)
        weights = face_weights(conducts[level_index], padded)
        scale = 0.25**level_index
        inverses.append(1.0 / (scale * weights[6]))
        operators.append(partial(local_operate, weights=weights, scale=scale))
    sources = [right_side]
    smoothed = []
    for level_index in range(joined):
        operate = operators[level_index]
        iterate = chebyshev(
            sources[level_index], None, PRE, SMOOTH_LO, SMOOTH_HI, operate, inverses[level_index]
        )
        smoothed.append(iterate)
        sources.append(restrict(sources[level_index] - operate(iterate)))
    whole_source, whole_conduct = collect(sources[joined], conducts[joined])
    correction = own_block(cycle(joined, whole_source, whole_conduct), sources[joined].shape)
    for level_index in reversed(range(joined)):
        iterate = smoothed[level_index] + prolong(correction)
        correction = chebyshev(
            sources[level_index],
            iterate,
            POST,
            SMOOTH_LO,
            SMOOTH_HI,
            operators[level_index],
            inverses[level_index],
        )
    residual = right_side - operators[0](correction)
    return (correction, residual)


def solution(mesh):
    in_specs = (P("gx", "gy", None), P("gx", "gy", None))
    out_specs = (P("gx", "gy", None), P("gx", "gy", None))
    return jax.shard_map(
        per_device, mesh=mesh, in_specs=in_specs, out_specs=out_specs, check_vma=False
    )
```

profile of v0, /device:TPU:0, one launch (start us, length us, event | category | flops | bytes accessed | tf_op | source)
XLA Modules:
  0.0 564.4 jit_solution(12364084085292544761)
XLA Ops:
  5.2 35.6 %reshape.68 = f32[16,2,8,2,128,2]{5,4,3,2,1,0:T(8,128)} reshape(f32[32,16,256]{2,1,0:T(8,128)} %param.3) | data formatting | bytes 1048576 | tf_op jit(solution)/shard_map/reshape | solution.py:96
  40.8 12.2 %reduce_sum.86 = f32[16,8,128]{2,1,0:T(8,128)S(1)} reduce(f32[16,2,8,2,128,2]{5,4,3,2,1,0:T(8,128)} %reshape.68, f32[]{:T(128)} %constant.35.clone.1), dimensions={1,3,5}, to_apply=%region_0.0 | reduce | flops 114688 | bytes 589828 | tf_op jit(solution)/shard_map/reduce_sum | solution.py:96
  53.6 5.2 collective-permute-start.8
  60.2 3.4 collective-permute-start.2
  65.7 5.5 div.203
  76.8 4.0 collective-permute-start.4
  82.1 3.3 collective-permute-done.5
  85.4 4.5 collective-permute-start.6
  91.9 4.1 collective-permute-start.20
  108.0 4.5 collective-permute-start.14
  113.9 4.6 collective-permute-start.10
  119.9 4.6 fusion.13
  124.4 35.6 %reshape.69 = f32[16,2,8,2,128,2]{5,4,3,2,1,0:T(8,128)} reshape(f32[32,16,256]{2,1,0:T(8,128)} %fusion.13) | data formatting | bytes 1048576 | tf_op jit(solution)/shard_map/reshape | solution.py:96
  160.0 12.2 %reduce_sum.87 = f32[16,8,128]{2,1,0:T(8,128)S(1)} reduce(f32[16,2,8,2,128,2]{5,4,3,2,1,0:T(8,128)} %reshape.69, f32[]{:T(128)} %constant.35.clone.1), dimensions={1,3,5}, to_apply=%region_1.0 | reduce | flops 114688 | bytes 589828 | tf_op jit(solution)/shard_map/reduce_sum | solution.py:96
  174.0 3.7 collective-permute-start.16
  179.6 3.2 collective-permute-done.17
  182.9 4.6 collective-permute-start.18
  189.3 4.5 collective-permute-start.32
  200.9 4.8 collective-permute-start.26
  208.4 5.1 collective-permute-start.22
  215.2 5.6 reshape.70
  225.5 3.4 collective-permute-start.28
  234.5 4.9 collective-permute-start.30
  240.7 21.5 %all-gather.2 = f32[8,16,2]{1,2,0:T(2,128)S(1)} all-gather(f32[1,16,2]{1,2,0:T(2,128)S(1)} %multiply_bitcast_fusion.1), channel_id=2, replica_groups=mesh['gx'=4,'gy'=8] {'gy'}, dimensions={0}, use_global_device_ids=true | all-gather | bytes 1152 | tf_op jit(solution)/shard_map/all_gather | solution.py:116
  263.0 8.1 %all_gather.13 = f32[8,8,16]{2,1,0:T(8,128)S(1)} all-gather(f32[2,8,16]{2,1,0:T(8,128)} %reshape.75), channel_id=1, replica_groups=mesh['gx'=4,'gy'=8] {'gx'}, dimensions={0}, use_global_device_ids=true | all-gather | bytes 5120 | tf_op jit(solution)/shard_map/all_gather | solution.py:120
  282.4 5.1 collective-permute-start.34
  295.2 3.4 collective-permute-start.40
  302.0 4.5 collective-permute-start.42
  313.4 3.4 collective-permute-start.44
  321.7 5.2 collective-permute-start.46
  328.2 4.5 collective-permute-done.47
  337.8 17.3 %all-gather.3 = f32[8,16,2]{1,2,0:T(2,128)S(1)} all-gather(f32[1,16,2]{1,2,0:T(2,128)S(1)} %multiply_bitcast_fusion), channel_id=3, replica_groups=mesh['gx'=4,'gy'=8] {'gy'}, dimensions={0}, use_global_device_ids=true | all-gather | bytes 1152 | tf_op jit(solution)/shard_map/all_gather | solution.py:115
  358.3 5.4 all_gather.15
  372.5 3.3 collective-permute-start.50
  377.2 4.2 collective-permute-done.51
  393.2 4.2 collective-permute-done.55
  412.1 4.2 collective-permute-done.59
  428.3 4.2 collective-permute-done.63
  436.0 4.0 reshape.73
  451.9 4.2 collective-permute-done.67
  464.1 4.8 collective-permute-start.70
  470.3 4.2 collective-permute-done.71
  475.5 11.4 %broadcast_in_dim.36 = f32[16,2,8,2,128,2]{5,4,3,2,1,0:T(8,128)} broadcast(f32[16,8,128]{2,1,0:T(8,128)S(1)} %fusion.118), dimensions={0,2,4} | broadcast | bytes 589824 | tf_op jit(solution)/shard_map/broadcast_in_dim | solution.py:101
  486.9 24.6 %reshape.74 = f32[32,16,256]{2,1,0:T(8,128)} reshape(f32[16,2,8,2,128,2]{5,4,3,2,1,0:T(8,128)} %broadcast_in_dim.36) | data formatting | bytes 1048576 | tf_op jit(solution)/shard_map/reshape | solution.py:102
  519.8 4.2 collective-permute-start.74
  525.6 4.2 collective-permute-done.75
  542.1 4.2 collective-permute-done.79
  558.7 4.2 collective-permute-done.83
  (325 shorter events, 214.4 us)
Async XLA Ops:
  1.4 58.7 %collective-permute-start = (f32[1,16,256]{2,1,0:T(8,128)S(1)}, f32[1,16,256]{2,1,0:T(8,128)S(1)}, u32[]{:S(2)}, u32[]{:S(2)}) collective-permute-start(f32[1,16,256]{2,1,0:T(8,128)S(1)} %get-tuple-element.81), channel_id=1, source_target_pairs={{0,8},{8,16},{16,24},{1,9},{9,17},{17,25},{2,10},{10,18},{18,26},{... | collective-permute-start | bytes 49160 | tf_op jit(solution)/shard_map/ppermute | solution.py:27
  3.7 56.4 %collective-permute-start.1 = (f32[1,16,256]{2,1,0:T(8,128)S(1)}, f32[1,16,256]{2,1,0:T(8,128)S(1)}, u32[]{:S(2)}, u32[]{:S(2)}) collective-permute-start(f32[1,16,256]{2,1,0:T(8,128)S(1)} %get-tuple-element.80), channel_id=1, source_target_pairs={{8,0},{16,8},{24,16},{9,1},{17,9},{25,17},{10,2},{18,10},{26,18},{... | collective-permute-start | bytes 49160 | tf_op jit(solution)/shard_map/ppermute | solution.py:28
  53.6 59.0 %collective-permute-start.8 = (f32[1,8,128]{2,1,0:T(8,128)}, f32[1,8,128]{2,1,0:T(8,128)S(1)}, u32[]{:S(2)}, u32[]{:S(2)}) collective-permute-start(f32[1,8,128]{2,1,0:T(8,128)} %get-tuple-element.102), channel_id=1, source_target_pairs={{0,8},{8,16},{16,24},{1,9},{9,17},{17,25},{2,10},{10,18},{18,26},{... | collective-permute-start | bytes 12296 | tf_op jit(solution)/shard_map/ppermute | solution.py:27
  58.8 55.2 %collective-permute-start.9 = (f32[1,8,128]{2,1,0:T(8,128)}, f32[1,8,128]{2,1,0:T(8,128)S(1)}, u32[]{:S(2)}, u32[]{:S(2)}) collective-permute-start(f32[1,8,128]{2,1,0:T(8,128)} %get-tuple-element.103), channel_id=1, source_target_pairs={{8,0},{16,8},{24,16},{9,1},{17,9},{25,17},{10,2},{18,10},{26,18},{... | collective-permute-start | bytes 12296 | tf_op jit(solution)/shard_map/ppermute | solution.py:28
  60.2 13.6 %collective-permute-start.2 = (f32[34,1,256]{2,1,0:T(1,128)S(1)}, f32[34,1,256]{2,1,0:T(1,128)S(1)}, u32[]{:S(2)}, u32[]{:S(2)}) collective-permute-start(f32[34,1,256]{2,1,0:T(1,128)S(1)} %get-tuple-element.67), channel_id=1, source_target_pairs={{0,1},{1,2},{2,3},{3,4},{4,5},{5,6},{6,7},{8,9},{9,10},{10,11},{11... | collective-permute-start | bytes 104456 | tf_op jit(solution)/shard_map/ppermute | solution.py:27
  63.6 10.2 %collective-permute-start.3 = (f32[34,1,256]{2,1,0:T(1,128)S(1)}, f32[34,1,256]{2,1,0:T(1,128)S(1)}, u32[]{:S(2)}, u32[]{:S(2)}) collective-permute-start(f32[34,1,256]{2,1,0:T(1,128)S(1)} %get-tuple-element.66), channel_id=1, source_target_pairs={{1,0},{2,1},{3,2},{4,3},{5,4},{6,5},{7,6},{9,8},{10,9},{11,10},{12... | collective-permute-start | bytes 104456 | tf_op jit(solution)/shard_map/ppermute | solution.py:28
  76.8 5.3 collective-permute-start.4
  85.4 10.5 %collective-permute-start.6 = (f32[34,1,256]{2,1,0:T(1,128)S(1)}, f32[34,1,256]{2,1,0:T(1,128)S(1)}, u32[]{:S(2)}, u32[]{:S(2)}) collective-permute-start(f32[34,1,256]{2,1,0:T(1,128)S(1)} %get-tuple-element.64), channel_id=1, source_target_pairs={{0,1},{1,2},{2,3},{3,4},{4,5},{5,6},{6,7},{8,9},{9,10},{10,11},{11... | collective-permute-start | bytes 104456 | tf_op jit(solution)/shard_map/ppermute | solution.py:27
  90.0 6.3 %collective-permute-start.7 = (f32[34,1,256]{2,1,0:T(1,128)S(1)}, f32[34,1,256]{2,1,0:T(1,128)S(1)}, u32[]{:S(2)}, u32[]{:S(2)}) collective-permute-start(f32[34,1,256]{2,1,0:T(1,128)S(1)} %get-tuple-element.65), channel_id=1, source_target_pairs={{1,0},{2,1},{3,2},{4,3},{5,4},{6,5},{7,6},{9,8},{10,9},{11,10},{12... | collective-permute-start | bytes 104456 | tf_op jit(solution)/shard_map/ppermute | solution.py:28
  91.9 113.9 %collective-permute-start.20 = (f32[1,4,64]{2,1,0:T(4,128)}, f32[1,4,64]{2,1,0:T(4,128)S(1)}, u32[]{:S(2)}, u32[]{:S(2)}) collective-permute-start(f32[1,4,64]{2,1,0:T(4,128)} %get-tuple-element.126), channel_id=1, source_target_pairs={{0,8},{8,16},{16,24},{1,9},{9,17},{17,25},{2,10},{10,18},{18,26},{... | collective-permute-start | bytes 3080 | tf_op jit(solution)/shard_map/ppermute | solution.py:27
  97.9 7.8 %collective-permute-start.12 = (f32[1,16,256]{2,1,0:T(8,128)S(1)}, f32[1,16,256]{2,1,0:T(8,128)S(1)}, u32[]{:S(2)}, u32[]{:S(2)}) collective-permute-start(f32[1,16,256]{2,1,0:T(8,128)S(1)} %get-tuple-element.74), channel_id=1, source_target_pairs={{0,8},{8,16},{16,24},{1,9},{9,17},{17,25},{2,10},{10,18},{18,26},{... | collective-permute-start | bytes 49160 | tf_op jit(solution)/shard_map/ppermute | solution.py:27
  101.1 5.8 %collective-permute-start.13 = (f32[1,16,256]{2,1,0:T(8,128)S(1)}, f32[1,16,256]{2,1,0:T(8,128)S(1)}, u32[]{:S(2)}, u32[]{:S(2)}) collective-permute-start(f32[1,16,256]{2,1,0:T(8,128)S(1)} %get-tuple-element.75), channel_id=1, source_target_pairs={{8,0},{16,8},{24,16},{9,1},{17,9},{25,17},{10,2},{18,10},{26,18},{... | collective-permute-start | bytes 49160 | tf_op jit(solution)/shard_map/ppermute | solution.py:28
  105.6 101.4 %collective-permute-start.21 = (f32[1,4,64]{2,1,0:T(4,128)}, f32[1,4,64]{2,1,0:T(4,128)}, u32[]{:S(2)}, u32[]{:S(2)}) collective-permute-start(f32[1,4,64]{2,1,0:T(4,128)} %get-tuple-element.127), channel_id=1, source_target_pairs={{8,0},{16,8},{24,16},{9,1},{17,9},{25,17},{10,2},{18,10},{26,18},{... | collective-permute-start | bytes 3080 | tf_op jit(solution)/shard_map/ppermute | solution.py:28
  108.0 10.5 %collective-permute-start.14 = (f32[34,1,256]{2,1,0:T(1,128)S(1)}, f32[34,1,256]{2,1,0:T(1,128)S(1)}, u32[]{:S(2)}, u32[]{:S(2)}) collective-permute-start(f32[34,1,256]{2,1,0:T(1,128)S(1)} %get-tuple-element.62), channel_id=1, source_target_pairs={{0,1},{1,2},{2,3},{3,4},{4,5},{5,6},{6,7},{8,9},{9,10},{10,11},{11... | collective-permute-start | bytes 104456 | tf_op jit(solution)/shard_map/ppermute | solution.py:27
  112.6 7.3 %collective-permute-start.15 = (f32[34,1,256]{2,1,0:T(1,128)S(1)}, f32[34,1,256]{2,1,0:T(1,128)S(1)}, u32[]{:S(2)}, u32[]{:S(2)}) collective-permute-start(f32[34,1,256]{2,1,0:T(1,128)S(1)} %get-tuple-element.63), channel_id=1, source_target_pairs={{1,0},{2,1},{3,2},{4,3},{5,4},{6,5},{7,6},{9,8},{10,9},{11,10},{12... | collective-permute-start | bytes 104456 | tf_op jit(solution)/shard_map/ppermute | solution.py:28
  113.9 58.3 %collective-permute-start.10 = (f32[18,1,128]{2,1,0:T(1,128)S(1)}, f32[18,1,128]{2,1,0:T(1,128)S(1)}, u32[]{:S(2)}, u32[]{:S(2)}) collective-permute-start(f32[18,1,128]{2,1,0:T(1,128)S(1)} %get-tuple-element.91), channel_id=1, source_target_pairs={{0,1},{1,2},{2,3},{3,4},{4,5},{5,6},{6,7},{8,9},{9,10},{10,11},{11... | collective-permute-start | bytes 27656 | tf_op jit(solution)/shard_map/ppermute | solution.py:27
  118.6 53.7 %collective-permute-start.11 = (f32[18,1,128]{2,1,0:T(1,128)S(1)}, f32[18,1,128]{2,1,0:T(1,128)S(1)}, u32[]{:S(2)}, u32[]{:S(2)}) collective-permute-start(f32[18,1,128]{2,1,0:T(1,128)S(1)} %get-tuple-element.90), channel_id=1, source_target_pairs={{1,0},{2,1},{3,2},{4,3},{5,4},{6,5},{7,6},{9,8},{10,9},{11,10},{12... | collective-permute-start | bytes 27656 | tf_op jit(solution)/shard_map/ppermute | solution.py:28
  174.0 5.6 collective-permute-start.16
  182.9 11.0 %collective-permute-start.18 = (f32[18,1,128]{2,1,0:T(1,128)S(1)}, f32[18,1,128]{2,1,0:T(1,128)S(1)}, u32[]{:S(2)}, u32[]{:S(2)}) collective-permute-start(f32[18,1,128]{2,1,0:T(1,128)S(1)} %get-tuple-element.88), channel_id=1, source_target_pairs={{0,1},{1,2},{2,3},{3,4},{4,5},{5,6},{6,7},{8,9},{9,10},{10,11},{11... | collective-permute-start | bytes 27656 | tf_op jit(solution)/shard_map/ppermute | solution.py:27
  187.4 6.5 %collective-permute-start.19 = (f32[18,1,128]{2,1,0:T(1,128)S(1)}, f32[18,1,128]{2,1,0:T(1,128)S(1)}, u32[]{:S(2)}, u32[]{:S(2)}) collective-permute-start(f32[18,1,128]{2,1,0:T(1,128)S(1)} %get-tuple-element.89), channel_id=1, source_target_pairs={{1,0},{2,1},{3,2},{4,3},{5,4},{6,5},{7,6},{9,8},{10,9},{11,10},{12... | collective-permute-start | bytes 27656 | tf_op jit(solution)/shard_map/ppermute | solution.py:28
  189.3 86.5 %collective-permute-start.32 = (f32[1,2,32]{2,0,1:T(1,128)}, f32[1,2,32]{2,0,1:T(1,128)}, u32[]{:S(2)}, u32[]{:S(2)}) collective-permute-start(f32[1,2,32]{2,0,1:T(1,128)} %get-tuple-element.150), channel_id=1, source_target_pairs={{0,8},{8,16},{16,24},{1,9},{9,17},{17,25},{2,10},{10,18},{18,26},{... | collective-permute-start | bytes 776 | tf_op jit(solution)/shard_map/ppermute | solution.py:27
  199.2 76.7 %collective-permute-start.33 = (f32[1,2,32]{2,0,1:T(1,128)}, f32[1,2,32]{2,0,1:T(1,128)}, u32[]{:S(2)}, u32[]{:S(2)}) collective-permute-start(f32[1,2,32]{2,0,1:T(1,128)} %get-tuple-element.151), channel_id=1, source_target_pairs={{8,0},{16,8},{24,16},{9,1},{17,9},{25,17},{10,2},{18,10},{26,18},{... | collective-permute-start | bytes 776 | tf_op jit(solution)/shard_map/ppermute | solution.py:28
  200.9 12.6 %collective-permute-start.26 = (f32[18,1,128]{2,1,0:T(1,128)S(1)}, f32[18,1,128]{2,1,0:T(1,128)S(1)}, u32[]{:S(2)}, u32[]{:S(2)}) collective-permute-start(f32[18,1,128]{2,1,0:T(1,128)S(1)} %get-tuple-element.86), channel_id=1, source_target_pairs={{0,1},{1,2},{2,3},{3,4},{4,5},{5,6},{6,7},{8,9},{9,10},{10,11},{11... | collective-permute-start | bytes 27656 | tf_op jit(solution)/shard_map/ppermute | solution.py:27
  205.8 9.3 %collective-permute-start.27 = (f32[18,1,128]{2,1,0:T(1,128)S(1)}, f32[18,1,128]{2,1,0:T(1,128)S(1)}, u32[]{:S(2)}, u32[]{:S(2)}) collective-permute-start(f32[18,1,128]{2,1,0:T(1,128)S(1)} %get-tuple-element.87), channel_id=1, source_target_pairs={{1,0},{2,1},{3,2},{4,3},{5,4},{6,5},{7,6},{9,8},{10,9},{11,10},{12... | collective-permute-start | bytes 27656 | tf_op jit(solution)/shard_map/ppermute | solution.py:28
  208.4 14.9 %collective-permute-start.22 = (f32[10,1,64]{2,1,0:T(1,128)}, f32[10,1,64]{2,1,0:T(1,128)}, u32[]{:S(2)}, u32[]{:S(2)}) collective-permute-start(f32[10,1,64]{2,1,0:T(1,128)} %get-tuple-element.115), channel_id=1, source_target_pairs={{0,1},{1,2},{2,3},{3,4},{4,5},{5,6},{6,7},{8,9},{9,10},{10,11},{11... | collective-permute-start | bytes 7688 | tf_op jit(solution)/shard_map/ppermute | solution.py:27
  213.6 9.8 %collective-permute-start.23 = (f32[10,1,64]{2,1,0:T(1,128)}, f32[10,1,64]{2,1,0:T(1,128)}, u32[]{:S(2)}, u32[]{:S(2)}) collective-permute-start(f32[10,1,64]{2,1,0:T(1,128)} %get-tuple-element.114), channel_id=1, source_target_pairs={{1,0},{2,1},{3,2},{4,3},{5,4},{6,5},{7,6},{9,8},{10,9},{11,10},{12... | collective-permute-start | bytes 7688 | tf_op jit(solution)/shard_map/ppermute | solution.py:28
  225.5 8.4 %collective-permute-start.28 = (f32[1,4,64]{2,1,0:T(4,128)}, f32[1,4,64]{2,1,0:T(4,128)S(1)}, u32[]{:S(2)}, u32[]{:S(2)}) collective-permute-start(f32[1,4,64]{2,1,0:T(4,128)} %get-tuple-element.122), channel_id=1, source_target_pairs={{0,8},{8,16},{16,24},{1,9},{9,17},{17,25},{2,10},{10,18},{18,26},{... | collective-permute-start | bytes 3080 | tf_op jit(solution)/shard_map/ppermute | solution.py:27
  234.5 36.6 %collective-permute-start.30 = (f32[10,1,64]{2,1,0:T(1,128)}, f32[10,1,64]{2,1,0:T(1,128)}, u32[]{:S(2)}, u32[]{:S(2)}) collective-permute-start(f32[10,1,64]{2,1,0:T(1,128)} %get-tuple-element.112), channel_id=1, source_target_pairs={{0,1},{1,2},{2,3},{3,4},{4,5},{5,6},{6,7},{8,9},{9,10},{10,11},{11... | collective-permute-start | bytes 7688 | tf_op jit(solution)/shard_map/ppermute | solution.py:27
  239.4 31.7 %collective-permute-start.31 = (f32[10,1,64]{2,1,0:T(1,128)}, f32[10,1,64]{2,1,0:T(1,128)}, u32[]{:S(2)}, u32[]{:S(2)}) collective-permute-start(f32[10,1,64]{2,1,0:T(1,128)} %get-tuple-element.113), channel_id=1, source_target_pairs={{1,0},{2,1},{3,2},{4,3},{5,4},{6,5},{7,6},{9,8},{10,9},{11,10},{12... | collective-permute-start | bytes 7688 | tf_op jit(solution)/shard_map/ppermute | solution.py:28
  278.9 9.9 %collective-permute-start.38 = (f32[10,1,64]{2,1,0:T(1,128)S(1)}, f32[10,1,64]{2,1,0:T(1,128)S(1)}, u32[]{:S(2)}, u32[]{:S(2)}) collective-permute-start(f32[10,1,64]{2,1,0:T(1,128)S(1)} %get-tuple-element.110), channel_id=1, source_target_pairs={{0,1},{1,2},{2,3},{3,4},{4,5},{5,6},{6,7},{8,9},{9,10},{10,11},{11... | collective-permute-start | bytes 7688 | tf_op jit(solution)/shard_map/ppermute | solution.py:27
  280.5 8.3 %collective-permute-start.39 = (f32[10,1,64]{2,1,0:T(1,128)S(1)}, f32[10,1,64]{2,1,0:T(1,128)S(1)}, u32[]{:S(2)}, u32[]{:S(2)}) collective-permute-start(f32[10,1,64]{2,1,0:T(1,128)S(1)} %get-tuple-element.111), channel_id=1, source_target_pairs={{1,0},{2,1},{3,2},{4,3},{5,4},{6,5},{7,6},{9,8},{10,9},{11,10},{12... | collective-permute-start | bytes 7688 | tf_op jit(solution)/shard_map/ppermute | solution.py:28
  282.4 11.7 %collective-permute-start.34 = (f32[6,1,32]{2,0,1:T(8,128)}, f32[6,1,32]{2,0,1:T(8,128)}, u32[]{:S(2)}, u32[]{:S(2)}) collective-permute-start(f32[6,1,32]{2,0,1:T(8,128)} %get-tuple-element.137), channel_id=1, source_target_pairs={{0,1},{1,2},{2,3},{3,4},{4,5},{5,6},{6,7},{8,9},{9,10},{10,11},{11... | collective-permute-start | bytes 2312 | tf_op jit(solution)/shard_map/ppermute | solution.py:27
  287.5 6.6 %collective-permute-start.35 = (f32[6,1,32]{2,0,1:T(8,128)}, f32[6,1,32]{2,0,1:T(8,128)}, u32[]{:S(2)}, u32[]{:S(2)}) collective-permute-start(f32[6,1,32]{2,0,1:T(8,128)} %get-tuple-element.136), channel_id=1, source_target_pairs={{1,0},{2,1},{3,2},{4,3},{5,4},{6,5},{7,6},{9,8},{10,9},{11,10},{12... | collective-permute-start | bytes 2312 | tf_op jit(solution)/shard_map/ppermute | solution.py:28
  302.0 7.7 %collective-permute-start.42 = (f32[6,1,32]{2,0,1:T(8,128)S(1)}, f32[6,1,32]{2,0,1:T(8,128)S(1)}, u32[]{:S(2)}, u32[]{:S(2)}) collective-permute-start(f32[6,1,32]{2,0,1:T(8,128)S(1)} %get-tuple-element.134), channel_id=1, source_target_pairs={{0,1},{1,2},{2,3},{3,4},{4,5},{5,6},{6,7},{8,9},{9,10},{10,11},{11... | collective-permute-start | bytes 2312 | tf_op jit(solution)/shard_map/ppermute | solution.py:27
  306.6 5.5 collective-permute-start.43
  321.7 6.5 %collective-permute-start.46 = (f32[6,1,32]{2,0,1:T(8,128)}, f32[6,1,32]{2,0,1:T(8,128)}, u32[]{:S(2)}, u32[]{:S(2)}) collective-permute-start(f32[6,1,32]{2,0,1:T(8,128)} %get-tuple-element.132), channel_id=1, source_target_pairs={{0,1},{1,2},{2,3},{3,4},{4,5},{5,6},{6,7},{8,9},{9,10},{10,11},{11... | collective-permute-start | bytes 2312 | tf_op jit(solution)/shard_map/ppermute | solution.py:27
  326.9 5.8 %collective-permute-start.47 = (f32[6,1,32]{2,0,1:T(8,128)}, f32[6,1,32]{2,0,1:T(8,128)}, u32[]{:S(2)}, u32[]{:S(2)}) collective-permute-start(f32[6,1,32]{2,0,1:T(8,128)} %get-tuple-element.133), channel_id=1, source_target_pairs={{1,0},{2,1},{3,2},{4,3},{5,4},{6,5},{7,6},{9,8},{10,9},{11,10},{12... | collective-permute-start | bytes 2312 | tf_op jit(solution)/shard_map/ppermute | solution.py:28
  375.8 5.5 collective-permute-start.51
  391.8 5.5 collective-permute-start.55
  410.8 5.5 collective-permute-start.59
  426.9 5.5 collective-permute-start.63
  450.6 5.6 collective-permute-start.67
  464.1 6.1 %collective-permute-start.70 = (f32[18,1,128]{2,1,0:T(1,128)S(1)}, f32[18,1,128]{2,1,0:T(1,128)S(1)}, u32[]{:S(2)}, u32[]{:S(2)}) collective-permute-start(f32[18,1,128]{2,1,0:T(1,128)S(1)} %get-tuple-element.82), channel_id=1, source_target_pairs={{0,1},{1,2},{2,3},{3,4},{4,5},{5,6},{6,7},{8,9},{9,10},{10,11},{11... | collective-permute-start | bytes 27656 | tf_op jit(solution)/shard_map/ppermute | solution.py:27
  468.9 5.6 collective-permute-start.71
  519.8 5.8 %collective-permute-start.74 = (f32[34,1,256]{2,1,0:T(1,128)S(1)}, f32[34,1,256]{2,1,0:T(1,128)S(1)}, u32[]{:S(2)}, u32[]{:S(2)}) collective-permute-start(f32[34,1,256]{2,1,0:T(1,128)S(1)} %get-tuple-element.60), channel_id=1, source_target_pairs={{0,1},{1,2},{2,3},{3,4},{4,5},{5,6},{6,7},{8,9},{9,10},{10,11},{11... | collective-permute-start | bytes 104456 | tf_op jit(solution)/shard_map/ppermute | solution.py:27
  524.0 5.8 %collective-permute-start.75 = (f32[34,1,256]{2,1,0:T(1,128)S(1)}, f32[34,1,256]{2,1,0:T(1,128)S(1)}, u32[]{:S(2)}, u32[]{:S(2)}) collective-permute-start(f32[34,1,256]{2,1,0:T(1,128)S(1)} %get-tuple-element.61), channel_id=1, source_target_pairs={{1,0},{2,1},{3,2},{4,3},{5,4},{6,5},{7,6},{9,8},{10,9},{11,10},{12... | collective-permute-start | bytes 104456 | tf_op jit(solution)/shard_map/ppermute | solution.py:28
  540.5 5.8 %collective-permute-start.79 = (f32[34,1,256]{2,1,0:T(1,128)S(1)}, f32[34,1,256]{2,1,0:T(1,128)S(1)}, u32[]{:S(2)}, u32[]{:S(2)}) collective-permute-start(f32[34,1,256]{2,1,0:T(1,128)S(1)} %get-tuple-element.59), channel_id=1, source_target_pairs={{1,0},{2,1},{3,2},{4,3},{5,4},{6,5},{7,6},{9,8},{10,9},{11,10},{12... | collective-permute-start | bytes 104456 | tf_op jit(solution)/shard_map/ppermute | solution.py:28
  557.1 5.8 %collective-permute-start.83 = (f32[34,1,256]{2,1,0:T(1,128)S(1)}, f32[34,1,256]{2,1,0:T(1,128)S(1)}, u32[]{:S(2)}, u32[]{:S(2)}) collective-permute-start(f32[34,1,256]{2,1,0:T(1,128)S(1)} %get-tuple-element.57), channel_id=1, source_target_pairs={{1,0},{2,1},{3,2},{4,3},{5,4},{6,5},{7,6},{9,8},{10,9},{11,10},{12... | collective-permute-start | bytes 104456 | tf_op jit(solution)/shard_map/ppermute | solution.py:28
  (72 other events, 1518.2 us)
where the time goes:
time: 570 us; the launch traced here: 564 us
  starting transfers between devices  205 us (36%)
  local copies, waits for them, and re-layouts  149 us (26%)
  waiting for transfers between devices  84.2 us (15%)
  other arithmetic  72 us (13%)
  blocking collectives  52.3 us (9%)
    ppermute x42, starting transfers between devices, with_halo(): before = lax.ppermute(last, axis, up)  150 us
    ppermute x42, waiting for transfers between devices, with_halo(): after = lax.ppermute(leading, axis, down)  83.2 us
    reshape x4, local copies, waits for them, and re-layouts, restrict(): field.reshape(size_x // 2, 2, size_y // 2, 2, size_z // 2, 2)  78.8 us
    ppermute x42, starting transfers between devices, with_halo(): after = lax.ppermute(leading, axis, down)  54.7 us
    reduce_sum x10, other arithmetic, restrict(): jnp.mean(field.reshape(size_x // 2, 2, size_y // 2, 2, size_z // 2, 2), a...  36.9 us
    reshape x3, local copies, waits for them, and re-layouts, prolong(): return grown.reshape(2 * size_x, 2 * size_y, 2 * size_z)  29.9 us
    all_gather x1, blocking collectives, collect(): lax.all_gather(conduct, 'gy', axis=1, tiled=True)  21.5 us
    all_gather x1, blocking collectives, collect(): lax.all_gather(source, 'gy', axis=1, tiled=True)  17.3 us
  transfers between devices with their start and end apart: 84, of which 32 were waited for; matrix products, arithmetic and copies ran while one was open for 26% of the time, Pallas kernels for 0%

commit v1 on v0

v1 whole, which is shorter than its diff:
```python
import math
from functools import partial

import jax
import jax.numpy as jnp
from jax import lax
from jax.experimental import pallas as pl
from jax.experimental.pallas import tpu as pltpu
from jax.sharding import PartitionSpec as P

F32 = jnp.float32
BF16 = jnp.bfloat16

THETA = 1.25
DELTA = 0.75
SIGMA = THETA / DELTA
RHO0 = 1.0 / SIGMA
RHO1 = 1.0 / (2.0 * SIGMA - RHO0)
KEEP = RHO1 * RHO0
GAIN = 2.0 * RHO1 / DELTA
BOTTOM = 8
BOTTOM_THETA = (2.0 + 0.05) / 2.0
BOTTOM_DELTA = (2.0 - 0.05) / 2.0

K0, B0, S0 = 3, 2, 3
K1, B1 = 6, 5
R0, R1 = 4, 8
SPARE = 4 * 1024 * 1024


def rotate(value, axis, shift):
    size = lax.axis_size(axis)
    return lax.ppermute(value, axis, [(i, (i + shift) % size) for i in range(size)])


def inside(axis, side):
    index = lax.axis_index(axis)
    if side < 0:
        return index > 0
    return index < lax.axis_size(axis) - 1


def masked(flag, value):
    return jnp.where(flag, value, jnp.zeros_like(value))


def iota(shape, dim):
    return lax.broadcasted_iota(jnp.int32, shape, dim)


def pick(x, matrix):
    high = x.astype(BF16)
    low = (x - high.astype(F32)).astype(BF16)
    return jnp.dot(high, matrix, preferred_element_type=F32) + jnp.dot(
        low, matrix, preferred_element_type=F32
    )


def halving(fine, coarse, scale, first=0, valid=None):
    row, col = iota((fine, coarse), 0), iota((fine, coarse), 1)
    hit = row // 2 + first == col
    if valid is not None:
        hit = hit & (row < valid)
    return jnp.where(hit, scale, 0.0).astype(BF16)


def doubling(coarse, fine, valid):
    row, col = iota((coarse, fine), 0), iota((coarse, fine), 1)
    return jnp.where((row == col // 2) & (row < valid), 1.0, 0.0).astype(BF16)


def face(a, b):
    product, total = a * b, a + b
    return jnp.where(product > 0.0, 2.0 * product / total, total)


def up(x, axis):
    return pltpu.roll(x, x.shape[axis] - 1, axis)


def down(x, axis):
    return pltpu.roll(x, 1, axis)


def sided(k, axis, edged):
    size = k.shape[axis]
    after = up(k, axis)
    place = iota(k.shape, axis)
    if edged:
        after = jnp.where(place == size - 1, 0.0, after)
    w = face(k, after)
    low = down(w, axis)
    if edged:
        low = jnp.where(place == 0, k, low)
        return jnp.where(place == size - 1, 0.0, w), w + low
    return w, w + low


def weigh(k, wl, ws, wz, total, inverse, row_edge, lane_edge, unroll):
    planes = k.shape[0]

    def body(i, before):
        here = k[i]
        lead = face(here, k[i + 1])
        rows, row_sum = sided(here, 0, row_edge)
        lanes, lane_sum = sided(here, 1, lane_edge)
        wl[i] = lead
        ws[i] = rows
        wz[i] = lanes
        whole = (before + lead) + (row_sum + lane_sum)
        total[i] = whole
        inverse[i] = jnp.where(here > 0.0, 1.0 / whole, 0.0)
        return lead

    lax.fori_loop(0, planes - 1, body, jnp.zeros(k.shape[1:], F32), unroll=unroll)


def beside(x, wl, ws, wz, i):
    here = x[i]
    rows, lanes = ws[i], wz[i]
    out = wl[i] * x[i + 1] + wl[i - 1] * x[i - 1]
    out = out + (rows * up(here, 0) + down(rows * here, 0))
    return out + (lanes * up(here, 1) + down(lanes * here, 1))


def loop(low, high, body, unroll):
    def step(i, carry):
        body(i)
        return carry

    lax.fori_loop(low, high, step, 0, unroll=unroll)


def pre_smooth(b, first, second, w, inverse, scale, depth, unroll):
    planes = b.shape[0]

    def start(i):
        first[i] = b[i] * inverse[i] * (1.0 / (scale * THETA))

    loop(depth, planes - depth, start, unroll)

    def sweep(i):
        near = beside(first, *w, i)
        second[i] = (1.0 + KEEP + GAIN * (THETA - 1.0)) * first[i] + GAIN * (inverse[i] * near)

    loop(depth + 1, planes - depth - 1, sweep, unroll)


def post_smooth(b, first, second, w, inverse, scale, depth, unroll, store):
    planes = b.shape[0]

    def sweep(i):
        x = first[i]
        near = beside(first, *w, i)
        second[i] = x + ((b[i] * (1.0 / scale) + near) * inverse[i] - x) * (1.0 / THETA)

    loop(depth, planes - depth, sweep, unroll)

    def last(i):
        x = second[i]
        near = beside(second, *w, i)
        step = KEEP * (x - first[i]) + GAIN * ((b[i] * (1.0 / scale) + near) * inverse[i] - x)
        store(i, x + step)

    loop(depth + 1, planes - depth - 1, last, unroll)


def slab_kernel(b, k, up_out, down_out):
    rows = k.shape[1]
    for r in range(K0):
        up_out[r] = k[:, rows - K0 + r, :]
        down_out[r] = k[:, r, :]
    for r in range(B0):
        up_out[K0 + r] = b[:, rows - B0 + r, :]
        down_out[K0 + r] = b[:, r, :]


def widen(out, own, low, high, first, count, start):
    planes, rows, lanes = own.shape
    end = start + rows
    out[:, 0:start, :] = jnp.zeros((planes, start, lanes), F32)
    out[:, end:, :] = jnp.zeros((planes, out.shape[1] - end, lanes), F32)
    out[:, start:end, :] = own[...]
    below, above = inside("gy", -1), inside("gy", 1)
    for r in range(count):
        out[:, start - count + r, :] = masked(below, low(first, r))
        out[:, end + r, :] = masked(above, high(first, r))


def widen_kernel(b, k, low, high, k_out, b_out, up_out, down_out):
    widen(k_out, k, lambda f, r: low[f + r], lambda f, r: high[f + r], 0, K0, R0)
    widen(b_out, b, lambda f, r: low[f + r], lambda f, r: high[f + r], K0, B0, R0)
    planes = k.shape[0]
    up_out[0:K0] = k_out[planes - K0 :]
    up_out[K0:] = b_out[planes - B0 :]
    down_out[0:K0] = k_out[0:K0]
    down_out[K0:] = b_out[0:B0]


def join(out, own, low, high, first, count, halo):
    planes = own.shape[0]
    left, right = inside("gx", -1), inside("gx", 1)
    out[halo : halo + planes] = own[...]
    for r in range(halo):
        below, above = halo - 1 - r, halo + planes + r
        if r < count:
            out[below] = masked(left, low[first + count - 1 - r])
            out[above] = masked(right, high[first + r])
        else:
            out[below] = jnp.zeros_like(out[below])
            out[above] = jnp.zeros_like(out[above])


def fine_down_kernel(
    k_own, b_own, low, high,
    k, b, s_out, b1_out, k1_out, up_out, down_out,
    wl, ws, wz, total, inverse, first, second, pairs, halves,
):
    join(k, k_own, low, high, 0, K0, K0)
    join(b, b_own, low, high, K0, B0, K0)
    w = (wl, ws, wz)
    weigh(k, wl, ws, wz, total, inverse, False, True, 1)
    planes, rows, lanes = b.shape
    pre_smooth(b, first, second, w, inverse, 1.0, 1, 2)
    own = planes - 2 * K0
    half = own // 2

    def residual(i):
        return b[i] - total[i] * second[i] + beside(second, *w, i)

    def restrict(j):
        i = 2 * j + K0
        pairs[j] = residual(i) + residual(i + 1)
        pairs[half + j] = k[i] + k[i + 1]

    loop(0, half, restrict, 1)
    matrix = halving(lanes, lanes // 2, 0.125)
    halves[...] = pick(pairs[...].reshape(2 * half * rows, lanes), matrix).reshape(halves.shape)
    count = (rows - 2 * R0) // 2
    both = halves[:, pl.ds(R0, count, stride=2), :] + halves[:, pl.ds(R0 + 1, count, stride=2), :]
    b1_out[...] = both[:half]
    k1_out[...] = both[half:]
    s_out[...] = second[K0 : K0 + own, R0 : rows - R0, :]
    for out, k_from, b_from, s_from in (
        (up_out, count - K1, count - B1, 2 * count - S0),
        (down_out, 0, 0, 0),
    ):
        at = 0
        for r in range(K1):
            out[at : at + half] = k1_out[:, k_from + r, :]
            at += half
        for r in range(B1):
            out[at : at + half] = b1_out[:, b_from + r, :]
            at += half
        for r in range(S0):
            for h in range(2):
                out[at : at + own] = s_out[:, s_from + r, h * lanes // 2 : (h + 1) * lanes // 2]
                at += own


def widen_both_kernel(b1, k1, s, low, high, k_out, b_out, s_out, up_out, down_out):
    half, own, lanes = b1.shape[0], s.shape[0], b1.shape[2]

    def block(ref):
        return lambda first, r: ref[first + r * half : first + (r + 1) * half]

    def wide(ref):
        def get(first, r):
            at = first + 2 * r * own
            return jnp.concatenate([ref[at : at + own], ref[at + own : at + 2 * own]], axis=1)

        return get

    widen(k_out, k1, block(low), block(high), 0, K1, R1)
    widen(b_out, b1, block(low), block(high), K1 * half, B1, R1)
    widen(s_out, s, wide(low), wide(high), (K1 + B1) * half, S0, R0)
    for out, k_from, b_from, s_from in (
        (up_out, half - K1, half - B1, own - S0),
        (down_out, 0, 0, 0),
    ):
        out[0:K1] = k_out[k_from : k_from + K1]
        out[K1 : K1 + B1] = b_out[b_from : b_from + B1]
        for r in range(S0):
            for h in range(2):
                out[K1 + B1 + 2 * r + h] = s_out[s_from + r, :, h * lanes : (h + 1) * lanes]


def middle_down_kernel(
    k_own, b_own, low, high,
    k, b, second, out,
    wl, ws, wz, total, inverse, first, pairs, halves,
):
    scale = 0.25
    join(k, k_own, low, high, 0, K1, K1)
    join(b, b_own, low, high, K1, B1, K1)
    w = (wl, ws, wz)
    weigh(k, wl, ws, wz, total, inverse, False, True, 1)
    second[...] = jnp.zeros_like(second)
    pre_smooth(b, first, second, w, inverse, scale, 1, 2)
    planes, rows, lanes = b.shape
    half = (planes - 2 * K1) // 2

    def residual(i):
        return b[i] - scale * (total[i] * second[i] - beside(second, *w, i))

    def restrict(j):
        i = 2 * j + K1
        pairs[j] = residual(i) + residual(i + 1)
        pairs[half + j] = k[i] + k[i + 1]

    loop(0, half, restrict, 2)
    size = half * rows
    fields = pick(pairs[0:half].reshape(size, lanes), halving(lanes, lanes, 0.125))
    conducts = pick(pairs[half:].reshape(size, lanes), halving(lanes, lanes, 0.125, lanes // 2))
    halves[...] = (fields + conducts).reshape(halves.shape)
    count = (rows - 2 * R1) // 2
    both = halves[:, pl.ds(R1, count, stride=2), :] + halves[:, pl.ds(R1 + 1, count, stride=2), :]
    for i in range(half):
        out[0, pl.ds(i, count, stride=half), :] = both[i]

    def copy(d):
        out[d] = out[0]

    loop(1, out.shape[0], copy, 1)


def coarse_down(k, b, w, total, inverse, first, second, scale, valid, k_next, b_next):
    planes, rows, lanes = k.shape
    row_edge = True
    weigh(k, *w, total, inverse, row_edge, False, 2)
    for ref in (first, second):
        for end in (0, planes - 1):
            ref[end] = jnp.zeros((rows, lanes), F32)
    pre_smooth_whole(b, first, second, w, inverse, scale, 2)
    half = (planes - 2) // 2

    def residual(i):
        return b[i] - scale * (total[i] * second[i] - beside(second, *w, i))

    def restrict(j):
        i = 2 * j + 1
        first[j] = residual(i) + residual(i + 1)
        first[half + j] = k[i] + k[i + 1]

    loop(0, half, restrict, 2)
    size = 2 * half * rows
    matrix = halving(lanes, lanes, 0.125, 0, valid)
    pairs = first[0 : 2 * half].reshape(size, lanes)
    halves = total.at[0 : 2 * half]
    halves[...] = pick(pairs, matrix).reshape(halves.shape)
    count = rows // 2
    both = halves[:, pl.ds(0, count, stride=2), :] + halves[:, pl.ds(1, count, stride=2), :]
    b_next[1 : half + 1] = both[:half]
    k_next[1 : half + 1] = both[half:]
    for end in (0, half + 1):
        k_next[end] = jnp.zeros(k_next.shape[1:], F32)
        b_next[end] = jnp.zeros(b_next.shape[1:], F32)


def pre_smooth_whole(b, first, second, w, inverse, scale, unroll):
    planes = b.shape[0]

    def start(i):
        first[i] = b[i] * inverse[i] * (1.0 / (scale * THETA))

    loop(1, planes - 1, start, unroll)

    def sweep(i):
        near = beside(first, *w, i)
        second[i] = (1.0 + KEEP + GAIN * (THETA - 1.0)) * first[i] + GAIN * (inverse[i] * near)

    loop(1, planes - 1, sweep, unroll)


def coarse_up(correction, b, w, inverse, first, second, scale, valid, grown):
    planes, rows, lanes = b.shape
    half, count = correction.shape[0], correction.shape[1]
    wide = pick(correction.reshape(half * count, lanes), doubling(lanes, lanes, valid // 2))
    wide = wide.reshape(half, count, lanes)
    grown[:, pl.ds(0, count, stride=2), :] = wide
    grown[:, pl.ds(1, count, stride=2), :] = wide
    for end in (0, planes - 1):
        first[end] = jnp.zeros((rows, lanes), F32)

    def add(j):
        i = 2 * j + 1
        first[i] = second[i] + grown[j]
        first[i + 1] = second[i + 1] + grown[j]

    loop(0, half, add, 2)

    def sweep(i):
        x = first[i]
        near = beside(first, *w, i)
        second[i] = x + ((b[i] * (1.0 / scale) + near) * inverse[i] - x) * (1.0 / THETA)

    loop(1, planes - 1, sweep, 2)

    def last(i):
        x = second[i]
        near = beside(second, *w, i)
        step = KEEP * (x - first[i]) + GAIN * ((b[i] * (1.0 / scale) + near) * inverse[i] - x)
        first[i] = x + step

    loop(1, planes - 1, last, 2)


def bottom(k, b, scale):
    planes, rows, lanes = k.shape
    none = jnp.zeros((1, rows, lanes), F32)

    def after(v):
        return jnp.concatenate([v[1:], none], axis=0)

    def before(v):
        return jnp.concatenate([none, v[:-1]], axis=0)

    lead = face(k, after(k))
    lead_low = jnp.concatenate([k[:1], lead[:-1]], axis=0)
    row = iota(k.shape, 1)
    next_row = jnp.where(row == rows - 1, 0.0, up(k, 1))
    row_w = face(k, next_row)
    row_low = jnp.where(row == 0, k, down(row_w, 1))
    lane_w = face(k, up(k, 2))
    lane_low = down(lane_w, 2)
    whole = ((lead + lead_low) + (row_w + row_low)) + (lane_w + lane_low)
    inverse = jnp.where(k > 0.0, 1.0 / whole, 0.0)
    source = b * inverse * (1.0 / scale)
    lead_i, lead_low_i = lead * inverse, lead_low * inverse
    row_i = jnp.where(row == rows - 1, 0.0, row_w) * inverse
    row_low_i = jnp.where(row == 0, 0.0, row_low) * inverse
    lane_i, lane_low_i = lane_w * inverse, lane_low * inverse
    sigma = BOTTOM_THETA / BOTTOM_DELTA
    rho = 1.0 / sigma
    step = source * (1.0 / BOTTOM_THETA)
    x = step
    for _ in range(BOTTOM - 1):
        following = 1.0 / (2.0 * sigma - rho)
        near = (lead_i * after(x) + lead_low_i * before(x)) + (
            row_i * up(x, 1) + row_low_i * down(x, 1)
        )
        near = near + (lane_i * up(x, 2) + lane_low_i * down(x, 2))
        step = (following * rho) * step + (2.0 * following / BOTTOM_DELTA) * (source - x + near)
        x = x + step
        rho = following
    return x


def coarse_kernel(
    valid, received, region,
    k2, b2, wl2, ws2, wz2, total2, inverse2, first2, second2,
    k3, b3, wl3, ws3, wz3, total3, inverse3, first3, second3,
    k4, b4, grown2, grown3,
):
    planes, rows, lanes = k2.shape
    across, along = lax.axis_size("gx"), lax.axis_size("gy")
    block_x, block_y = rows // across, (planes - 2) // along
    lane = iota((block_x, lanes), 1)
    zero = jnp.zeros((rows, lanes), F32)
    for end in (0, planes - 1):
        k2[end] = zero
        b2[end] = zero

    def place(column):
        for row in range(across):
            for j in range(block_y):
                piece = received[row * along + column, j * block_x : (j + 1) * block_x, :]
                field = jnp.where(lane < valid, piece, 0.0)
                conduct = jnp.where(lane < valid, pltpu.roll(piece, lanes - valid, 1), 0.0)
                b2[1 + column * block_y + j, row * block_x : (row + 1) * block_x, :] = field
                k2[1 + column * block_y + j, row * block_x : (row + 1) * block_x, :] = conduct

    loop(0, along, place, 1)
    w2, w3 = (wl2, ws2, wz2), (wl3, ws3, wz3)
    coarse_down(
        k2, b2, w2, total2, inverse2, first2, second2, 0.25**2, valid, k3, b3
    )
    coarse_down(
        k3, b3, w3, total3, inverse3, first3, second3, 0.25**3, valid // 2, k4, b4
    )
    own4 = k4.shape[0] - 2
    x4 = bottom(k4[1 : own4 + 1], b4[1 : own4 + 1], 0.25**4)

    coarse_up(x4, b3, w3, inverse3, first3, second3, 0.25**3, valid // 2, grown3)
    own3 = k3.shape[0] - 2
    coarse_up(
        first3[1 : own3 + 1], b2, w2, inverse2, first2, second2, 0.25**2, valid, grown2
    )
    column, row = lax.axis_index("gy"), lax.axis_index("gx")
    margin = (region.shape[0] - block_y) // 2
    for q in range(region.shape[0]):
        plane = column * block_y + q - margin
        for side in range(3):
            block = row + side - 1
            there = (plane >= 0) & (plane < planes - 2) & (block >= 0) & (block < across)
            start = pl.multiple_of(jnp.clip(block, 0, across - 1) * block_x, block_x)
            value = first2[1 + jnp.clip(plane, 0, planes - 3), pl.ds(start, block_x), :]
            region[q, side * block_x : (side + 1) * block_x, :] = masked(there, value)


def fine_up_kernel(
    valid, region, k1, b1, s1, k, b, s_own, low, high,
    field_out, residual_out,
    wl1, ws1, wz1, total1, inverse1, first1, second1, grown,
    s, wl, ws, wz, total, inverse, second, tall,
):
    planes1, rows1, lanes1 = k1.shape
    planes, rows, lanes = k.shape
    weigh(k1, wl1, ws1, wz1, total1, inverse1, False, True, 1)
    weigh(k, wl, ws, wz, total, inverse, False, True, 1)
    w1, w = (wl1, ws1, wz1), (wl, ws, wz)
    count_y, count_x = region.shape[0], region.shape[1]
    block_x = count_x // 3
    wide = pick(region[...].reshape(count_y * count_x, lanes1), doubling(lanes1, lanes1, valid))
    wide = wide.reshape(count_y, count_x, lanes1)
    margin = 2
    grown[...] = jnp.zeros_like(grown)
    for q in range(block_x + 2 * margin):
        line = wide[:, block_x - margin + q, :]
        at = R1 - 2 * margin
        grown[q, pl.ds(at, count_y, stride=2), :] = line
        grown[q, pl.ds(at + 1, count_y, stride=2), :] = line
    begin = K1 - 2 * margin
    first1[...] = s1[...]

    def add1(q):
        for side in range(2):
            first1[begin + 2 * q + side] = first1[begin + 2 * q + side] + grown[q]

    loop(0, block_x + 2 * margin, add1, 1)
    depth = K1 - 3

    def store1(i, value):
        first1[i] = value

    post_smooth(b1, first1, second1, w1, inverse1, 0.25, depth, 2, store1)
    join(s, s_own, low, high, 0, S0, S0)
    own1 = planes1 - 2 * K1
    count = own1 + 4
    begin = K1 - 2
    part = (rows - 2 * R0) // 2 + 4
    source = first1[begin : begin + count, R1 - 2 : R1 - 2 + part, :]
    tall[:, pl.ds(0, part, stride=2), :] = source
    tall[:, pl.ds(1, part, stride=2), :] = source
    matrix = doubling(lanes1, lanes, lanes1)

    def add(q):
        grown_plane = pick(tall[q], matrix)
        for side in range(2):
            i = 2 * q + side - 1

            @pl.when((i >= 0) & (i < planes))
            def _():
                s[i] = s[i] + grown_plane

    loop(0, count, add, 1)

    def store(i, value):
        s[i] = value

    post_smooth(b, s, second, w, inverse, 1.0, 1, 2, store)
    own = planes - 2 * K0

    def finish(j):
        i = j + K0
        x = s[i]
        rest = b[i] - total[i] * x + beside(s, *w, i)
        field_out[j] = x[R0 : rows - R0, :]
        residual_out[j] = rest[R0 : rows - R0, :]

    loop(0, own, finish, 2)


def call(kernel, outs, scratch=()):
    def run(*operands):
        shapes = [operand.shape for operand in operands] + list(outs) + list(scratch)
        words = sum(math.prod(s[:-2]) * (-(-s[-2] // 8) * 8) * s[-1] for s in shapes)
        return pl.pallas_call(
            kernel,
            out_shape=[jax.ShapeDtypeStruct(shape, F32) for shape in outs],
            scratch_shapes=[pltpu.VMEM(shape, F32) for shape in scratch],
            compiler_params=pltpu.CompilerParams(vmem_limit_bytes=4 * words + SPARE),
        )(*operands)

    return run


def per_device(right_side, coefficient):
    bx, by, nz = right_side.shape
    across, along = lax.axis_size("gx"), lax.axis_size("gy")
    devices = across * along
    hx, hy, hz = bx // 2, by // 2, nz // 2
    tall, tall1 = by + 2 * R0, hy + 2 * R1

    slab = (K0 + B0, bx, nz)
    up_rows, down_rows = call(slab_kernel, [slab, slab])(right_side, coefficient)
    low, high = rotate(up_rows, "gy", 1), rotate(down_rows, "gy", -1)

    plane = (bx, tall, nz)
    slab = (K0 + B0, tall, nz)
    k_own, b_own, up_planes, down_planes = call(widen_kernel, [plane, plane, slab, slab])(
        right_side, coefficient, low, high
    )
    low, high = rotate(up_planes, "gx", 1), rotate(down_planes, "gx", -1)

    block = (bx + 2 * K0, tall, nz)
    level1 = (hx, hy, hz)
    message = ((K1 + B1) * hx + S0 * 2 * bx, hz)
    k, b, s, b1, k1, up_rows, down_rows = call(
        fine_down_kernel,
        [block, block, (bx, by, nz), level1, level1, message, message],
        [block] * 7 + [(bx, tall, nz), (bx, tall, hz)],
    )(k_own, b_own, low, high)
    low, high = rotate(up_rows, "gy", 1), rotate(down_rows, "gy", -1)

    message = (K1 + B1 + 2 * S0, tall1, hz)
    k1_own, b1_own, s_own, up_planes, down_planes = call(
        widen_both_kernel,
        [(hx, tall1, hz), (hx, tall1, hz), plane, message, message],
    )(b1, k1, s, low, high)
    low, high = rotate(up_planes, "gx", 1), rotate(down_planes, "gx", -1)

    block1 = (hx + 2 * K1, tall1, hz)
    piece = (hx // 2) * (hy // 2)
    k1, b1, s1, copies = call(
        middle_down_kernel,
        [block1, block1, block1, (devices, piece, hz)],
        [block1] * 6 + [(hx, tall1, hz), (hx // 2, tall1, hz)],
    )(k1_own, b1_own, low, high)
    received = lax.all_to_all(copies, ("gx", "gy"), 0, 0, tiled=True)

    x2, y2 = across * hx // 2, along * hy // 2
    level2, level3, level4 = (
        (y2 // s + 2, x2 // s, hz) for s in (1, 2, 4)
    )
    margin = 2
    (region,) = call(
        partial(coarse_kernel, nz // 4),
        [(hy // 2 + 2 * margin, 3 * hx // 2, hz)],
        [level2] * 9 + [level3] * 9 + [level4] * 2 + [(y2 // 2, x2, hz), (y2 // 4, x2 // 2, hz)],
    )(received)
    s_low, s_high = spread(low, K1 + B1, tall), spread(high, K1 + B1, tall)
    field, residual = call(
        partial(fine_up_kernel, nz // 4),
        [(bx, by, nz)] * 2,
        [block1] * 7 + [(hx // 2 + 2 * margin, tall1, hz)] + [block] * 7
        + [(hx + 4, tall, hz)],
    )(region, k1, b1, s1, k, b, s_own, s_low, s_high)
    return field, residual


def spread(message, first, rows):
    parts = message[first:, :rows]
    return jnp.concatenate([parts[0::2], parts[1::2]], axis=2)


def solution(mesh):
    in_specs = (P("gx", "gy", None), P("gx", "gy", None))
    out_specs = (P("gx", "gy", None), P("gx", "gy", None))

    return jax.shard_map(
        per_device, mesh=mesh, in_specs=in_specs, out_specs=out_specs, check_vma=False
    )
```

time: 570 us -> 118 us (0.21)
  starting transfers between devices: 205 us -> 19.1 us
  local copies, waits for them, and re-layouts: 149 us -> 8.19 us
  other arithmetic: 72 us -> 1.27 us
  Pallas kernels: 0 us -> 53.6 us
  blocking collectives: 52.3 us -> 0 us
  waiting for transfers between devices: 84.2 us -> 35.1 us
    ppermute x84 -> x8, starting transfers between devices: 205 us -> 14.5 us  [rotate(): lax.ppermute(value, axis, [(i, (i + shift) % size) for i in range(size)])]
    reshape x7 -> x0, local copies, waits for them, and re-layouts: 109 us -> none  [the longest x4 78.8 us: restrict(): field.reshape(size_x // 2, 2, size_y // 2, 2, size_z // 2, 2)]
    ppermute x84 -> x8, waiting for transfers between devices: 84.2 us -> 21.2 us  [rotate(): lax.ppermute(value, axis, [(i, (i + shift) % size) for i in range(size)])]
    pallas_call x0 -> x7, Pallas kernels: none -> 53.6 us  [run(): pl.pallas_call(kernel, out_shape=[jax.ShapeDtypeStruct(shape, F32) for sh...]
    all_gather x4 -> x0, blocking collectives: 52.3 us -> none  [the longest x1 21.5 us: collect(): lax.all_gather(conduct, 'gy', axis=1, tiled=True)]
    reduce_sum x10 -> x0, other arithmetic: 36.9 us -> none  [restrict(): jnp.mean(field.reshape(size_x // 2, 2, size_y // 2, 2, size_z // 2, 2), a...]
    broadcast_in_dim x5 -> x0, local copies, waits for them, and re-layouts: 15.1 us -> none  [prolong(): jnp.broadcast_to(field[:, None, :, None, :, None], (size_x, 2, size_y, 2,...]
    add x24 -> x0, other arithmetic: 14.9 us -> none  [the longest x15 7.74 us: chebyshev(): iterate = iterate + update]
  transfers between devices with their start and end apart: 84 -> 9, of which waited for: 32 -> 9; matrix products, arithmetic and copies ran while one was open for 26% -> 1% of each run, Pallas kernels for 0% -> 0%
where the time goes in v1:
time: 118 us
  Pallas kernels  53.6 us (45%)
  waiting for transfers between devices  35.1 us (30%)
  starting transfers between devices  19.1 us (16%)
  local copies, waits for them, and re-layouts  8.19 us (7%)
  other arithmetic  1.27 us (1%)
    pallas_call x7, Pallas kernels, run(): pl.pallas_call(kernel, out_shape=[jax.ShapeDtypeStruct(shape, F32) for sh...  53.6 us
    ppermute x8, waiting for transfers between devices, rotate(): lax.ppermute(value, axis, [(i, (i + shift) % size) for i in range(size)])  21.2 us
    ppermute x8, starting transfers between devices, rotate(): lax.ppermute(value, axis, [(i, (i + shift) % size) for i in range(size)])  14.5 us
    all_to_all x1, waiting for transfers between devices, per_device(): received = lax.all_to_all(copies, ('gx', 'gy'), 0, 0, tiled=True)  13.9 us
    unnamed x30, local copies, waits for them, and re-layouts  7.04 us
    all_to_all x1, starting transfers between devices, per_device(): received = lax.all_to_all(copies, ('gx', 'gy'), 0, 0, tiled=True)  4.61 us
  transfers between devices with their start and end apart: 9, of which 9 were waited for; matrix products, arithmetic and copies ran while one was open for 1% of the time, Pallas kernels for 0%

profile of v1, /device:TPU:0, one launch (start us, length us, event | category | flops | bytes accessed | tf_op | source)
XLA Modules:
  0.0 118.0 jit_solution(18150289904470682570)
XLA Ops:
  0.6 0.0 copy-start
  0.6 1.0 copy-done
  1.7 1.0 copy-done.2
  2.7 0.1 shard_map.41
  2.8 3.0 %collective-permute-start = (f32[5,32,256]{2,1,0:T(8,128)S(1)}, f32[5,32,256]{2,1,0:T(8,128)S(1)}, u32[]{:S(2)}, u32[]{:S(2)}) collective-permute-start(f32[5,32,256]{2,1,0:T(8,128)S(1)} %get-tuple-element.24), channel_id=1, source_target_pairs={{0,1},{1,2},{2,3},{3,4},{4,5},{5,6},{6,7},{7,0},{8,9},{9,10},{10,1... | collective-permute-start | bytes 491528 | tf_op jit(solution)/shard_map/ppermute | solution.py:33
  5.8 3.1 %collective-permute-start.1 = (f32[5,32,256]{2,1,0:T(8,128)S(1)}, f32[5,32,256]{2,1,0:T(8,128)S(1)}, u32[]{:S(2)}, u32[]{:S(2)}) collective-permute-start(f32[5,32,256]{2,1,0:T(8,128)S(1)} %get-tuple-element.25), channel_id=1, source_target_pairs={{0,7},{1,0},{2,1},{3,2},{4,3},{5,4},{6,5},{7,6},{8,15},{9,8},{10,9... | collective-permute-start | bytes 491528 | tf_op jit(solution)/shard_map/ppermute | solution.py:33
  8.9 4.2 %collective-permute-done.low = f32[5,32,256]{2,1,0:T(8,128)S(1)} collective-permute-done((f32[5,32,256]{2,1,0:T(8,128)S(1)}, f32[5,32,256]{2,1,0:T(8,128)S(1)}, u32[]{:S(2)}, u32[]{:S(2)}) %collective-permute-start) | collective-permute-done | bytes 163872 | tf_op jit(solution)/shard_map/ppermute | solution.py:33
  13.2 1.8 %collective-permute-done.1.high = f32[5,32,256]{2,1,0:T(8,128)S(1)} collective-permute-done((f32[5,32,256]{2,1,0:T(8,128)S(1)}, f32[5,32,256]{2,1,0:T(8,128)S(1)}, u32[]{:S(2)}, u32[]{:S(2)}) %collective-permute-start.1) | collective-permute-done | bytes 163872 | tf_op jit(solution)/shard_map/ppermute | solution.py:33
  15.0 0.0 copy-done.1
  15.0 0.0 copy-done.3
  15.0 0.3 shard_map.42
  15.3 0.1 collective-permute-start.2
  15.4 1.7 %collective-permute-start.3 = (f32[5,24,256]{2,1,0:T(8,128)S(1)}, f32[5,24,256]{2,1,0:T(8,128)S(1)}, u32[]{:S(2)}, u32[]{:S(2)}) collective-permute-start(f32[5,24,256]{2,1,0:T(8,128)S(1)} %get-tuple-element.29), channel_id=1, source_target_pairs={{0,24},{8,0},{16,8},{24,16},{1,25},{9,1},{17,9},{25,17},{2,26},{10... | collective-permute-start | bytes 368648 | tf_op jit(solution)/shard_map/ppermute | solution.py:33
  17.1 2.6 %collective-permute-done.2.low = f32[5,24,256]{2,1,0:T(8,128)S(1)} collective-permute-done((f32[5,24,256]{2,1,0:T(8,128)S(1)}, f32[5,24,256]{2,1,0:T(8,128)S(1)}, u32[]{:S(2)}, u32[]{:S(2)}) %collective-permute-start.2) | collective-permute-done | bytes 122912 | tf_op jit(solution)/shard_map/ppermute | solution.py:33
  19.7 0.4 collective-permute-done.3.high
  20.0 10.3 %shard_map.43 = (f32[38,24,256]{2,1,0:T(8,128)S(1)}, f32[38,24,256]{2,1,0:T(8,128)S(1)}, f32[32,16,256]{2,1,0:T(8,128)S(1)}, f32[16,8,128]{2,1,0:T(8,128)S(1)}, ...) custom-call(f32[32,24,256]{2,1,0:T(8,128)S(1)} %get-tuple-element.26.k_own, ...), custom_call_target="tpu_custom_call" | custom-call | tf_op jit(solution)/shard_map/pallas_call | solution.py:578
  30.4 0.3 collective-permute-start.4
  30.7 4.4 %collective-permute-start.5 = (f32[368,128]{1,0:T(8,128)S(1)}, f32[368,128]{1,0:T(8,128)S(1)}, u32[]{:S(2)}, u32[]{:S(2)}) collective-permute-start(f32[368,128]{1,0:T(8,128)S(1)} %get-tuple-element.34), channel_id=1, source_target_pairs={{0,7},{1,0},{2,1},{3,2},{4,3},{5,4},{6,5},{7,6},{8,15},{9,8},{10,9... | collective-permute-start | bytes 565256 | tf_op jit(solution)/shard_map/ppermute | solution.py:33
  35.1 5.4 %collective-permute-done.4.low = f32[368,128]{1,0:T(8,128)S(1)} collective-permute-done((f32[368,128]{1,0:T(8,128)S(1)}, f32[368,128]{1,0:T(8,128)S(1)}, u32[]{:S(2)}, u32[]{:S(2)}) %collective-permute-start.4) | collective-permute-done | bytes 188448 | tf_op jit(solution)/shard_map/ppermute | solution.py:33
  40.5 1.9 %collective-permute-done.5.high = f32[368,128]{1,0:T(8,128)S(1)} collective-permute-done((f32[368,128]{1,0:T(8,128)S(1)}, f32[368,128]{1,0:T(8,128)S(1)}, u32[]{:S(2)}, u32[]{:S(2)}) %collective-permute-start.5) | collective-permute-done | bytes 188448 | tf_op jit(solution)/shard_map/ppermute | solution.py:33
  42.4 0.3 shard_map.44
  42.8 0.2 collective-permute-start.6
  42.9 1.6 %collective-permute-start.7 = (f32[17,24,128]{2,1,0:T(8,128)S(1)}, f32[17,24,128]{2,1,0:T(8,128)S(1)}, u32[]{:S(2)}, u32[]{:S(2)}) collective-permute-start(f32[17,24,128]{2,1,0:T(8,128)S(1)} %get-tuple-element.38), channel_id=1, source_target_pairs={{0,24},{8,0},{16,8},{24,16},{1,25},{9,1},{17,9},{25,17},{2,26},{10... | collective-permute-start | bytes 626696 | tf_op jit(solution)/shard_map/ppermute | solution.py:33
  44.5 3.7 %collective-permute-done.6.low = f32[17,24,128]{2,1,0:T(8,128)S(1)} collective-permute-done((f32[17,24,128]{2,1,0:T(8,128)S(1)}, f32[17,24,128]{2,1,0:T(8,128)S(1)}, u32[]{:S(2)}, u32[]{:S(2)}) %collective-permute-start.6) | collective-permute-done | bytes 208928 | tf_op jit(solution)/shard_map/ppermute | solution.py:33
  48.3 1.2 collective-permute-done.7.high
  49.4 6.3 %shard_map.45 = (f32[28,24,128]{2,1,0:T(8,128)S(1)}, f32[28,24,128]{2,1,0:T(8,128)S(1)}, f32[28,24,128]{2,1,0:T(8,128)S(1)}, f32[32,32,128]{2,1,0:T(8,128)S(1)}) custom-call(f32[16,24,128]{2,1,0:T(8,128)S(1)} %get-tuple-element.35.k_own, f32[16,24,128]{2,1,0:T(8,128)S(1)} %get-tuple-element.36.b_own, f32[17,24,128]{2,1,0:T(8,128)S(1)} %collective-permute-done.6.low, ...), custom_call_target="tpu_custom_call" | custom-call | tf_op jit(solution)/shard_map/pallas_call | solution.py:578
  55.7 0.0 copy-done.6
  55.7 0.0 copy-start.4
  55.7 0.8 copy-done.4
  56.5 0.7 copy-done.7
  57.3 0.7 copy-done.9
  58.0 0.7 copy-done.11
  58.7 4.6 %all-to-all-start = ((f32[32,32,128]{2,1,0:T(8,128)}), f32[32,32,128]{2,1,0:T(8,128)S(1)}, u32[]{:S(2)}, u32[]{:S(2)}) async-start(f32[32,32,128]{2,1,0:T(8,128)} %copy-done.4), calls=%async_computation | async-start | bytes 1048576 | tf_op jit(solution)/shard_map/all_to_all | solution.py:630
  63.3 0.0 copy-done.5
  63.4 0.0 slice-start
  63.4 0.9 slice-done
  64.2 0.6 pad_maximum_fusion.low
  64.9 0.3 slice-done.1
  65.2 0.6 pad_maximum_fusion.1.high
  65.8 13.9 %all-to-all-done.received = f32[32,32,128]{2,1,0:T(8,128)S(1)} async-done(((f32[32,32,128]{2,1,0:T(8,128)}), f32[32,32,128]{2,1,0:T(8,128)S(1)}, u32[]{:S(2)}, u32[]{:S(2)}) %all-to-all-start) | async-done | bytes 524320 | tf_op jit(solution)/shard_map/all_to_all | solution.py:630
  79.7 14.5 %shard_map.46.region = f32[8,24,128]{2,1,0:T(8,128)S(1)} custom-call(f32[32,32,128]{2,1,0:T(8,128)S(1)} %all-to-all-done.received), custom_call_target="tpu_custom_call" | custom-call | tf_op jit(solution)/shard_map/pallas_call | solution.py:578
  94.2 0.0 copy-done.8
  94.2 0.0 copy-done.13
  94.2 0.0 copy-done.14
  94.2 0.0 copy-start.10
  94.2 1.0 copy-done.10
  95.2 1.0 copy-done.12
  96.2 21.8 %shard_map.47 = (f32[32,16,256]{2,1,0:T(8,128)}, f32[32,16,256]{2,1,0:T(8,128)}) custom-call(f32[8,24,128]{2,1,0:T(8,128)S(1)} %shard_map.46.region, f32[28,24,128]{2,1,0:T(8,128)S(1)} %copy-done.8, f32[28,24,128]{2,1,0:T(8,128)S(1)} %copy-done.10, f32[28,24,128]{2,1,0:T(8,128)S(1)} %copy-done.12, f32[38,24,256]{2,1,0:T(8,128)S(1)} %get-tuple-element.43.k, ...), custom_call_target="tpu_custom_call" | custom-call | tf_op jit(solution)/shard_map/pallas_call | solution.py:578
  (15 shorter events, 0.0 us)
Async XLA Ops:
  0.6 1.0 copy-start
  1.7 1.0 copy-start.2
  2.7 12.3 %copy-start.1 = (f32[32,16,256]{2,1,0:T(8,128)S(1)}, f32[32,16,256]{2,1,0:T(8,128)}, u32[]{:S(2)}) copy-start(f32[32,16,256]{2,1,0:T(8,128)} %b.3) | copy-start | bytes 1572868
  2.7 12.3 %copy-start.3 = (f32[32,16,256]{2,1,0:T(8,128)S(1)}, f32[32,16,256]{2,1,0:T(8,128)}, u32[]{:S(2)}) copy-start(f32[32,16,256]{2,1,0:T(8,128)} %k.3) | copy-start | bytes 1572868
  2.8 10.3 %collective-permute-start = (f32[5,32,256]{2,1,0:T(8,128)S(1)}, f32[5,32,256]{2,1,0:T(8,128)S(1)}, u32[]{:S(2)}, u32[]{:S(2)}) collective-permute-start(f32[5,32,256]{2,1,0:T(8,128)S(1)} %get-tuple-element.24), channel_id=1, source_target_pairs={{0,1},{1,2},{2,3},{3,4},{4,5},{5,6},{6,7},{7,0},{8,9},{9,10},{10,1... | collective-permute-start | bytes 491528 | tf_op jit(solution)/shard_map/ppermute | solution.py:33
  5.8 9.2 %collective-permute-start.1 = (f32[5,32,256]{2,1,0:T(8,128)S(1)}, f32[5,32,256]{2,1,0:T(8,128)S(1)}, u32[]{:S(2)}, u32[]{:S(2)}) collective-permute-start(f32[5,32,256]{2,1,0:T(8,128)S(1)} %get-tuple-element.25), channel_id=1, source_target_pairs={{0,7},{1,0},{2,1},{3,2},{4,3},{5,4},{6,5},{7,6},{8,15},{9,8},{10,9... | collective-permute-start | bytes 491528 | tf_op jit(solution)/shard_map/ppermute | solution.py:33
  15.3 4.4 %collective-permute-start.2 = (f32[5,24,256]{2,1,0:T(8,128)S(1)}, f32[5,24,256]{2,1,0:T(8,128)S(1)}, u32[]{:S(2)}, u32[]{:S(2)}) collective-permute-start(f32[5,24,256]{2,1,0:T(8,128)S(1)} %get-tuple-element.28), channel_id=1, source_target_pairs={{0,8},{8,16},{16,24},{24,0},{1,9},{9,17},{17,25},{25,1},{2,10},{10... | collective-permute-start | bytes 368648 | tf_op jit(solution)/shard_map/ppermute | solution.py:33
  15.4 4.6 %collective-permute-start.3 = (f32[5,24,256]{2,1,0:T(8,128)S(1)}, f32[5,24,256]{2,1,0:T(8,128)S(1)}, u32[]{:S(2)}, u32[]{:S(2)}) collective-permute-start(f32[5,24,256]{2,1,0:T(8,128)S(1)} %get-tuple-element.29), channel_id=1, source_target_pairs={{0,24},{8,0},{16,8},{24,16},{1,25},{9,1},{17,9},{25,17},{2,26},{10... | collective-permute-start | bytes 368648 | tf_op jit(solution)/shard_map/ppermute | solution.py:33
  30.4 10.1 %collective-permute-start.4 = (f32[368,128]{1,0:T(8,128)S(1)}, f32[368,128]{1,0:T(8,128)S(1)}, u32[]{:S(2)}, u32[]{:S(2)}) collective-permute-start(f32[368,128]{1,0:T(8,128)S(1)} %get-tuple-element.33), channel_id=1, source_target_pairs={{0,1},{1,2},{2,3},{3,4},{4,5},{5,6},{6,7},{7,0},{8,9},{9,10},{10,1... | collective-permute-start | bytes 565256 | tf_op jit(solution)/shard_map/ppermute | solution.py:33
  30.7 11.7 %collective-permute-start.5 = (f32[368,128]{1,0:T(8,128)S(1)}, f32[368,128]{1,0:T(8,128)S(1)}, u32[]{:S(2)}, u32[]{:S(2)}) collective-permute-start(f32[368,128]{1,0:T(8,128)S(1)} %get-tuple-element.34), channel_id=1, source_target_pairs={{0,7},{1,0},{2,1},{3,2},{4,3},{5,4},{6,5},{7,6},{8,15},{9,8},{10,9... | collective-permute-start | bytes 565256 | tf_op jit(solution)/shard_map/ppermute | solution.py:33
  42.8 5.5 %collective-permute-start.6 = (f32[17,24,128]{2,1,0:T(8,128)S(1)}, f32[17,24,128]{2,1,0:T(8,128)S(1)}, u32[]{:S(2)}, u32[]{:S(2)}) collective-permute-start(f32[17,24,128]{2,1,0:T(8,128)S(1)} %get-tuple-element.37), channel_id=1, source_target_pairs={{0,8},{8,16},{16,24},{24,0},{1,9},{9,17},{17,25},{25,1},{2,10},{10... | collective-permute-start | bytes 626696 | tf_op jit(solution)/shard_map/ppermute | solution.py:33
  42.9 6.5 %collective-permute-start.7 = (f32[17,24,128]{2,1,0:T(8,128)S(1)}, f32[17,24,128]{2,1,0:T(8,128)S(1)}, u32[]{:S(2)}, u32[]{:S(2)}) collective-permute-start(f32[17,24,128]{2,1,0:T(8,128)S(1)} %get-tuple-element.38), channel_id=1, source_target_pairs={{0,24},{8,0},{16,8},{24,16},{1,25},{9,1},{17,9},{25,17},{2,26},{10... | collective-permute-start | bytes 626696 | tf_op jit(solution)/shard_map/ppermute | solution.py:33
  48.3 15.1 %copy-start.5 = (f32[17,24,128]{2,1,0:T(8,128)}, f32[17,24,128]{2,1,0:T(8,128)S(1)}, u32[]{:S(2)}) copy-start(f32[17,24,128]{2,1,0:T(8,128)S(1)} %collective-permute-done.6.low) | copy-start | bytes 626692
  49.4 6.3 %copy-start.6 = (f32[17,24,128]{2,1,0:T(8,128)}, f32[17,24,128]{2,1,0:T(8,128)S(1)}, u32[]{:S(2)}) copy-start(f32[17,24,128]{2,1,0:T(8,128)S(1)} %collective-permute-done.7.high) | copy-start | bytes 626692
  55.7 0.8 copy-start.4
  56.5 0.7 copy-start.7
  57.2 0.7 copy-start.9
  58.0 0.7 copy-start.11
  58.7 21.0 %all-to-all-start = ((f32[32,32,128]{2,1,0:T(8,128)}), f32[32,32,128]{2,1,0:T(8,128)S(1)}, u32[]{:S(2)}, u32[]{:S(2)}) async-start(f32[32,32,128]{2,1,0:T(8,128)} %copy-done.4), calls=%async_computation | async-start | bytes 1048576 | tf_op jit(solution)/shard_map/all_to_all | solution.py:630
  63.4 0.9 slice-start
  64.2 0.9 slice-start.1
  65.8 28.4 %copy-start.8 = (f32[28,24,128]{2,1,0:T(8,128)S(1)}, f32[28,24,128]{2,1,0:T(8,128)}, u32[]{:S(2)}) copy-start(f32[28,24,128]{2,1,0:T(8,128)} %copy-done.7) | copy-start | bytes 1032196
  79.7 14.5 %copy-start.13 = (f32[3,24,256]{2,1,0:T(8,128)S(1)}, f32[3,24,256]{2,1,0:T(8,128)}, u32[]{:S(2)}) copy-start(f32[3,24,256]{2,1,0:T(8,128)} %pad_maximum_fusion.low) | copy-start | bytes 221188
  79.7 14.5 %copy-start.14 = (f32[3,24,256]{2,1,0:T(8,128)S(1)}, f32[3,24,256]{2,1,0:T(8,128)}, u32[]{:S(2)}) copy-start(f32[3,24,256]{2,1,0:T(8,128)} %pad_maximum_fusion.1.high) | copy-start | bytes 221188
  94.2 1.0 copy-start.10
  95.2 1.0 copy-start.12

commit v2 on v1

v2 whole, which is shorter than its diff:
```python
import math
from functools import partial

import jax
import jax.numpy as jnp
from jax import lax
from jax.experimental import pallas as pl
from jax.experimental.pallas import tpu as pltpu
from jax.sharding import PartitionSpec as P

F32 = jnp.float32
BF16 = jnp.bfloat16

THETA = 1.25
DELTA = 0.75
SIGMA = THETA / DELTA
RHO0 = 1.0 / SIGMA
RHO1 = 1.0 / (2.0 * SIGMA - RHO0)
KEEP = RHO1 * RHO0
GAIN = 2.0 * RHO1 / DELTA
BOTTOM = 8
BOTTOM_THETA = (2.0 + 0.05) / 2.0
BOTTOM_DELTA = (2.0 - 0.05) / 2.0

K0, B0, S0 = 3, 2, 3
K1, B1, S1 = 4, 3, 4
EDGE = 2
UNROLL = 8
SPARE = 4 * 1024 * 1024


def rotate(value, axis, shift):
    size = lax.axis_size(axis)
    return lax.ppermute(value, axis, [(i, (i + shift) % size) for i in range(size)])


def inside(axis, side):
    index = lax.axis_index(axis)
    if side < 0:
        return index > 0
    return index < lax.axis_size(axis) - 1


def masked(flag, value):
    return jnp.where(flag, value, jnp.zeros_like(value))


def iota(shape, dim):
    return lax.broadcasted_iota(jnp.int32, shape, dim)


def pick(x, matrix):
    high = x.astype(BF16)
    low = (x - high.astype(F32)).astype(BF16)
    return jnp.dot(high, matrix, preferred_element_type=F32) + jnp.dot(
        low, matrix, preferred_element_type=F32
    )


def halving(fine, coarse, valid):
    row, col = iota((fine, coarse), 0), iota((fine, coarse), 1)
    return jnp.where((row // 2 == col) & (row < valid), 0.125, 0.0).astype(BF16)


def doubling(coarse, fine, valid):
    row, col = iota((coarse, fine), 0), iota((coarse, fine), 1)
    return jnp.where((row == col // 2) & (row < valid), 1.0, 0.0).astype(BF16)


def face(a, b):
    product, total = a * b, a + b
    return jnp.where(product > 0.0, 2.0 * product / total, total)


def up(x, axis):
    return pltpu.roll(x, x.shape[axis] - 1, axis)


def down(x, axis):
    return pltpu.roll(x, 1, axis)


def sided(k, axis, edged):
    size = k.shape[axis]
    after = up(k, axis)
    place = iota(k.shape, axis)
    if edged:
        after = jnp.where(place == size - 1, 0.0, after)
    w = face(k, after)
    low = down(w, axis)
    if edged:
        low = jnp.where(place == 0, k, low)
        return jnp.where(place == size - 1, 0.0, w), w + low
    return w, w + low


def loop(low, high, body):
    def step(i, carry):
        body(i)
        return carry

    lax.fori_loop(low, high, step, 0, unroll=min(UNROLL, high - low))


def weigh(k, wl, ws, wz, total, inverse, row_edge, lane_edge):
    planes = k.shape[0]

    def body(i, before):
        here = k[i]
        lead = face(here, k[i + 1])
        rows, row_sum = sided(here, 0, row_edge)
        lanes, lane_sum = sided(here, 1, lane_edge)
        wl[i] = lead
        ws[i] = rows
        wz[i] = lanes
        whole = (before + lead) + (row_sum + lane_sum)
        total[i] = whole
        inverse[i] = jnp.where(here > 0.0, 1.0 / whole, 0.0)
        return lead

    lax.fori_loop(0, planes - 1, body, jnp.zeros(k.shape[1:], F32), unroll=UNROLL)


def beside(x, w, i):
    wl, ws, wz = w
    here = x[i]
    rows, lanes = ws[i], wz[i]
    out = wl[i] * x[i + 1] + wl[i - 1] * x[i - 1]
    out = out + (rows * up(here, 0) + down(rows * here, 0))
    return out + (lanes * up(here, 1) + down(lanes * here, 1))


def pre_smooth(b, first, second, w, inverse, scale, outer, inner):
    def start(i):
        first[i] = b[i] * inverse[i] * (1.0 / (scale * THETA))

    loop(*outer, start)

    def sweep(i):
        near = beside(first, w, i)
        second[i] = (1.0 + KEEP + GAIN * (THETA - 1.0)) * first[i] + GAIN * (inverse[i] * near)

    loop(*inner, sweep)


def post_smooth(b, first, second, w, inverse, scale, outer, inner):
    def sweep(i):
        x = first[i]
        near = beside(first, w, i)
        second[i] = x + ((b[i] * (1.0 / scale) + near) * inverse[i] - x) * (1.0 / THETA)

    loop(*outer, sweep)

    def last(i):
        x = second[i]
        near = beside(second, w, i)
        step = KEEP * (x - first[i]) + GAIN * ((b[i] * (1.0 / scale) + near) * inverse[i] - x)
        first[i] = x + step

    loop(*inner, last)


def residual(b, field, w, total, scale, i):
    return b[i] - scale * (total[i] * field[i] - beside(field, w, i))


def coarser(pairs, halves, valid):
    planes, rows, lanes = pairs.shape
    matrix = halving(lanes, halves.shape[2], valid)
    halves[...] = pick(pairs.reshape(planes * rows, lanes), matrix).reshape(halves.shape)
    count = rows // 2
    return halves[:, pl.ds(0, count, stride=2), :] + halves[:, pl.ds(1, count, stride=2), :]


def packed(pairs, halves, valid):
    planes, rows, lanes = pairs.shape
    matrix = halving(lanes, halves.shape[2], valid)
    halves[...] = pick(pairs.reshape(planes * rows, lanes), matrix).reshape(halves.shape)
    count = rows // 4
    quarter = [halves[:, pl.ds(r, count, stride=4), :] for r in range(4)]
    odd = pltpu.roll(quarter[2] + quarter[3], halves.shape[2] // 2, 2)
    return (quarter[0] + quarter[1]) + odd


def spread_copies(out, rows):
    size, count = rows.shape[0], rows.shape[1]
    for i in range(size):
        out[0, pl.ds(i, count, stride=size), :] = rows[i]

    def copy(d):
        out[d] = out[0]

    loop(1, out.shape[0], copy)


def slab_kernel(b, k, up_out, down_out):
    rows = k.shape[1]
    for r in range(K0):
        up_out[r] = k[:, rows - K0 + r, :]
        down_out[r] = k[:, r, :]
    for r in range(B0):
        up_out[K0 + r] = b[:, rows - B0 + r, :]
        down_out[K0 + r] = b[:, r, :]


def conduct_kernel(k, k1, copies, pairs, halves, pairs1, halves1):
    def add(j):
        pairs[j] = k[2 * j] + k[2 * j + 1]

    loop(0, pairs.shape[0], add)
    k1[...] = coarser(pairs[...], halves, k.shape[2])

    def add1(j):
        pairs1[j] = k1[2 * j] + k1[2 * j + 1]

    loop(0, pairs1.shape[0], add1)
    spread_copies(copies, packed(pairs1[...], halves1, k1.shape[2]))


def widen(out, own, low, high, count):
    planes, rows, lanes = own.shape
    size = out.shape[1]
    out[:, 0:rows, :] = own[...]
    out[:, rows:, :] = jnp.zeros((planes, size - rows, lanes), F32)
    below, above = inside("gy", -1), inside("gy", 1)
    for r in range(count):
        out[:, size - count + r, :] = masked(below, low(r))
        out[:, rows + r, :] = masked(above, high(r))


def widen_kernel(b, k, low, high, k_out, b_out, up_out, down_out):
    widen(k_out, k, lambda r: low[r], lambda r: high[r], K0)
    widen(b_out, b, lambda r: low[K0 + r], lambda r: high[K0 + r], B0)
    planes = k.shape[0]
    up_out[0:K0] = k_out[planes - K0 :]
    up_out[K0:] = b_out[planes - B0 :]
    down_out[0:K0] = k_out[0:K0]
    down_out[K0:] = b_out[0:B0]


def join(out, own, low, high, count, halo):
    planes = own.shape[0]
    left, right = inside("gx", -1), inside("gx", 1)
    out[halo : halo + planes] = own[...]
    for r in range(halo):
        below, above = halo - 1 - r, halo + planes + r
        if r < count:
            out[below] = masked(left, low(count - 1 - r))
            out[above] = masked(right, high(r))
        else:
            out[below] = jnp.zeros(out.shape[1:], F32)
            out[above] = jnp.zeros(out.shape[1:], F32)


def fine_down_kernel(
    k_own, b_own, low, high, k1,
    wl, ws, wz, total, inverse, b, s_out, b1_out, up_out, down_out,
    k, first, second, pairs, halves,
):
    join(k, k_own, lambda r: low[r], lambda r: high[r], K0, K0)
    join(b, b_own, lambda r: low[K0 + r], lambda r: high[K0 + r], B0, K0)
    w = (wl, ws, wz)
    weigh(k, wl, ws, wz, total, inverse, False, True)
    planes, lanes = b.shape[0], b.shape[2]
    own, rows = planes - 2 * K0, s_out.shape[1]
    pre_smooth(b, first, second, w, inverse, 1.0, (1, planes - 1), (2, planes - 2))

    def restrict(j):
        i = 2 * j + K0
        both = residual(b, second, w, total, 1.0, i) + residual(b, second, w, total, 1.0, i + 1)
        pairs[j] = both[0:rows]

    loop(0, own // 2, restrict)
    b1_out[...] = coarser(pairs[...], halves, lanes)
    s_out[...] = second[K0 : K0 + own, 0:rows, :]
    half, count = b1_out.shape[0], b1_out.shape[1]
    for out, k_from, b_from in ((up_out, count - K1, count - B1), (down_out, 0, 0)):
        for r in range(K1):
            out[r] = k1[:, k_from + r, :]
        for r in range(B1):
            out[K1 + r] = b1_out[:, b_from + r, :]


def widen_middle_kernel(k1, b1, low, high, k_out, b_out, up_out, down_out):
    widen(k_out, k1, lambda r: low[r], lambda r: high[r], K1)
    widen(b_out, b1, lambda r: low[K1 + r], lambda r: high[K1 + r], B1)
    planes = k1.shape[0]
    up_out[0:K1] = k_out[planes - K1 :]
    up_out[K1:] = b_out[planes - B1 :]
    down_out[0:K1] = k_out[0:K1]
    down_out[K1:] = b_out[0:B1]


def middle_down_kernel(
    k_own, b_own, low, high, s,
    wl, ws, wz, total, inverse, b, s_out, copies, up_out, down_out,
    k, first, second, pairs, halves,
):
    scale = 0.25
    join(k, k_own, lambda r: low[r], lambda r: high[r], K1, K1)
    join(b, b_own, lambda r: low[K1 + r], lambda r: high[K1 + r], B1, K1)
    w = (wl, ws, wz)
    weigh(k, wl, ws, wz, total, inverse, False, True)
    planes, lanes = b.shape[0], b.shape[2]
    own, rows = planes - 2 * K1, s_out.shape[1]
    pre_smooth(b, first, second, w, inverse, scale, (1, planes - 1), (2, planes - 2))

    def restrict(j):
        i = 2 * j + K1
        both = residual(b, second, w, total, scale, i) + residual(b, second, w, total, scale, i + 1)
        pairs[j] = both[0:rows]

    loop(0, own // 2, restrict)
    spread_copies(copies, packed(pairs[...], halves, lanes))
    s_out[...] = second[K1 : K1 + own, 0:rows, :]
    fine, fine_rows = s.shape[0], s.shape[1]
    for out, from0, from1 in ((up_out, fine_rows - S0, rows - S1), (down_out, 0, 0)):
        for r in range(S0):
            for h in range(2):
                at = (2 * r + h) * fine
                out[at : at + fine] = s[:, from0 + r, h * lanes : (h + 1) * lanes]
        for r in range(S1):
            at = 2 * S0 * fine + r * own
            out[at : at + own] = s_out[:, from1 + r, :]


def widen_fields_kernel(s, s1, low, high, s_out, s1_out, up_out, down_out):
    fine, own, lanes = s.shape[0], s1.shape[0], s1.shape[2]

    def wide(ref):
        def get(r):
            at = 2 * r * fine
            return jnp.concatenate([ref[at : at + fine], ref[at + fine : at + 2 * fine]], axis=1)

        return get

    def block(ref):
        def get(r):
            at = 2 * S0 * fine + r * own
            return ref[at : at + own]

        return get

    widen(s_out, s, wide(low), wide(high), S0)
    widen(s1_out, s1, block(low), block(high), S1)
    rows, rows1 = s_out.shape[1], s1_out.shape[1]
    for out, from0, from1 in ((up_out, fine - S0, own - S1), (down_out, 0, 0)):
        for r in range(S0):
            for h in range(2):
                at = (2 * r + h) * rows
                out[at : at + rows] = s_out[from0 + r, :, h * lanes : (h + 1) * lanes]
        for r in range(S1):
            at = 2 * S0 * rows + r * rows1
            out[at : at + rows1] = s1_out[from1 + r]


def unpack(received, out, block_x, block_y, across, along):
    planes, rows, lanes = out.shape
    lane = iota((block_x, lanes), 1)
    for end in (0, planes - 1):
        out[end] = jnp.zeros((rows, lanes), F32)

    def place(column):
        for row in range(across):
            for j in range(block_y // 2):
                piece = received[row * along + column, j * block_x : (j + 1) * block_x, :]
                at = 1 + column * block_y + 2 * j
                span = slice(row * block_x, (row + 1) * block_x)
                out[at, span, :] = jnp.where(lane < lanes // 2, piece, 0.0)
                other = pltpu.roll(piece, lanes // 2, 1)
                out[at + 1, span, :] = jnp.where(lane < lanes // 2, other, 0.0)

    loop(0, along, place)


def clear_ends(ref):
    for end in (0, ref.shape[0] - 1):
        ref[end] = jnp.zeros(ref.shape[1:], F32)


def coarse_weights_kernel(
    valid, received,
    wl2, ws2, wz2, total2, inverse2, wl3, ws3, wz3, total3, inverse3, k4,
    k2, k3, pairs2, halves2, pairs3, halves3,
):
    planes, rows, lanes = k2.shape
    across, along = lax.axis_size("gx"), lax.axis_size("gy")
    unpack(received, k2, rows // across, (planes - 2) // along, across, along)

    def add2(j):
        pairs2[j] = k2[2 * j + 1] + k2[2 * j + 2]

    loop(0, pairs2.shape[0], add2)
    clear_ends(k3)
    k3[1 : k3.shape[0] - 1] = coarser(pairs2[...], halves2, valid)

    def add3(j):
        pairs3[j] = k3[2 * j + 1] + k3[2 * j + 2]

    loop(0, pairs3.shape[0], add3)
    k4[...] = coarser(pairs3[...], halves3, valid // 2)
    weigh(k2, wl2, ws2, wz2, total2, inverse2, True, False)
    weigh(k3, wl3, ws3, wz3, total3, inverse3, True, False)


def coarse_down(b, w, total, inverse, first, second, scale, valid, pairs, halves):
    ends = (1, b.shape[0] - 1)
    clear_ends(first)
    clear_ends(second)
    pre_smooth(b, first, second, w, inverse, scale, ends, ends)

    def restrict(j):
        i = 2 * j + 1
        pairs[j] = residual(b, second, w, total, scale, i) + residual(
            b, second, w, total, scale, i + 1
        )

    loop(0, pairs.shape[0], restrict)
    return coarser(pairs[...], halves, valid)


def coarse_up(correction, b, w, inverse, first, second, scale, valid, grown):
    planes, rows, lanes = b.shape
    half, count = correction.shape[0], correction.shape[1]
    wide = pick(correction.reshape(half * count, lanes), doubling(lanes, lanes, valid // 2))
    wide = wide.reshape(half, count, lanes)
    grown[:, pl.ds(0, count, stride=2), :] = wide
    grown[:, pl.ds(1, count, stride=2), :] = wide

    def add(j):
        i = 2 * j + 1
        first[i] = second[i] + grown[j]
        first[i + 1] = second[i + 1] + grown[j]

    loop(0, half, add)
    ends = (1, planes - 1)
    post_smooth(b, first, second, w, inverse, scale, ends, ends)


def bottom(k, b, scale):
    planes, rows, lanes = k.shape
    none = jnp.zeros((1, rows, lanes), F32)

    def after(v):
        return jnp.concatenate([v[1:], none], axis=0)

    def before(v):
        return jnp.concatenate([none, v[:-1]], axis=0)

    lead = face(k, after(k))
    lead_low = jnp.concatenate([k[:1], lead[:-1]], axis=0)
    row = iota(k.shape, 1)
    row_w = face(k, jnp.where(row == rows - 1, 0.0, up(k, 1)))
    row_low = jnp.where(row == 0, k, down(row_w, 1))
    lane_w = face(k, up(k, 2))
    lane_low = down(lane_w, 2)
    whole = ((lead + lead_low) + (row_w + row_low)) + (lane_w + lane_low)
    inverse = jnp.where(k > 0.0, 1.0 / whole, 0.0)
    source = b * inverse * (1.0 / scale)
    lead_i, lead_low_i = lead * inverse, lead_low * inverse
    row_i = jnp.where(row == rows - 1, 0.0, row_w) * inverse
    row_low_i = jnp.where(row == 0, 0.0, row_low) * inverse
    lane_i, lane_low_i = lane_w * inverse, lane_low * inverse
    sigma = BOTTOM_THETA / BOTTOM_DELTA
    rho = 1.0 / sigma
    step = source * (1.0 / BOTTOM_THETA)
    x = step
    for _ in range(BOTTOM - 1):
        following = 1.0 / (2.0 * sigma - rho)
        near = (lead_i * after(x) + lead_low_i * before(x)) + (
            row_i * up(x, 1) + row_low_i * down(x, 1)
        )
        near = near + (lane_i * up(x, 2) + lane_low_i * down(x, 2))
        step = (following * rho) * step + (2.0 * following / BOTTOM_DELTA) * (source - x + near)
        x = x + step
        rho = following
    return x


def coarse_kernel(
    valid, received, wl2, ws2, wz2, total2, inverse2, wl3, ws3, wz3, total3, inverse3, k4,
    region,
    b2, first2, second2, pairs2, halves2, b3, first3, second3, pairs3, halves3, grown2, grown3,
):
    planes, rows, lanes = b2.shape
    across, along = lax.axis_size("gx"), lax.axis_size("gy")
    block_x, block_y = rows // across, (planes - 2) // along
    unpack(received, b2, block_x, block_y, across, along)
    w2, w3 = (wl2, ws2, wz2), (wl3, ws3, wz3)
    clear_ends(b3)
    own3 = b3.shape[0] - 2
    b3[1 : own3 + 1] = coarse_down(
        b2, w2, total2, inverse2, first2, second2, 0.25**2, valid, pairs2, halves2
    )
    b4 = coarse_down(
        b3, w3, total3, inverse3, first3, second3, 0.25**3, valid // 2, pairs3, halves3
    )
    x4 = bottom(k4[...], b4, 0.25**4)
    coarse_up(x4, b3, w3, inverse3, first3, second3, 0.25**3, valid // 2, grown3)
    coarse_up(
        first3[1 : own3 + 1], b2, w2, inverse2, first2, second2, 0.25**2, valid, grown2
    )
    column, row = lax.axis_index("gy"), lax.axis_index("gx")
    for q in range(region.shape[0]):
        plane = column * block_y + q - EDGE
        for side in range(3):
            block = row + side - 1
            there = (plane >= 0) & (plane < planes - 2) & (block >= 0) & (block < across)
            start = pl.multiple_of(jnp.clip(block, 0, across - 1) * block_x, block_x)
            value = first2[1 + jnp.clip(plane, 0, planes - 3), pl.ds(start, block_x), :]
            region[q, side * block_x : (side + 1) * block_x, :] = masked(there, value)


def fine_up_kernel(
    valid, region, wl1, ws1, wz1, inverse1, b1, s1_own,
    wl, ws, wz, total, inverse, b, s_own, low, high,
    field_out, residual_out,
    first1, second1, grown, s, second, tall, thick,
):
    planes1, rows1, lanes1 = b1.shape
    planes, rows, lanes = b.shape
    w1, w = (wl1, ws1, wz1), (wl, ws, wz)

    def wide(ref):
        def get(r):
            at = 2 * r * rows
            return jnp.concatenate([ref[at : at + rows], ref[at + rows : at + 2 * rows]], axis=1)

        return get

    def block(ref):
        def get(r):
            at = 2 * S0 * rows + r * rows1
            return ref[at : at + rows1]

        return get

    join(s, s_own, wide(low), wide(high), S0, S0)
    join(first1, s1_own, block(low), block(high), S1, S1)
    count_y, count_x = region.shape[0], region.shape[1]
    block_x = count_x // 3
    expanded = pick(region[...].reshape(count_y * count_x, lanes1), doubling(lanes1, lanes1, valid))
    expanded = expanded.reshape(count_y, count_x, lanes1)
    own_y = count_y - 2 * EDGE
    for q in range(block_x + 2 * EDGE):
        line = expanded[:, block_x - EDGE + q, :]
        line = jnp.concatenate([line[EDGE:], line[:EDGE]], axis=0)
        grown[q, pl.ds(0, count_y, stride=2), :] = line
        grown[q, pl.ds(1, count_y, stride=2), :] = line

    def add1(q):
        for side in range(2):
            first1[2 * q + side] = first1[2 * q + side] + grown[q]

    loop(0, block_x + 2 * EDGE, add1)
    post_smooth(
        b1, first1, second1, w1, inverse1, 0.25, (1, planes1 - 1), (2, planes1 - 2)
    )
    begin, count = S1 - EDGE, planes1 - 2 * S1 + 2 * EDGE
    own1 = rows1 - 2 * S1
    edge = 2 * EDGE
    for half, at, where in ((own1 + EDGE, 0, 0), (EDGE, rows1 - EDGE, 2 * (own1 + EDGE))):
        part = first1[begin : begin + count, at : at + half, :]
        tall[:, pl.ds(where, half, stride=2), :] = part
        tall[:, pl.ds(where + 1, half, stride=2), :] = part
    matrix = doubling(lanes1, lanes, lanes1)
    thick[...] = pick(tall[...].reshape(count * rows, lanes1), matrix).reshape(thick.shape)
    s[0] = s[0] + thick[0]
    s[planes - 1] = s[planes - 1] + thick[count - 1]

    def add(q):
        for side in range(2):
            i = 2 * q + side - 1
            s[i] = s[i] + thick[q]

    loop(1, count - 1, add)
    post_smooth(b, s, second, w, inverse, 1.0, (1, planes - 1), (2, planes - 2))
    own, own_rows = field_out.shape[0], field_out.shape[1]

    def finish(j):
        i = j + K0
        field_out[j] = s[i, 0:own_rows, :]
        residual_out[j] = residual(b, s, w, total, 1.0, i)[0:own_rows]

    loop(0, own, finish)


def call(kernel, outs, scratch=()):
    def run(*operands):
        shapes = [operand.shape for operand in operands] + list(outs) + list(scratch)
        words = sum(math.prod(s[:-2]) * (-(-s[-2] // 8) * 8) * s[-1] for s in shapes)
        return pl.pallas_call(
            kernel,
            out_shape=[jax.ShapeDtypeStruct(shape, F32) for shape in outs],
            scratch_shapes=[pltpu.VMEM(shape, F32) for shape in scratch],
            compiler_params=pltpu.CompilerParams(vmem_limit_bytes=4 * words + SPARE),
        )(*operands)

    return run


def eight(rows):
    return -(-rows // 8) * 8


def per_device(right_side, coefficient):
    bx, by, nz = right_side.shape
    across, along = lax.axis_size("gx"), lax.axis_size("gy")
    devices = across * along
    hx, hy, hz = bx // 2, by // 2, nz // 2
    qx, qy = hx // 2, hy // 2
    both = ("gx", "gy")
    tall, tall1 = eight(by + 2 * K0), eight(hy + 2 * K1)
    pieces = (devices, qx * qy // 2, hz)

    slab = (K0 + B0, bx, nz)
    up_rows, down_rows = call(slab_kernel, [slab, slab])(right_side, coefficient)
    low, high = rotate(up_rows, "gy", 1), rotate(down_rows, "gy", -1)
    k1, copies = call(
        conduct_kernel,
        [(hx, hy, hz), pieces],
        [(hx, by, nz), (hx, by, hz), (qx, hy, hz), (qx, hy, hz)],
    )(coefficient)
    k2 = lax.all_to_all(copies, both, 0, 0, tiled=True)

    plane = (bx, tall, nz)
    slab = (K0 + B0, tall, nz)
    k_own, b_own, up_planes, down_planes = call(widen_kernel, [plane, plane, slab, slab])(
        right_side, coefficient, low, high
    )
    low, high = rotate(up_planes, "gx", 1), rotate(down_planes, "gx", -1)

    block = (bx + 2 * K0, tall, nz)
    slab = (K1 + B1, hx, hz)
    *w0, b, s, b1, up_rows, down_rows = call(
        fine_down_kernel,
        [block] * 6 + [(bx, by, nz), (hx, hy, hz), slab, slab],
        [block] * 3 + [(hx, by, nz), (hx, by, hz)],
    )(k_own, b_own, low, high, k1)
    low, high = rotate(up_rows, "gy", 1), rotate(down_rows, "gy", -1)
    slab = (K1 + B1, tall1, hz)
    k1_own, b1_own, up_planes, down_planes = call(
        widen_middle_kernel, [(hx, tall1, hz), (hx, tall1, hz), slab, slab]
    )(k1, b1, low, high)
    low, high = rotate(up_planes, "gx", 1), rotate(down_planes, "gx", -1)

    block1 = (hx + 2 * K1, tall1, hz)
    slab = (2 * S0 * bx + S1 * hx, hz)
    *w1, b1, s1, copies, up_rows, down_rows = call(
        middle_down_kernel,
        [block1] * 6 + [(hx, hy, hz), pieces, slab, slab],
        [block1] * 3 + [(qx, hy, hz), (qx, hy, hz)],
    )(k1_own, b1_own, low, high, s)
    b2 = lax.all_to_all(copies, both, 0, 0, tiled=True)
    low, high = rotate(up_rows, "gy", 1), rotate(down_rows, "gy", -1)
    slab = (2 * S0 * tall + S1 * tall1, hz)
    s_own, s1_own, up_planes, down_planes = call(
        widen_fields_kernel, [plane, (hx, tall1, hz), slab, slab]
    )(s, s1, low, high)
    low, high = rotate(up_planes, "gx", 1), rotate(down_planes, "gx", -1)

    x2, y2 = across * qx, along * qy
    level2, level3, level4 = ((y2 // s + 2, x2 // s, hz) for s in (1, 2, 4))
    half2, half3 = (y2 // 2, x2, hz), (y2 // 4, x2 // 2, hz)
    valid = nz // 4
    weights = call(
        partial(coarse_weights_kernel, valid),
        [level2] * 5 + [level3] * 5 + [(y2 // 4, x2 // 4, hz)],
        [level2, level3, half2, half2, half3, half3],
    )(k2)
    (region,) = call(
        partial(coarse_kernel, valid),
        [(qy + 2 * EDGE, 3 * qx, hz)],
        [level2] * 3 + [half2] * 2 + [level3] * 3 + [half3] * 2 + [half2, half3],
    )(b2, *weights)

    wl1, ws1, wz1, _, inverse1 = w1
    count = hx + 2 * EDGE
    field, rest = call(
        partial(fine_up_kernel, valid),
        [(bx, by, nz)] * 2,
        [block1, block1, (qx + 2 * EDGE, tall1, hz), block, block, (count, tall, hz)]
        + [(count, tall, nz)],
    )(region, wl1, ws1, wz1, inverse1, b1, s1_own, *w0, b, s_own, low, high)
    return field, rest


def solution(mesh):
    in_specs = (P("gx", "gy", None), P("gx", "gy", None))
    out_specs = (P("gx", "gy", None), P("gx", "gy", None))
    return jax.shard_map(
        per_device, mesh=mesh, in_specs=in_specs, out_specs=out_specs, check_vma=False
    )
```

time: 118 us -> 106 us (0.90)
  Pallas kernels: 53.6 us -> 23.3 us
  local copies, waits for them, and re-layouts: 8.19 us -> 24.5 us
  starting transfers between devices: 19.1 us -> 33.4 us
  waiting for transfers between devices: 35.1 us -> 23.5 us
  other arithmetic: 1.27 us -> 0 us
    pallas_call x7 -> x10, Pallas kernels: 53.6 us -> 23.3 us  [run(): pl.pallas_call(kernel, out_shape=[jax.ShapeDtypeStruct(shape, F32) for sh...]
    unnamed x30 -> x72, local copies, waits for them, and re-layouts: 7.04 us -> 24.5 us
    all_to_all x1 -> x2, waiting for transfers between devices: 13.9 us -> 0.01 us  [the longest x1 0.01 us: per_device(): k2 = lax.all_to_all(copies, both, 0, 0, tiled=True)]
    all_to_all x1 -> x2, starting transfers between devices: 4.61 us -> 13.8 us  [the longest x1 7.3 us: per_device(): k2 = lax.all_to_all(copies, both, 0, 0, tiled=True)]
    ppermute x8 -> x12, starting transfers between devices: 14.5 us -> 19.6 us  [rotate(): lax.ppermute(value, axis, [(i, (i + shift) % size) for i in range(size)])]
    ppermute x8 -> x12, waiting for transfers between devices: 21.2 us -> 23.5 us  [rotate(): lax.ppermute(value, axis, [(i, (i + shift) % size) for i in range(size)])]
    concatenate x2 -> x0, other arithmetic: 1.27 us -> none  [spread(): return jnp.concatenate([parts[0::2], parts[1::2]], axis=2)]
  transfers between devices with their start and end apart: 9 -> 14, of which waited for: 9 -> 6; matrix products, arithmetic and copies ran while one was open for 1% -> 0% of each run, Pallas kernels for 0% -> 15%
where the time goes in v2:
time: 106 us
  starting transfers between devices  33.4 us (32%)
  local copies, waits for them, and re-layouts  24.5 us (23%)
  waiting for transfers between devices  23.5 us (22%)
  Pallas kernels  23.3 us (22%)
    unnamed x72, local copies, waits for them, and re-layouts  24.5 us
    ppermute x12, waiting for transfers between devices, rotate(): lax.ppermute(value, axis, [(i, (i + shift) % size) for i in range(size)])  23.5 us
    pallas_call x10, Pallas kernels, run(): pl.pallas_call(kernel, out_shape=[jax.ShapeDtypeStruct(shape, F32) for sh...  23.3 us
    ppermute x12, starting transfers between devices, rotate(): lax.ppermute(value, axis, [(i, (i + shift) % size) for i in range(size)])  19.6 us
    all_to_all x1, starting transfers between devices, per_device(): k2 = lax.all_to_all(copies, both, 0, 0, tiled=True)  7.3 us
    all_to_all x1, starting transfers between devices, per_device(): b2 = lax.all_to_all(copies, both, 0, 0, tiled=True)  6.54 us
  transfers between devices with their start and end apart: 14, of which 6 were waited for; matrix products, arithmetic and copies ran while one was open for 0% of the time, Pallas kernels for 15%

profile of v2, /device:TPU:0, one launch (start us, length us, event | category | flops | bytes accessed | tf_op | source)
XLA Modules:
  0.0 105.7 jit_solution(14683971594280469222)
XLA Ops:
  0.6 1.0 copy-done
  1.7 1.2 %shard_map.41 = (f32[16,8,128]{2,1,0:T(8,128)S(1)}, f32[32,16,128]{2,1,0:T(8,128)}) custom-call(f32[32,16,256]{2,1,0:T(8,128)S(1)} %copy-done), custom_call_target="tpu_custom_call" | custom-call | tf_op jit(solution)/shard_map/pallas_call | solution.py:592
  2.9 7.3 %all-to-all-start.1 = ((f32[32,16,128]{2,1,0:T(8,128)}), f32[32,16,128]{2,1,0:T(8,128)S(1)}, u32[]{:S(2)}, u32[]{:S(2)}) async-start(f32[32,16,128]{2,1,0:T(8,128)} %get-tuple-element.64), calls=%async_computation.1 | async-start | bytes 524288 | tf_op jit(solution)/shard_map/all_to_all | solution.py:624
  10.4 1.8 %collective-permute-start = (f32[5,32,256]{2,1,0:T(8,128)S(1)}, f32[5,32,256]{2,1,0:T(8,128)S(1)}, u32[]{:S(2)}, u32[]{:S(2)}) collective-permute-start(f32[5,32,256]{2,1,0:T(8,128)S(1)} %get-tuple-element.49), channel_id=1, source_target_pairs={{0,1},{1,2},{2,3},{3,4},{4,5},{5,6},{6,7},{7,0},{8,9},{9,10},{10,1... | collective-permute-start | bytes 491528 | tf_op jit(solution)/shard_map/ppermute | solution.py:34
  12.2 3.0 %collective-permute-start.1 = (f32[5,32,256]{2,1,0:T(8,128)S(1)}, f32[5,32,256]{2,1,0:T(8,128)S(1)}, u32[]{:S(2)}, u32[]{:S(2)}) collective-permute-start(f32[5,32,256]{2,1,0:T(8,128)S(1)} %get-tuple-element.50), channel_id=1, source_target_pairs={{0,7},{1,0},{2,1},{3,2},{4,3},{5,4},{6,5},{7,6},{8,15},{9,8},{10,9... | collective-permute-start | bytes 491528 | tf_op jit(solution)/shard_map/ppermute | solution.py:34
  15.1 8.4 %collective-permute-done.low = f32[5,32,256]{2,1,0:T(8,128)S(1)} collective-permute-done((f32[5,32,256]{2,1,0:T(8,128)S(1)}, f32[5,32,256]{2,1,0:T(8,128)S(1)}, u32[]{:S(2)}, u32[]{:S(2)}) %collective-permute-start) | collective-permute-done | bytes 163872 | tf_op jit(solution)/shard_map/ppermute | solution.py:34
  23.9 1.7 %collective-permute-start.3 = (f32[5,24,256]{2,1,0:T(8,128)S(1)}, f32[5,24,256]{2,1,0:T(8,128)S(1)}, u32[]{:S(2)}, u32[]{:S(2)}) collective-permute-start(f32[5,24,256]{2,1,0:T(8,128)S(1)} %get-tuple-element.54), channel_id=1, source_target_pairs={{0,24},{8,0},{16,8},{24,16},{1,25},{9,1},{17,9},{25,17},{2,26},{10... | collective-permute-start | bytes 368648 | tf_op jit(solution)/shard_map/ppermute | solution.py:34
  25.6 2.6 %collective-permute-done.2.low = f32[5,24,256]{2,1,0:T(8,128)S(1)} collective-permute-done((f32[5,24,256]{2,1,0:T(8,128)S(1)}, f32[5,24,256]{2,1,0:T(8,128)S(1)}, u32[]{:S(2)}, u32[]{:S(2)}) %collective-permute-start.2) | collective-permute-done | bytes 122912 | tf_op jit(solution)/shard_map/ppermute | solution.py:34
  28.5 4.0 %shard_map.44 = (f32[38,24,256]{2,1,0:T(8,128)S(1)}, f32[38,24,256]{2,1,0:T(8,128)S(1)}, f32[38,24,256]{2,1,0:T(8,128)S(1)}, f32[38,24,256]{2,1,0:T(8,128)S(1)},...) custom-call(f32[32,24,256]{2,1,0:T(8,128)S(1)} %get-tuple-element.51, ...), custom_call_target="tpu_custom_call" | custom-call | tf_op jit(solution)/shard_map/pallas_call | solution.py:592
  32.5 1.0 copy-done.3
  33.5 0.9 copy-done.5
  34.5 0.9 copy-done.7
  35.4 0.9 copy-done.9
  36.7 4.3 %collective-permute-start.5 = (f32[7,16,128]{2,1,0:T(8,128)S(1)}, f32[7,16,128]{2,1,0:T(8,128)S(1)}, u32[]{:S(2)}, u32[]{:S(2)}) collective-permute-start(f32[7,16,128]{2,1,0:T(8,128)S(1)} %get-tuple-element.57), channel_id=1, source_target_pairs={{0,7},{1,0},{2,1},{3,2},{4,3},{5,4},{6,5},{7,6},{8,15},{9,8},{10,9... | collective-permute-start | bytes 172040 | tf_op jit(solution)/shard_map/ppermute | solution.py:34
  41.0 2.5 %collective-permute-done.4.low = f32[7,16,128]{2,1,0:T(8,128)S(1)} collective-permute-done((f32[7,16,128]{2,1,0:T(8,128)S(1)}, f32[7,16,128]{2,1,0:T(8,128)S(1)}, u32[]{:S(2)}, u32[]{:S(2)}) %collective-permute-start.4) | collective-permute-done | bytes 57376 | tf_op jit(solution)/shard_map/ppermute | solution.py:34
  43.8 1.6 %collective-permute-start.7 = (f32[7,16,128]{2,1,0:T(8,128)S(1)}, f32[7,16,128]{2,1,0:T(8,128)S(1)}, u32[]{:S(2)}, u32[]{:S(2)}) collective-permute-start(f32[7,16,128]{2,1,0:T(8,128)S(1)} %get-tuple-element.61), channel_id=1, source_target_pairs={{0,24},{8,0},{16,8},{24,16},{1,25},{9,1},{17,9},{25,17},{2,26},{10... | collective-permute-start | bytes 172040 | tf_op jit(solution)/shard_map/ppermute | solution.py:34
  45.4 1.9 %collective-permute-done.6.low = f32[7,16,128]{2,1,0:T(8,128)S(1)} collective-permute-done((f32[7,16,128]{2,1,0:T(8,128)S(1)}, f32[7,16,128]{2,1,0:T(8,128)S(1)}, u32[]{:S(2)}, u32[]{:S(2)}) %collective-permute-start.6) | collective-permute-done | bytes 57376 | tf_op jit(solution)/shard_map/ppermute | solution.py:34
  47.3 3.3 %shard_map.46 = (f32[24,16,128]{2,1,0:T(8,128)S(1)}, f32[24,16,128]{2,1,0:T(8,128)S(1)}, f32[24,16,128]{2,1,0:T(8,128)S(1)}, f32[24,16,128]{2,1,0:T(8,128)}, f32...) custom-call(f32[16,16,128]{2,1,0:T(8,128)S(1)} %get-tuple-element.58, ...), custom_call_target="tpu_custom_call" | custom-call | tf_op jit(solution)/shard_map/pallas_call | solution.py:592
  50.6 0.7 copy-done.23
  51.3 0.7 copy-done.25
  52.0 0.7 copy-done.27
  53.3 6.5 %all-to-all-start = ((f32[32,16,128]{2,1,0:T(8,128)}), f32[32,16,128]{2,1,0:T(8,128)S(1)}, u32[]{:S(2)}, u32[]{:S(2)}) async-start(f32[32,16,128]{2,1,0:T(8,128)} %get-tuple-element.63), calls=%async_computation | async-start | bytes 524288 | tf_op jit(solution)/shard_map/all_to_all | solution.py:654
  59.9 1.8 %collective-permute-start.8 = (f32[256,128]{1,0:T(8,128)}, f32[256,128]{1,0:T(8,128)S(1)}, u32[]{:S(2)}, u32[]{:S(2)}) collective-permute-start(f32[256,128]{1,0:T(8,128)} %copy-done.35), channel_id=1, source_target_pairs={{0,1},{1,2},{2,3},{3,4},{4,5},{5,6},{6,7},{7,0},{8,9},{9,10},{10,1... | collective-permute-start | bytes 393224 | tf_op jit(solution)/shard_map/ppermute | solution.py:34
  61.7 3.0 %collective-permute-start.9 = (f32[256,128]{1,0:T(8,128)S(1)}, f32[256,128]{1,0:T(8,128)S(1)}, u32[]{:S(2)}, u32[]{:S(2)}) collective-permute-start(f32[256,128]{1,0:T(8,128)S(1)} %get-tuple-element.83), channel_id=1, source_target_pairs={{0,7},{1,0},{2,1},{3,2},{4,3},{5,4},{6,5},{7,6},{8,15},{9,8},{10,9... | collective-permute-start | bytes 393224 | tf_op jit(solution)/shard_map/ppermute | solution.py:34
  64.6 7.9 %collective-permute-done.8.low = f32[256,128]{1,0:T(8,128)S(1)} collective-permute-done((f32[256,128]{1,0:T(8,128)}, f32[256,128]{1,0:T(8,128)S(1)}, u32[]{:S(2)}, u32[]{:S(2)}) %collective-permute-start.8) | collective-permute-done | bytes 131104 | tf_op jit(solution)/shard_map/ppermute | solution.py:34
  72.5 0.9 shard_map.49
  73.4 0.9 copy-done.11
  74.3 0.7 copy-done.33
  75.0 1.7 %collective-permute-start.11 = (f32[208,128]{1,0:T(8,128)}, f32[208,128]{1,0:T(8,128)}, u32[]{:S(2)}, u32[]{:S(2)}) collective-permute-start(f32[208,128]{1,0:T(8,128)} %get-tuple-element.93), channel_id=1, source_target_pairs={{0,24},{8,0},{16,8},{24,16},{1,25},{9,1},{17,9},{25,17},{2,26},{10... | collective-permute-start | bytes 319496 | tf_op jit(solution)/shard_map/ppermute | solution.py:34
  76.7 2.1 %shard_map.47 = (f32[34,32,128]{2,1,0:T(8,128)S(1)}, f32[34,32,128]{2,1,0:T(8,128)S(1)}, f32[34,32,128]{2,1,0:T(8,128)S(1)}, f32[34,32,128]{2,1,0:T(8,128)S(1)},...) custom-call(f32[32,16,128]{2,1,0:T(8,128)S(1)} %all-to-all-done.1.re, ...), custom_call_target="tpu_custom_call" | custom-call | tf_op jit(solution)/shard_map/pallas_call | solution.py:592
  78.8 0.8 copy-done.13
  79.6 0.8 copy-done.15
  80.5 0.8 copy-done.17
  81.3 0.8 copy-done.19
  82.1 0.8 copy-done.21
  83.5 0.7 copy-done.31
  84.2 1.1 copy-done.14
  85.2 1.1 copy-done.16
  86.3 1.1 copy-done.18
  87.3 1.1 copy-done.20
  88.4 1.1 copy-done.22
  89.5 0.9 copy-done.30
  90.4 0.9 copy-done.32
  91.3 4.7 %shard_map.48.region = f32[8,24,128]{2,1,0:T(8,128)S(1)} custom-call(f32[32,16,128]{2,1,0:T(8,128)S(1)} %all-to-all-done.received, f32[34,32,128]{2,1,0:T(8,128)S(1)} %copy-done.14, f32[34,32,128]{2,1,0:T(8,128)S(1)} %copy-done.16, f32[34,32,128]{2,1,0:T(8,128)S(1)} %copy-done.18, f32[34,32,128]{2,1,0:T(8,128)S(1)} %copy-done.20, ...), custom_call_target="tpu_custom_call" | custom-call | tf_op jit(solution)/shard_map/pallas_call | solution.py:592
  96.1 1.1 %copy-done.12 = f32[32,24,256]{2,1,0:T(8,128)S(1)} copy-done((f32[32,24,256]{2,1,0:T(8,128)S(1)}, f32[32,24,256]{2,1,0:T(8,128)}, u32[]{:S(2)}) %copy-start.12) | copy-done | bytes 786456
  97.2 0.9 copy-done.28
  98.1 0.9 copy-done.34
  99.0 6.6 %shard_map.50 = (f32[32,16,256]{2,1,0:T(8,128)}, f32[32,16,256]{2,1,0:T(8,128)}) custom-call(f32[8,24,128]{2,1,0:T(8,128)S(1)} %shard_map.48.region, f32[24,16,128]{2,1,0:T(8,128)S(1)} %get-tuple-element.76.wl1, f32[24,16,128]{2,1,0:T(8,128)S(1)} %get-tuple-element.77.ws1, f32[24,16,128]{2,1,0:T(8,128)S(1)} %copy-done.24, f32[24,16,128]{2,1,0:T(8,128)S(1)} %copy-done.26, ...), custom_call_target="tpu_custom_call" | custom-call | tf_op jit(solution)/shard_map/pallas_call | solution.py:592
  (62 shorter events, 2.8 us)
Async XLA Ops:
  0.6 1.0 copy-start
  1.7 8.5 %copy-start.1 = (f32[32,16,256]{2,1,0:T(8,128)S(1)}, f32[32,16,256]{2,1,0:T(8,128)}, u32[]{:S(2)}) copy-start(f32[32,16,256]{2,1,0:T(8,128)} %k.5) | copy-start | bytes 1572868
  1.7 8.6 %copy-start.2 = (f32[32,16,256]{2,1,0:T(8,128)S(1)}, f32[32,16,256]{2,1,0:T(8,128)}, u32[]{:S(2)}) copy-start(f32[32,16,256]{2,1,0:T(8,128)} %b.3) | copy-start | bytes 1572868
  2.9 50.4 %all-to-all-start.1 = ((f32[32,16,128]{2,1,0:T(8,128)}), f32[32,16,128]{2,1,0:T(8,128)S(1)}, u32[]{:S(2)}, u32[]{:S(2)}) async-start(f32[32,16,128]{2,1,0:T(8,128)} %get-tuple-element.64), calls=%async_computation.1 | async-start | bytes 524288 | tf_op jit(solution)/shard_map/all_to_all | solution.py:624
  10.4 13.2 %collective-permute-start = (f32[5,32,256]{2,1,0:T(8,128)S(1)}, f32[5,32,256]{2,1,0:T(8,128)S(1)}, u32[]{:S(2)}, u32[]{:S(2)}) collective-permute-start(f32[5,32,256]{2,1,0:T(8,128)S(1)} %get-tuple-element.49), channel_id=1, source_target_pairs={{0,1},{1,2},{2,3},{3,4},{4,5},{5,6},{6,7},{7,0},{8,9},{9,10},{10,1... | collective-permute-start | bytes 491528 | tf_op jit(solution)/shard_map/ppermute | solution.py:34
  12.2 11.4 %collective-permute-start.1 = (f32[5,32,256]{2,1,0:T(8,128)S(1)}, f32[5,32,256]{2,1,0:T(8,128)S(1)}, u32[]{:S(2)}, u32[]{:S(2)}) collective-permute-start(f32[5,32,256]{2,1,0:T(8,128)S(1)} %get-tuple-element.50), channel_id=1, source_target_pairs={{0,7},{1,0},{2,1},{3,2},{4,3},{5,4},{6,5},{7,6},{8,15},{9,8},{10,9... | collective-permute-start | bytes 491528 | tf_op jit(solution)/shard_map/ppermute | solution.py:34
  23.8 4.4 %collective-permute-start.2 = (f32[5,24,256]{2,1,0:T(8,128)S(1)}, f32[5,24,256]{2,1,0:T(8,128)S(1)}, u32[]{:S(2)}, u32[]{:S(2)}) collective-permute-start(f32[5,24,256]{2,1,0:T(8,128)S(1)} %get-tuple-element.53), channel_id=1, source_target_pairs={{0,8},{8,16},{16,24},{24,0},{1,9},{9,17},{17,25},{25,1},{2,10},{10... | collective-permute-start | bytes 368648 | tf_op jit(solution)/shard_map/ppermute | solution.py:34
  23.9 4.6 %collective-permute-start.3 = (f32[5,24,256]{2,1,0:T(8,128)S(1)}, f32[5,24,256]{2,1,0:T(8,128)S(1)}, u32[]{:S(2)}, u32[]{:S(2)}) collective-permute-start(f32[5,24,256]{2,1,0:T(8,128)S(1)} %get-tuple-element.54), channel_id=1, source_target_pairs={{0,24},{8,0},{16,8},{24,16},{1,25},{9,1},{17,9},{25,17},{2,26},{10... | collective-permute-start | bytes 368648 | tf_op jit(solution)/shard_map/ppermute | solution.py:34
  32.5 1.0 copy-start.3
  33.5 0.9 copy-start.5
  34.5 0.9 copy-start.7
  35.4 0.9 copy-start.9
  36.3 7.2 %collective-permute-start.4 = (f32[7,16,128]{2,1,0:T(8,128)S(1)}, f32[7,16,128]{2,1,0:T(8,128)S(1)}, u32[]{:S(2)}, u32[]{:S(2)}) collective-permute-start(f32[7,16,128]{2,1,0:T(8,128)S(1)} %get-tuple-element.56), channel_id=1, source_target_pairs={{0,1},{1,2},{2,3},{3,4},{4,5},{5,6},{6,7},{7,0},{8,9},{9,10},{10,1... | collective-permute-start | bytes 172040 | tf_op jit(solution)/shard_map/ppermute | solution.py:34
  36.7 6.8 %collective-permute-start.5 = (f32[7,16,128]{2,1,0:T(8,128)S(1)}, f32[7,16,128]{2,1,0:T(8,128)S(1)}, u32[]{:S(2)}, u32[]{:S(2)}) collective-permute-start(f32[7,16,128]{2,1,0:T(8,128)S(1)} %get-tuple-element.57), channel_id=1, source_target_pairs={{0,7},{1,0},{2,1},{3,2},{4,3},{5,4},{6,5},{7,6},{8,15},{9,8},{10,9... | collective-permute-start | bytes 172040 | tf_op jit(solution)/shard_map/ppermute | solution.py:34
  43.6 3.7 %collective-permute-start.6 = (f32[7,16,128]{2,1,0:T(8,128)S(1)}, f32[7,16,128]{2,1,0:T(8,128)S(1)}, u32[]{:S(2)}, u32[]{:S(2)}) collective-permute-start(f32[7,16,128]{2,1,0:T(8,128)S(1)} %get-tuple-element.60), channel_id=1, source_target_pairs={{0,8},{8,16},{16,24},{24,0},{1,9},{9,17},{17,25},{25,1},{2,10},{10... | collective-permute-start | bytes 172040 | tf_op jit(solution)/shard_map/ppermute | solution.py:34
  43.8 3.5 %collective-permute-start.7 = (f32[7,16,128]{2,1,0:T(8,128)S(1)}, f32[7,16,128]{2,1,0:T(8,128)S(1)}, u32[]{:S(2)}, u32[]{:S(2)}) collective-permute-start(f32[7,16,128]{2,1,0:T(8,128)S(1)} %get-tuple-element.61), channel_id=1, source_target_pairs={{0,24},{8,0},{16,8},{24,16},{1,25},{9,1},{17,9},{25,17},{2,26},{10... | collective-permute-start | bytes 172040 | tf_op jit(solution)/shard_map/ppermute | solution.py:34
  50.6 0.7 copy-start.23
  51.3 0.7 copy-start.25
  52.0 0.7 copy-start.27
  53.3 30.9 %all-to-all-start = ((f32[32,16,128]{2,1,0:T(8,128)}), f32[32,16,128]{2,1,0:T(8,128)S(1)}, u32[]{:S(2)}, u32[]{:S(2)}) async-start(f32[32,16,128]{2,1,0:T(8,128)} %get-tuple-element.63), calls=%async_computation | async-start | bytes 524288 | tf_op jit(solution)/shard_map/all_to_all | solution.py:654
  59.9 12.7 %collective-permute-start.8 = (f32[256,128]{1,0:T(8,128)}, f32[256,128]{1,0:T(8,128)S(1)}, u32[]{:S(2)}, u32[]{:S(2)}) collective-permute-start(f32[256,128]{1,0:T(8,128)} %copy-done.35), channel_id=1, source_target_pairs={{0,1},{1,2},{2,3},{3,4},{4,5},{5,6},{6,7},{7,0},{8,9},{9,10},{10,1... | collective-permute-start | bytes 393224 | tf_op jit(solution)/shard_map/ppermute | solution.py:34
  61.7 10.8 %collective-permute-start.9 = (f32[256,128]{1,0:T(8,128)S(1)}, f32[256,128]{1,0:T(8,128)S(1)}, u32[]{:S(2)}, u32[]{:S(2)}) collective-permute-start(f32[256,128]{1,0:T(8,128)S(1)} %get-tuple-element.83), channel_id=1, source_target_pairs={{0,7},{1,0},{2,1},{3,2},{4,3},{5,4},{6,5},{7,6},{8,15},{9,8},{10,9... | collective-permute-start | bytes 393224 | tf_op jit(solution)/shard_map/ppermute | solution.py:34
  73.4 0.9 copy-start.11
  74.3 0.7 copy-start.33
  75.0 21.0 %collective-permute-start.10 = (f32[208,128]{1,0:T(8,128)}, f32[208,128]{1,0:T(8,128)}, u32[]{:S(2)}, u32[]{:S(2)}) collective-permute-start(f32[208,128]{1,0:T(8,128)} %get-tuple-element.92), channel_id=1, source_target_pairs={{0,8},{8,16},{16,24},{24,0},{1,9},{9,17},{17,25},{25,1},{2,10},{10... | collective-permute-start | bytes 319496 | tf_op jit(solution)/shard_map/ppermute | solution.py:34
  75.0 21.0 %collective-permute-start.11 = (f32[208,128]{1,0:T(8,128)}, f32[208,128]{1,0:T(8,128)}, u32[]{:S(2)}, u32[]{:S(2)}) collective-permute-start(f32[208,128]{1,0:T(8,128)} %get-tuple-element.93), channel_id=1, source_target_pairs={{0,24},{8,0},{16,8},{24,16},{1,25},{9,1},{17,9},{25,17},{2,26},{10... | collective-permute-start | bytes 319496 | tf_op jit(solution)/shard_map/ppermute | solution.py:34
  76.7 19.3 %copy-start.26 = (f32[24,16,128]{2,1,0:T(8,128)S(1)}, f32[24,16,128]{2,1,0:T(8,128)}, u32[]{:S(2)}) copy-start(f32[24,16,128]{2,1,0:T(8,128)} %copy-done.25) | copy-start | bytes 589828
  78.8 0.9 copy-start.13
  79.6 0.8 copy-start.15
  80.4 0.8 copy-start.17
  81.3 0.8 copy-start.19
  82.1 0.8 copy-start.21
  83.5 0.7 copy-start.31
  84.2 1.1 copy-start.14
  85.2 1.1 copy-start.16
  86.3 1.1 copy-start.18
  87.3 1.1 copy-start.20
  88.4 1.1 copy-start.22
  89.5 0.9 copy-start.30
  90.4 0.9 copy-start.32
  91.3 4.7 %copy-start.4 = (f32[38,24,256]{2,1,0:T(8,128)S(1)}, f32[38,24,256]{2,1,0:T(8,128)}, u32[]{:S(2)}) copy-start(f32[38,24,256]{2,1,0:T(8,128)} %copy-done.3) | copy-start | bytes 2801668
  91.3 4.7 %copy-start.6 = (f32[38,24,256]{2,1,0:T(8,128)S(1)}, f32[38,24,256]{2,1,0:T(8,128)}, u32[]{:S(2)}) copy-start(f32[38,24,256]{2,1,0:T(8,128)} %copy-done.5) | copy-start | bytes 2801668
  91.3 4.7 %copy-start.8 = (f32[38,24,256]{2,1,0:T(8,128)S(1)}, f32[38,24,256]{2,1,0:T(8,128)}, u32[]{:S(2)}) copy-start(f32[38,24,256]{2,1,0:T(8,128)} %copy-done.7) | copy-start | bytes 2801668
  91.3 4.8 %copy-start.10 = (f32[38,24,256]{2,1,0:T(8,128)S(1)}, f32[38,24,256]{2,1,0:T(8,128)}, u32[]{:S(2)}) copy-start(f32[38,24,256]{2,1,0:T(8,128)} %copy-done.9) | copy-start | bytes 2801668
  91.3 4.8 %copy-start.24 = (f32[24,16,128]{2,1,0:T(8,128)S(1)}, f32[24,16,128]{2,1,0:T(8,128)}, u32[]{:S(2)}) copy-start(f32[24,16,128]{2,1,0:T(8,128)} %copy-done.23) | copy-start | bytes 589828
  96.0 1.1 %copy-start.12 = (f32[32,24,256]{2,1,0:T(8,128)S(1)}, f32[32,24,256]{2,1,0:T(8,128)}, u32[]{:S(2)}) copy-start(f32[32,24,256]{2,1,0:T(8,128)} %copy-done.11) | copy-start | bytes 2359300
  97.2 0.9 copy-start.28
  98.1 0.9 copy-start.34
  (2 other events, 1.3 us)

commit v3 on v2

--- a/solution.py
+++ b/solution.py
@@ -27,6 +27,7 @@
 EDGE = 2
 UNROLL = 8
 SPARE = 4 * 1024 * 1024
+VMEM_BYTES = 64 * 1024 * 1024
 
 
 def rotate(value, axis, shift):
@@ -65,6 +66,23 @@
 def doubling(coarse, fine, valid):
     row, col = iota((coarse, fine), 0), iota((coarse, fine), 1)
     return jnp.where((row == col // 2) & (row < valid), 1.0, 0.0).astype(BF16)
+
+
+def move(refs, stash, sems, back):
+    copies = []
+    for i, ref in enumerate(refs):
+        planes = ref.shape[0]
+        there = stash.at[i * planes : (i + 1) * planes]
+        source, target = (there, ref) if back else (ref, there)
+        copies.append(pltpu.make_async_copy(source, target, sems.at[i]))
+    for copy in copies:
+        copy.start()
+    return copies
+
+
+def wait(copies):
+    for copy in copies:
+        copy.wait()
 
 
 def face(a, b):
@@ -114,8 +132,9 @@
         ws[i] = rows
         wz[i] = lanes
         whole = (before + lead) + (row_sum + lane_sum)
-        total[i] = whole
-        inverse[i] = jnp.where(here > 0.0, 1.0 / whole, 0.0)
+        there = here > 0.0
+        total[i] = jnp.where(there, whole, 0.0)
+        inverse[i] = jnp.where(there, 1.0 / whole, 0.0)
         return lead
 
     lax.fori_loop(0, planes - 1, body, jnp.zeros(k.shape[1:], F32), unroll=UNROLL)
@@ -182,10 +201,11 @@
     return (quarter[0] + quarter[1]) + odd
 
 
-def spread_copies(out, rows):
-    size, count = rows.shape[0], rows.shape[1]
-    for i in range(size):
-        out[0, pl.ds(i, count, stride=size), :] = rows[i]
+def spread_copies(out, *fields):
+    for f, rows in enumerate(fields):
+        size, count = rows.shape[0], rows.shape[1]
+        for i in range(size):
+            out[0, pl.ds(f * size * count + i, count, stride=size), :] = rows[i]
 
     def copy(d):
         out[d] = out[0]
@@ -203,7 +223,7 @@
         down_out[K0 + r] = b[:, r, :]
 
 
-def conduct_kernel(k, k1, copies, pairs, halves, pairs1, halves1):
+def conduct_kernel(k, k1, k2, pairs, halves, pairs1, halves1):
     def add(j):
         pairs[j] = k[2 * j] + k[2 * j + 1]
 
@@ -214,7 +234,7 @@
         pairs1[j] = k1[2 * j] + k1[2 * j + 1]
 
     loop(0, pairs1.shape[0], add1)
-    spread_copies(copies, packed(pairs1[...], halves1, k1.shape[2]))
+    k2[...] = packed(pairs1[...], halves1, k1.shape[2])
 
 
 def widen(out, own, low, high, count):
@@ -254,13 +274,14 @@
 
 def fine_down_kernel(
     k_own, b_own, low, high, k1,
-    wl, ws, wz, total, inverse, b, s_out, b1_out, up_out, down_out,
-    k, first, second, pairs, halves,
+    stash, s_out, b1_out, up_out, down_out,
+    wl, ws, wz, total, inverse, b, k, first, second, pairs, halves, sems,
 ):
     join(k, k_own, lambda r: low[r], lambda r: high[r], K0, K0)
     join(b, b_own, lambda r: low[K0 + r], lambda r: high[K0 + r], B0, K0)
     w = (wl, ws, wz)
     weigh(k, wl, ws, wz, total, inverse, False, True)
+    copies = move((wl, ws, wz, total, b), stash, sems, False)
     planes, lanes = b.shape[0], b.shape[2]
     own, rows = planes - 2 * K0, s_out.shape[1]
     pre_smooth(b, first, second, w, inverse, 1.0, (1, planes - 1), (2, planes - 2))
@@ -279,6 +300,7 @@
             out[r] = k1[:, k_from + r, :]
         for r in range(B1):
             out[K1 + r] = b1_out[:, b_from + r, :]
+    wait(copies)
 
 
 def widen_middle_kernel(k1, b1, low, high, k_out, b_out, up_out, down_out):
@@ -292,9 +314,9 @@
 
 
 def middle_down_kernel(
-    k_own, b_own, low, high, s,
-    wl, ws, wz, total, inverse, b, s_out, copies, up_out, down_out,
-    k, first, second, pairs, halves,
+    k_own, b_own, low, high, s, k2,
+    wl, ws, wz, inverse, b, s_out, copies, up_out, down_out,
+    total, k, first, second, pairs, halves,
 ):
     scale = 0.25
     join(k, k_own, lambda r: low[r], lambda r: high[r], K1, K1)
@@ -311,7 +333,7 @@
         pairs[j] = both[0:rows]
 
     loop(0, own // 2, restrict)
-    spread_copies(copies, packed(pairs[...], halves, lanes))
+    spread_copies(copies, k2[...], packed(pairs[...], halves, lanes))
     s_out[...] = second[K1 : K1 + own, 0:rows, :]
     fine, fine_rows = s.shape[0], s.shape[1]
     for out, from0, from1 in ((up_out, fine_rows - S0, rows - S1), (down_out, 0, 0)):
@@ -354,7 +376,7 @@
             out[at : at + rows1] = s1_out[from1 + r]
 
 
-def unpack(received, out, block_x, block_y, across, along):
+def unpack(received, out, first, block_x, block_y, across, along):
     planes, rows, lanes = out.shape
     lane = iota((block_x, lanes), 1)
     for end in (0, planes - 1):
@@ -363,7 +385,7 @@
     def place(column):
         for row in range(across):
             for j in range(block_y // 2):
-                piece = received[row * along + column, j * block_x : (j + 1) * block_x, :]
+                piece = received[row * along + column, pl.ds(first + j * block_x, block_x), :]
                 at = 1 + column * block_y + 2 * j
                 span = slice(row * block_x, (row + 1) * block_x)
                 out[at, span, :] = jnp.where(lane < lanes // 2, piece, 0.0)
@@ -376,31 +398,6 @@
 def clear_ends(ref):
     for end in (0, ref.shape[0] - 1):
         ref[end] = jnp.zeros(ref.shape[1:], F32)
-
-
-def coarse_weights_kernel(
-    valid, received,
-    wl2, ws2, wz2, total2, inverse2, wl3, ws3, wz3, total3, inverse3, k4,
-    k2, k3, pairs2, halves2, pairs3, halves3,
-):
-    planes, rows, lanes = k2.shape
-    across, along = lax.axis_size("gx"), lax.axis_size("gy")
-    unpack(received, k2, rows // across, (planes - 2) // along, across, along)
-
-    def add2(j):
-        pairs2[j] = k2[2 * j + 1] + k2[2 * j + 2]
-
-    loop(0, pairs2.shape[0], add2)
-    clear_ends(k3)
-    k3[1 : k3.shape[0] - 1] = coarser(pairs2[...], halves2, valid)
-
-    def add3(j):
-        pairs3[j] = k3[2 * j + 1] + k3[2 * j + 2]
-
-    loop(0, pairs3.shape[0], add3)
-    k4[...] = coarser(pairs3[...], halves3, valid // 2)
-    weigh(k2, wl2, ws2, wz2, total2, inverse2, True, False)
-    weigh(k3, wl3, ws3, wz3, total3, inverse3, True, False)
 
 
 def coarse_down(b, w, total, inverse, first, second, scale, valid, pairs, halves):
@@ -478,28 +475,42 @@
 
 
 def coarse_kernel(
-    valid, received, wl2, ws2, wz2, total2, inverse2, wl3, ws3, wz3, total3, inverse3, k4,
-    region,
-    b2, first2, second2, pairs2, halves2, b3, first3, second3, pairs3, halves3, grown2, grown3,
+    valid, received, region,
+    wl2, ws2, wz2, total2, inverse2, k2, b2, first2, second2, pairs2, halves2,
+    wl3, ws3, wz3, total3, inverse3, k3, b3, first3, second3, pairs3, halves3,
 ):
     planes, rows, lanes = b2.shape
     across, along = lax.axis_size("gx"), lax.axis_size("gy")
     block_x, block_y = rows // across, (planes - 2) // along
-    unpack(received, b2, block_x, block_y, across, along)
+    unpack(received, k2, 0, block_x, block_y, across, along)
+    unpack(received, b2, block_x * block_y // 2, block_x, block_y, across, along)
+
+    def add2(j):
+        pairs2[j] = k2[2 * j + 1] + k2[2 * j + 2]
+
+    loop(0, pairs2.shape[0], add2)
+    clear_ends(k3)
+    own3 = k3.shape[0] - 2
+    k3[1 : own3 + 1] = coarser(pairs2[...], halves2, valid)
+
+    def add3(j):
+        pairs3[j] = k3[2 * j + 1] + k3[2 * j + 2]
+
+    loop(0, pairs3.shape[0], add3)
+    k4 = coarser(pairs3[...], halves3, valid // 2)
+    weigh(k2, wl2, ws2, wz2, total2, inverse2, True, False)
+    weigh(k3, wl3, ws3, wz3, total3, inverse3, True, False)
     w2, w3 = (wl2, ws2, wz2), (wl3, ws3, wz3)
     clear_ends(b3)
-    own3 = b3.shape[0] - 2
     b3[1 : own3 + 1] = coarse_down(
         b2, w2, total2, inverse2, first2, second2, 0.25**2, valid, pairs2, halves2
     )
     b4 = coarse_down(
         b3, w3, total3, inverse3, first3, second3, 0.25**3, valid // 2, pairs3, halves3
     )
-    x4 = bottom(k4[...], b4, 0.25**4)
-    coarse_up(x4, b3, w3, inverse3, first3, second3, 0.25**3, valid // 2, grown3)
-    coarse_up(
-        first3[1 : own3 + 1], b2, w2, inverse2, first2, second2, 0.25**2, valid, grown2
-    )
+    x4 = bottom(k4, b4, 0.25**4)
+    coarse_up(x4, b3, w3, inverse3, first3, second3, 0.25**3, valid // 2, pairs3)
+    coarse_up(first3[1 : own3 + 1], b2, w2, inverse2, first2, second2, 0.25**2, valid, pairs2)
     column, row = lax.axis_index("gy"), lax.axis_index("gx")
     for q in range(region.shape[0]):
         plane = column * block_y + q - EDGE
@@ -512,11 +523,11 @@
 
 
 def fine_up_kernel(
-    valid, region, wl1, ws1, wz1, inverse1, b1, s1_own,
-    wl, ws, wz, total, inverse, b, s_own, low, high,
+    valid, region, wl1, ws1, wz1, inverse1, b1, s1_own, stash, s_own, low, high,
     field_out, residual_out,
-    first1, second1, grown, s, second, tall, thick,
+    wl, ws, wz, total, b, inverse, first1, second1, grown, s, second, tall, thick, sems,
 ):
+    copies = move((wl, ws, wz, total, b), stash, sems, True)
     planes1, rows1, lanes1 = b1.shape
     planes, rows, lanes = b.shape
     w1, w = (wl1, ws1, wz1), (wl, ws, wz)
@@ -574,6 +585,12 @@
             s[i] = s[i] + thick[q]
 
     loop(1, count - 1, add)
+    wait(copies)
+
+    def invert(i):
+        inverse[i] = jnp.where(total[i] > 0.0, 1.0 / total[i], 0.0)
+
+    loop(1, planes - 1, invert)
     post_smooth(b, s, second, w, inverse, 1.0, (1, planes - 1), (2, planes - 2))
     own, own_rows = field_out.shape[0], field_out.shape[1]
 
@@ -585,14 +602,20 @@
     loop(0, own, finish)
 
 
-def call(kernel, outs, scratch=()):
+def call(kernel, outs, scratch=(), held=0, kept=(), sems=()):
     def run(*operands):
-        shapes = [operand.shape for operand in operands] + list(outs) + list(scratch)
-        words = sum(math.prod(s[:-2]) * (-(-s[-2] // 8) * 8) * s[-1] for s in shapes)
+        inputs = [o.shape for i, o in enumerate(operands) if i not in kept]
+        shapes = inputs + list(outs[held:]) + list(scratch)
+        words = sum(math.prod(s[:-2]) * eight(s[-2]) * s[-1] for s in shapes)
+        places = [pltpu.HBM if i in kept else pltpu.VMEM for i in range(len(operands))]
+        out_places = [pltpu.HBM if i < held else pltpu.VMEM for i in range(len(outs))]
         return pl.pallas_call(
             kernel,
             out_shape=[jax.ShapeDtypeStruct(shape, F32) for shape in outs],
-            scratch_shapes=[pltpu.VMEM(shape, F32) for shape in scratch],
+            in_specs=[pl.BlockSpec(memory_space=place) for place in places],
+            out_specs=[pl.BlockSpec(memory_space=place) for place in out_places],
+            scratch_shapes=[pltpu.VMEM(shape, F32) for shape in scratch]
+            + [pltpu.SemaphoreType.DMA((n,)) for n in sems],
             compiler_params=pltpu.CompilerParams(vmem_limit_bytes=4 * words + SPARE),
         )(*operands)
 
@@ -611,17 +634,16 @@
     qx, qy = hx // 2, hy // 2
     both = ("gx", "gy")
     tall, tall1 = eight(by + 2 * K0), eight(hy + 2 * K1)
-    pieces = (devices, qx * qy // 2, hz)
+    pieces = (devices, qx * qy, hz)
 
     slab = (K0 + B0, bx, nz)
     up_rows, down_rows = call(slab_kernel, [slab, slab])(right_side, coefficient)
     low, high = rotate(up_rows, "gy", 1), rotate(down_rows, "gy", -1)
-    k1, copies = call(
+    k1, k2 = call(
         conduct_kernel,
-        [(hx, hy, hz), pieces],
+        [(hx, hy, hz), (qx, qy // 2, hz)],
         [(hx, by, nz), (hx, by, hz), (qx, hy, hz), (qx, hy, hz)],
     )(coefficient)
-    k2 = lax.all_to_all(copies, both, 0, 0, tiled=True)
 
     plane = (bx, tall, nz)
     slab = (K0 + B0, tall, nz)
@@ -632,10 +654,13 @@
 
     block = (bx + 2 * K0, tall, nz)
     slab = (K1 + B1, hx, hz)
-    *w0, b, s, b1, up_rows, down_rows = call(
+    planes = 5 * block[0] + VMEM_BYTES // (4 * tall * nz)
+    stash, s, b1, up_rows, down_rows = call(
         fine_down_kernel,
-        [block] * 6 + [(bx, by, nz), (hx, hy, hz), slab, slab],
-        [block] * 3 + [(hx, by, nz), (hx, by, hz)],
+        [(planes, tall, nz), (bx, by, nz), (hx, hy, hz), slab, slab],
+        [block] * 9 + [(hx, by, nz), (hx, by, hz)],
+        held=1,
+        sems=(5,),
     )(k_own, b_own, low, high, k1)
     low, high = rotate(up_rows, "gy", 1), rotate(down_rows, "gy", -1)
     slab = (K1 + B1, tall1, hz)
@@ -646,12 +671,12 @@
 
     block1 = (hx + 2 * K1, tall1, hz)
     slab = (2 * S0 * bx + S1 * hx, hz)
-    *w1, b1, s1, copies, up_rows, down_rows = call(
+    *kept1, s1, copies, up_rows, down_rows = call(
         middle_down_kernel,
-        [block1] * 6 + [(hx, hy, hz), pieces, slab, slab],
-        [block1] * 3 + [(qx, hy, hz), (qx, hy, hz)],
-    )(k1_own, b1_own, low, high, s)
-    b2 = lax.all_to_all(copies, both, 0, 0, tiled=True)
+        [block1] * 5 + [(hx, hy, hz), pieces, slab, slab],
+        [block1] * 4 + [(qx, hy, hz), (qx, hy, hz)],
+    )(k1_own, b1_own, low, high, s, k2)
+    received = lax.all_to_all(copies, both, 0, 0, tiled=True)
     low, high = rotate(up_rows, "gy", 1), rotate(down_rows, "gy", -1)
     slab = (2 * S0 * tall + S1 * tall1, hz)
     s_own, s1_own, up_planes, down_planes = call(
@@ -660,28 +685,24 @@
     low, high = rotate(up_planes, "gx", 1), rotate(down_planes, "gx", -1)
 
     x2, y2 = across * qx, along * qy
-    level2, level3, level4 = ((y2 // s + 2, x2 // s, hz) for s in (1, 2, 4))
+    level2, level3 = ((y2 // s + 2, x2 // s, hz) for s in (1, 2))
     half2, half3 = (y2 // 2, x2, hz), (y2 // 4, x2 // 2, hz)
     valid = nz // 4
-    weights = call(
-        partial(coarse_weights_kernel, valid),
-        [level2] * 5 + [level3] * 5 + [(y2 // 4, x2 // 4, hz)],
-        [level2, level3, half2, half2, half3, half3],
-    )(k2)
     (region,) = call(
         partial(coarse_kernel, valid),
         [(qy + 2 * EDGE, 3 * qx, hz)],
-        [level2] * 3 + [half2] * 2 + [level3] * 3 + [half3] * 2 + [half2, half3],
-    )(b2, *weights)
-
-    wl1, ws1, wz1, _, inverse1 = w1
+        [level2] * 9 + [half2] * 2 + [level3] * 9 + [half3] * 2,
+    )(received)
+
     count = hx + 2 * EDGE
     field, rest = call(
         partial(fine_up_kernel, valid),
         [(bx, by, nz)] * 2,
-        [block1, block1, (qx + 2 * EDGE, tall1, hz), block, block, (count, tall, hz)]
-        + [(count, tall, nz)],
-    )(region, wl1, ws1, wz1, inverse1, b1, s1_own, *w0, b, s_own, low, high)
+        [block] * 6 + [block1, block1, (qx + 2 * EDGE, tall1, hz)]
+        + [block, block, (count, tall, hz), (count, tall, nz)],
+        kept=(7,),
+        sems=(5,),
+    )(region, *kept1, s1_own, stash, s_own, low, high)
     return field, rest
 
 

time: 106 us -> 79.9 us (0.75)
  local copies, waits for them, and re-layouts: 24.5 us -> 4.16 us
  starting transfers between devices: 33.4 us -> 27.6 us
  waiting for transfers between devices: 23.5 us -> 25.2 us
  Pallas kernels: 23.3 us -> 21.8 us
    unnamed x72 -> x8, local copies, waits for them, and re-layouts: 24.5 us -> 4.16 us
    all_to_all x2 -> x1, starting transfers between devices: 13.8 us -> 6.54 us  [per_device(): received = lax.all_to_all(copies, both, 0, 0, tiled=True)]
    pallas_call x10 -> x9, Pallas kernels: 23.3 us -> 21.8 us  [run(): pl.pallas_call(kernel, out_shape=[jax.ShapeDtypeStruct(shape, F32) for sh...]
    ppermute x12, starting transfers between devices: 19.6 us -> 21 us  [rotate(): lax.ppermute(value, axis, [(i, (i + shift) % size) for i in range(size)])]
    ppermute x12, waiting for transfers between devices: 23.5 us -> 24.9 us  [rotate(): lax.ppermute(value, axis, [(i, (i + shift) % size) for i in range(size)])]
  transfers between devices with their start and end apart: 14 -> 13, of which waited for: 6 -> 8; matrix products, arithmetic and copies ran while one was open for 0% -> 0% of each run, Pallas kernels for 15% -> 9%
where the time goes in v3:
time: 79.9 us; the launch traced here: 79.5 us
  starting transfers between devices  27.6 us (35%)
  waiting for transfers between devices  25.2 us (32%)
  Pallas kernels  21.8 us (27%)
  local copies, waits for them, and re-layouts  4.16 us (5%)
    ppermute x12, waiting for transfers between devices, rotate(): lax.ppermute(value, axis, [(i, (i + shift) % size) for i in range(size)])  24.9 us
    pallas_call x9, Pallas kernels, run(): pl.pallas_call(kernel, out_shape=[jax.ShapeDtypeStruct(shape, F32) for sh...  21.8 us
    ppermute x12, starting transfers between devices, rotate(): lax.ppermute(value, axis, [(i, (i + shift) % size) for i in range(size)])  21 us
    all_to_all x1, starting transfers between devices, per_device(): received = lax.all_to_all(copies, both, 0, 0, tiled=True)  6.54 us
    unnamed x8, local copies, waits for them, and re-layouts  4.16 us
  transfers between devices with their start and end apart: 13, of which 8 were waited for; matrix products, arithmetic and copies ran while one was open for 0% of the time, Pallas kernels for 9%

profile of v3, /device:TPU:0, one launch (start us, length us, event | category | flops | bytes accessed | tf_op | source)
XLA Modules:
  0.0 79.5 jit_solution(6972944390884455867)
XLA Ops:
  0.6 0.0 copy-start
  0.6 1.0 %copy-done = f32[32,16,256]{2,1,0:T(8,128)S(1)} copy-done((f32[32,16,256]{2,1,0:T(8,128)S(1)}, f32[32,16,256]{2,1,0:T(8,128)}, u32[]{:S(2)}) %copy-start) | copy-done | bytes 524312
  1.7 0.0 copy-start.2
  1.7 1.0 %copy-done.2 = f32[32,16,256]{2,1,0:T(8,128)S(1)} copy-done((f32[32,16,256]{2,1,0:T(8,128)S(1)}, f32[32,16,256]{2,1,0:T(8,128)}, u32[]{:S(2)}) %copy-start.2) | copy-done | bytes 524312
  2.7 0.1 shard_map.42
  2.8 3.0 %collective-permute-start = (f32[5,32,256]{2,1,0:T(8,128)S(1)}, f32[5,32,256]{2,1,0:T(8,128)S(1)}, u32[]{:S(2)}, u32[]{:S(2)}) collective-permute-start(f32[5,32,256]{2,1,0:T(8,128)S(1)} %get-tuple-element.33), channel_id=1, source_target_pairs={{0,1},{1,2},{2,3},{3,4},{4,5},{5,6},{6,7},{7,0},{8,9},{9,10},{10,1... | collective-permute-start | bytes 491528 | tf_op jit(solution)/shard_map/ppermute | solution.py:35
  5.8 3.1 %collective-permute-start.1 = (f32[5,32,256]{2,1,0:T(8,128)S(1)}, f32[5,32,256]{2,1,0:T(8,128)S(1)}, u32[]{:S(2)}, u32[]{:S(2)}) collective-permute-start(f32[5,32,256]{2,1,0:T(8,128)S(1)} %get-tuple-element.34), channel_id=1, source_target_pairs={{0,7},{1,0},{2,1},{3,2},{4,3},{5,4},{6,5},{7,6},{8,15},{9,8},{10,9... | collective-permute-start | bytes 491528 | tf_op jit(solution)/shard_map/ppermute | solution.py:35
  8.9 4.2 %collective-permute-done.low = f32[5,32,256]{2,1,0:T(8,128)S(1)} collective-permute-done((f32[5,32,256]{2,1,0:T(8,128)S(1)}, f32[5,32,256]{2,1,0:T(8,128)S(1)}, u32[]{:S(2)}, u32[]{:S(2)}) %collective-permute-start) | collective-permute-done | bytes 163872 | tf_op jit(solution)/shard_map/ppermute | solution.py:35
  13.2 1.8 %collective-permute-done.1.high = f32[5,32,256]{2,1,0:T(8,128)S(1)} collective-permute-done((f32[5,32,256]{2,1,0:T(8,128)S(1)}, f32[5,32,256]{2,1,0:T(8,128)S(1)}, u32[]{:S(2)}, u32[]{:S(2)}) %collective-permute-start.1) | collective-permute-done | bytes 163872 | tf_op jit(solution)/shard_map/ppermute | solution.py:35
  15.0 0.0 copy-start.1
  15.0 1.0 %copy-done.1 = f32[32,16,256]{2,1,0:T(8,128)S(1)} copy-done((f32[32,16,256]{2,1,0:T(8,128)S(1)}, f32[32,16,256]{2,1,0:T(8,128)}, u32[]{:S(2)}) %copy-start.1) | copy-done | bytes 524312
  16.0 0.0 copy-start.3
  16.0 1.0 %copy-done.3 = f32[32,16,256]{2,1,0:T(8,128)S(1)} copy-done((f32[32,16,256]{2,1,0:T(8,128)S(1)}, f32[32,16,256]{2,1,0:T(8,128)}, u32[]{:S(2)}) %copy-start.3) | copy-done | bytes 524312
  17.1 0.2 shard_map.43
  17.3 0.1 collective-permute-start.2
  17.4 1.7 %collective-permute-start.3 = (f32[5,24,256]{2,1,0:T(8,128)S(1)}, f32[5,24,256]{2,1,0:T(8,128)S(1)}, u32[]{:S(2)}, u32[]{:S(2)}) collective-permute-start(f32[5,24,256]{2,1,0:T(8,128)S(1)} %get-tuple-element.38), channel_id=1, source_target_pairs={{0,24},{8,0},{16,8},{24,16},{1,25},{9,1},{17,9},{25,17},{2,26},{10... | collective-permute-start | bytes 368648 | tf_op jit(solution)/shard_map/ppermute | solution.py:35
  19.1 0.5 shard_map.41
  19.6 2.1 %collective-permute-done.2.low = f32[5,24,256]{2,1,0:T(8,128)S(1)} collective-permute-done((f32[5,24,256]{2,1,0:T(8,128)S(1)}, f32[5,24,256]{2,1,0:T(8,128)S(1)}, u32[]{:S(2)}, u32[]{:S(2)}) %collective-permute-start.2) | collective-permute-done | bytes 122912 | tf_op jit(solution)/shard_map/ppermute | solution.py:35
  21.7 0.4 collective-permute-done.3.high
  22.0 4.3 %shard_map.44 = (f32[2920,24,256]{2,1,0:T(8,128)}, f32[32,16,256]{2,1,0:T(8,128)S(1)}, f32[16,8,128]{2,1,0:T(8,128)S(1)}, f32[7,16,128]{2,1,0:T(8,128)S(1)}, f32[7,16,128]{2,1,0:T(8,128)S(1)}) custom-call(f32[32,24,256]{2,1,0:T(8,128)S(1)} %get-tuple-element.35.k_own, f32[32,24,256]{2,1,0:T(8,128)S(1)} %get-tuple-element.36.b_own, ...), custom_call_target="tpu_custom_call" | custom-call | tf_op jit(solution)/shard_map/pallas_call | solution.py:612
  26.4 0.3 collective-permute-start.4
  26.7 4.4 %collective-permute-start.5 = (f32[7,16,128]{2,1,0:T(8,128)S(1)}, f32[7,16,128]{2,1,0:T(8,128)S(1)}, u32[]{:S(2)}, u32[]{:S(2)}) collective-permute-start(f32[7,16,128]{2,1,0:T(8,128)S(1)} %get-tuple-element.41), channel_id=1, source_target_pairs={{0,7},{1,0},{2,1},{3,2},{4,3},{5,4},{6,5},{7,6},{8,15},{9,8},{10,9... | collective-permute-start | bytes 172040 | tf_op jit(solution)/shard_map/ppermute | solution.py:35
  31.1 2.5 %collective-permute-done.4.low = f32[7,16,128]{2,1,0:T(8,128)S(1)} collective-permute-done((f32[7,16,128]{2,1,0:T(8,128)S(1)}, f32[7,16,128]{2,1,0:T(8,128)S(1)}, u32[]{:S(2)}, u32[]{:S(2)}) %collective-permute-start.4) | collective-permute-done | bytes 57376 | tf_op jit(solution)/shard_map/ppermute | solution.py:35
  33.6 0.0 collective-permute-done.5.high
  33.6 0.1 shard_map.45
  33.7 0.2 collective-permute-start.6
  33.9 1.6 %collective-permute-start.7 = (f32[7,16,128]{2,1,0:T(8,128)S(1)}, f32[7,16,128]{2,1,0:T(8,128)S(1)}, u32[]{:S(2)}, u32[]{:S(2)}) collective-permute-start(f32[7,16,128]{2,1,0:T(8,128)S(1)} %get-tuple-element.45), channel_id=1, source_target_pairs={{0,24},{8,0},{16,8},{24,16},{1,25},{9,1},{17,9},{25,17},{2,26},{10... | collective-permute-start | bytes 172040 | tf_op jit(solution)/shard_map/ppermute | solution.py:35
  35.5 1.9 %collective-permute-done.6.low = f32[7,16,128]{2,1,0:T(8,128)S(1)} collective-permute-done((f32[7,16,128]{2,1,0:T(8,128)S(1)}, f32[7,16,128]{2,1,0:T(8,128)S(1)}, u32[]{:S(2)}, u32[]{:S(2)}) %collective-permute-start.6) | collective-permute-done | bytes 57376 | tf_op jit(solution)/shard_map/ppermute | solution.py:35
  37.4 0.0 collective-permute-done.7.high
  37.4 3.4 %shard_map.46 = (f32[24,16,128]{2,1,0:T(8,128)S(1)}, f32[24,16,128]{2,1,0:T(8,128)S(1)}, f32[24,16,128]{2,1,0:T(8,128)S(1)}, f32[24,16,128]{2,1,0:T(8,128)S(1)},...) custom-call(f32[16,16,128]{2,1,0:T(8,128)S(1)} %get-tuple-element.42, ...), custom_call_target="tpu_custom_call" | custom-call | tf_op jit(solution)/shard_map/pallas_call | solution.py:612
  40.7 6.5 %all-to-all-start = ((f32[32,32,128]{2,1,0:T(8,128)}), f32[32,32,128]{2,1,0:T(8,128)S(1)}, u32[]{:S(2)}, u32[]{:S(2)}) async-start(f32[32,32,128]{2,1,0:T(8,128)} %get-tuple-element.48), calls=%async_computation | async-start | bytes 1048576 | tf_op jit(solution)/shard_map/all_to_all | solution.py:679
  47.3 1.8 %collective-permute-start.8 = (f32[256,128]{1,0:T(8,128)S(1)}, f32[256,128]{1,0:T(8,128)S(1)}, u32[]{:S(2)}, u32[]{:S(2)}) collective-permute-start(f32[256,128]{1,0:T(8,128)S(1)} %get-tuple-element.55), channel_id=1, source_target_pairs={{0,1},{1,2},{2,3},{3,4},{4,5},{5,6},{6,7},{7,0},{8,9},{9,10},{10,1... | collective-permute-start | bytes 393224 | tf_op jit(solution)/shard_map/ppermute | solution.py:35
  49.1 3.0 %collective-permute-start.9 = (f32[256,128]{1,0:T(8,128)S(1)}, f32[256,128]{1,0:T(8,128)S(1)}, u32[]{:S(2)}, u32[]{:S(2)}) collective-permute-start(f32[256,128]{1,0:T(8,128)S(1)} %get-tuple-element.56), channel_id=1, source_target_pairs={{0,7},{1,0},{2,1},{3,2},{4,3},{5,4},{6,5},{7,6},{8,15},{9,8},{10,9... | collective-permute-start | bytes 393224 | tf_op jit(solution)/shard_map/ppermute | solution.py:35
  52.1 12.1 %collective-permute-done.8.low = f32[256,128]{1,0:T(8,128)S(1)} collective-permute-done((f32[256,128]{1,0:T(8,128)S(1)}, f32[256,128]{1,0:T(8,128)S(1)}, u32[]{:S(2)}, u32[]{:S(2)}) %collective-permute-start.8) | collective-permute-done | bytes 131104 | tf_op jit(solution)/shard_map/ppermute | solution.py:35
  64.1 0.0 collective-permute-done.9.high
  64.1 0.2 shard_map.48
  64.3 0.1 collective-permute-start.10
  64.4 1.7 %collective-permute-start.11 = (f32[208,128]{1,0:T(8,128)S(1)}, f32[208,128]{1,0:T(8,128)S(1)}, u32[]{:S(2)}, u32[]{:S(2)}) collective-permute-start(f32[208,128]{1,0:T(8,128)S(1)} %get-tuple-element.61), channel_id=1, source_target_pairs={{0,24},{8,0},{16,8},{24,16},{1,25},{9,1},{17,9},{25,17},{2,26},{10... | collective-permute-start | bytes 319496 | tf_op jit(solution)/shard_map/ppermute | solution.py:35
  66.1 0.3 all-to-all-done.received
  66.4 6.7 %shard_map.47.region = f32[8,24,128]{2,1,0:T(8,128)S(1)} custom-call(f32[32,32,128]{2,1,0:T(8,128)S(1)} %all-to-all-done.received), custom_call_target="tpu_custom_call" | custom-call | tf_op jit(solution)/shard_map/pallas_call | solution.py:612
  73.2 0.0 collective-permute-done.10.low
  73.2 0.0 collective-permute-done.11.high
  73.2 6.3 %shard_map.49 = (f32[32,16,256]{2,1,0:T(8,128)}, f32[32,16,256]{2,1,0:T(8,128)}) custom-call(f32[8,24,128]{2,1,0:T(8,128)S(1)} %shard_map.47.region, f32[24,16,128]{2,1,0:T(8,128)S(1)} %get-tuple-element.49.wl1, f32[24,16,128]{2,1,0:T(8,128)S(1)} %get-tuple-element.50.ws1, f32[24,16,128]{2,1,0:T(8,128)S(1)} %get-tuple-element.51.wz1, ...), custom_call_target="tpu_custom_call" | custom-call | tf_op jit(solution)/shard_map/pallas_call | solution.py:612
Async XLA Ops:
  0.6 1.0 %copy-start = (f32[32,16,256]{2,1,0:T(8,128)S(1)}, f32[32,16,256]{2,1,0:T(8,128)}, u32[]{:S(2)}) copy-start(f32[32,16,256]{2,1,0:T(8,128)} %k.5) | copy-start | bytes 1572868
  1.7 1.0 %copy-start.2 = (f32[32,16,256]{2,1,0:T(8,128)S(1)}, f32[32,16,256]{2,1,0:T(8,128)}, u32[]{:S(2)}) copy-start(f32[32,16,256]{2,1,0:T(8,128)} %b.3) | copy-start | bytes 1572868
  2.8 10.3 %collective-permute-start = (f32[5,32,256]{2,1,0:T(8,128)S(1)}, f32[5,32,256]{2,1,0:T(8,128)S(1)}, u32[]{:S(2)}, u32[]{:S(2)}) collective-permute-start(f32[5,32,256]{2,1,0:T(8,128)S(1)} %get-tuple-element.33), channel_id=1, source_target_pairs={{0,1},{1,2},{2,3},{3,4},{4,5},{5,6},{6,7},{7,0},{8,9},{9,10},{10,1... | collective-permute-start | bytes 491528 | tf_op jit(solution)/shard_map/ppermute | solution.py:35
  5.8 9.2 %collective-permute-start.1 = (f32[5,32,256]{2,1,0:T(8,128)S(1)}, f32[5,32,256]{2,1,0:T(8,128)S(1)}, u32[]{:S(2)}, u32[]{:S(2)}) collective-permute-start(f32[5,32,256]{2,1,0:T(8,128)S(1)} %get-tuple-element.34), channel_id=1, source_target_pairs={{0,7},{1,0},{2,1},{3,2},{4,3},{5,4},{6,5},{7,6},{8,15},{9,8},{10,9... | collective-permute-start | bytes 491528 | tf_op jit(solution)/shard_map/ppermute | solution.py:35
  15.0 1.0 %copy-start.1 = (f32[32,16,256]{2,1,0:T(8,128)S(1)}, f32[32,16,256]{2,1,0:T(8,128)}, u32[]{:S(2)}) copy-start(f32[32,16,256]{2,1,0:T(8,128)} %k.5) | copy-start | bytes 1572868
  16.0 1.0 %copy-start.3 = (f32[32,16,256]{2,1,0:T(8,128)S(1)}, f32[32,16,256]{2,1,0:T(8,128)}, u32[]{:S(2)}) copy-start(f32[32,16,256]{2,1,0:T(8,128)} %b.3) | copy-start | bytes 1572868
  17.3 4.4 %collective-permute-start.2 = (f32[5,24,256]{2,1,0:T(8,128)S(1)}, f32[5,24,256]{2,1,0:T(8,128)S(1)}, u32[]{:S(2)}, u32[]{:S(2)}) collective-permute-start(f32[5,24,256]{2,1,0:T(8,128)S(1)} %get-tuple-element.37), channel_id=1, source_target_pairs={{0,8},{8,16},{16,24},{24,0},{1,9},{9,17},{17,25},{25,1},{2,10},{10... | collective-permute-start | bytes 368648 | tf_op jit(solution)/shard_map/ppermute | solution.py:35
  17.4 4.6 %collective-permute-start.3 = (f32[5,24,256]{2,1,0:T(8,128)S(1)}, f32[5,24,256]{2,1,0:T(8,128)S(1)}, u32[]{:S(2)}, u32[]{:S(2)}) collective-permute-start(f32[5,24,256]{2,1,0:T(8,128)S(1)} %get-tuple-element.38), channel_id=1, source_target_pairs={{0,24},{8,0},{16,8},{24,16},{1,25},{9,1},{17,9},{25,17},{2,26},{10... | collective-permute-start | bytes 368648 | tf_op jit(solution)/shard_map/ppermute | solution.py:35
  26.4 7.2 %collective-permute-start.4 = (f32[7,16,128]{2,1,0:T(8,128)S(1)}, f32[7,16,128]{2,1,0:T(8,128)S(1)}, u32[]{:S(2)}, u32[]{:S(2)}) collective-permute-start(f32[7,16,128]{2,1,0:T(8,128)S(1)} %get-tuple-element.40), channel_id=1, source_target_pairs={{0,1},{1,2},{2,3},{3,4},{4,5},{5,6},{6,7},{7,0},{8,9},{9,10},{10,1... | collective-permute-start | bytes 172040 | tf_op jit(solution)/shard_map/ppermute | solution.py:35
  26.7 6.9 %collective-permute-start.5 = (f32[7,16,128]{2,1,0:T(8,128)S(1)}, f32[7,16,128]{2,1,0:T(8,128)S(1)}, u32[]{:S(2)}, u32[]{:S(2)}) collective-permute-start(f32[7,16,128]{2,1,0:T(8,128)S(1)} %get-tuple-element.41), channel_id=1, source_target_pairs={{0,7},{1,0},{2,1},{3,2},{4,3},{5,4},{6,5},{7,6},{8,15},{9,8},{10,9... | collective-permute-start | bytes 172040 | tf_op jit(solution)/shard_map/ppermute | solution.py:35
  33.7 3.7 %collective-permute-start.6 = (f32[7,16,128]{2,1,0:T(8,128)S(1)}, f32[7,16,128]{2,1,0:T(8,128)S(1)}, u32[]{:S(2)}, u32[]{:S(2)}) collective-permute-start(f32[7,16,128]{2,1,0:T(8,128)S(1)} %get-tuple-element.44), channel_id=1, source_target_pairs={{0,8},{8,16},{16,24},{24,0},{1,9},{9,17},{17,25},{25,1},{2,10},{10... | collective-permute-start | bytes 172040 | tf_op jit(solution)/shard_map/ppermute | solution.py:35
  33.9 3.5 %collective-permute-start.7 = (f32[7,16,128]{2,1,0:T(8,128)S(1)}, f32[7,16,128]{2,1,0:T(8,128)S(1)}, u32[]{:S(2)}, u32[]{:S(2)}) collective-permute-start(f32[7,16,128]{2,1,0:T(8,128)S(1)} %get-tuple-element.45), channel_id=1, source_target_pairs={{0,24},{8,0},{16,8},{24,16},{1,25},{9,1},{17,9},{25,17},{2,26},{10... | collective-permute-start | bytes 172040 | tf_op jit(solution)/shard_map/ppermute | solution.py:35
  40.7 25.7 %all-to-all-start = ((f32[32,32,128]{2,1,0:T(8,128)}), f32[32,32,128]{2,1,0:T(8,128)S(1)}, u32[]{:S(2)}, u32[]{:S(2)}) async-start(f32[32,32,128]{2,1,0:T(8,128)} %get-tuple-element.48), calls=%async_computation | async-start | bytes 1048576 | tf_op jit(solution)/shard_map/all_to_all | solution.py:679
  47.3 16.9 %collective-permute-start.8 = (f32[256,128]{1,0:T(8,128)S(1)}, f32[256,128]{1,0:T(8,128)S(1)}, u32[]{:S(2)}, u32[]{:S(2)}) collective-permute-start(f32[256,128]{1,0:T(8,128)S(1)} %get-tuple-element.55), channel_id=1, source_target_pairs={{0,1},{1,2},{2,3},{3,4},{4,5},{5,6},{6,7},{7,0},{8,9},{9,10},{10,1... | collective-permute-start | bytes 393224 | tf_op jit(solution)/shard_map/ppermute | solution.py:35
  49.1 15.0 %collective-permute-start.9 = (f32[256,128]{1,0:T(8,128)S(1)}, f32[256,128]{1,0:T(8,128)S(1)}, u32[]{:S(2)}, u32[]{:S(2)}) collective-permute-start(f32[256,128]{1,0:T(8,128)S(1)} %get-tuple-element.56), channel_id=1, source_target_pairs={{0,7},{1,0},{2,1},{3,2},{4,3},{5,4},{6,5},{7,6},{8,15},{9,8},{10,9... | collective-permute-start | bytes 393224 | tf_op jit(solution)/shard_map/ppermute | solution.py:35
  64.3 8.9 %collective-permute-start.10 = (f32[208,128]{1,0:T(8,128)S(1)}, f32[208,128]{1,0:T(8,128)S(1)}, u32[]{:S(2)}, u32[]{:S(2)}) collective-permute-start(f32[208,128]{1,0:T(8,128)S(1)} %get-tuple-element.60), channel_id=1, source_target_pairs={{0,8},{8,16},{16,24},{24,0},{1,9},{9,17},{17,25},{25,1},{2,10},{10... | collective-permute-start | bytes 319496 | tf_op jit(solution)/shard_map/ppermute | solution.py:35
  64.4 8.8 %collective-permute-start.11 = (f32[208,128]{1,0:T(8,128)S(1)}, f32[208,128]{1,0:T(8,128)S(1)}, u32[]{:S(2)}, u32[]{:S(2)}) collective-permute-start(f32[208,128]{1,0:T(8,128)S(1)} %get-tuple-element.61), channel_id=1, source_target_pairs={{0,24},{8,0},{16,8},{24,16},{1,25},{9,1},{17,9},{25,17},{2,26},{10... | collective-permute-start | bytes 319496 | tf_op jit(solution)/shard_map/ppermute | solution.py:35

commit v4 on v3

--- a/solution.py
+++ b/solution.py
@@ -25,7 +25,7 @@
 K0, B0, S0 = 3, 2, 3
 K1, B1, S1 = 4, 3, 4
 EDGE = 2
-UNROLL = 8
+REGISTERS = 48
 SPARE = 4 * 1024 * 1024
 VMEM_BYTES = 64 * 1024 * 1024
 
@@ -98,26 +98,30 @@
     return pltpu.roll(x, 1, axis)
 
 
-def sided(k, axis, edged):
-    size = k.shape[axis]
+def sided(k, axis, edge):
     after = up(k, axis)
+    if edge is None:
+        w = face(k, after)
+        return w, w + down(w, axis)
     place = iota(k.shape, axis)
-    if edged:
-        after = jnp.where(place == size - 1, 0.0, after)
-    w = face(k, after)
-    low = down(w, axis)
-    if edged:
-        low = jnp.where(place == 0, k, low)
-        return jnp.where(place == size - 1, 0.0, w), w + low
-    return w, w + low
-
-
-def loop(low, high, body):
+    if edge < k.shape[axis]:
+        place = lax.rem(place, edge)
+    last = place == edge - 1
+    w = face(k, jnp.where(last, 0.0, after))
+    return jnp.where(last, 0.0, w), w + jnp.where(place == 0, k, down(w, axis))
+
+
+def unrolled(plane, count):
+    registers = max(1, plane[0] * plane[1] // 1024)
+    return max(1, min(count, REGISTERS // registers))
+
+
+def loop(low, high, body, plane):
     def step(i, carry):
         body(i)
         return carry
 
-    lax.fori_loop(low, high, step, 0, unroll=min(UNROLL, high - low))
+    lax.fori_loop(low, high, step, 0, unroll=unrolled(plane, high - low))
 
 
 def weigh(k, wl, ws, wz, total, inverse, row_edge, lane_edge):
@@ -126,8 +130,8 @@
     def body(i, before):
         here = k[i]
         lead = face(here, k[i + 1])
-        rows, row_sum = sided(here, 0, row_edge)
-        lanes, lane_sum = sided(here, 1, lane_edge)
+        rows, row_sum = sided(here, 0, here.shape[0] if row_edge else None)
+        lanes, lane_sum = sided(here, 1, here.shape[1] if lane_edge else None)
         wl[i] = lead
         ws[i] = rows
         wz[i] = lanes
@@ -137,10 +141,12 @@
         inverse[i] = jnp.where(there, 1.0 / whole, 0.0)
         return lead
 
-    lax.fori_loop(0, planes - 1, body, jnp.zeros(k.shape[1:], F32), unroll=UNROLL)
+    lax.fori_loop(0, planes - 1, body, jnp.zeros(k.shape[1:], F32), unroll=unrolled(k.shape[1:], planes - 1))
 
 
 def beside(x, w, i):
+    if len(w) == 4:
+        return beside_packed(x, w, i)
     wl, ws, wz = w
     here = x[i]
     rows, lanes = ws[i], wz[i]
@@ -153,13 +159,13 @@
     def start(i):
         first[i] = b[i] * inverse[i] * (1.0 / (scale * THETA))
 
-    loop(*outer, start)
+    loop(*outer, start, b.shape[1:])
 
     def sweep(i):
         near = beside(first, w, i)
         second[i] = (1.0 + KEEP + GAIN * (THETA - 1.0)) * first[i] + GAIN * (inverse[i] * near)
 
-    loop(*inner, sweep)
+    loop(*inner, sweep, b.shape[1:])
 
 
 def post_smooth(b, first, second, w, inverse, scale, outer, inner):
@@ -168,7 +174,7 @@
         near = beside(first, w, i)
         second[i] = x + ((b[i] * (1.0 / scale) + near) * inverse[i] - x) * (1.0 / THETA)
 
-    loop(*outer, sweep)
+    loop(*outer, sweep, b.shape[1:])
 
     def last(i):
         x = second[i]
@@ -176,16 +182,15 @@
         step = KEEP * (x - first[i]) + GAIN * ((b[i] * (1.0 / scale) + near) * inverse[i] - x)
         first[i] = x + step
 
-    loop(*inner, last)
+    loop(*inner, last, b.shape[1:])
 
 
 def residual(b, field, w, total, scale, i):
     return b[i] - scale * (total[i] * field[i] - beside(field, w, i))
 
 
-def coarser(pairs, halves, valid):
+def coarser(pairs, halves, matrix):
     planes, rows, lanes = pairs.shape
-    matrix = halving(lanes, halves.shape[2], valid)
     halves[...] = pick(pairs.reshape(planes * rows, lanes), matrix).reshape(halves.shape)
     count = rows // 2
     return halves[:, pl.ds(0, count, stride=2), :] + halves[:, pl.ds(1, count, stride=2), :]
@@ -201,20 +206,27 @@
     return (quarter[0] + quarter[1]) + odd
 
 
-def spread_copies(out, *fields):
+def spread_copies(out, held, sems, *fields):
     for f, rows in enumerate(fields):
         size, count = rows.shape[0], rows.shape[1]
         for i in range(size):
-            out[0, pl.ds(f * size * count + i, count, stride=size), :] = rows[i]
-
-    def copy(d):
-        out[d] = out[0]
-
-    loop(1, out.shape[0], copy)
-
-
-def slab_kernel(b, k, up_out, down_out):
+            held[0, pl.ds(f * size * count + i, count, stride=size), :] = rows[i]
+    group = held.shape[0]
+    for d in range(1, group):
+        held[d] = held[0]
+    copies = []
+    for d in range(out.shape[0] // group):
+        there = out.at[d * group : (d + 1) * group]
+        copies.append(pltpu.make_async_copy(held, there, sems.at[d]))
+    for copy in copies:
+        copy.start()
+    return copies
+
+
+def slab_kernel(b, k, up_out, down_out, b_out, k_out):
     rows = k.shape[1]
+    b_out[...] = b[...]
+    k_out[...] = k[...]
     for r in range(K0):
         up_out[r] = k[:, rows - K0 + r, :]
         down_out[r] = k[:, r, :]
@@ -223,18 +235,23 @@
         down_out[K0 + r] = b[:, r, :]
 
 
-def conduct_kernel(k, k1, k2, pairs, halves, pairs1, halves1):
+def conduct_kernel(k, message, k1, pairs, halves, pairs1, halves1, held, sems):
     def add(j):
         pairs[j] = k[2 * j] + k[2 * j + 1]
 
-    loop(0, pairs.shape[0], add)
-    k1[...] = coarser(pairs[...], halves, k.shape[2])
+    loop(0, pairs.shape[0], add, pairs.shape[1:])
+    lanes = k.shape[2]
+    k1[...] = coarser(pairs[...], halves, halving(lanes, lanes // 2, lanes))
 
     def add1(j):
         pairs1[j] = k1[2 * j] + k1[2 * j + 1]
 
-    loop(0, pairs1.shape[0], add1)
-    k2[...] = packed(pairs1[...], halves1, k1.shape[2])
+    loop(0, pairs1.shape[0], add1, pairs1.shape[1:])
+    wait(spread_copies(message, held, sems, packed(pairs1[...], halves1, k1.shape[2])))
+
+
+def after_kernel(message, _low, _high, out):
+    pass
 
 
 def widen(out, own, low, high, count):
@@ -291,8 +308,8 @@
         both = residual(b, second, w, total, 1.0, i) + residual(b, second, w, total, 1.0, i + 1)
         pairs[j] = both[0:rows]
 
-    loop(0, own // 2, restrict)
-    b1_out[...] = coarser(pairs[...], halves, lanes)
+    loop(0, own // 2, restrict, (2 * b.shape[1], b.shape[2]))
+    b1_out[...] = coarser(pairs[...], halves, halving(lanes, lanes // 2, lanes))
     s_out[...] = second[K0 : K0 + own, 0:rows, :]
     half, count = b1_out.shape[0], b1_out.shape[1]
     for out, k_from, b_from in ((up_out, count - K1, count - B1), (down_out, 0, 0)):
@@ -314,9 +331,9 @@
 
 
 def middle_down_kernel(
-    k_own, b_own, low, high, s, k2,
-    wl, ws, wz, inverse, b, s_out, copies, up_out, down_out,
-    total, k, first, second, pairs, halves,
+    k_own, b_own, low, high,
+    message, wl, ws, wz, inverse, b, s_out,
+    total, k, first, second, pairs, halves, held, sems,
 ):
     scale = 0.25
     join(k, k_own, lambda r: low[r], lambda r: high[r], K1, K1)
@@ -332,67 +349,66 @@
         both = residual(b, second, w, total, scale, i) + residual(b, second, w, total, scale, i + 1)
         pairs[j] = both[0:rows]
 
-    loop(0, own // 2, restrict)
-    spread_copies(copies, k2[...], packed(pairs[...], halves, lanes))
+    loop(0, own // 2, restrict, (2 * b.shape[1], b.shape[2]))
+    copies = spread_copies(message, held, sems, packed(pairs[...], halves, lanes))
     s_out[...] = second[K1 : K1 + own, 0:rows, :]
-    fine, fine_rows = s.shape[0], s.shape[1]
-    for out, from0, from1 in ((up_out, fine_rows - S0, rows - S1), (down_out, 0, 0)):
-        for r in range(S0):
-            for h in range(2):
-                at = (2 * r + h) * fine
-                out[at : at + fine] = s[:, from0 + r, h * lanes : (h + 1) * lanes]
-        for r in range(S1):
-            at = 2 * S0 * fine + r * own
-            out[at : at + own] = s_out[:, from1 + r, :]
-
-
-def widen_fields_kernel(s, s1, low, high, s_out, s1_out, up_out, down_out):
-    fine, own, lanes = s.shape[0], s1.shape[0], s1.shape[2]
-
-    def wide(ref):
-        def get(r):
-            at = 2 * r * fine
-            return jnp.concatenate([ref[at : at + fine], ref[at + fine : at + 2 * fine]], axis=1)
-
-        return get
-
-    def block(ref):
-        def get(r):
-            at = 2 * S0 * fine + r * own
-            return ref[at : at + own]
-
-        return get
-
-    widen(s_out, s, wide(low), wide(high), S0)
-    widen(s1_out, s1, block(low), block(high), S1)
-    rows, rows1 = s_out.shape[1], s1_out.shape[1]
+    wait(copies)
+
+
+def field_planes_kernel(s, s1, up_out, down_out):
+    fine, rows, own, rows1, lanes = s.shape[0], s.shape[1], s1.shape[0], s1.shape[1], s1.shape[2]
     for out, from0, from1 in ((up_out, fine - S0, own - S1), (down_out, 0, 0)):
         for r in range(S0):
             for h in range(2):
                 at = (2 * r + h) * rows
-                out[at : at + rows] = s_out[from0 + r, :, h * lanes : (h + 1) * lanes]
+                out[at : at + rows] = s[from0 + r, :, h * lanes : (h + 1) * lanes]
         for r in range(S1):
             at = 2 * S0 * rows + r * rows1
-            out[at : at + rows1] = s1_out[from1 + r]
+            out[at : at + rows1] = s1[from1 + r]
+
+
+def split_lanes(ref, rows):
+    def get(r):
+        at = 2 * r * rows
+        return jnp.concatenate([ref[at : at + rows], ref[at + rows : at + 2 * rows]], axis=1)
+
+    return get
+
+
+def from_row(ref, first, rows):
+    def get(r):
+        return ref[first + r * rows : first + (r + 1) * rows]
+
+    return get
+
+
+def field_rows_kernel(s, s1, low, high, s_out, s1_out, up_out, down_out):
+    rows, rows1, lanes = s.shape[1], s1.shape[1], s1.shape[2]
+    join(s_out, s, split_lanes(low, rows), split_lanes(high, rows), S0, S0)
+    first = 2 * S0 * rows
+    join(s1_out, s1, from_row(low, first, rows1), from_row(high, first, rows1), S1, S1)
+    fine, own = s_out.shape[0], s1_out.shape[0]
+    for out, from0, from1 in ((up_out, rows - S0, rows1 - S1), (down_out, 0, 0)):
+        for r in range(S0):
+            for h in range(2):
+                at = (2 * r + h) * fine
+                out[at : at + fine] = s_out[:, from0 + r, h * lanes : (h + 1) * lanes]
+        for r in range(S1):
+            at = 2 * S0 * fine + r * own
+            out[at : at + own] = s1_out[:, from1 + r, :]
 
 
 def unpack(received, out, first, block_x, block_y, across, along):
-    planes, rows, lanes = out.shape
-    lane = iota((block_x, lanes), 1)
-    for end in (0, planes - 1):
-        out[end] = jnp.zeros((rows, lanes), F32)
+    clear_ends(out)
 
     def place(column):
         for row in range(across):
             for j in range(block_y // 2):
                 piece = received[row * along + column, pl.ds(first + j * block_x, block_x), :]
-                at = 1 + column * block_y + 2 * j
-                span = slice(row * block_x, (row + 1) * block_x)
-                out[at, span, :] = jnp.where(lane < lanes // 2, piece, 0.0)
-                other = pltpu.roll(piece, lanes // 2, 1)
-                out[at + 1, span, :] = jnp.where(lane < lanes // 2, other, 0.0)
-
-    loop(0, along, place)
+                at = 1 + column * (block_y // 2) + j
+                out[at, row * block_x : (row + 1) * block_x, :] = piece
+
+    loop(0, along, place, (out.shape[1], block_y // 2 * out.shape[2]))
 
 
 def clear_ends(ref):
@@ -400,38 +416,62 @@
         ref[end] = jnp.zeros(ref.shape[1:], F32)
 
 
-def coarse_down(b, w, total, inverse, first, second, scale, valid, pairs, halves):
+def across_up(x, after):
+    half = x.shape[1] // 2
+    return pltpu.roll(jnp.where(iota(x.shape, 1) < half, after, x), half, 1)
+
+
+def across_down(x, before):
+    half = x.shape[1] // 2
+    return pltpu.roll(jnp.where(iota(x.shape, 1) < half, x, before), half, 1)
+
+
+def weigh_packed(k, wl, wl_low, ws, wz, total, inverse):
+    planes = k.shape[0]
+
+    def body(i, before):
+        here = k[i]
+        lead = face(here, across_up(here, k[i + 1]))
+        lead_low = across_down(lead, before)
+        rows, row_sum = sided(here, 0, here.shape[0])
+        lanes, lane_sum = sided(here, 1, here.shape[1] // 2)
+        wl[i] = lead
+        wl_low[i] = lead_low
+        ws[i] = rows
+        wz[i] = lanes
+        whole = (lead_low + lead) + (row_sum + lane_sum)
+        there = here > 0.0
+        total[i] = jnp.where(there, whole, 0.0)
+        inverse[i] = jnp.where(there, 1.0 / whole, 0.0)
+        return lead
+
+    lax.fori_loop(0, planes - 1, body, jnp.zeros(k.shape[1:], F32), unroll=unrolled(k.shape[1:], planes - 1))
+
+
+def beside_packed(x, w, i):
+    wl, wl_low, ws, wz = w
+    here = x[i]
+    rows, lanes = ws[i], wz[i]
+    out = wl[i] * across_up(here, x[i + 1]) + wl_low[i] * across_down(here, x[i - 1])
+    out = out + (rows * up(here, 0) + down(rows * here, 0))
+    return out + (lanes * up(here, 1) + down(lanes * here, 1))
+
+
+def coarse_pre(b, w, inverse, first, second, scale):
     ends = (1, b.shape[0] - 1)
     clear_ends(first)
     clear_ends(second)
     pre_smooth(b, first, second, w, inverse, scale, ends, ends)
 
-    def restrict(j):
-        i = 2 * j + 1
-        pairs[j] = residual(b, second, w, total, scale, i) + residual(
-            b, second, w, total, scale, i + 1
-        )
-
-    loop(0, pairs.shape[0], restrict)
-    return coarser(pairs[...], halves, valid)
-
-
-def coarse_up(correction, b, w, inverse, first, second, scale, valid, grown):
-    planes, rows, lanes = b.shape
-    half, count = correction.shape[0], correction.shape[1]
-    wide = pick(correction.reshape(half * count, lanes), doubling(lanes, lanes, valid // 2))
-    wide = wide.reshape(half, count, lanes)
-    grown[:, pl.ds(0, count, stride=2), :] = wide
-    grown[:, pl.ds(1, count, stride=2), :] = wide
-
-    def add(j):
-        i = 2 * j + 1
-        first[i] = second[i] + grown[j]
-        first[i + 1] = second[i + 1] + grown[j]
-
-    loop(0, half, add)
-    ends = (1, planes - 1)
-    post_smooth(b, first, second, w, inverse, scale, ends, ends)
+
+def widened(x, matrix):
+    planes, rows, lanes = x.shape
+    return pick(x.reshape(planes * rows, lanes), matrix).reshape(planes, rows, matrix.shape[1])
+
+
+def twice(out, x):
+    out[:, pl.ds(0, x.shape[1], stride=2), :] = x
+    out[:, pl.ds(1, x.shape[1], stride=2), :] = x
 
 
 def bottom(k, b, scale):
@@ -475,47 +515,72 @@
 
 
 def coarse_kernel(
-    valid, received, region,
-    wl2, ws2, wz2, total2, inverse2, k2, b2, first2, second2, pairs2, halves2,
+    valid, received_k, received, region,
+    wl2, low2, ws2, wz2, total2, inverse2, k2, b2, first2, second2, pairs2, halves2,
     wl3, ws3, wz3, total3, inverse3, k3, b3, first3, second3, pairs3, halves3,
 ):
     planes, rows, lanes = b2.shape
     across, along = lax.axis_size("gx"), lax.axis_size("gy")
-    block_x, block_y = rows // across, (planes - 2) // along
-    unpack(received, k2, 0, block_x, block_y, across, along)
-    unpack(received, b2, block_x * block_y // 2, block_x, block_y, across, along)
-
-    def add2(j):
-        pairs2[j] = k2[2 * j + 1] + k2[2 * j + 2]
-
-    loop(0, pairs2.shape[0], add2)
+    block_x, block_y = rows // across, 2 * (planes - 2) // along
+    unpack(received_k, k2, 0, block_x, block_y, across, along)
+    unpack(received, b2, 0, block_x, block_y, across, along)
+    own3, half = planes - 2, valid // 2
+    row, col = iota((lanes, lanes), 0), iota((lanes, lanes), 1)
+    matrix2 = jnp.where(lax.rem(row, valid) // 2 == col, 0.125, 0.0).astype(BF16)
+    matrix3 = halving(lanes, lanes, half)
     clear_ends(k3)
-    own3 = k3.shape[0] - 2
-    k3[1 : own3 + 1] = coarser(pairs2[...], halves2, valid)
+    k3[1 : own3 + 1] = coarser(k2[1 : own3 + 1], halves2, matrix2)
 
     def add3(j):
         pairs3[j] = k3[2 * j + 1] + k3[2 * j + 2]
 
-    loop(0, pairs3.shape[0], add3)
-    k4 = coarser(pairs3[...], halves3, valid // 2)
-    weigh(k2, wl2, ws2, wz2, total2, inverse2, True, False)
+    loop(0, pairs3.shape[0], add3, pairs3.shape[1:])
+    k4 = coarser(pairs3[...], halves3, matrix3)
+    weigh_packed(k2, wl2, low2, ws2, wz2, total2, inverse2)
     weigh(k3, wl3, ws3, wz3, total3, inverse3, True, False)
-    w2, w3 = (wl2, ws2, wz2), (wl3, ws3, wz3)
+    w2, w3 = (wl2, low2, ws2, wz2), (wl3, ws3, wz3)
+    scale2, scale3 = 0.25**2, 0.25**3
+    coarse_pre(b2, w2, inverse2, first2, second2, scale2)
+
+    def rest2(j):
+        pairs2[j] = residual(b2, second2, w2, total2, scale2, j + 1)
+
+    loop(0, own3, rest2, pairs2.shape[1:])
     clear_ends(b3)
-    b3[1 : own3 + 1] = coarse_down(
-        b2, w2, total2, inverse2, first2, second2, 0.25**2, valid, pairs2, halves2
-    )
-    b4 = coarse_down(
-        b3, w3, total3, inverse3, first3, second3, 0.25**3, valid // 2, pairs3, halves3
-    )
-    x4 = bottom(k4, b4, 0.25**4)
-    coarse_up(x4, b3, w3, inverse3, first3, second3, 0.25**3, valid // 2, pairs3)
-    coarse_up(first3[1 : own3 + 1], b2, w2, inverse2, first2, second2, 0.25**2, valid, pairs2)
-    column, row = lax.axis_index("gy"), lax.axis_index("gx")
+    b3[1 : own3 + 1] = coarser(pairs2[...], halves2, matrix2)
+    coarse_pre(b3, w3, inverse3, first3, second3, scale3)
+
+    def rest3(j):
+        i = 2 * j + 1
+        pairs3[j] = residual(b3, second3, w3, total3, scale3, i) + residual(
+            b3, second3, w3, total3, scale3, i + 1
+        )
+
+    loop(0, pairs3.shape[0], rest3, pairs3.shape[1:])
+    x4 = bottom(k4, coarser(pairs3[...], halves3, matrix3), 0.25**4)
+    twice(pairs3, widened(x4, doubling(lanes, lanes, half // 2)))
+
+    def add_up3(j):
+        for side in range(2):
+            i = 2 * j + 1 + side
+            first3[i] = second3[i] + pairs3[j]
+
+    loop(0, pairs3.shape[0], add_up3, pairs3.shape[1:])
+    ends = (1, own3 + 1)
+    post_smooth(b3, first3, second3, w3, inverse3, scale3, ends, ends)
+    matrix = jnp.where((lax.rem(col, valid) // 2 == row) & (row < half), 1.0, 0.0).astype(BF16)
+    twice(pairs2, widened(first3[1 : own3 + 1], matrix))
+
+    def add_up2(i):
+        first2[i] = second2[i] + pairs2[i - 1]
+
+    loop(1, own3 + 1, add_up2, pairs2.shape[1:])
+    post_smooth(b2, first2, second2, w2, inverse2, scale2, ends, ends)
+    column, place = lax.axis_index("gy"), lax.axis_index("gx")
     for q in range(region.shape[0]):
-        plane = column * block_y + q - EDGE
+        plane = column * (block_y // 2) + q - EDGE // 2
         for side in range(3):
-            block = row + side - 1
+            block = place + side - 1
             there = (plane >= 0) & (plane < planes - 2) & (block >= 0) & (block < across)
             start = pl.multiple_of(jnp.clip(block, 0, across - 1) * block_x, block_x)
             value = first2[1 + jnp.clip(plane, 0, planes - 3), pl.ds(start, block_x), :]
@@ -523,47 +588,32 @@
 
 
 def fine_up_kernel(
-    valid, region, wl1, ws1, wz1, inverse1, b1, s1_own, stash, s_own, low, high,
+    region, wl1, ws1, wz1, inverse1, b1, s1_own, stash, s_own, low, high,
     field_out, residual_out,
-    wl, ws, wz, total, b, inverse, first1, second1, grown, s, second, tall, thick, sems,
+    wl, ws, wz, total, b, inverse, first1, second1, grown, s, second, tall, thick, rest,
+    sems, out_sems,
 ):
     copies = move((wl, ws, wz, total, b), stash, sems, True)
     planes1, rows1, lanes1 = b1.shape
     planes, rows, lanes = b.shape
     w1, w = (wl1, ws1, wz1), (wl, ws, wz)
-
-    def wide(ref):
-        def get(r):
-            at = 2 * r * rows
-            return jnp.concatenate([ref[at : at + rows], ref[at + rows : at + 2 * rows]], axis=1)
-
-        return get
-
-    def block(ref):
-        def get(r):
-            at = 2 * S0 * rows + r * rows1
-            return ref[at : at + rows1]
-
-        return get
-
-    join(s, s_own, wide(low), wide(high), S0, S0)
-    join(first1, s1_own, block(low), block(high), S1, S1)
-    count_y, count_x = region.shape[0], region.shape[1]
-    block_x = count_x // 3
-    expanded = pick(region[...].reshape(count_y * count_x, lanes1), doubling(lanes1, lanes1, valid))
-    expanded = expanded.reshape(count_y, count_x, lanes1)
-    own_y = count_y - 2 * EDGE
+    widen(s, s_own, split_lanes(low, planes), split_lanes(high, planes), S0)
+    first = 2 * S0 * planes
+    widen(first1, s1_own, from_row(low, first, planes1), from_row(high, first, planes1), S1)
+    count_y, block_x = region.shape[0], region.shape[1] // 3
+    expanded = widened(region[...], doubling(lanes1, 2 * lanes1, lanes1))
     for q in range(block_x + 2 * EDGE):
         line = expanded[:, block_x - EDGE + q, :]
-        line = jnp.concatenate([line[EDGE:], line[:EDGE]], axis=0)
-        grown[q, pl.ds(0, count_y, stride=2), :] = line
-        grown[q, pl.ds(1, count_y, stride=2), :] = line
+        line = jnp.concatenate([line[EDGE // 2 :], line[: EDGE // 2]], axis=0)
+        for r in range(4):
+            half = line[:, (r // 2) * lanes1 : (r // 2 + 1) * lanes1]
+            grown[q, pl.ds(r, count_y, stride=4), :] = half
 
     def add1(q):
         for side in range(2):
             first1[2 * q + side] = first1[2 * q + side] + grown[q]
 
-    loop(0, block_x + 2 * EDGE, add1)
+    loop(0, block_x + 2 * EDGE, add1, b1.shape[1:])
     post_smooth(
         b1, first1, second1, w1, inverse1, 0.25, (1, planes1 - 1), (2, planes1 - 2)
     )
@@ -584,25 +634,35 @@
             i = 2 * q + side - 1
             s[i] = s[i] + thick[q]
 
-    loop(1, count - 1, add)
+    loop(1, count - 1, add, b.shape[1:])
     wait(copies)
 
     def invert(i):
         inverse[i] = jnp.where(total[i] > 0.0, 1.0 / total[i], 0.0)
 
-    loop(1, planes - 1, invert)
+    loop(1, planes - 1, invert, b.shape[1:])
     post_smooth(b, s, second, w, inverse, 1.0, (1, planes - 1), (2, planes - 2))
     own, own_rows = field_out.shape[0], field_out.shape[1]
+    mine = s.at[K0 : K0 + own, 0:own_rows]
+    copies = [pltpu.make_async_copy(mine, field_out, out_sems.at[0])]
+    copies[0].start()
 
     def finish(j):
-        i = j + K0
-        field_out[j] = s[i, 0:own_rows, :]
-        residual_out[j] = residual(b, s, w, total, 1.0, i)[0:own_rows]
-
-    loop(0, own, finish)
-
-
-def call(kernel, outs, scratch=(), held=0, kept=(), sems=()):
+        rest[j] = residual(b, s, w, total, 1.0, j + K0)[0:own_rows]
+
+    parts = out_sems.shape[0] - 1
+    for part in range(parts):
+        begin, end = own * part // parts, own * (part + 1) // parts
+        loop(begin, end, finish, b.shape[1:])
+        copy = pltpu.make_async_copy(
+            rest.at[begin:end], residual_out.at[begin:end], out_sems.at[1 + part]
+        )
+        copy.start()
+        copies.append(copy)
+    wait(copies)
+
+
+def call(kernel, outs, scratch=(), held=0, kept=(), sems=(), alias=None):
     def run(*operands):
         inputs = [o.shape for i, o in enumerate(operands) if i not in kept]
         shapes = inputs + list(outs[held:]) + list(scratch)
@@ -616,6 +676,7 @@
             out_specs=[pl.BlockSpec(memory_space=place) for place in out_places],
             scratch_shapes=[pltpu.VMEM(shape, F32) for shape in scratch]
             + [pltpu.SemaphoreType.DMA((n,)) for n in sems],
+            input_output_aliases=alias or {},
             compiler_params=pltpu.CompilerParams(vmem_limit_bytes=4 * words + SPARE),
         )(*operands)
 
@@ -634,15 +695,20 @@
     qx, qy = hx // 2, hy // 2
     both = ("gx", "gy")
     tall, tall1 = eight(by + 2 * K0), eight(hy + 2 * K1)
-    pieces = (devices, qx * qy, hz)
+    pieces = (devices, qx * qy // 2, hz)
 
     slab = (K0 + B0, bx, nz)
-    up_rows, down_rows = call(slab_kernel, [slab, slab])(right_side, coefficient)
+    up_rows, down_rows, right_side, coefficient = call(
+        slab_kernel, [slab, slab, (bx, by, nz), (bx, by, nz)]
+    )(right_side, coefficient)
     low, high = rotate(up_rows, "gy", 1), rotate(down_rows, "gy", -1)
-    k1, k2 = call(
+    group = 4
+    message, k1 = call(
         conduct_kernel,
-        [(hx, hy, hz), (qx, qy // 2, hz)],
-        [(hx, by, nz), (hx, by, hz), (qx, hy, hz), (qx, hy, hz)],
+        [pieces, (hx, hy, hz)],
+        [(hx, by, nz), (hx, by, hz), (qx, hy, hz), (qx, hy, hz), (group, *pieces[1:])],
+        held=1,
+        sems=(devices // group,),
     )(coefficient)
 
     plane = (bx, tall, nz)
@@ -651,6 +717,11 @@
         right_side, coefficient, low, high
     )
     low, high = rotate(up_planes, "gx", 1), rotate(down_planes, "gx", -1)
+
+    (message,) = call(after_kernel, [pieces], held=1, kept=(0, 1, 2), alias={0: 0})(
+        message, low, high
+    )
+    k2 = lax.all_to_all(message, both, 0, 0, tiled=True)
 
     block = (bx + 2 * K0, tall, nz)
     slab = (K1 + B1, hx, hz)
@@ -670,38 +741,42 @@
     low, high = rotate(up_planes, "gx", 1), rotate(down_planes, "gx", -1)
 
     block1 = (hx + 2 * K1, tall1, hz)
-    slab = (2 * S0 * bx + S1 * hx, hz)
-    *kept1, s1, copies, up_rows, down_rows = call(
+    message, *kept1, s1 = call(
         middle_down_kernel,
-        [block1] * 5 + [(hx, hy, hz), pieces, slab, slab],
-        [block1] * 4 + [(qx, hy, hz), (qx, hy, hz)],
-    )(k1_own, b1_own, low, high, s, k2)
-    received = lax.all_to_all(copies, both, 0, 0, tiled=True)
+        [pieces] + [block1] * 5 + [(hx, hy, hz)],
+        [block1] * 4 + [(qx, hy, hz), (qx, hy, hz), (group, *pieces[1:])],
+        held=1,
+        sems=(devices // group,),
+    )(k1_own, b1_own, low, high)
+    received = lax.all_to_all(message, both, 0, 0, tiled=True)
+
+    slab = (2 * S0 * by + S1 * hy, hz)
+    up_planes, down_planes = call(field_planes_kernel, [slab, slab])(s, s1)
+    low, high = rotate(up_planes, "gx", 1), rotate(down_planes, "gx", -1)
+    slab = (2 * S0 * block[0] + S1 * block1[0], hz)
+    s_own, s1_own, up_rows, down_rows = call(
+        field_rows_kernel, [(block[0], by, nz), (block1[0], hy, hz), slab, slab]
+    )(s, s1, low, high)
     low, high = rotate(up_rows, "gy", 1), rotate(down_rows, "gy", -1)
-    slab = (2 * S0 * tall + S1 * tall1, hz)
-    s_own, s1_own, up_planes, down_planes = call(
-        widen_fields_kernel, [plane, (hx, tall1, hz), slab, slab]
-    )(s, s1, low, high)
-    low, high = rotate(up_planes, "gx", 1), rotate(down_planes, "gx", -1)
 
     x2, y2 = across * qx, along * qy
-    level2, level3 = ((y2 // s + 2, x2 // s, hz) for s in (1, 2))
+    level2, level3 = (y2 // 2 + 2, x2, hz), (y2 // 2 + 2, x2 // 2, hz)
     half2, half3 = (y2 // 2, x2, hz), (y2 // 4, x2 // 2, hz)
-    valid = nz // 4
     (region,) = call(
-        partial(coarse_kernel, valid),
-        [(qy + 2 * EDGE, 3 * qx, hz)],
-        [level2] * 9 + [half2] * 2 + [level3] * 9 + [half3] * 2,
-    )(received)
+        partial(coarse_kernel, nz // 4),
+        [(qy // 2 + EDGE, 3 * qx, hz)],
+        [level2] * 10 + [half2] * 2 + [level3] * 9 + [half3] * 2,
+    )(k2, received)
 
     count = hx + 2 * EDGE
     field, rest = call(
-        partial(fine_up_kernel, valid),
+        fine_up_kernel,
         [(bx, by, nz)] * 2,
         [block] * 6 + [block1, block1, (qx + 2 * EDGE, tall1, hz)]
-        + [block, block, (count, tall, hz), (count, tall, nz)],
+        + [block, block, (count, tall, hz), (count, tall, nz), (bx, by, nz)],
+        held=2,
         kept=(7,),
-        sems=(5,),
+        sems=(5, 5),
     )(region, *kept1, s1_own, stash, s_own, low, high)
     return field, rest
 

time: 79.9 us -> 72.2 us (0.904)
  waiting for transfers between devices: 25.2 us -> 16.5 us
  starting transfers between devices: 27.6 us -> 32.4 us
  local copies, waits for them, and re-layouts: 4.16 us -> 2.08 us
  Pallas kernels: 21.8 us -> 20.2 us
    ppermute x12, waiting for transfers between devices: 24.9 us -> 15.8 us  [rotate(): lax.ppermute(value, axis, [(i, (i + shift) % size) for i in range(size)])]
    all_to_all x1 -> x2, starting transfers between devices: 6.54 us -> 11.2 us  [the longest x1 6.21 us: per_device(): received = lax.all_to_all(message, both, 0, 0, tiled=True)]
    unnamed x8 -> x4, local copies, waits for them, and re-layouts: 4.16 us -> 2.08 us
    pallas_call x9 -> x11, Pallas kernels: 21.8 us -> 20.2 us  [run(): pl.pallas_call(kernel, out_shape=[jax.ShapeDtypeStruct(shape, F32) for sh...]
  transfers between devices with their start and end apart: 13 -> 14, of which waited for: 8 -> 11; matrix products, arithmetic and copies ran while one was open for 0% -> 0% of each run, Pallas kernels for 9% -> 19%
where the time goes in v4:
time: 72.2 us; the launch traced here: 71.9 us
  starting transfers between devices  32.4 us (45%)
  Pallas kernels  20.2 us (28%)
  waiting for transfers between devices  16.5 us (23%)
  local copies, waits for them, and re-layouts  2.08 us (3%)
  between operations  0.75 us (1%)
    ppermute x12, starting transfers between devices, rotate(): lax.ppermute(value, axis, [(i, (i + shift) % size) for i in range(size)])  21.1 us
    pallas_call x11, Pallas kernels, run(): pl.pallas_call(kernel, out_shape=[jax.ShapeDtypeStruct(shape, F32) for sh...  20.2 us
    ppermute x12, waiting for transfers between devices, rotate(): lax.ppermute(value, axis, [(i, (i + shift) % size) for i in range(size)])  15.8 us
    all_to_all x1, starting transfers between devices, per_device(): received = lax.all_to_all(message, both, 0, 0, tiled=True)  6.21 us
    all_to_all x1, starting transfers between devices, per_device(): k2 = lax.all_to_all(message, both, 0, 0, tiled=True)  5.03 us
    unnamed x4, local copies, waits for them, and re-layouts  2.08 us
  transfers between devices with their start and end apart: 14, of which 11 were waited for; matrix products, arithmetic and copies ran while one was open for 0% of the time, Pallas kernels for 19%

profile of v4, /device:TPU:0, one launch (start us, length us, event | category | flops | bytes accessed | tf_op | source)
XLA Modules:
  0.0 71.9 jit_solution(16936021408170044048)
XLA Ops:
  0.6 0.0 copy-start
  0.6 1.0 %copy-done = f32[32,16,256]{2,1,0:T(8,128)S(1)} copy-done((f32[32,16,256]{2,1,0:T(8,128)S(1)}, f32[32,16,256]{2,1,0:T(8,128)}, u32[]{:S(2)}) %copy-start) | copy-done | bytes 524312
  1.7 0.0 copy-start.1
  1.7 1.0 %copy-done.1 = f32[32,16,256]{2,1,0:T(8,128)S(1)} copy-done((f32[32,16,256]{2,1,0:T(8,128)S(1)}, f32[32,16,256]{2,1,0:T(8,128)}, u32[]{:S(2)}) %copy-start.1) | copy-done | bytes 524312
  2.7 0.2 shard_map.41
  2.9 3.0 %collective-permute-start = (f32[5,32,256]{2,1,0:T(8,128)S(1)}, f32[5,32,256]{2,1,0:T(8,128)S(1)}, u32[]{:S(2)}, u32[]{:S(2)}) collective-permute-start(f32[5,32,256]{2,1,0:T(8,128)S(1)} %get-tuple-element.37), channel_id=1, source_target_pairs={{0,1},{1,2},{2,3},{3,4},{4,5},{5,6},{6,7},{7,0},{8,9},{9,10},{10,1... | collective-permute-start | bytes 491528 | tf_op jit(solution)/shard_map/ppermute | solution.py:35
  5.9 3.1 %collective-permute-start.1 = (f32[5,32,256]{2,1,0:T(8,128)S(1)}, f32[5,32,256]{2,1,0:T(8,128)S(1)}, u32[]{:S(2)}, u32[]{:S(2)}) collective-permute-start(f32[5,32,256]{2,1,0:T(8,128)S(1)} %get-tuple-element.38), channel_id=1, source_target_pairs={{0,7},{1,0},{2,1},{3,2},{4,3},{5,4},{6,5},{7,6},{8,15},{9,8},{10,9... | collective-permute-start | bytes 491528 | tf_op jit(solution)/shard_map/ppermute | solution.py:35
  9.0 4.2 %collective-permute-done.low = f32[5,32,256]{2,1,0:T(8,128)S(1)} collective-permute-done((f32[5,32,256]{2,1,0:T(8,128)S(1)}, f32[5,32,256]{2,1,0:T(8,128)S(1)}, u32[]{:S(2)}, u32[]{:S(2)}) %collective-permute-start) | collective-permute-done | bytes 163872 | tf_op jit(solution)/shard_map/ppermute | solution.py:35
  13.2 1.8 %collective-permute-done.1.high = f32[5,32,256]{2,1,0:T(8,128)S(1)} collective-permute-done((f32[5,32,256]{2,1,0:T(8,128)S(1)}, f32[5,32,256]{2,1,0:T(8,128)S(1)}, u32[]{:S(2)}, u32[]{:S(2)}) %collective-permute-start.1) | collective-permute-done | bytes 163872 | tf_op jit(solution)/shard_map/ppermute | solution.py:35
  15.1 0.2 shard_map.43
  15.3 0.1 collective-permute-start.2
  15.3 1.7 %collective-permute-start.3 = (f32[5,24,256]{2,1,0:T(8,128)S(1)}, f32[5,24,256]{2,1,0:T(8,128)S(1)}, u32[]{:S(2)}, u32[]{:S(2)}) collective-permute-start(f32[5,24,256]{2,1,0:T(8,128)S(1)} %get-tuple-element.40), channel_id=1, source_target_pairs={{0,24},{8,0},{16,8},{24,16},{1,25},{9,1},{17,9},{25,17},{2,26},{10... | collective-permute-start | bytes 368648 | tf_op jit(solution)/shard_map/ppermute | solution.py:35
  17.1 1.2 %shard_map.42 = (f32[32,16,128]{2,1,0:T(8,128)}, f32[16,8,128]{2,1,0:T(8,128)S(1)}) custom-call(f32[32,16,256]{2,1,0:T(8,128)S(1)} %get-tuple-element.34.k), custom_call_target="tpu_custom_call" | custom-call | tf_op jit(solution)/shard_map/pallas_call | solution.py:672
  18.3 1.3 %collective-permute-done.2._low.low = f32[5,24,256]{2,1,0:T(8,128)S(1)} collective-permute-done((f32[5,24,256]{2,1,0:T(8,128)S(1)}, f32[5,24,256]{2,1,0:T(8,128)S(1)}, u32[]{:S(2)}, u32[]{:S(2)}) %collective-permute-start.2) | collective-permute-done | bytes 122912 | tf_op jit(solution)/shard_map/ppermute | solution.py:35
  19.6 0.4 collective-permute-done.3._high.high
  20.0 5.0 %all-to-all-start = ((f32[32,16,128]{2,1,0:T(8,128)}), f32[32,16,128]{2,1,0:T(8,128)S(1)}, u32[]{:S(2)}, u32[]{:S(2)}) async-start(f32[32,16,128]{2,1,0:T(8,128)} %shard_map.44), calls=%async_computation | async-start | bytes 524288 | tf_op jit(solution)/shard_map/all_to_all | solution.py:724
  25.0 4.4 %shard_map.45 = (f32[2920,24,256]{2,1,0:T(8,128)}, f32[32,16,256]{2,1,0:T(8,128)S(1)}, f32[16,8,128]{2,1,0:T(8,128)S(1)}, f32[7,16,128]{2,1,0:T(8,128)S(1)}, f32[7,16,128]{2,1,0:T(8,128)S(1)}) custom-call(f32[32,24,256]{2,1,0:T(8,128)S(1)} %get-tuple-element.42.k_own, f32[32,24,256]{2,1,0:T(8,128)S(1)} %get-tuple-element.43.b_own, ...), custom_call_target="tpu_custom_call" | custom-call | tf_op jit(solution)/shard_map/pallas_call | solution.py:672
  29.4 1.8 %collective-permute-start.4 = (f32[7,16,128]{2,1,0:T(8,128)S(1)}, f32[7,16,128]{2,1,0:T(8,128)S(1)}, u32[]{:S(2)}, u32[]{:S(2)}) collective-permute-start(f32[7,16,128]{2,1,0:T(8,128)S(1)} %get-tuple-element.45), channel_id=1, source_target_pairs={{0,1},{1,2},{2,3},{3,4},{4,5},{5,6},{6,7},{7,0},{8,9},{9,10},{10,1... | collective-permute-start | bytes 172040 | tf_op jit(solution)/shard_map/ppermute | solution.py:35
  31.2 3.0 %collective-permute-start.5 = (f32[7,16,128]{2,1,0:T(8,128)S(1)}, f32[7,16,128]{2,1,0:T(8,128)S(1)}, u32[]{:S(2)}, u32[]{:S(2)}) collective-permute-start(f32[7,16,128]{2,1,0:T(8,128)S(1)} %get-tuple-element.46), channel_id=1, source_target_pairs={{0,7},{1,0},{2,1},{3,2},{4,3},{5,4},{6,5},{7,6},{8,15},{9,8},{10,9... | collective-permute-start | bytes 172040 | tf_op jit(solution)/shard_map/ppermute | solution.py:35
  34.2 2.2 %collective-permute-done.4.low = f32[7,16,128]{2,1,0:T(8,128)S(1)} collective-permute-done((f32[7,16,128]{2,1,0:T(8,128)S(1)}, f32[7,16,128]{2,1,0:T(8,128)S(1)}, u32[]{:S(2)}, u32[]{:S(2)}) %collective-permute-start.4) | collective-permute-done | bytes 57376 | tf_op jit(solution)/shard_map/ppermute | solution.py:35
  36.4 0.3 collective-permute-done.5.high
  36.7 0.1 shard_map.46
  36.8 0.1 collective-permute-start.6
  36.9 1.7 %collective-permute-start.7 = (f32[7,16,128]{2,1,0:T(8,128)S(1)}, f32[7,16,128]{2,1,0:T(8,128)S(1)}, u32[]{:S(2)}, u32[]{:S(2)}) collective-permute-start(f32[7,16,128]{2,1,0:T(8,128)S(1)} %get-tuple-element.50), channel_id=1, source_target_pairs={{0,24},{8,0},{16,8},{24,16},{1,25},{9,1},{17,9},{25,17},{2,26},{10... | collective-permute-start | bytes 172040 | tf_op jit(solution)/shard_map/ppermute | solution.py:35
  38.6 1.9 %collective-permute-done.6.low = f32[7,16,128]{2,1,0:T(8,128)S(1)} collective-permute-done((f32[7,16,128]{2,1,0:T(8,128)S(1)}, f32[7,16,128]{2,1,0:T(8,128)S(1)}, u32[]{:S(2)}, u32[]{:S(2)}) %collective-permute-start.6) | collective-permute-done | bytes 57376 | tf_op jit(solution)/shard_map/ppermute | solution.py:35
  40.5 0.0 collective-permute-done.7.high
  40.5 1.4 %shard_map.47 = (f32[32,16,128]{2,1,0:T(8,128)}, f32[24,16,128]{2,1,0:T(8,128)S(1)}, f32[24,16,128]{2,1,0:T(8,128)S(1)}, f32[24,16,128]{2,1,0:T(8,128)S(1)}, f32...) custom-call(f32[16,16,128]{2,1,0:T(8,128)S(1)} %get-tuple-element.47.k_own, ...), custom_call_target="tpu_custom_call" | custom-call | tf_op jit(solution)/shard_map/pallas_call | solution.py:672
  41.9 0.0 all-to-all-done.received_k
  42.0 6.2 %all-to-all-start.1 = ((f32[32,16,128]{2,1,0:T(8,128)}), f32[32,16,128]{2,1,0:T(8,128)S(1)}, u32[]{:S(2)}, u32[]{:S(2)}) async-start(f32[32,16,128]{2,1,0:T(8,128)} %get-tuple-element.51), calls=%async_computation.1 | async-start | bytes 524288 | tf_op jit(solution)/shard_map/all_to_all | solution.py:751
  48.2 0.3 collective-permute-start.8
  48.5 1.5 %collective-permute-start.9 = (f32[128,128]{1,0:T(8,128)S(1)}, f32[128,128]{1,0:T(8,128)S(1)}, u32[]{:S(2)}, u32[]{:S(2)}) collective-permute-start(f32[128,128]{1,0:T(8,128)S(1)} %get-tuple-element.60), channel_id=1, source_target_pairs={{0,24},{8,0},{16,8},{24,16},{1,25},{9,1},{17,9},{25,17},{2,26},{10... | collective-permute-start | bytes 196616 | tf_op jit(solution)/shard_map/ppermute | solution.py:35
  50.0 2.5 %collective-permute-done.8.low = f32[128,128]{1,0:T(8,128)S(1)} collective-permute-done((f32[128,128]{1,0:T(8,128)S(1)}, f32[128,128]{1,0:T(8,128)S(1)}, u32[]{:S(2)}, u32[]{:S(2)}) %collective-permute-start.8) | collective-permute-done | bytes 65568 | tf_op jit(solution)/shard_map/ppermute | solution.py:35
  52.5 0.5 collective-permute-done.9.high
  53.0 0.2 shard_map.50
  53.2 1.6 %collective-permute-start.10 = (f32[324,128]{1,0:T(8,128)S(1)}, f32[324,128]{1,0:T(8,128)S(1)}, u32[]{:S(2)}, u32[]{:S(2)}) collective-permute-start(f32[324,128]{1,0:T(8,128)S(1)} %get-tuple-element.64), channel_id=1, source_target_pairs={{0,1},{1,2},{2,3},{3,4},{4,5},{5,6},{6,7},{7,0},{8,9},{9,10},{10,1... | collective-permute-start | bytes 497672 | tf_op jit(solution)/shard_map/ppermute | solution.py:35
  54.8 3.3 %collective-permute-start.11 = (f32[324,128]{1,0:T(8,128)S(1)}, f32[324,128]{1,0:T(8,128)S(1)}, u32[]{:S(2)}, u32[]{:S(2)}) collective-permute-start(f32[324,128]{1,0:T(8,128)S(1)} %get-tuple-element.65), channel_id=1, source_target_pairs={{0,7},{1,0},{2,1},{3,2},{4,3},{5,4},{6,5},{7,6},{8,15},{9,8},{10,9... | collective-permute-start | bytes 497672 | tf_op jit(solution)/shard_map/ppermute | solution.py:35
  58.1 0.7 all-to-all-done.1.received
  58.8 6.1 %shard_map.48.region = f32[4,24,128]{2,1,0:T(8,128)S(1)} custom-call(f32[32,16,128]{2,1,0:T(8,128)S(1)} %all-to-all-done.received_k, f32[32,16,128]{2,1,0:T(8,128)S(1)} %all-to-all-done.1.received), custom_call_target="tpu_custom_call" | custom-call | tf_op jit(solution)/shard_map/pallas_call | solution.py:672
  64.9 0.0 collective-permute-done.10.low
  64.9 0.6 collective-permute-done.11.high
  65.6 6.3 %shard_map.51 = (f32[32,16,256]{2,1,0:T(8,128)}, f32[32,16,256]{2,1,0:T(8,128)}) custom-call(f32[4,24,128]{2,1,0:T(8,128)S(1)} %shard_map.48.region, f32[24,16,128]{2,1,0:T(8,128)S(1)} %get-tuple-element.52.wl1, f32[24,16,128]{2,1,0:T(8,128)S(1)} %get-tuple-element.53.ws1, f32[24,16,128]{2,1,0:T(8,128)S(1)} %get-tuple-element.54.wz1, ...), custom_call_target="tpu_custom_call" | custom-call | tf_op jit(solution)/shard_map/pallas_call | solution.py:672
  (2 shorter events, 0.0 us)
Async XLA Ops:
  0.6 1.0 %copy-start = (f32[32,16,256]{2,1,0:T(8,128)S(1)}, f32[32,16,256]{2,1,0:T(8,128)}, u32[]{:S(2)}) copy-start(f32[32,16,256]{2,1,0:T(8,128)} %b.1) | copy-start | bytes 1572868
  1.7 1.0 %copy-start.1 = (f32[32,16,256]{2,1,0:T(8,128)S(1)}, f32[32,16,256]{2,1,0:T(8,128)}, u32[]{:S(2)}) copy-start(f32[32,16,256]{2,1,0:T(8,128)} %k.1) | copy-start | bytes 1572868
  2.9 10.3 %collective-permute-start = (f32[5,32,256]{2,1,0:T(8,128)S(1)}, f32[5,32,256]{2,1,0:T(8,128)S(1)}, u32[]{:S(2)}, u32[]{:S(2)}) collective-permute-start(f32[5,32,256]{2,1,0:T(8,128)S(1)} %get-tuple-element.37), channel_id=1, source_target_pairs={{0,1},{1,2},{2,3},{3,4},{4,5},{5,6},{6,7},{7,0},{8,9},{9,10},{10,1... | collective-permute-start | bytes 491528 | tf_op jit(solution)/shard_map/ppermute | solution.py:35
  5.9 9.2 %collective-permute-start.1 = (f32[5,32,256]{2,1,0:T(8,128)S(1)}, f32[5,32,256]{2,1,0:T(8,128)S(1)}, u32[]{:S(2)}, u32[]{:S(2)}) collective-permute-start(f32[5,32,256]{2,1,0:T(8,128)S(1)} %get-tuple-element.38), channel_id=1, source_target_pairs={{0,7},{1,0},{2,1},{3,2},{4,3},{5,4},{6,5},{7,6},{8,15},{9,8},{10,9... | collective-permute-start | bytes 491528 | tf_op jit(solution)/shard_map/ppermute | solution.py:35
  15.3 4.4 %collective-permute-start.2 = (f32[5,24,256]{2,1,0:T(8,128)S(1)}, f32[5,24,256]{2,1,0:T(8,128)S(1)}, u32[]{:S(2)}, u32[]{:S(2)}) collective-permute-start(f32[5,24,256]{2,1,0:T(8,128)S(1)} %get-tuple-element.39), channel_id=1, source_target_pairs={{0,8},{8,16},{16,24},{24,0},{1,9},{9,17},{17,25},{25,1},{2,10},{10... | collective-permute-start | bytes 368648 | tf_op jit(solution)/shard_map/ppermute | solution.py:35
  15.3 4.6 %collective-permute-start.3 = (f32[5,24,256]{2,1,0:T(8,128)S(1)}, f32[5,24,256]{2,1,0:T(8,128)S(1)}, u32[]{:S(2)}, u32[]{:S(2)}) collective-permute-start(f32[5,24,256]{2,1,0:T(8,128)S(1)} %get-tuple-element.40), channel_id=1, source_target_pairs={{0,24},{8,0},{16,8},{24,16},{1,25},{9,1},{17,9},{25,17},{2,26},{10... | collective-permute-start | bytes 368648 | tf_op jit(solution)/shard_map/ppermute | solution.py:35
  20.0 21.9 %all-to-all-start = ((f32[32,16,128]{2,1,0:T(8,128)}), f32[32,16,128]{2,1,0:T(8,128)S(1)}, u32[]{:S(2)}, u32[]{:S(2)}) async-start(f32[32,16,128]{2,1,0:T(8,128)} %shard_map.44), calls=%async_computation | async-start | bytes 524288 | tf_op jit(solution)/shard_map/all_to_all | solution.py:724
  29.4 7.0 %collective-permute-start.4 = (f32[7,16,128]{2,1,0:T(8,128)S(1)}, f32[7,16,128]{2,1,0:T(8,128)S(1)}, u32[]{:S(2)}, u32[]{:S(2)}) collective-permute-start(f32[7,16,128]{2,1,0:T(8,128)S(1)} %get-tuple-element.45), channel_id=1, source_target_pairs={{0,1},{1,2},{2,3},{3,4},{4,5},{5,6},{6,7},{7,0},{8,9},{9,10},{10,1... | collective-permute-start | bytes 172040 | tf_op jit(solution)/shard_map/ppermute | solution.py:35
  31.2 5.5 %collective-permute-start.5 = (f32[7,16,128]{2,1,0:T(8,128)S(1)}, f32[7,16,128]{2,1,0:T(8,128)S(1)}, u32[]{:S(2)}, u32[]{:S(2)}) collective-permute-start(f32[7,16,128]{2,1,0:T(8,128)S(1)} %get-tuple-element.46), channel_id=1, source_target_pairs={{0,7},{1,0},{2,1},{3,2},{4,3},{5,4},{6,5},{7,6},{8,15},{9,8},{10,9... | collective-permute-start | bytes 172040 | tf_op jit(solution)/shard_map/ppermute | solution.py:35
  36.8 3.7 %collective-permute-start.6 = (f32[7,16,128]{2,1,0:T(8,128)S(1)}, f32[7,16,128]{2,1,0:T(8,128)S(1)}, u32[]{:S(2)}, u32[]{:S(2)}) collective-permute-start(f32[7,16,128]{2,1,0:T(8,128)S(1)} %get-tuple-element.49), channel_id=1, source_target_pairs={{0,8},{8,16},{16,24},{24,0},{1,9},{9,17},{17,25},{25,1},{2,10},{10... | collective-permute-start | bytes 172040 | tf_op jit(solution)/shard_map/ppermute | solution.py:35
  36.9 3.6 %collective-permute-start.7 = (f32[7,16,128]{2,1,0:T(8,128)S(1)}, f32[7,16,128]{2,1,0:T(8,128)S(1)}, u32[]{:S(2)}, u32[]{:S(2)}) collective-permute-start(f32[7,16,128]{2,1,0:T(8,128)S(1)} %get-tuple-element.50), channel_id=1, source_target_pairs={{0,24},{8,0},{16,8},{24,16},{1,25},{9,1},{17,9},{25,17},{2,26},{10... | collective-permute-start | bytes 172040 | tf_op jit(solution)/shard_map/ppermute | solution.py:35
  42.0 16.9 %all-to-all-start.1 = ((f32[32,16,128]{2,1,0:T(8,128)}), f32[32,16,128]{2,1,0:T(8,128)S(1)}, u32[]{:S(2)}, u32[]{:S(2)}) async-start(f32[32,16,128]{2,1,0:T(8,128)} %get-tuple-element.51), calls=%async_computation.1 | async-start | bytes 524288 | tf_op jit(solution)/shard_map/all_to_all | solution.py:751
  48.2 4.3 %collective-permute-start.8 = (f32[128,128]{1,0:T(8,128)S(1)}, f32[128,128]{1,0:T(8,128)S(1)}, u32[]{:S(2)}, u32[]{:S(2)}) collective-permute-start(f32[128,128]{1,0:T(8,128)S(1)} %get-tuple-element.59), channel_id=1, source_target_pairs={{0,8},{8,16},{16,24},{24,0},{1,9},{9,17},{17,25},{25,1},{2,10},{10... | collective-permute-start | bytes 196616 | tf_op jit(solution)/shard_map/ppermute | solution.py:35
  48.5 4.5 %collective-permute-start.9 = (f32[128,128]{1,0:T(8,128)S(1)}, f32[128,128]{1,0:T(8,128)S(1)}, u32[]{:S(2)}, u32[]{:S(2)}) collective-permute-start(f32[128,128]{1,0:T(8,128)S(1)} %get-tuple-element.60), channel_id=1, source_target_pairs={{0,24},{8,0},{16,8},{24,16},{1,25},{9,1},{17,9},{25,17},{2,26},{10... | collective-permute-start | bytes 196616 | tf_op jit(solution)/shard_map/ppermute | solution.py:35
  53.2 11.7 %collective-permute-start.10 = (f32[324,128]{1,0:T(8,128)S(1)}, f32[324,128]{1,0:T(8,128)S(1)}, u32[]{:S(2)}, u32[]{:S(2)}) collective-permute-start(f32[324,128]{1,0:T(8,128)S(1)} %get-tuple-element.64), channel_id=1, source_target_pairs={{0,1},{1,2},{2,3},{3,4},{4,5},{5,6},{6,7},{7,0},{8,9},{9,10},{10,1... | collective-permute-start | bytes 497672 | tf_op jit(solution)/shard_map/ppermute | solution.py:35
  54.8 10.7 %collective-permute-start.11 = (f32[324,128]{1,0:T(8,128)S(1)}, f32[324,128]{1,0:T(8,128)S(1)}, u32[]{:S(2)}, u32[]{:S(2)}) collective-permute-start(f32[324,128]{1,0:T(8,128)S(1)} %get-tuple-element.65), channel_id=1, source_target_pairs={{0,7},{1,0},{2,1},{3,2},{4,3},{5,4},{6,5},{7,6},{8,15},{9,8},{10,9... | collective-permute-start | bytes 497672 | tf_op jit(solution)/shard_map/ppermute | solution.py:35

commit v5 on v4

--- a/solution.py
+++ b/solution.py
@@ -68,13 +68,12 @@
     return jnp.where((row == col // 2) & (row < valid), 1.0, 0.0).astype(BF16)
 
 
-def move(refs, stash, sems, back):
+def fetch(refs, stash, sems):
     copies = []
     for i, ref in enumerate(refs):
         planes = ref.shape[0]
         there = stash.at[i * planes : (i + 1) * planes]
-        source, target = (there, ref) if back else (ref, there)
-        copies.append(pltpu.make_async_copy(source, target, sems.at[i]))
+        copies.append(pltpu.make_async_copy(there, ref, sems.at[i]))
     for copy in copies:
         copy.start()
     return copies
@@ -124,8 +123,9 @@
     lax.fori_loop(low, high, step, 0, unroll=unrolled(plane, high - low))
 
 
-def weigh(k, wl, ws, wz, total, inverse, row_edge, lane_edge):
-    planes = k.shape[0]
+def weigh(k, wl, ws, wz, total, inverse, row_edge, lane_edge, span=None, before=None):
+    plane = k.shape[1:]
+    low, high = span or (0, k.shape[0] - 1)
 
     def body(i, before):
         here = k[i]
@@ -141,7 +141,8 @@
         inverse[i] = jnp.where(there, 1.0 / whole, 0.0)
         return lead
 
-    lax.fori_loop(0, planes - 1, body, jnp.zeros(k.shape[1:], F32), unroll=unrolled(k.shape[1:], planes - 1))
+    before = jnp.zeros(plane, F32) if before is None else before
+    lax.fori_loop(low, high, body, before, unroll=unrolled(plane, high - low))
 
 
 def beside(x, w, i):
@@ -159,13 +160,15 @@
     def start(i):
         first[i] = b[i] * inverse[i] * (1.0 / (scale * THETA))
 
-    loop(*outer, start, b.shape[1:])
+    for span in outer:
+        loop(*span, start, b.shape[1:])
 
     def sweep(i):
         near = beside(first, w, i)
         second[i] = (1.0 + KEEP + GAIN * (THETA - 1.0)) * first[i] + GAIN * (inverse[i] * near)
 
-    loop(*inner, sweep, b.shape[1:])
+    for span in inner:
+        loop(*span, sweep, b.shape[1:])
 
 
 def post_smooth(b, first, second, w, inverse, scale, outer, inner):
@@ -250,10 +253,6 @@
     wait(spread_copies(message, held, sems, packed(pairs1[...], halves1, k1.shape[2])))
 
 
-def after_kernel(message, _low, _high, out):
-    pass
-
-
 def widen(out, own, low, high, count):
     planes, rows, lanes = own.shape
     size = out.shape[1]
@@ -289,38 +288,101 @@
             out[above] = jnp.zeros(out.shape[1:], F32)
 
 
-def fine_down_kernel(
-    k_own, b_own, low, high, k1,
-    stash, s_out, b1_out, up_out, down_out,
-    wl, ws, wz, total, inverse, b, k, first, second, pairs, halves, sems,
-):
-    join(k, k_own, lambda r: low[r], lambda r: high[r], K0, K0)
-    join(b, b_own, lambda r: low[K0 + r], lambda r: high[K0 + r], B0, K0)
-    w = (wl, ws, wz)
-    weigh(k, wl, ws, wz, total, inverse, False, True)
-    copies = move((wl, ws, wz, total, b), stash, sems, False)
-    planes, lanes = b.shape[0], b.shape[2]
-    own, rows = planes - 2 * K0, s_out.shape[1]
-    pre_smooth(b, first, second, w, inverse, 1.0, (1, planes - 1), (2, planes - 2))
+def fine_inner_kernel(k_own, b_own, wl, ws, wz, total, inverse, b, first, second, pairs, k):
+    own, planes = k_own.shape[0], b.shape[0]
+    k[K0 : K0 + own] = k_own[...]
+    b[K0 : K0 + own] = b_own[...]
+    low, high, rows = K0, planes - K0, pairs.shape[1]
+    weigh(k, wl, ws, wz, total, inverse, False, True, (low, high - 1))
+    pre_smooth(
+        b, first, second, (wl, ws, wz), inverse, 1.0, [(low + 1, high - 1)], [(low + 2, high - 2)]
+    )
+    fine_restrict(b, second, (wl, ws, wz), total, pairs, (2, own // 2 - 2))
+
+
+def fine_restrict(b, field, w, total, pairs, span):
+    rows = pairs.shape[1]
 
     def restrict(j):
         i = 2 * j + K0
-        both = residual(b, second, w, total, 1.0, i) + residual(b, second, w, total, 1.0, i + 1)
+        both = residual(b, field, w, total, 1.0, i) + residual(b, field, w, total, 1.0, i + 1)
         pairs[j] = both[0:rows]
 
-    loop(0, own // 2, restrict, (2 * b.shape[1], b.shape[2]))
+    loop(*span, restrict, (2 * b.shape[1], b.shape[2]))
+
+
+def fine_outer_kernel(
+    k_own, low, high, k1,
+    wl_in, ws_in, wz_in, total_in, inverse_in, b_in, first_in, second_in, pairs_in,
+    wl_out, ws_out, wz_out, total_out, b_out, s_out, b1_out, up_out, down_out,
+    wl, ws, wz, total, inverse, b, first, second, pairs, k, halves,
+):
+    planes, rows, lanes = b.shape[0], s_out.shape[1], b.shape[2]
+    own, end = planes - 2 * K0, planes - K0
+    for mine, inner in (
+        (wl, wl_in), (ws, ws_in), (wz, wz_in), (total, total_in), (inverse, inverse_in), (b, b_in),
+        (first, first_in), (second, second_in),
+    ):
+        mine[K0 : K0 + 5] = inner[K0 : K0 + 5]
+        mine[end - 5 : end] = inner[end - 5 : end]
+    left, right = inside("gx", -1), inside("gx", 1)
+    for r in range(K0):
+        k[r] = masked(left, low[r])
+        k[end + r] = masked(right, high[r])
+    for r in range(B0):
+        b[K0 - B0 + r] = masked(left, low[K0 + r])
+        b[end + r] = masked(right, high[K0 + r])
+    for r in range(2):
+        k[K0 + r] = k_own[r]
+        k[end - 2 + r] = k_own[own - 2 + r]
+    w = (wl, ws, wz)
+    weigh(k, wl, ws, wz, total, inverse, False, True, (0, K0 + 1))
+    weigh(k, wl, ws, wz, total, inverse, False, True, (end - 1, planes - 1), wl[end - 2])
+    pre_smooth(
+        b, first, second, w, inverse, 1.0,
+        [(1, K0 + 1), (end - 1, planes - 1)], [(2, K0 + 2), (end - 2, planes - 2)],
+    )
+    pairs[2 : own // 2 - 2] = pairs_in[2 : own // 2 - 2]
+    fine_restrict(b, second, w, total, pairs, (0, 2))
+    fine_restrict(b, second, w, total, pairs, (own // 2 - 2, own // 2))
     b1_out[...] = coarser(pairs[...], halves, halving(lanes, lanes // 2, lanes))
-    s_out[...] = second[K0 : K0 + own, 0:rows, :]
+    s_out[2 : own - 2] = second_in[K0 + 2 : end - 2, 0:rows, :]
+    for at in (0, own - 2):
+        s_out[at : at + 2] = second[K0 + at : K0 + at + 2, 0:rows, :]
+    for out, mine in ((wl_out, wl), (ws_out, ws), (wz_out, wz), (total_out, total), (b_out, b)):
+        out[0 : K0 + 1] = mine[0 : K0 + 1]
+        out[K0 + 1 :] = mine[end - 1 :]
     half, count = b1_out.shape[0], b1_out.shape[1]
     for out, k_from, b_from in ((up_out, count - K1, count - B1), (down_out, 0, 0)):
         for r in range(K1):
             out[r] = k1[:, k_from + r, :]
         for r in range(B1):
             out[K1 + r] = b1_out[:, b_from + r, :]
+
+
+def stash_kernel(*refs):
+    inner, outer, (stash, sems) = refs[:5], refs[5:10], refs[10:]
+    planes, edge = inner[0].shape[0], K0 + 1
+    copies = []
+    for i in range(5):
+        for j, (source, first, at, count) in enumerate((
+            (inner[i], edge, edge, planes - 2 * edge),
+            (outer[i], 0, 0, edge),
+            (outer[i], edge, planes - edge, edge),
+        )):
+            copies.append(
+                pltpu.make_async_copy(
+                    source.at[first : first + count],
+                    stash.at[i * planes + at : i * planes + at + count],
+                    sems.at[3 * i + j],
+                )
+            )
+    for copy in copies:
+        copy.start()
     wait(copies)
 
 
-def widen_middle_kernel(k1, b1, low, high, k_out, b_out, up_out, down_out):
+def widen_middle_kernel(k1, b1, low, high, _stash, k_out, b_out, up_out, down_out):
     widen(k_out, k1, lambda r: low[r], lambda r: high[r], K1)
     widen(b_out, b1, lambda r: low[K1 + r], lambda r: high[K1 + r], B1)
     planes = k1.shape[0]
@@ -342,7 +404,7 @@
     weigh(k, wl, ws, wz, total, inverse, False, True)
     planes, lanes = b.shape[0], b.shape[2]
     own, rows = planes - 2 * K1, s_out.shape[1]
-    pre_smooth(b, first, second, w, inverse, scale, (1, planes - 1), (2, planes - 2))
+    pre_smooth(b, first, second, w, inverse, scale, [(1, planes - 1)], [(2, planes - 2)])
 
     def restrict(j):
         i = 2 * j + K1
@@ -458,7 +520,7 @@
 
 
 def coarse_pre(b, w, inverse, first, second, scale):
-    ends = (1, b.shape[0] - 1)
+    ends = [(1, b.shape[0] - 1)]
     clear_ends(first)
     clear_ends(second)
     pre_smooth(b, first, second, w, inverse, scale, ends, ends)
@@ -515,10 +577,11 @@
 
 
 def coarse_kernel(
-    valid, received_k, received, region,
+    valid, received_k, received, stash, region, wl, ws, wz, total, b,
     wl2, low2, ws2, wz2, total2, inverse2, k2, b2, first2, second2, pairs2, halves2,
-    wl3, ws3, wz3, total3, inverse3, k3, b3, first3, second3, pairs3, halves3,
+    wl3, ws3, wz3, total3, inverse3, k3, b3, first3, second3, pairs3, halves3, sems,
 ):
+    copies = fetch((wl, ws, wz, total, b), stash, sems)
     planes, rows, lanes = b2.shape
     across, along = lax.axis_size("gx"), lax.axis_size("gy")
     block_x, block_y = rows // across, 2 * (planes - 2) // along
@@ -585,15 +648,15 @@
             start = pl.multiple_of(jnp.clip(block, 0, across - 1) * block_x, block_x)
             value = first2[1 + jnp.clip(plane, 0, planes - 3), pl.ds(start, block_x), :]
             region[q, side * block_x : (side + 1) * block_x, :] = masked(there, value)
+    wait(copies)
 
 
 def fine_up_kernel(
-    region, wl1, ws1, wz1, inverse1, b1, s1_own, stash, s_own, low, high,
+    region, wl1, ws1, wz1, inverse1, b1, s1_own, wl, ws, wz, total, b, s_own, low, high,
     field_out, residual_out,
-    wl, ws, wz, total, b, inverse, first1, second1, grown, s, second, tall, thick, rest,
-    sems, out_sems,
+    inverse, first1, second1, grown, s, second, tall, thick, rest,
+    out_sems,
 ):
-    copies = move((wl, ws, wz, total, b), stash, sems, True)
     planes1, rows1, lanes1 = b1.shape
     planes, rows, lanes = b.shape
     w1, w = (wl1, ws1, wz1), (wl, ws, wz)
@@ -635,7 +698,6 @@
             s[i] = s[i] + thick[q]
 
     loop(1, count - 1, add, b.shape[1:])
-    wait(copies)
 
     def invert(i):
         inverse[i] = jnp.where(total[i] > 0.0, 1.0 / total[i], 0.0)
@@ -662,7 +724,7 @@
     wait(copies)
 
 
-def call(kernel, outs, scratch=(), held=0, kept=(), sems=(), alias=None):
+def call(kernel, outs, scratch=(), held=0, kept=(), sems=(), alias=None, cost=0):
     def run(*operands):
         inputs = [o.shape for i, o in enumerate(operands) if i not in kept]
         shapes = inputs + list(outs[held:]) + list(scratch)
@@ -677,6 +739,7 @@
             scratch_shapes=[pltpu.VMEM(shape, F32) for shape in scratch]
             + [pltpu.SemaphoreType.DMA((n,)) for n in sems],
             input_output_aliases=alias or {},
+            cost_estimate=pl.CostEstimate(flops=cost, bytes_accessed=cost, transcendentals=0) if cost else None,
             compiler_params=pltpu.CompilerParams(vmem_limit_bytes=4 * words + SPARE),
         )(*operands)
 
@@ -713,31 +776,31 @@
 
     plane = (bx, tall, nz)
     slab = (K0 + B0, tall, nz)
-    k_own, b_own, up_planes, down_planes = call(widen_kernel, [plane, plane, slab, slab])(
+    k_own, b_own, up_planes, down_planes = call(widen_kernel, [plane, plane, slab, slab], cost=1000000000000)(
         right_side, coefficient, low, high
     )
     low, high = rotate(up_planes, "gx", 1), rotate(down_planes, "gx", -1)
 
-    (message,) = call(after_kernel, [pieces], held=1, kept=(0, 1, 2), alias={0: 0})(
-        message, low, high
+    k2 = lax.all_to_all(message, both, 0, 0, tiled=True)
+
+    block = (bx + 2 * K0, tall, nz)
+    inner = call(fine_inner_kernel, [block] * 8 + [(hx, by, nz)], [block])(k_own, b_own)
+    slab = (K1 + B1, hx, hz)
+    edges = (2 * K0 + 2, tall, nz)
+    *outer, s, b1, up_rows, down_rows = call(
+        fine_outer_kernel,
+        [edges] * 5 + [(bx, by, nz), (hx, hy, hz), slab, slab],
+        [block] * 8 + [(hx, by, nz), block, (hx, by, hz)],
+    )(k_own, low, high, k1, *inner)
+    planes = 5 * block[0] + VMEM_BYTES // (4 * tall * nz)
+    (stash,) = call(stash_kernel, [(planes, tall, nz)], held=1, sems=(15,))(
+        *inner[:4], inner[5], *outer
     )
-    k2 = lax.all_to_all(message, both, 0, 0, tiled=True)
-
-    block = (bx + 2 * K0, tall, nz)
-    slab = (K1 + B1, hx, hz)
-    planes = 5 * block[0] + VMEM_BYTES // (4 * tall * nz)
-    stash, s, b1, up_rows, down_rows = call(
-        fine_down_kernel,
-        [(planes, tall, nz), (bx, by, nz), (hx, hy, hz), slab, slab],
-        [block] * 9 + [(hx, by, nz), (hx, by, hz)],
-        held=1,
-        sems=(5,),
-    )(k_own, b_own, low, high, k1)
     low, high = rotate(up_rows, "gy", 1), rotate(down_rows, "gy", -1)
     slab = (K1 + B1, tall1, hz)
     k1_own, b1_own, up_planes, down_planes = call(
-        widen_middle_kernel, [(hx, tall1, hz), (hx, tall1, hz), slab, slab]
-    )(k1, b1, low, high)
+        widen_middle_kernel, [(hx, tall1, hz), (hx, tall1, hz), slab, slab], kept=(4,)
+    )(k1, b1, low, high, stash)
     low, high = rotate(up_planes, "gx", 1), rotate(down_planes, "gx", -1)
 
     block1 = (hx + 2 * K1, tall1, hz)
@@ -762,22 +825,23 @@
     x2, y2 = across * qx, along * qy
     level2, level3 = (y2 // 2 + 2, x2, hz), (y2 // 2 + 2, x2 // 2, hz)
     half2, half3 = (y2 // 2, x2, hz), (y2 // 4, x2 // 2, hz)
-    (region,) = call(
+    region, *weights = call(
         partial(coarse_kernel, nz // 4),
-        [(qy // 2 + EDGE, 3 * qx, hz)],
+        [(qy // 2 + EDGE, 3 * qx, hz)] + [block] * 5,
         [level2] * 10 + [half2] * 2 + [level3] * 9 + [half3] * 2,
-    )(k2, received)
+        kept=(2,),
+        sems=(5,),
+    )(k2, received, stash)
 
     count = hx + 2 * EDGE
     field, rest = call(
         fine_up_kernel,
         [(bx, by, nz)] * 2,
-        [block] * 6 + [block1, block1, (qx + 2 * EDGE, tall1, hz)]
+        [block] + [block1, block1, (qx + 2 * EDGE, tall1, hz)]
         + [block, block, (count, tall, hz), (count, tall, nz), (bx, by, nz)],
         held=2,
-        kept=(7,),
-        sems=(5, 5),
-    )(region, *kept1, s1_own, stash, s_own, low, high)
+        sems=(5,),
+    )(region, *kept1, s1_own, *weights, s_own, low, high)
     return field, rest
 
 

time: 72.2 us -> 63.9 us (0.89)
  waiting for transfers between devices: 16.5 us -> 7.74 us
  Pallas kernels: 20.2 us -> 22 us
  starting transfers between devices: 32.4 us -> 30.9 us
    ppermute x12, waiting for transfers between devices: 15.8 us -> 7.03 us  [rotate(): lax.ppermute(value, axis, [(i, (i + shift) % size) for i in range(size)])]
    pallas_call x11 -> x12, Pallas kernels: 20.2 us -> 22 us  [run(): pl.pallas_call(kernel, out_shape=[jax.ShapeDtypeStruct(shape, F32) for sh...]
    all_to_all x1, starting transfers between devices: 5.03 us -> 3.42 us  [per_device(): k2 = lax.all_to_all(message, both, 0, 0, tiled=True)]
  transfers between devices with their start and end apart: 14 -> 14, of which waited for: 11 -> 8; matrix products, arithmetic and copies ran while one was open for 0% -> 0% of each run, Pallas kernels for 19% -> 27%
where the time goes in v5:
time: 63.9 us; the launch traced here: 63.5 us
  starting transfers between devices  30.9 us (48%)
  Pallas kernels  22 us (34%)
  waiting for transfers between devices  7.74 us (12%)
  local copies, waits for them, and re-layouts  2.08 us (3%)
  between operations  0.77 us (1%)
    pallas_call x12, Pallas kernels, run(): pl.pallas_call(kernel, out_shape=[jax.ShapeDtypeStruct(shape, F32) for sh...  22 us
    ppermute x12, starting transfers between devices, rotate(): lax.ppermute(value, axis, [(i, (i + shift) % size) for i in range(size)])  21.1 us
    ppermute x12, waiting for transfers between devices, rotate(): lax.ppermute(value, axis, [(i, (i + shift) % size) for i in range(size)])  7.03 us
    all_to_all x1, starting transfers between devices, per_device(): received = lax.all_to_all(message, both, 0, 0, tiled=True)  6.4 us
    all_to_all x1, starting transfers between devices, per_device(): k2 = lax.all_to_all(message, both, 0, 0, tiled=True)  3.42 us
    unnamed x4, local copies, waits for them, and re-layouts  2.08 us
  transfers between devices with their start and end apart: 14, of which 8 were waited for; matrix products, arithmetic and copies ran while one was open for 0% of the time, Pallas kernels for 27%

profile of v5, /device:TPU:0, one launch (start us, length us, event | category | flops | bytes accessed | tf_op | source)
XLA Modules:
  0.0 63.5 jit_solution(6343279145780741132)
XLA Ops:
  0.6 0.0 copy-start
  0.6 1.0 %copy-done = f32[32,16,256]{2,1,0:T(8,128)S(1)} copy-done((f32[32,16,256]{2,1,0:T(8,128)S(1)}, f32[32,16,256]{2,1,0:T(8,128)}, u32[]{:S(2)}) %copy-start) | copy-done | bytes 524312
  1.7 0.0 copy-start.1
  1.7 1.0 %copy-done.1 = f32[32,16,256]{2,1,0:T(8,128)S(1)} copy-done((f32[32,16,256]{2,1,0:T(8,128)S(1)}, f32[32,16,256]{2,1,0:T(8,128)}, u32[]{:S(2)}) %copy-start.1) | copy-done | bytes 524312
  2.7 0.2 shard_map.41
  2.9 3.0 %collective-permute-start = (f32[5,32,256]{2,1,0:T(8,128)S(1)}, f32[5,32,256]{2,1,0:T(8,128)S(1)}, u32[]{:S(2)}, u32[]{:S(2)}) collective-permute-start(f32[5,32,256]{2,1,0:T(8,128)S(1)} %get-tuple-element.57), channel_id=1, source_target_pairs={{0,1},{1,2},{2,3},{3,4},{4,5},{5,6},{6,7},{7,0},{8,9},{9,10},{10,1... | collective-permute-start | bytes 491528 | tf_op jit(solution)/shard_map/ppermute | solution.py:35
  5.9 3.1 %collective-permute-start.1 = (f32[5,32,256]{2,1,0:T(8,128)S(1)}, f32[5,32,256]{2,1,0:T(8,128)S(1)}, u32[]{:S(2)}, u32[]{:S(2)}) collective-permute-start(f32[5,32,256]{2,1,0:T(8,128)S(1)} %get-tuple-element.58), channel_id=1, source_target_pairs={{0,7},{1,0},{2,1},{3,2},{4,3},{5,4},{6,5},{7,6},{8,15},{9,8},{10,9... | collective-permute-start | bytes 491528 | tf_op jit(solution)/shard_map/ppermute | solution.py:35
  9.0 1.2 %shard_map.42 = (f32[32,16,128]{2,1,0:T(8,128)}, f32[16,8,128]{2,1,0:T(8,128)S(1)}) custom-call(f32[32,16,256]{2,1,0:T(8,128)S(1)} %get-tuple-element.53.k), custom_call_target="tpu_custom_call" | custom-call | tf_op jit(solution)/shard_map/pallas_call | solution.py:734
  10.2 3.4 %all-to-all-start = ((f32[32,16,128]{2,1,0:T(8,128)}), f32[32,16,128]{2,1,0:T(8,128)}, u32[]{:S(2)}, u32[]{:S(2)}) async-start(f32[32,16,128]{2,1,0:T(8,128)} %get-tuple-element.54), calls=%async_computation | async-start | bytes 524288 | tf_op jit(solution)/shard_map/all_to_all | solution.py:784
  13.7 0.0 collective-permute-done.low
  13.7 1.4 %collective-permute-done.1.high = f32[5,32,256]{2,1,0:T(8,128)S(1)} collective-permute-done((f32[5,32,256]{2,1,0:T(8,128)S(1)}, f32[5,32,256]{2,1,0:T(8,128)S(1)}, u32[]{:S(2)}, u32[]{:S(2)}) %collective-permute-start.1) | collective-permute-done | bytes 163872 | tf_op jit(solution)/shard_map/ppermute | solution.py:35
  15.1 0.2 shard_map.43
  15.3 0.1 collective-permute-start.2
  15.3 1.7 %collective-permute-start.3 = (f32[5,24,256]{2,1,0:T(8,128)S(1)}, f32[5,24,256]{2,1,0:T(8,128)S(1)}, u32[]{:S(2)}, u32[]{:S(2)}) collective-permute-start(f32[5,24,256]{2,1,0:T(8,128)S(1)} %get-tuple-element.61), channel_id=1, source_target_pairs={{0,24},{8,0},{16,8},{24,16},{1,25},{9,1},{17,9},{25,17},{2,26},{10... | collective-permute-start | bytes 368648 | tf_op jit(solution)/shard_map/ppermute | solution.py:35
  17.1 3.8 %shard_map.44 = (f32[38,24,256]{2,1,0:T(8,128)S(1)}, f32[38,24,256]{2,1,0:T(8,128)S(1)}, f32[38,24,256]{2,1,0:T(8,128)S(1)}, f32[38,24,256]{2,1,0:T(8,128)S(1)},...) custom-call(f32[32,24,256]{2,1,0:T(8,128)S(1)} %get-tuple-element.59, ...), custom_call_target="tpu_custom_call" | custom-call | tf_op jit(solution)/shard_map/pallas_call | solution.py:734
  20.9 0.0 collective-permute-done.2.low
  20.9 0.4 collective-permute-done.3.high
  21.3 0.7 %shard_map.45 = (f32[8,24,256]{2,1,0:T(8,128)S(1)}, f32[8,24,256]{2,1,0:T(8,128)S(1)}, f32[8,24,256]{2,1,0:T(8,128)S(1)}, f32[8,24,256]{2,1,0:T(8,128)S(1)}, f32...) custom-call(f32[32,24,256]{2,1,0:T(8,128)S(1)} %get-tuple-element.59, ...), custom_call_target="tpu_custom_call" | custom-call | tf_op jit(solution)/shard_map/pallas_call | solution.py:734
  22.1 0.3 collective-permute-start.4
  22.3 4.5 %collective-permute-start.5 = (f32[7,16,128]{2,1,0:T(8,128)S(1)}, f32[7,16,128]{2,1,0:T(8,128)S(1)}, u32[]{:S(2)}, u32[]{:S(2)}) collective-permute-start(f32[7,16,128]{2,1,0:T(8,128)S(1)} %get-tuple-element.74), channel_id=1, source_target_pairs={{0,7},{1,0},{2,1},{3,2},{4,3},{5,4},{6,5},{7,6},{8,15},{9,8},{10,9... | collective-permute-start | bytes 172040 | tf_op jit(solution)/shard_map/ppermute | solution.py:35
  26.8 2.3 %shard_map.46._stash.stash = f32[2920,24,256]{2,1,0:T(8,128)} custom-call(f32[38,24,256]{2,1,0:T(8,128)S(1)} %get-tuple-element.63.wl_in.refs_0_, f32[38,24,256]{2,1,0:T(8,128)S(1)} %get-tuple-element.64.ws_in.refs_1_, f32[38,24,256]{2,1,0:T(8,128)S(1)} %get-tuple-element.65.wz_in.refs_2_, f32[38,24,256]{2,1,0:T(8,128)S(1)} %get-tuple-element.66.total_in.refs_3_, ...), custom_call_target="tpu_custom_call" | custom-call | tf_op jit(solution)/shard_map/pallas_call | solution.py:734
  29.1 0.2 collective-permute-done.4.low
  29.3 0.0 collective-permute-done.5.high
  29.3 0.1 shard_map.47
  29.4 0.7 %collective-permute-start.6 = (f32[7,16,128]{2,1,0:T(8,128)S(1)}, f32[7,16,128]{2,1,0:T(8,128)S(1)}, u32[]{:S(2)}, u32[]{:S(2)}) collective-permute-start(f32[7,16,128]{2,1,0:T(8,128)S(1)} %get-tuple-element.82), channel_id=1, source_target_pairs={{0,8},{8,16},{16,24},{24,0},{1,9},{9,17},{17,25},{25,1},{2,10},{10... | collective-permute-start | bytes 172040 | tf_op jit(solution)/shard_map/ppermute | solution.py:35
  30.1 1.1 %collective-permute-start.7 = (f32[7,16,128]{2,1,0:T(8,128)S(1)}, f32[7,16,128]{2,1,0:T(8,128)S(1)}, u32[]{:S(2)}, u32[]{:S(2)}) collective-permute-start(f32[7,16,128]{2,1,0:T(8,128)S(1)} %get-tuple-element.83), channel_id=1, source_target_pairs={{0,24},{8,0},{16,8},{24,16},{1,25},{9,1},{17,9},{25,17},{2,26},{10... | collective-permute-start | bytes 172040 | tf_op jit(solution)/shard_map/ppermute | solution.py:35
  31.2 1.9 %collective-permute-done.6.low = f32[7,16,128]{2,1,0:T(8,128)S(1)} collective-permute-done((f32[7,16,128]{2,1,0:T(8,128)S(1)}, f32[7,16,128]{2,1,0:T(8,128)S(1)}, u32[]{:S(2)}, u32[]{:S(2)}) %collective-permute-start.6) | collective-permute-done | bytes 57376 | tf_op jit(solution)/shard_map/ppermute | solution.py:35
  33.1 0.1 collective-permute-done.7.high
  33.2 1.4 %shard_map.48 = (f32[32,16,128]{2,1,0:T(8,128)}, f32[24,16,128]{2,1,0:T(8,128)S(1)}, f32[24,16,128]{2,1,0:T(8,128)S(1)}, f32[24,16,128]{2,1,0:T(8,128)S(1)}, f32...) custom-call(f32[16,16,128]{2,1,0:T(8,128)S(1)} %get-tuple-element.80.k_own, ...), custom_call_target="tpu_custom_call" | custom-call | tf_op jit(solution)/shard_map/pallas_call | solution.py:734
  34.6 0.0 all-to-all-done.received_k
  34.7 6.4 %all-to-all-start.1 = ((f32[32,16,128]{2,1,0:T(8,128)}), f32[32,16,128]{2,1,0:T(8,128)S(1)}, u32[]{:S(2)}, u32[]{:S(2)}) async-start(f32[32,16,128]{2,1,0:T(8,128)} %get-tuple-element.84), calls=%async_computation.1 | async-start | bytes 524288 | tf_op jit(solution)/shard_map/all_to_all | solution.py:814
  41.1 0.3 collective-permute-start.8
  41.4 1.5 %collective-permute-start.9 = (f32[128,128]{1,0:T(8,128)S(1)}, f32[128,128]{1,0:T(8,128)S(1)}, u32[]{:S(2)}, u32[]{:S(2)}) collective-permute-start(f32[128,128]{1,0:T(8,128)S(1)} %get-tuple-element.94), channel_id=1, source_target_pairs={{0,24},{8,0},{16,8},{24,16},{1,25},{9,1},{17,9},{25,17},{2,26},{10... | collective-permute-start | bytes 196616 | tf_op jit(solution)/shard_map/ppermute | solution.py:35
  42.9 2.5 %collective-permute-done.8.low = f32[128,128]{1,0:T(8,128)S(1)} collective-permute-done((f32[128,128]{1,0:T(8,128)S(1)}, f32[128,128]{1,0:T(8,128)S(1)}, u32[]{:S(2)}, u32[]{:S(2)}) %collective-permute-start.8) | collective-permute-done | bytes 65568 | tf_op jit(solution)/shard_map/ppermute | solution.py:35
  45.4 0.5 collective-permute-done.9.high
  45.9 0.2 shard_map.51
  46.1 1.6 %collective-permute-start.10 = (f32[324,128]{1,0:T(8,128)S(1)}, f32[324,128]{1,0:T(8,128)S(1)}, u32[]{:S(2)}, u32[]{:S(2)}) collective-permute-start(f32[324,128]{1,0:T(8,128)S(1)} %get-tuple-element.102), channel_id=1, source_target_pairs={{0,1},{1,2},{2,3},{3,4},{4,5},{5,6},{6,7},{7,0},{8,9},{9,10},{10,1... | collective-permute-start | bytes 497672 | tf_op jit(solution)/shard_map/ppermute | solution.py:35
  47.7 3.3 %collective-permute-start.11 = (f32[324,128]{1,0:T(8,128)S(1)}, f32[324,128]{1,0:T(8,128)S(1)}, u32[]{:S(2)}, u32[]{:S(2)}) collective-permute-start(f32[324,128]{1,0:T(8,128)S(1)} %get-tuple-element.103), channel_id=1, source_target_pairs={{0,7},{1,0},{2,1},{3,2},{4,3},{5,4},{6,5},{7,6},{8,15},{9,8},{10,9... | collective-permute-start | bytes 497672 | tf_op jit(solution)/shard_map/ppermute | solution.py:35
  51.0 0.7 %all-to-all-done.1.received = f32[32,16,128]{2,1,0:T(8,128)S(1)} async-done(((f32[32,16,128]{2,1,0:T(8,128)}), f32[32,16,128]{2,1,0:T(8,128)S(1)}, u32[]{:S(2)}, u32[]{:S(2)}) %all-to-all-start.1) | async-done | bytes 262176 | tf_op jit(solution)/shard_map/all_to_all | solution.py:814
  51.7 7.1 %shard_map.49 = (f32[4,24,128]{2,1,0:T(8,128)S(1)}, f32[38,24,256]{2,1,0:T(8,128)S(1)}, f32[38,24,256]{2,1,0:T(8,128)S(1)}, f32[38,24,256]{2,1,0:T(8,128)S(1)}, ...) custom-call(f32[32,16,128]{2,1,0:T(8,128)} %all-to-all-done.received_k, ...), custom_call_target="tpu_custom_call" | custom-call | tf_op jit(solution)/shard_map/pallas_call | solution.py:734
  58.8 0.0 collective-permute-done.10.low
  58.8 0.0 collective-permute-done.11.high
  58.9 4.6 %shard_map.52 = (f32[32,16,256]{2,1,0:T(8,128)}, f32[32,16,256]{2,1,0:T(8,128)}) custom-call(f32[4,24,128]{2,1,0:T(8,128)S(1)} %get-tuple-element.85.region, f32[24,16,128]{2,1,0:T(8,128)S(1)} %get-tuple-element.86.wl1, f32[24,16,128]{2,1,0:T(8,128)S(1)} %get-tuple-element.87.ws1, f32[24,16,128]{2,1,0:T(8,128)S(1)} %get-tuple-element.88.wz1, ...), custom_call_target="tpu_custom_call" | custom-call | tf_op jit(solution)/shard_map/pallas_call | solution.py:734
  (1 shorter events, 0.0 us)
Async XLA Ops:
  0.6 1.0 %copy-start = (f32[32,16,256]{2,1,0:T(8,128)S(1)}, f32[32,16,256]{2,1,0:T(8,128)}, u32[]{:S(2)}) copy-start(f32[32,16,256]{2,1,0:T(8,128)} %b.1) | copy-start | bytes 1572868
  1.7 1.0 %copy-start.1 = (f32[32,16,256]{2,1,0:T(8,128)S(1)}, f32[32,16,256]{2,1,0:T(8,128)}, u32[]{:S(2)}) copy-start(f32[32,16,256]{2,1,0:T(8,128)} %k.1) | copy-start | bytes 1572868
  2.9 10.8 %collective-permute-start = (f32[5,32,256]{2,1,0:T(8,128)S(1)}, f32[5,32,256]{2,1,0:T(8,128)S(1)}, u32[]{:S(2)}, u32[]{:S(2)}) collective-permute-start(f32[5,32,256]{2,1,0:T(8,128)S(1)} %get-tuple-element.57), channel_id=1, source_target_pairs={{0,1},{1,2},{2,3},{3,4},{4,5},{5,6},{6,7},{7,0},{8,9},{9,10},{10,1... | collective-permute-start | bytes 491528 | tf_op jit(solution)/shard_map/ppermute | solution.py:35
  5.9 9.2 %collective-permute-start.1 = (f32[5,32,256]{2,1,0:T(8,128)S(1)}, f32[5,32,256]{2,1,0:T(8,128)S(1)}, u32[]{:S(2)}, u32[]{:S(2)}) collective-permute-start(f32[5,32,256]{2,1,0:T(8,128)S(1)} %get-tuple-element.58), channel_id=1, source_target_pairs={{0,7},{1,0},{2,1},{3,2},{4,3},{5,4},{6,5},{7,6},{8,15},{9,8},{10,9... | collective-permute-start | bytes 491528 | tf_op jit(solution)/shard_map/ppermute | solution.py:35
  10.2 24.4 %all-to-all-start = ((f32[32,16,128]{2,1,0:T(8,128)}), f32[32,16,128]{2,1,0:T(8,128)}, u32[]{:S(2)}, u32[]{:S(2)}) async-start(f32[32,16,128]{2,1,0:T(8,128)} %get-tuple-element.54), calls=%async_computation | async-start | bytes 524288 | tf_op jit(solution)/shard_map/all_to_all | solution.py:784
  15.3 5.6 %collective-permute-start.2 = (f32[5,24,256]{2,1,0:T(8,128)S(1)}, f32[5,24,256]{2,1,0:T(8,128)S(1)}, u32[]{:S(2)}, u32[]{:S(2)}) collective-permute-start(f32[5,24,256]{2,1,0:T(8,128)S(1)} %get-tuple-element.60), channel_id=1, source_target_pairs={{0,8},{8,16},{16,24},{24,0},{1,9},{9,17},{17,25},{25,1},{2,10},{10... | collective-permute-start | bytes 368648 | tf_op jit(solution)/shard_map/ppermute | solution.py:35
  15.3 6.0 %collective-permute-start.3 = (f32[5,24,256]{2,1,0:T(8,128)S(1)}, f32[5,24,256]{2,1,0:T(8,128)S(1)}, u32[]{:S(2)}, u32[]{:S(2)}) collective-permute-start(f32[5,24,256]{2,1,0:T(8,128)S(1)} %get-tuple-element.61), channel_id=1, source_target_pairs={{0,24},{8,0},{16,8},{24,16},{1,25},{9,1},{17,9},{25,17},{2,26},{10... | collective-permute-start | bytes 368648 | tf_op jit(solution)/shard_map/ppermute | solution.py:35
  22.1 7.2 %collective-permute-start.4 = (f32[7,16,128]{2,1,0:T(8,128)S(1)}, f32[7,16,128]{2,1,0:T(8,128)S(1)}, u32[]{:S(2)}, u32[]{:S(2)}) collective-permute-start(f32[7,16,128]{2,1,0:T(8,128)S(1)} %get-tuple-element.73), channel_id=1, source_target_pairs={{0,1},{1,2},{2,3},{3,4},{4,5},{5,6},{6,7},{7,0},{8,9},{9,10},{10,1... | collective-permute-start | bytes 172040 | tf_op jit(solution)/shard_map/ppermute | solution.py:35
  22.3 7.0 %collective-permute-start.5 = (f32[7,16,128]{2,1,0:T(8,128)S(1)}, f32[7,16,128]{2,1,0:T(8,128)S(1)}, u32[]{:S(2)}, u32[]{:S(2)}) collective-permute-start(f32[7,16,128]{2,1,0:T(8,128)S(1)} %get-tuple-element.74), channel_id=1, source_target_pairs={{0,7},{1,0},{2,1},{3,2},{4,3},{5,4},{6,5},{7,6},{8,15},{9,8},{10,9... | collective-permute-start | bytes 172040 | tf_op jit(solution)/shard_map/ppermute | solution.py:35
  29.4 3.7 %collective-permute-start.6 = (f32[7,16,128]{2,1,0:T(8,128)S(1)}, f32[7,16,128]{2,1,0:T(8,128)S(1)}, u32[]{:S(2)}, u32[]{:S(2)}) collective-permute-start(f32[7,16,128]{2,1,0:T(8,128)S(1)} %get-tuple-element.82), channel_id=1, source_target_pairs={{0,8},{8,16},{16,24},{24,0},{1,9},{9,17},{17,25},{25,1},{2,10},{10... | collective-permute-start | bytes 172040 | tf_op jit(solution)/shard_map/ppermute | solution.py:35
  30.1 3.1 %collective-permute-start.7 = (f32[7,16,128]{2,1,0:T(8,128)S(1)}, f32[7,16,128]{2,1,0:T(8,128)S(1)}, u32[]{:S(2)}, u32[]{:S(2)}) collective-permute-start(f32[7,16,128]{2,1,0:T(8,128)S(1)} %get-tuple-element.83), channel_id=1, source_target_pairs={{0,24},{8,0},{16,8},{24,16},{1,25},{9,1},{17,9},{25,17},{2,26},{10... | collective-permute-start | bytes 172040 | tf_op jit(solution)/shard_map/ppermute | solution.py:35
  34.7 17.1 %all-to-all-start.1 = ((f32[32,16,128]{2,1,0:T(8,128)}), f32[32,16,128]{2,1,0:T(8,128)S(1)}, u32[]{:S(2)}, u32[]{:S(2)}) async-start(f32[32,16,128]{2,1,0:T(8,128)} %get-tuple-element.84), calls=%async_computation.1 | async-start | bytes 524288 | tf_op jit(solution)/shard_map/all_to_all | solution.py:814
  41.1 4.3 %collective-permute-start.8 = (f32[128,128]{1,0:T(8,128)S(1)}, f32[128,128]{1,0:T(8,128)S(1)}, u32[]{:S(2)}, u32[]{:S(2)}) collective-permute-start(f32[128,128]{1,0:T(8,128)S(1)} %get-tuple-element.93), channel_id=1, source_target_pairs={{0,8},{8,16},{16,24},{24,0},{1,9},{9,17},{17,25},{25,1},{2,10},{10... | collective-permute-start | bytes 196616 | tf_op jit(solution)/shard_map/ppermute | solution.py:35
  41.4 4.5 %collective-permute-start.9 = (f32[128,128]{1,0:T(8,128)S(1)}, f32[128,128]{1,0:T(8,128)S(1)}, u32[]{:S(2)}, u32[]{:S(2)}) collective-permute-start(f32[128,128]{1,0:T(8,128)S(1)} %get-tuple-element.94), channel_id=1, source_target_pairs={{0,24},{8,0},{16,8},{24,16},{1,25},{9,1},{17,9},{25,17},{2,26},{10... | collective-permute-start | bytes 196616 | tf_op jit(solution)/shard_map/ppermute | solution.py:35
  46.1 12.7 %collective-permute-start.10 = (f32[324,128]{1,0:T(8,128)S(1)}, f32[324,128]{1,0:T(8,128)S(1)}, u32[]{:S(2)}, u32[]{:S(2)}) collective-permute-start(f32[324,128]{1,0:T(8,128)S(1)} %get-tuple-element.102), channel_id=1, source_target_pairs={{0,1},{1,2},{2,3},{3,4},{4,5},{5,6},{6,7},{7,0},{8,9},{9,10},{10,1... | collective-permute-start | bytes 497672 | tf_op jit(solution)/shard_map/ppermute | solution.py:35
  47.7 11.1 %collective-permute-start.11 = (f32[324,128]{1,0:T(8,128)S(1)}, f32[324,128]{1,0:T(8,128)S(1)}, u32[]{:S(2)}, u32[]{:S(2)}) collective-permute-start(f32[324,128]{1,0:T(8,128)S(1)} %get-tuple-element.103), channel_id=1, source_target_pairs={{0,7},{1,0},{2,1},{3,2},{4,3},{5,4},{6,5},{7,6},{8,15},{9,8},{10,9... | collective-permute-start | bytes 497672 | tf_op jit(solution)/shard_map/ppermute | solution.py:35

commit v6 on v5

--- a/solution.py
+++ b/solution.py
@@ -25,7 +25,7 @@
 K0, B0, S0 = 3, 2, 3
 K1, B1, S1 = 4, 3, 4
 EDGE = 2
-REGISTERS = 48
+REGISTERS = [48]
 SPARE = 4 * 1024 * 1024
 VMEM_BYTES = 64 * 1024 * 1024
 
@@ -110,9 +110,28 @@
     return jnp.where(last, 0.0, w), w + jnp.where(place == 0, k, down(w, axis))
 
 
-def unrolled(plane, count):
-    registers = max(1, plane[0] * plane[1] // 1024)
-    return max(1, min(count, REGISTERS // registers))
+def blocks_of(plane, count):
+    most = max(1, REGISTERS[0] // max(1, plane[0] * plane[1] // 1024))
+    best = None
+    for blocks in range(max(1, count // (2 * most)), count + 1):
+        steps = count // blocks
+        cost = (count - blocks * steps) * 0.5 + abs(steps - most)
+        if best is None or cost < best[0]:
+            best = (cost, blocks, steps)
+    return best[1:]
+
+
+def carried(low, high, body, carry, plane):
+    blocks, steps = blocks_of(plane, high - low)
+    end = low + blocks * steps
+    if blocks == 1:
+        end = low
+        steps = high - low
+    elif blocks * steps:
+        carry = lax.fori_loop(low, end, body, carry, unroll=steps)
+    for i in range(end, high):
+        carry = body(i, carry)
+    return carry
 
 
 def loop(low, high, body, plane):
@@ -120,7 +139,7 @@
         body(i)
         return carry
 
-    lax.fori_loop(low, high, step, 0, unroll=unrolled(plane, high - low))
+    carried(low, high, step, 0, plane)
 
 
 def weigh(k, wl, ws, wz, total, inverse, row_edge, lane_edge, span=None, before=None):
@@ -142,7 +161,7 @@
         return lead
 
     before = jnp.zeros(plane, F32) if before is None else before
-    lax.fori_loop(low, high, body, before, unroll=unrolled(plane, high - low))
+    carried(low, high, body, before, plane)
 
 
 def beside(x, w, i):
@@ -311,10 +330,20 @@
     loop(*span, restrict, (2 * b.shape[1], b.shape[2]))
 
 
+def put_rows(out, at, parts):
+    lanes = out.shape[1]
+    for part in parts:
+        rows = part.shape[0]
+        for h in range(part.shape[1] // lanes):
+            out[at : at + rows] = part[:, h * lanes : (h + 1) * lanes]
+            at += rows
+    return at
+
+
 def fine_outer_kernel(
     k_own, low, high, k1,
     wl_in, ws_in, wz_in, total_in, inverse_in, b_in, first_in, second_in, pairs_in,
-    wl_out, ws_out, wz_out, total_out, b_out, s_out, b1_out, up_out, down_out,
+    wl_out, ws_out, wz_out, total_out, b_out, s_out, b1_out, up_out, down_out, s_up, s_down,
     wl, ws, wz, total, inverse, b, first, second, pairs, k, halves,
 ):
     planes, rows, lanes = b.shape[0], s_out.shape[1], b.shape[2]
@@ -352,6 +381,8 @@
     for out, mine in ((wl_out, wl), (ws_out, ws), (wz_out, wz), (total_out, total), (b_out, b)):
         out[0 : K0 + 1] = mine[0 : K0 + 1]
         out[K0 + 1 :] = mine[end - 1 :]
+    put_rows(s_up, 0, [s_out[:, rows - S0 + r, :] for r in range(S0)])
+    put_rows(s_down, 0, [s_out[:, r, :] for r in range(S0)])
     half, count = b1_out.shape[0], b1_out.shape[1]
     for out, k_from, b_from in ((up_out, count - K1, count - B1), (down_out, 0, 0)):
         for r in range(K1):
@@ -393,9 +424,9 @@
 
 
 def middle_down_kernel(
-    k_own, b_own, low, high,
-    message, wl, ws, wz, inverse, b, s_out,
-    total, k, first, second, pairs, halves, held, sems,
+    k_own, b_own, low, high, _s_low, _s_high,
+    message, k, b, s_out,
+    wl, ws, wz, inverse, total, first, second, pairs, halves, held, sems,
 ):
     scale = 0.25
     join(k, k_own, lambda r: low[r], lambda r: high[r], K1, K1)
@@ -417,21 +448,9 @@
     wait(copies)
 
 
-def field_planes_kernel(s, s1, up_out, down_out):
-    fine, rows, own, rows1, lanes = s.shape[0], s.shape[1], s1.shape[0], s1.shape[1], s1.shape[2]
-    for out, from0, from1 in ((up_out, fine - S0, own - S1), (down_out, 0, 0)):
-        for r in range(S0):
-            for h in range(2):
-                at = (2 * r + h) * rows
-                out[at : at + rows] = s[from0 + r, :, h * lanes : (h + 1) * lanes]
-        for r in range(S1):
-            at = 2 * S0 * rows + r * rows1
-            out[at : at + rows1] = s1[from1 + r]
-
-
-def split_lanes(ref, rows):
+def split_lanes(ref, first, rows):
     def get(r):
-        at = 2 * r * rows
+        at = first + 2 * r * rows
         return jnp.concatenate([ref[at : at + rows], ref[at + rows : at + 2 * rows]], axis=1)
 
     return get
@@ -444,20 +463,21 @@
     return get
 
 
-def field_rows_kernel(s, s1, low, high, s_out, s1_out, up_out, down_out):
-    rows, rows1, lanes = s.shape[1], s1.shape[1], s1.shape[2]
-    join(s_out, s, split_lanes(low, rows), split_lanes(high, rows), S0, S0)
+def field_planes_kernel(s, s1, low, high, s_out, up_out, down_out):
+    fine, own = s.shape[0], s1.shape[0]
+    widen(s_out, s, split_lanes(low, 0, fine), split_lanes(high, 0, fine), S0)
+    for out, from0, from1 in ((up_out, fine - S0, own - S1), (down_out, 0, 0)):
+        at = put_rows(out, 0, [s_out[from0 + r] for r in range(S0)])
+        put_rows(out, at, [s1[from1 + r] for r in range(S1)])
+
+
+def field_rows_kernel(s, s1, low, high, _weights, s_out, s1_out, up_out, down_out):
+    rows, rows1 = s.shape[1], s1.shape[1]
+    join(s_out, s, split_lanes(low, 0, rows), split_lanes(high, 0, rows), S0, S0)
     first = 2 * S0 * rows
     join(s1_out, s1, from_row(low, first, rows1), from_row(high, first, rows1), S1, S1)
-    fine, own = s_out.shape[0], s1_out.shape[0]
-    for out, from0, from1 in ((up_out, rows - S0, rows1 - S1), (down_out, 0, 0)):
-        for r in range(S0):
-            for h in range(2):
-                at = (2 * r + h) * fine
-                out[at : at + fine] = s_out[:, from0 + r, h * lanes : (h + 1) * lanes]
-        for r in range(S1):
-            at = 2 * S0 * fine + r * own
-            out[at : at + own] = s1_out[:, from1 + r, :]
+    put_rows(up_out, 0, [s1_out[:, rows1 - S1 + r, :] for r in range(S1)])
+    put_rows(down_out, 0, [s1_out[:, r, :] for r in range(S1)])
 
 
 def unpack(received, out, first, block_x, block_y, across, along):
@@ -507,7 +527,7 @@
         inverse[i] = jnp.where(there, 1.0 / whole, 0.0)
         return lead
 
-    lax.fori_loop(0, planes - 1, body, jnp.zeros(k.shape[1:], F32), unroll=unrolled(k.shape[1:], planes - 1))
+    carried(0, planes - 1, body, jnp.zeros(k.shape[1:], F32), k.shape[1:])
 
 
 def beside_packed(x, w, i):
@@ -576,31 +596,74 @@
     return x
 
 
+def mean_matrix(lanes, valid):
+    row, col = iota((lanes, lanes), 0), iota((lanes, lanes), 1)
+    return jnp.where(lax.rem(row, valid) // 2 == col, 0.125, 0.0).astype(BF16)
+
+
+def coarse_weights_kernel(
+    valid, received, wl2, ws2, wz2, total2, level3, k4,
+    low2, inverse2, k2, halves2, wl3, ws3, wz3, total3, inverse3, k3, pairs3, halves3,
+):
+    planes, rows, lanes = k2.shape
+    across, along = lax.axis_size("gx"), lax.axis_size("gy")
+    unpack(received, k2, 0, rows // across, 2 * (planes - 2) // along, across, along)
+    own3 = planes - 2
+    clear_ends(k3)
+    k3[1 : own3 + 1] = coarser(k2[1 : own3 + 1], halves2, mean_matrix(lanes, valid))
+
+    def add3(j):
+        pairs3[j] = k3[2 * j + 1] + k3[2 * j + 2]
+
+    loop(0, pairs3.shape[0], add3, pairs3.shape[1:])
+    k4[...] = coarser(pairs3[...], halves3, halving(lanes, lanes, valid // 2))
+    weigh_packed(k2, wl2, low2, ws2, wz2, total2, inverse2)
+    weigh(k3, wl3, ws3, wz3, total3, inverse3, True, False)
+
+    def pack(i):
+        lane = iota(level3.shape[1:], 1)
+        parts = [jnp.where(lane < valid // 2, ref[i], 0.0) for ref in (wl3, ws3, wz3, total3)]
+        level3[i] = sum(
+            (pltpu.roll(part, f * (valid // 2), 1) for f, part in enumerate(parts) if f), parts[0]
+        )
+
+    loop(0, planes - 1, pack, level3.shape[1:])
+
+
+def invert(total):
+    return jnp.where(total > 0.0, 1.0 / total, 0.0)
+
+
 def coarse_kernel(
-    valid, received_k, received, stash, region, wl, ws, wz, total, b,
-    wl2, low2, ws2, wz2, total2, inverse2, k2, b2, first2, second2, pairs2, halves2,
-    wl3, ws3, wz3, total3, inverse3, k3, b3, first3, second3, pairs3, halves3, sems,
+    valid, received, wl2, ws2, wz2, total2, level3, k4, stash,
+    region, wl, ws, wz, total, b,
+    low2, inverse2, b2, first2, second2, pairs2, halves2,
+    wl3, ws3, wz3, total3, inverse3, b3, first3, second3, pairs3, halves3, sems,
 ):
     copies = fetch((wl, ws, wz, total, b), stash, sems)
     planes, rows, lanes = b2.shape
     across, along = lax.axis_size("gx"), lax.axis_size("gy")
     block_x, block_y = rows // across, 2 * (planes - 2) // along
-    unpack(received_k, k2, 0, block_x, block_y, across, along)
+    own3, half = planes - 2, valid // 2
     unpack(received, b2, 0, block_x, block_y, across, along)
-    own3, half = planes - 2, valid // 2
     row, col = iota((lanes, lanes), 0), iota((lanes, lanes), 1)
-    matrix2 = jnp.where(lax.rem(row, valid) // 2 == col, 0.125, 0.0).astype(BF16)
-    matrix3 = halving(lanes, lanes, half)
-    clear_ends(k3)
-    k3[1 : own3 + 1] = coarser(k2[1 : own3 + 1], halves2, matrix2)
-
-    def add3(j):
-        pairs3[j] = k3[2 * j + 1] + k3[2 * j + 2]
-
-    loop(0, pairs3.shape[0], add3, pairs3.shape[1:])
-    k4 = coarser(pairs3[...], halves3, matrix3)
-    weigh_packed(k2, wl2, low2, ws2, wz2, total2, inverse2)
-    weigh(k3, wl3, ws3, wz3, total3, inverse3, True, False)
+    matrix2, matrix3 = mean_matrix(lanes, valid), halving(lanes, lanes, half)
+
+    def complete(i):
+        low2[i] = across_down(wl2[i], wl2[i - 1])
+        inverse2[i] = invert(total2[i])
+
+    def unpack3(i):
+        lane = iota(level3.shape[1:], 1)
+        for f, ref in enumerate((wl3, ws3, wz3, total3)):
+            part = level3[i]
+            if f:
+                part = pltpu.roll(part, lanes - f * half, 1)
+            ref[i] = jnp.where(lane < half, part, 0.0)
+        inverse3[i] = invert(total3[i])
+
+    loop(1, own3 + 1, complete, b2.shape[1:])
+    loop(0, own3 + 1, unpack3, level3.shape[1:])
     w2, w3 = (wl2, low2, ws2, wz2), (wl3, ws3, wz3)
     scale2, scale3 = 0.25**2, 0.25**3
     coarse_pre(b2, w2, inverse2, first2, second2, scale2)
@@ -620,7 +683,7 @@
         )
 
     loop(0, pairs3.shape[0], rest3, pairs3.shape[1:])
-    x4 = bottom(k4, coarser(pairs3[...], halves3, matrix3), 0.25**4)
+    x4 = bottom(k4[...], coarser(pairs3[...], halves3, matrix3), 0.25**4)
     twice(pairs3, widened(x4, doubling(lanes, lanes, half // 2)))
 
     def add_up3(j):
@@ -652,17 +715,16 @@
 
 
 def fine_up_kernel(
-    region, wl1, ws1, wz1, inverse1, b1, s1_own, wl, ws, wz, total, b, s_own, low, high,
+    region, k1, b1, s1_own, wl, ws, wz, total, b, s_own, low, high,
     field_out, residual_out,
-    inverse, first1, second1, grown, s, second, tall, thick, rest,
+    wl1, ws1, wz1, total1, inverse1, inverse, first1, second1, grown, s, second, tall, thick, rest,
     out_sems,
 ):
     planes1, rows1, lanes1 = b1.shape
     planes, rows, lanes = b.shape
     w1, w = (wl1, ws1, wz1), (wl, ws, wz)
-    widen(s, s_own, split_lanes(low, planes), split_lanes(high, planes), S0)
-    first = 2 * S0 * planes
-    widen(first1, s1_own, from_row(low, first, planes1), from_row(high, first, planes1), S1)
+    weigh(k1, wl1, ws1, wz1, total1, inverse1, False, True)
+    widen(first1, s1_own, from_row(low, 0, planes1), from_row(high, 0, planes1), S1)
     count_y, block_x = region.shape[0], region.shape[1] // 3
     expanded = widened(region[...], doubling(lanes1, 2 * lanes1, lanes1))
     for q in range(block_x + 2 * EDGE):
@@ -689,20 +751,20 @@
         tall[:, pl.ds(where + 1, half, stride=2), :] = part
     matrix = doubling(lanes1, lanes, lanes1)
     thick[...] = pick(tall[...].reshape(count * rows, lanes1), matrix).reshape(thick.shape)
-    s[0] = s[0] + thick[0]
-    s[planes - 1] = s[planes - 1] + thick[count - 1]
+    s[0] = s_own[0] + thick[0]
+    s[planes - 1] = s_own[planes - 1] + thick[count - 1]
 
     def add(q):
         for side in range(2):
             i = 2 * q + side - 1
-            s[i] = s[i] + thick[q]
+            s[i] = s_own[i] + thick[q]
 
     loop(1, count - 1, add, b.shape[1:])
 
-    def invert(i):
-        inverse[i] = jnp.where(total[i] > 0.0, 1.0 / total[i], 0.0)
-
-    loop(1, planes - 1, invert, b.shape[1:])
+    def complete(i):
+        inverse[i] = invert(total[i])
+
+    loop(1, planes - 1, complete, b.shape[1:])
     post_smooth(b, s, second, w, inverse, 1.0, (1, planes - 1), (2, planes - 2))
     own, own_rows = field_out.shape[0], field_out.shape[1]
     mine = s.at[K0 : K0 + own, 0:own_rows]
@@ -724,7 +786,11 @@
     wait(copies)
 
 
-def call(kernel, outs, scratch=(), held=0, kept=(), sems=(), alias=None, cost=0):
+def call(kernel, outs, scratch=(), held=0, kept=(), sems=(), cost=0, registers=48):
+    def body(*refs):
+        REGISTERS[0] = registers
+        kernel(*refs)
+
     def run(*operands):
         inputs = [o.shape for i, o in enumerate(operands) if i not in kept]
         shapes = inputs + list(outs[held:]) + list(scratch)
@@ -732,13 +798,12 @@
         places = [pltpu.HBM if i in kept else pltpu.VMEM for i in range(len(operands))]
         out_places = [pltpu.HBM if i < held else pltpu.VMEM for i in range(len(outs))]
         return pl.pallas_call(
-            kernel,
+            body,
             out_shape=[jax.ShapeDtypeStruct(shape, F32) for shape in outs],
             in_specs=[pl.BlockSpec(memory_space=place) for place in places],
             out_specs=[pl.BlockSpec(memory_space=place) for place in out_places],
             scratch_shapes=[pltpu.VMEM(shape, F32) for shape in scratch]
             + [pltpu.SemaphoreType.DMA((n,)) for n in sems],
-            input_output_aliases=alias or {},
             cost_estimate=pl.CostEstimate(flops=cost, bytes_accessed=cost, transcendentals=0) if cost else None,
             compiler_params=pltpu.CompilerParams(vmem_limit_bytes=4 * words + SPARE),
         )(*operands)
@@ -784,12 +849,15 @@
     k2 = lax.all_to_all(message, both, 0, 0, tiled=True)
 
     block = (bx + 2 * K0, tall, nz)
-    inner = call(fine_inner_kernel, [block] * 8 + [(hx, by, nz)], [block])(k_own, b_own)
+    inner = call(fine_inner_kernel, [block] * 8 + [(hx, by, nz)], [block], registers=72)(
+        k_own, b_own
+    )
     slab = (K1 + B1, hx, hz)
     edges = (2 * K0 + 2, tall, nz)
-    *outer, s, b1, up_rows, down_rows = call(
+    field_slab = (2 * S0 * bx, hz)
+    *outer, s, b1, up_rows, down_rows, s_up, s_down = call(
         fine_outer_kernel,
-        [edges] * 5 + [(bx, by, nz), (hx, hy, hz), slab, slab],
+        [edges] * 5 + [(bx, by, nz), (hx, hy, hz), slab, slab, field_slab, field_slab],
         [block] * 8 + [(hx, by, nz), block, (hx, by, hz)],
     )(k_own, low, high, k1, *inner)
     planes = 5 * block[0] + VMEM_BYTES // (4 * tall * nz)
@@ -797,6 +865,7 @@
         *inner[:4], inner[5], *outer
     )
     low, high = rotate(up_rows, "gy", 1), rotate(down_rows, "gy", -1)
+    s_low, s_high = rotate(s_up, "gy", 1), rotate(s_down, "gy", -1)
     slab = (K1 + B1, tall1, hz)
     k1_own, b1_own, up_planes, down_planes = call(
         widen_middle_kernel, [(hx, tall1, hz), (hx, tall1, hz), slab, slab], kept=(4,)
@@ -804,44 +873,55 @@
     low, high = rotate(up_planes, "gx", 1), rotate(down_planes, "gx", -1)
 
     block1 = (hx + 2 * K1, tall1, hz)
-    message, *kept1, s1 = call(
+    message, k1, b1, s1 = call(
         middle_down_kernel,
-        [pieces] + [block1] * 5 + [(hx, hy, hz)],
-        [block1] * 4 + [(qx, hy, hz), (qx, hy, hz), (group, *pieces[1:])],
+        [pieces] + [block1] * 2 + [(hx, hy, hz)],
+        [block1] * 7 + [(qx, hy, hz), (qx, hy, hz), (group, *pieces[1:])],
         held=1,
         sems=(devices // group,),
-    )(k1_own, b1_own, low, high)
+    )(k1_own, b1_own, low, high, s_low, s_high)
     received = lax.all_to_all(message, both, 0, 0, tiled=True)
-
-    slab = (2 * S0 * by + S1 * hy, hz)
-    up_planes, down_planes = call(field_planes_kernel, [slab, slab])(s, s1)
-    low, high = rotate(up_planes, "gx", 1), rotate(down_planes, "gx", -1)
-    slab = (2 * S0 * block[0] + S1 * block1[0], hz)
-    s_own, s1_own, up_rows, down_rows = call(
-        field_rows_kernel, [(block[0], by, nz), (block1[0], hy, hz), slab, slab]
-    )(s, s1, low, high)
-    low, high = rotate(up_rows, "gy", 1), rotate(down_rows, "gy", -1)
 
     x2, y2 = across * qx, along * qy
     level2, level3 = (y2 // 2 + 2, x2, hz), (y2 // 2 + 2, x2 // 2, hz)
     half2, half3 = (y2 // 2, x2, hz), (y2 // 4, x2 // 2, hz)
+    valid = nz // 4
+    coarse = call(
+        partial(coarse_weights_kernel, valid),
+        [level2] * 4 + [level3, (y2 // 4, x2 // 4, hz)],
+        [level2] * 3 + [half2] + [level3] * 6 + [half3] * 2,
+        registers=48,
+    )(k2)
+    slab = (2 * S0 * tall + S1 * hy, hz)
+    s_rows, up_planes, down_planes = call(field_planes_kernel, [plane, slab, slab])(
+        s, s1, s_low, s_high
+    )
+    low, high = rotate(up_planes, "gx", 1), rotate(down_planes, "gx", -1)
+    slab = (S1 * block1[0], hz)
+    s_own, s1_own, up_rows, down_rows = call(
+        field_rows_kernel, [block, (block1[0], hy, hz), slab, slab]
+    )(s_rows, s1, low, high, coarse[-1])
+    low, high = rotate(up_rows, "gy", 1), rotate(down_rows, "gy", -1)
+
     region, *weights = call(
-        partial(coarse_kernel, nz // 4),
+        partial(coarse_kernel, valid),
         [(qy // 2 + EDGE, 3 * qx, hz)] + [block] * 5,
-        [level2] * 10 + [half2] * 2 + [level3] * 9 + [half3] * 2,
-        kept=(2,),
+        [level2] * 5 + [half2] * 2 + [level3] * 8 + [half3] * 2,
+        kept=(7,),
         sems=(5,),
-    )(k2, received, stash)
+        registers=40,
+    )(received, *coarse, stash)
 
     count = hx + 2 * EDGE
     field, rest = call(
         fine_up_kernel,
         [(bx, by, nz)] * 2,
-        [block] + [block1, block1, (qx + 2 * EDGE, tall1, hz)]
+        [block1] * 5 + [block, block1, block1, (qx + 2 * EDGE, tall1, hz)]
         + [block, block, (count, tall, hz), (count, tall, nz), (bx, by, nz)],
         held=2,
         sems=(5,),
-    )(region, *kept1, s1_own, *weights, s_own, low, high)
+        registers=96,
+    )(region, k1, b1, s1_own, *weights, s_own, low, high)
     return field, rest
 
 

time: 63.9 us -> 61.1 us (0.956)
  Pallas kernels: 22 us -> 19 us
  starting transfers between devices: 30.9 us -> 32.1 us
  waiting for transfers between devices: 7.74 us -> 6.71 us
    ppermute x12 -> x14, starting transfers between devices: 21.1 us -> 25.8 us  [rotate(): lax.ppermute(value, axis, [(i, (i + shift) % size) for i in range(size)])]
    all_to_all x1, starting transfers between devices: 6.4 us -> 2.94 us  [per_device(): received = lax.all_to_all(message, both, 0, 0, tiled=True)]
    pallas_call x12 -> x13, Pallas kernels: 22 us -> 19 us  [run(): pl.pallas_call(body, out_shape=[jax.ShapeDtypeStruct(shape, F32) for shap...]
    all_to_all x1, waiting for transfers between devices: 0.71 us -> 0.01 us  [per_device(): received = lax.all_to_all(message, both, 0, 0, tiled=True)]
    ppermute x12 -> x14, waiting for transfers between devices: 7.03 us -> 6.71 us  [rotate(): lax.ppermute(value, axis, [(i, (i + shift) % size) for i in range(size)])]
  transfers between devices with their start and end apart: 14 -> 16, of which waited for: 8 -> 7; matrix products, arithmetic and copies ran while one was open for 0% -> 0% of each run, Pallas kernels for 27% -> 25%
where the time goes in v6:
time: 61.1 us; the launch traced here: 60.7 us
  starting transfers between devices  32.1 us (53%)
  Pallas kernels  19 us (31%)
  waiting for transfers between devices  6.71 us (11%)
  local copies, waits for them, and re-layouts  2.08 us (3%)
  between operations  0.78 us (1%)
    ppermute x14, starting transfers between devices, rotate(): lax.ppermute(value, axis, [(i, (i + shift) % size) for i in range(size)])  25.8 us
    pallas_call x13, Pallas kernels, run(): pl.pallas_call(body, out_shape=[jax.ShapeDtypeStruct(shape, F32) for shap...  19 us
    ppermute x14, waiting for transfers between devices, rotate(): lax.ppermute(value, axis, [(i, (i + shift) % size) for i in range(size)])  6.71 us
    all_to_all x1, starting transfers between devices, per_device(): k2 = lax.all_to_all(message, both, 0, 0, tiled=True)  3.42 us
    all_to_all x1, starting transfers between devices, per_device(): received = lax.all_to_all(message, both, 0, 0, tiled=True)  2.94 us
    unnamed x4, local copies, waits for them, and re-layouts  2.08 us
  transfers between devices with their start and end apart: 16, of which 7 were waited for; matrix products, arithmetic and copies ran while one was open for 0% of the time, Pallas kernels for 25%

profile of v6, /device:TPU:0, one launch (start us, length us, event | category | flops | bytes accessed | tf_op | source)
XLA Modules:
  0.0 60.7 jit_solution(17858766232007096956)
XLA Ops:
  0.6 0.0 copy-start
  0.6 1.0 %copy-done = f32[32,16,256]{2,1,0:T(8,128)S(1)} copy-done((f32[32,16,256]{2,1,0:T(8,128)S(1)}, f32[32,16,256]{2,1,0:T(8,128)}, u32[]{:S(2)}) %copy-start) | copy-done | bytes 524312
  1.7 1.0 %copy-done.1 = f32[32,16,256]{2,1,0:T(8,128)S(1)} copy-done((f32[32,16,256]{2,1,0:T(8,128)S(1)}, f32[32,16,256]{2,1,0:T(8,128)}, u32[]{:S(2)}) %copy-start.1) | copy-done | bytes 524312
  2.7 0.2 shard_map.41
  2.9 3.0 %collective-permute-start = (f32[5,32,256]{2,1,0:T(8,128)S(1)}, f32[5,32,256]{2,1,0:T(8,128)S(1)}, u32[]{:S(2)}, u32[]{:S(2)}) collective-permute-start(f32[5,32,256]{2,1,0:T(8,128)S(1)} %get-tuple-element.62), channel_id=1, source_target_pairs={{0,1},{1,2},{2,3},{3,4},{4,5},{5,6},{6,7},{7,0},{8,9},{9,10},{10,1... | collective-permute-start | bytes 491528 | tf_op jit(solution)/shard_map/ppermute | solution.py:35
  5.9 3.1 %collective-permute-start.1 = (f32[5,32,256]{2,1,0:T(8,128)S(1)}, f32[5,32,256]{2,1,0:T(8,128)S(1)}, u32[]{:S(2)}, u32[]{:S(2)}) collective-permute-start(f32[5,32,256]{2,1,0:T(8,128)S(1)} %get-tuple-element.63), channel_id=1, source_target_pairs={{0,7},{1,0},{2,1},{3,2},{4,3},{5,4},{6,5},{7,6},{8,15},{9,8},{10,9... | collective-permute-start | bytes 491528 | tf_op jit(solution)/shard_map/ppermute | solution.py:35
  9.0 1.2 %shard_map.42 = (f32[32,16,128]{2,1,0:T(8,128)}, f32[16,8,128]{2,1,0:T(8,128)S(1)}) custom-call(f32[32,16,256]{2,1,0:T(8,128)S(1)} %get-tuple-element.59.refs_0_.refs_1_), custom_call_target="tpu_custom_call" | custom-call | tf_op jit(solution)/shard_map/pallas_call | solution.py:800
  10.2 3.4 %all-to-all-start.1 = ((f32[32,16,128]{2,1,0:T(8,128)}), f32[32,16,128]{2,1,0:T(8,128)}, u32[]{:S(2)}, u32[]{:S(2)}) async-start(f32[32,16,128]{2,1,0:T(8,128)} %get-tuple-element.92), calls=%async_computation.1 | async-start | bytes 524288 | tf_op jit(solution)/shard_map/all_to_all | solution.py:849
  13.6 0.0 collective-permute-done.refs_2_
  13.6 1.4 %collective-permute-done.1.refs_3_ = f32[5,32,256]{2,1,0:T(8,128)S(1)} collective-permute-done((f32[5,32,256]{2,1,0:T(8,128)S(1)}, f32[5,32,256]{2,1,0:T(8,128)S(1)}, u32[]{:S(2)}, u32[]{:S(2)}) %collective-permute-start.1) | collective-permute-done | bytes 163872 | tf_op jit(solution)/shard_map/ppermute | solution.py:35
  15.1 0.2 shard_map.43
  15.3 0.1 collective-permute-start.2
  15.3 1.7 %collective-permute-start.3 = (f32[5,24,256]{2,1,0:T(8,128)S(1)}, f32[5,24,256]{2,1,0:T(8,128)S(1)}, u32[]{:S(2)}, u32[]{:S(2)}) collective-permute-start(f32[5,24,256]{2,1,0:T(8,128)S(1)} %get-tuple-element.66), channel_id=1, source_target_pairs={{0,24},{8,0},{16,8},{24,16},{1,25},{9,1},{17,9},{25,17},{2,26},{10... | collective-permute-start | bytes 368648 | tf_op jit(solution)/shard_map/ppermute | solution.py:35
  17.1 2.5 %shard_map.44 = (f32[38,24,256]{2,1,0:T(8,128)S(1)}, f32[38,24,256]{2,1,0:T(8,128)S(1)}, f32[38,24,256]{2,1,0:T(8,128)S(1)}, f32[38,24,256]{2,1,0:T(8,128)S(1)},...) custom-call(f32[32,24,256]{2,1,0:T(8,128)S(1)} %get-tuple-element.64, ...), custom_call_target="tpu_custom_call" | custom-call | tf_op jit(solution)/shard_map/pallas_call | solution.py:800
  19.6 1.1 %collective-permute-done.2.refs_1_ = f32[5,24,256]{2,1,0:T(8,128)S(1)} collective-permute-done((f32[5,24,256]{2,1,0:T(8,128)S(1)}, f32[5,24,256]{2,1,0:T(8,128)S(1)}, u32[]{:S(2)}, u32[]{:S(2)}) %collective-permute-start.2) | collective-permute-done | bytes 122912 | tf_op jit(solution)/shard_map/ppermute | solution.py:35
  20.7 0.6 collective-permute-done.3.refs_2_
  21.3 0.8 %shard_map.45 = (f32[8,24,256]{2,1,0:T(8,128)S(1)}, f32[8,24,256]{2,1,0:T(8,128)S(1)}, f32[8,24,256]{2,1,0:T(8,128)S(1)}, f32[8,24,256]{2,1,0:T(8,128)S(1)}, f32...) custom-call(f32[32,24,256]{2,1,0:T(8,128)S(1)} %get-tuple-element.64, ...), custom_call_target="tpu_custom_call" | custom-call | tf_op jit(solution)/shard_map/pallas_call | solution.py:800
  22.1 0.2 collective-permute-start.4
  22.3 4.6 %collective-permute-start.5 = (f32[7,16,128]{2,1,0:T(8,128)S(1)}, f32[7,16,128]{2,1,0:T(8,128)S(1)}, u32[]{:S(2)}, u32[]{:S(2)}) collective-permute-start(f32[7,16,128]{2,1,0:T(8,128)S(1)} %get-tuple-element.79), channel_id=1, source_target_pairs={{0,7},{1,0},{2,1},{3,2},{4,3},{5,4},{6,5},{7,6},{8,15},{9,8},{10,9... | collective-permute-start | bytes 172040 | tf_op jit(solution)/shard_map/ppermute | solution.py:35
  26.9 0.0 collective-permute-start.8
  26.9 4.7 %collective-permute-start.9 = (f32[192,128]{1,0:T(8,128)S(1)}, f32[192,128]{1,0:T(8,128)S(1)}, u32[]{:S(2)}, u32[]{:S(2)}) collective-permute-start(f32[192,128]{1,0:T(8,128)S(1)} %get-tuple-element.90), channel_id=1, source_target_pairs={{0,7},{1,0},{2,1},{3,2},{4,3},{5,4},{6,5},{7,6},{8,15},{9,8},{10,9... | collective-permute-start | bytes 294920 | tf_op jit(solution)/shard_map/ppermute | solution.py:35
  31.6 2.3 %shard_map.46.refs_4_.refs_7_ = f32[2920,24,256]{2,1,0:T(8,128)} custom-call(f32[38,24,256]{2,1,0:T(8,128)S(1)} %get-tuple-element.68.refs_4_.refs_0_, f32[38,24,256]{2,1,0:T(8,128)S(1)} %get-tuple-element.69.refs_5_.refs_1_, f32[38,24,256]{2,1,0:T(8,128)S(1)} %get-tuple-element.70.refs_6_.refs_2_, f32[38,24,256]{2,1,0:T(8,128)S(1)} %get-tuple-element.71.refs_7_.refs_3_, ...), custom_call_target="tpu_custom_call" | custom-call | tf_op jit(solution)/shard_map/pallas_call | solution.py:800
  33.9 0.0 collective-permute-done.4.refs_2_
  33.9 0.0 collective-permute-done.5.refs_3_
  33.9 0.1 shard_map.47
  34.0 0.3 collective-permute-start.6
  34.3 1.5 %collective-permute-start.7 = (f32[7,16,128]{2,1,0:T(8,128)S(1)}, f32[7,16,128]{2,1,0:T(8,128)S(1)}, u32[]{:S(2)}, u32[]{:S(2)}) collective-permute-start(f32[7,16,128]{2,1,0:T(8,128)S(1)} %get-tuple-element.88), channel_id=1, source_target_pairs={{0,24},{8,0},{16,8},{24,16},{1,25},{9,1},{17,9},{25,17},{2,26},{10... | collective-permute-start | bytes 172040 | tf_op jit(solution)/shard_map/ppermute | solution.py:35
  35.8 0.0 collective-permute-done.8.refs_4_.refs_2_
  35.8 0.0 collective-permute-done.9.refs_5_.refs_3_
  35.8 1.9 %collective-permute-done.6.refs_2_ = f32[7,16,128]{2,1,0:T(8,128)S(1)} collective-permute-done((f32[7,16,128]{2,1,0:T(8,128)S(1)}, f32[7,16,128]{2,1,0:T(8,128)S(1)}, u32[]{:S(2)}, u32[]{:S(2)}) %collective-permute-start.6) | collective-permute-done | bytes 57376 | tf_op jit(solution)/shard_map/ppermute | solution.py:35
  37.6 0.1 collective-permute-done.7.refs_3_
  37.7 1.4 %shard_map.48 = (f32[32,16,128]{2,1,0:T(8,128)}, f32[24,16,128]{2,1,0:T(8,128)S(1)}, f32[24,16,128]{2,1,0:T(8,128)S(1)}, f32[16,8,128]{2,1,0:T(8,128)S(1)}) custom-call(f32[16,16,128]{2,1,0:T(8,128)S(1)} %get-tuple-element.85.refs_0_, f32[16,16,128]{2,1,0:T(8,128)S(1)} %get-tuple-element.86.refs_1_, f32[7,16,128]{2,1,0:T(8,128)S(1)} %collective-permute-done.6.refs_2_, ...), custom_call_target="tpu_custom_call" | custom-call | tf_op jit(solution)/shard_map/pallas_call | solution.py:800
  39.1 0.0 all-to-all-done.1.refs_0_
  39.2 2.9 %all-to-all-start = ((f32[32,16,128]{2,1,0:T(8,128)}), f32[32,16,128]{2,1,0:T(8,128)S(1)}, u32[]{:S(2)}, u32[]{:S(2)}) async-start(f32[32,16,128]{2,1,0:T(8,128)} %get-tuple-element.91), calls=%async_computation | async-start | bytes 524288 | tf_op jit(solution)/shard_map/all_to_all | solution.py:883
  42.1 0.1 shard_map.51
  42.2 1.4 %collective-permute-start.10 = (f32[176,128]{1,0:T(8,128)S(1)}, f32[176,128]{1,0:T(8,128)S(1)}, u32[]{:S(2)}, u32[]{:S(2)}) collective-permute-start(f32[176,128]{1,0:T(8,128)S(1)} %get-tuple-element.105), channel_id=1, source_target_pairs={{0,8},{8,16},{16,24},{24,0},{1,9},{9,17},{17,25},{25,1},{2,10},{10... | collective-permute-start | bytes 270344 | tf_op jit(solution)/shard_map/ppermute | solution.py:35
  43.7 0.4 collective-permute-start.11
  44.0 2.3 %shard_map.49 = (f32[18,32,128]{2,1,0:T(8,128)S(1)}, f32[18,32,128]{2,1,0:T(8,128)S(1)}, f32[18,32,128]{2,1,0:T(8,128)S(1)}, f32[18,32,128]{2,1,0:T(8,128)S(1)},...) custom-call(f32[32,16,128]{2,1,0:T(8,128)} %all-to-all-done.1.refs_0_), custom_call_target="tpu_custom_call" | custom-call | tf_op jit(solution)/shard_map/pallas_call | solution.py:800
  46.3 0.8 %collective-permute-done.10.refs_2_ = f32[176,128]{1,0:T(8,128)S(1)} collective-permute-done((f32[176,128]{1,0:T(8,128)S(1)}, f32[176,128]{1,0:T(8,128)S(1)}, u32[]{:S(2)}, u32[]{:S(2)}) %collective-permute-start.10) | collective-permute-done | bytes 90144 | tf_op jit(solution)/shard_map/ppermute | solution.py:35
  47.1 0.9 %collective-permute-done.11.refs_3_ = f32[176,128]{1,0:T(8,128)S(1)} collective-permute-done((f32[176,128]{1,0:T(8,128)S(1)}, f32[176,128]{1,0:T(8,128)S(1)}, u32[]{:S(2)}, u32[]{:S(2)}) %collective-permute-start.11) | collective-permute-done | bytes 90144 | tf_op jit(solution)/shard_map/ppermute | solution.py:35
  48.0 0.1 shard_map.52
  48.2 1.1 %collective-permute-start.12 = (f32[96,128]{1,0:T(8,128)S(1)}, f32[96,128]{1,0:T(8,128)S(1)}, u32[]{:S(2)}, u32[]{:S(2)}) collective-permute-start(f32[96,128]{1,0:T(8,128)S(1)} %get-tuple-element.114), channel_id=1, source_target_pairs={{0,1},{1,2},{2,3},{3,4},{4,5},{5,6},{6,7},{7,0},{8,9},{9,10},{10,1... | collective-permute-start | bytes 147464 | tf_op jit(solution)/shard_map/ppermute | solution.py:35
  49.3 3.7 %collective-permute-start.13 = (f32[96,128]{1,0:T(8,128)S(1)}, f32[96,128]{1,0:T(8,128)S(1)}, u32[]{:S(2)}, u32[]{:S(2)}) collective-permute-start(f32[96,128]{1,0:T(8,128)S(1)} %get-tuple-element.115), channel_id=1, source_target_pairs={{0,7},{1,0},{2,1},{3,2},{4,3},{5,4},{6,5},{7,6},{8,15},{9,8},{10,9... | collective-permute-start | bytes 147464 | tf_op jit(solution)/shard_map/ppermute | solution.py:35
  52.9 0.0 all-to-all-done.refs_0_
  52.9 3.9 %shard_map.50 = (f32[4,24,128]{2,1,0:T(8,128)S(1)}, f32[38,24,256]{2,1,0:T(8,128)S(1)}, f32[38,24,256]{2,1,0:T(8,128)S(1)}, f32[38,24,256]{2,1,0:T(8,128)S(1)}, ...) custom-call(f32[32,16,128]{2,1,0:T(8,128)S(1)} %all-to-all-done.refs_0_, ...), custom_call_target="tpu_custom_call" | custom-call | tf_op jit(solution)/shard_map/pallas_call | solution.py:800
  56.8 0.0 collective-permute-done.12.refs_10_
  56.8 0.0 collective-permute-done.13.refs_11_
  56.8 3.8 %shard_map.53 = (f32[32,16,256]{2,1,0:T(8,128)}, f32[32,16,256]{2,1,0:T(8,128)}) custom-call(f32[4,24,128]{2,1,0:T(8,128)S(1)} %get-tuple-element.99.refs_0_, f32[24,16,128]{2,1,0:T(8,128)S(1)} %get-tuple-element.100.refs_1_, f32[24,16,128]{2,1,0:T(8,128)S(1)} %get-tuple-element.101.refs_2_, f32[24,8,128]{2,1,0:T(8,128)S(1)} %get-tuple-element.107.refs_3_, ...), custom_call_target="tpu_custom_call" | custom-call | tf_op jit(solution)/shard_map/pallas_call | solution.py:800
  (1 shorter events, 0.0 us)
Async XLA Ops:
  0.6 1.0 %copy-start = (f32[32,16,256]{2,1,0:T(8,128)S(1)}, f32[32,16,256]{2,1,0:T(8,128)}, u32[]{:S(2)}) copy-start(f32[32,16,256]{2,1,0:T(8,128)} %refs_0_.1) | copy-start | bytes 1572868
  1.7 1.0 %copy-start.1 = (f32[32,16,256]{2,1,0:T(8,128)S(1)}, f32[32,16,256]{2,1,0:T(8,128)}, u32[]{:S(2)}) copy-start(f32[32,16,256]{2,1,0:T(8,128)} %refs_1_.1) | copy-start | bytes 1572868
  2.9 10.7 %collective-permute-start = (f32[5,32,256]{2,1,0:T(8,128)S(1)}, f32[5,32,256]{2,1,0:T(8,128)S(1)}, u32[]{:S(2)}, u32[]{:S(2)}) collective-permute-start(f32[5,32,256]{2,1,0:T(8,128)S(1)} %get-tuple-element.62), channel_id=1, source_target_pairs={{0,1},{1,2},{2,3},{3,4},{4,5},{5,6},{6,7},{7,0},{8,9},{9,10},{10,1... | collective-permute-start | bytes 491528 | tf_op jit(solution)/shard_map/ppermute | solution.py:35
  5.9 9.2 %collective-permute-start.1 = (f32[5,32,256]{2,1,0:T(8,128)S(1)}, f32[5,32,256]{2,1,0:T(8,128)S(1)}, u32[]{:S(2)}, u32[]{:S(2)}) collective-permute-start(f32[5,32,256]{2,1,0:T(8,128)S(1)} %get-tuple-element.63), channel_id=1, source_target_pairs={{0,7},{1,0},{2,1},{3,2},{4,3},{5,4},{6,5},{7,6},{8,15},{9,8},{10,9... | collective-permute-start | bytes 491528 | tf_op jit(solution)/shard_map/ppermute | solution.py:35
  10.2 28.9 %all-to-all-start.1 = ((f32[32,16,128]{2,1,0:T(8,128)}), f32[32,16,128]{2,1,0:T(8,128)}, u32[]{:S(2)}, u32[]{:S(2)}) async-start(f32[32,16,128]{2,1,0:T(8,128)} %get-tuple-element.92), calls=%async_computation.1 | async-start | bytes 524288 | tf_op jit(solution)/shard_map/all_to_all | solution.py:849
  15.3 5.4 %collective-permute-start.2 = (f32[5,24,256]{2,1,0:T(8,128)S(1)}, f32[5,24,256]{2,1,0:T(8,128)S(1)}, u32[]{:S(2)}, u32[]{:S(2)}) collective-permute-start(f32[5,24,256]{2,1,0:T(8,128)S(1)} %get-tuple-element.65), channel_id=1, source_target_pairs={{0,8},{8,16},{16,24},{24,0},{1,9},{9,17},{17,25},{25,1},{2,10},{10... | collective-permute-start | bytes 368648 | tf_op jit(solution)/shard_map/ppermute | solution.py:35
  15.3 6.0 %collective-permute-start.3 = (f32[5,24,256]{2,1,0:T(8,128)S(1)}, f32[5,24,256]{2,1,0:T(8,128)S(1)}, u32[]{:S(2)}, u32[]{:S(2)}) collective-permute-start(f32[5,24,256]{2,1,0:T(8,128)S(1)} %get-tuple-element.66), channel_id=1, source_target_pairs={{0,24},{8,0},{16,8},{24,16},{1,25},{9,1},{17,9},{25,17},{2,26},{10... | collective-permute-start | bytes 368648 | tf_op jit(solution)/shard_map/ppermute | solution.py:35
  22.1 11.8 %collective-permute-start.4 = (f32[7,16,128]{2,1,0:T(8,128)S(1)}, f32[7,16,128]{2,1,0:T(8,128)S(1)}, u32[]{:S(2)}, u32[]{:S(2)}) collective-permute-start(f32[7,16,128]{2,1,0:T(8,128)S(1)} %get-tuple-element.78), channel_id=1, source_target_pairs={{0,1},{1,2},{2,3},{3,4},{4,5},{5,6},{6,7},{7,0},{8,9},{9,10},{10,1... | collective-permute-start | bytes 172040 | tf_op jit(solution)/shard_map/ppermute | solution.py:35
  22.3 11.6 %collective-permute-start.5 = (f32[7,16,128]{2,1,0:T(8,128)S(1)}, f32[7,16,128]{2,1,0:T(8,128)S(1)}, u32[]{:S(2)}, u32[]{:S(2)}) collective-permute-start(f32[7,16,128]{2,1,0:T(8,128)S(1)} %get-tuple-element.79), channel_id=1, source_target_pairs={{0,7},{1,0},{2,1},{3,2},{4,3},{5,4},{6,5},{7,6},{8,15},{9,8},{10,9... | collective-permute-start | bytes 172040 | tf_op jit(solution)/shard_map/ppermute | solution.py:35
  26.9 8.9 %collective-permute-start.8 = (f32[192,128]{1,0:T(8,128)S(1)}, f32[192,128]{1,0:T(8,128)S(1)}, u32[]{:S(2)}, u32[]{:S(2)}) collective-permute-start(f32[192,128]{1,0:T(8,128)S(1)} %get-tuple-element.89), channel_id=1, source_target_pairs={{0,1},{1,2},{2,3},{3,4},{4,5},{5,6},{6,7},{7,0},{8,9},{9,10},{10,1... | collective-permute-start | bytes 294920 | tf_op jit(solution)/shard_map/ppermute | solution.py:35
  26.9 8.9 %collective-permute-start.9 = (f32[192,128]{1,0:T(8,128)S(1)}, f32[192,128]{1,0:T(8,128)S(1)}, u32[]{:S(2)}, u32[]{:S(2)}) collective-permute-start(f32[192,128]{1,0:T(8,128)S(1)} %get-tuple-element.90), channel_id=1, source_target_pairs={{0,7},{1,0},{2,1},{3,2},{4,3},{5,4},{6,5},{7,6},{8,15},{9,8},{10,9... | collective-permute-start | bytes 294920 | tf_op jit(solution)/shard_map/ppermute | solution.py:35
  34.0 3.7 %collective-permute-start.6 = (f32[7,16,128]{2,1,0:T(8,128)S(1)}, f32[7,16,128]{2,1,0:T(8,128)S(1)}, u32[]{:S(2)}, u32[]{:S(2)}) collective-permute-start(f32[7,16,128]{2,1,0:T(8,128)S(1)} %get-tuple-element.87), channel_id=1, source_target_pairs={{0,8},{8,16},{16,24},{24,0},{1,9},{9,17},{17,25},{25,1},{2,10},{10... | collective-permute-start | bytes 172040 | tf_op jit(solution)/shard_map/ppermute | solution.py:35
  34.3 3.4 %collective-permute-start.7 = (f32[7,16,128]{2,1,0:T(8,128)S(1)}, f32[7,16,128]{2,1,0:T(8,128)S(1)}, u32[]{:S(2)}, u32[]{:S(2)}) collective-permute-start(f32[7,16,128]{2,1,0:T(8,128)S(1)} %get-tuple-element.88), channel_id=1, source_target_pairs={{0,24},{8,0},{16,8},{24,16},{1,25},{9,1},{17,9},{25,17},{2,26},{10... | collective-permute-start | bytes 172040 | tf_op jit(solution)/shard_map/ppermute | solution.py:35
  39.2 13.8 %all-to-all-start = ((f32[32,16,128]{2,1,0:T(8,128)}), f32[32,16,128]{2,1,0:T(8,128)S(1)}, u32[]{:S(2)}, u32[]{:S(2)}) async-start(f32[32,16,128]{2,1,0:T(8,128)} %get-tuple-element.91), calls=%async_computation | async-start | bytes 524288 | tf_op jit(solution)/shard_map/all_to_all | solution.py:883
  42.2 4.9 %collective-permute-start.10 = (f32[176,128]{1,0:T(8,128)S(1)}, f32[176,128]{1,0:T(8,128)S(1)}, u32[]{:S(2)}, u32[]{:S(2)}) collective-permute-start(f32[176,128]{1,0:T(8,128)S(1)} %get-tuple-element.105), channel_id=1, source_target_pairs={{0,8},{8,16},{16,24},{24,0},{1,9},{9,17},{17,25},{25,1},{2,10},{10... | collective-permute-start | bytes 270344 | tf_op jit(solution)/shard_map/ppermute | solution.py:35
  43.7 4.4 %collective-permute-start.11 = (f32[176,128]{1,0:T(8,128)S(1)}, f32[176,128]{1,0:T(8,128)S(1)}, u32[]{:S(2)}, u32[]{:S(2)}) collective-permute-start(f32[176,128]{1,0:T(8,128)S(1)} %get-tuple-element.106), channel_id=1, source_target_pairs={{0,24},{8,0},{16,8},{24,16},{1,25},{9,1},{17,9},{25,17},{2,26},{10... | collective-permute-start | bytes 270344 | tf_op jit(solution)/shard_map/ppermute | solution.py:35
  48.2 8.7 %collective-permute-start.12 = (f32[96,128]{1,0:T(8,128)S(1)}, f32[96,128]{1,0:T(8,128)S(1)}, u32[]{:S(2)}, u32[]{:S(2)}) collective-permute-start(f32[96,128]{1,0:T(8,128)S(1)} %get-tuple-element.114), channel_id=1, source_target_pairs={{0,1},{1,2},{2,3},{3,4},{4,5},{5,6},{6,7},{7,0},{8,9},{9,10},{10,1... | collective-permute-start | bytes 147464 | tf_op jit(solution)/shard_map/ppermute | solution.py:35
  49.3 7.5 %collective-permute-start.13 = (f32[96,128]{1,0:T(8,128)S(1)}, f32[96,128]{1,0:T(8,128)S(1)}, u32[]{:S(2)}, u32[]{:S(2)}) collective-permute-start(f32[96,128]{1,0:T(8,128)S(1)} %get-tuple-element.115), channel_id=1, source_target_pairs={{0,7},{1,0},{2,1},{3,2},{4,3},{5,4},{6,5},{7,6},{8,15},{9,8},{10,9... | collective-permute-start | bytes 147464 | tf_op jit(solution)/shard_map/ppermute | solution.py:35

commit v7 on v6

--- a/solution.py
+++ b/solution.py
@@ -28,11 +28,62 @@
 REGISTERS = [48]
 SPARE = 4 * 1024 * 1024
 VMEM_BYTES = 64 * 1024 * 1024
-
-
-def rotate(value, axis, shift):
-    size = lax.axis_size(axis)
-    return lax.ppermute(value, axis, [(i, (i + shift) % size) for i in range(size)])
+LONG = 10**12
+
+
+def swap(first, second, axis):
+    axes = ("gx", "gy")
+    sizes = [lax.axis_size(name) for name in axes]
+    along = axes.index(axis)
+    size, other = sizes[along], sizes[1 - along]
+
+    def place(i, j):
+        return i * sizes[1] + j if along == 0 else j * sizes[1] + i
+
+    def pairs(begin):
+        found = []
+        for j in range(other):
+            for i in range(begin, size - 1, 2):
+                found += [(place(i, j), place(i + 1, j)), (place(i + 1, j), place(i, j))]
+        met = {source for source, _ in found}
+        for i in range(size):
+            for j in range(other):
+                beside = j + 1 - 2 * (j % 2)
+                target = place(i, beside) if beside < other else place(i, j)
+                if place(i, j) not in met:
+                    found.append((place(i, j), target))
+        return found
+
+    return lax.ppermute(first, axes, pairs(0)), lax.ppermute(second, axes, pairs(1))
+
+
+def is_even(axis):
+    return lax.rem(lax.axis_index(axis), 2) == 0
+
+
+class Either:
+    def __init__(self, flag, one, two):
+        self.flag, self.one, self.two, self.shape = flag, one, two, one.shape
+
+    def __getitem__(self, index):
+        return jnp.where(self.flag, self.one[index], self.two[index])
+
+
+def sides(axis, first, second):
+    even = is_even(axis)
+    return Either(even, second, first), Either(even, first, second)
+
+
+def send(axis, first, second, fill):
+    even = is_even(axis)
+
+    @pl.when(even)
+    def _():
+        fill(first, second)
+
+    @pl.when(jnp.logical_not(even))
+    def _():
+        fill(second, first)
 
 
 def inside(axis, side):
@@ -245,16 +296,20 @@
     return copies
 
 
-def slab_kernel(b, k, up_out, down_out, b_out, k_out):
+def slab_kernel(b, k, first, second, b_out, k_out):
     rows = k.shape[1]
     b_out[...] = b[...]
     k_out[...] = k[...]
-    for r in range(K0):
-        up_out[r] = k[:, rows - K0 + r, :]
-        down_out[r] = k[:, r, :]
-    for r in range(B0):
-        up_out[K0 + r] = b[:, rows - B0 + r, :]
-        down_out[K0 + r] = b[:, r, :]
+
+    def fill(after, before):
+        for r in range(K0):
+            after[r] = k[:, rows - K0 + r, :]
+            before[r] = k[:, r, :]
+        for r in range(B0):
+            after[K0 + r] = b[:, rows - B0 + r, :]
+            before[K0 + r] = b[:, r, :]
+
+    send("gy", first, second, fill)
 
 
 def conduct_kernel(k, message, k1, pairs, halves, pairs1, halves1, held, sems):
@@ -283,14 +338,19 @@
         out[:, rows + r, :] = masked(above, high(r))
 
 
-def widen_kernel(b, k, low, high, k_out, b_out, up_out, down_out):
+def widen_kernel(b, k, from_first, from_second, k_out, b_out, first, second):
+    low, high = sides("gy", from_first, from_second)
     widen(k_out, k, lambda r: low[r], lambda r: high[r], K0)
     widen(b_out, b, lambda r: low[K0 + r], lambda r: high[K0 + r], B0)
     planes = k.shape[0]
-    up_out[0:K0] = k_out[planes - K0 :]
-    up_out[K0:] = b_out[planes - B0 :]
-    down_out[0:K0] = k_out[0:K0]
-    down_out[K0:] = b_out[0:B0]
+
+    def fill(after, before):
+        after[0:K0] = k_out[planes - K0 :]
+        after[K0:] = b_out[planes - B0 :]
+        before[0:K0] = k_out[0:K0]
+        before[K0:] = b_out[0:B0]
+
+    send("gx", first, second, fill)
 
 
 def join(out, own, low, high, count, halo):
@@ -341,11 +401,12 @@
 
 
 def fine_outer_kernel(
-    k_own, low, high, k1,
+    k_own, from_first, from_second, k1,
     wl_in, ws_in, wz_in, total_in, inverse_in, b_in, first_in, second_in, pairs_in,
-    wl_out, ws_out, wz_out, total_out, b_out, s_out, b1_out, up_out, down_out, s_up, s_down,
+    wl_out, ws_out, wz_out, total_out, b_out, s_out, b1_out, first_out, second_out, s_first, s_second,
     wl, ws, wz, total, inverse, b, first, second, pairs, k, halves,
 ):
+    low, high = sides("gx", from_first, from_second)
     planes, rows, lanes = b.shape[0], s_out.shape[1], b.shape[2]
     own, end = planes - 2 * K0, planes - K0
     for mine, inner in (
@@ -381,14 +442,21 @@
     for out, mine in ((wl_out, wl), (ws_out, ws), (wz_out, wz), (total_out, total), (b_out, b)):
         out[0 : K0 + 1] = mine[0 : K0 + 1]
         out[K0 + 1 :] = mine[end - 1 :]
-    put_rows(s_up, 0, [s_out[:, rows - S0 + r, :] for r in range(S0)])
-    put_rows(s_down, 0, [s_out[:, r, :] for r in range(S0)])
-    half, count = b1_out.shape[0], b1_out.shape[1]
-    for out, k_from, b_from in ((up_out, count - K1, count - B1), (down_out, 0, 0)):
-        for r in range(K1):
-            out[r] = k1[:, k_from + r, :]
-        for r in range(B1):
-            out[K1 + r] = b1_out[:, b_from + r, :]
+    count = b1_out.shape[1]
+
+    def fill(after, before):
+        for out, k_from, b_from in ((after, count - K1, count - B1), (before, 0, 0)):
+            for r in range(K1):
+                out[r] = k1[:, k_from + r, :]
+            for r in range(B1):
+                out[K1 + r] = b1_out[:, b_from + r, :]
+
+    def fill_field(after, before):
+        put_rows(after, 0, [s_out[:, rows - S0 + r, :] for r in range(S0)])
+        put_rows(before, 0, [s_out[:, r, :] for r in range(S0)])
+
+    send("gy", first_out, second_out, fill)
+    send("gy", s_first, s_second, fill_field)
 
 
 def stash_kernel(*refs):
@@ -413,22 +481,30 @@
     wait(copies)
 
 
-def widen_middle_kernel(k1, b1, low, high, _stash, k_out, b_out, up_out, down_out):
+def widen_middle_kernel(
+    k1, b1, from_first, from_second, _stash, k_out, b_out, first, second
+):
+    low, high = sides("gy", from_first, from_second)
     widen(k_out, k1, lambda r: low[r], lambda r: high[r], K1)
     widen(b_out, b1, lambda r: low[K1 + r], lambda r: high[K1 + r], B1)
     planes = k1.shape[0]
-    up_out[0:K1] = k_out[planes - K1 :]
-    up_out[K1:] = b_out[planes - B1 :]
-    down_out[0:K1] = k_out[0:K1]
-    down_out[K1:] = b_out[0:B1]
+
+    def fill(after, before):
+        after[0:K1] = k_out[planes - K1 :]
+        after[K1:] = b_out[planes - B1 :]
+        before[0:K1] = k_out[0:K1]
+        before[K1:] = b_out[0:B1]
+
+    send("gx", first, second, fill)
 
 
 def middle_down_kernel(
-    k_own, b_own, low, high, _s_low, _s_high,
+    k_own, b_own, from_first, from_second, _s_first, _s_second,
     message, k, b, s_out,
     wl, ws, wz, inverse, total, first, second, pairs, halves, held, sems,
 ):
     scale = 0.25
+    low, high = sides("gx", from_first, from_second)
     join(k, k_own, lambda r: low[r], lambda r: high[r], K1, K1)
     join(b, b_own, lambda r: low[K1 + r], lambda r: high[K1 + r], B1, K1)
     w = (wl, ws, wz)
@@ -463,21 +539,33 @@
     return get
 
 
-def field_planes_kernel(s, s1, low, high, s_out, up_out, down_out):
+def field_planes_kernel(s, s1, from_first, from_second, s_out, first, second):
+    low, high = sides("gy", from_first, from_second)
     fine, own = s.shape[0], s1.shape[0]
     widen(s_out, s, split_lanes(low, 0, fine), split_lanes(high, 0, fine), S0)
-    for out, from0, from1 in ((up_out, fine - S0, own - S1), (down_out, 0, 0)):
-        at = put_rows(out, 0, [s_out[from0 + r] for r in range(S0)])
-        put_rows(out, at, [s1[from1 + r] for r in range(S1)])
-
-
-def field_rows_kernel(s, s1, low, high, _weights, s_out, s1_out, up_out, down_out):
+
+    def fill(after, before):
+        for out, from0, from1 in ((after, fine - S0, own - S1), (before, 0, 0)):
+            at = put_rows(out, 0, [s_out[from0 + r] for r in range(S0)])
+            put_rows(out, at, [s1[from1 + r] for r in range(S1)])
+
+    send("gx", first, second, fill)
+
+
+def field_rows_kernel(
+    s, s1, from_first, from_second, _weights, s_out, s1_out, first, second
+):
+    low, high = sides("gx", from_first, from_second)
     rows, rows1 = s.shape[1], s1.shape[1]
     join(s_out, s, split_lanes(low, 0, rows), split_lanes(high, 0, rows), S0, S0)
-    first = 2 * S0 * rows
-    join(s1_out, s1, from_row(low, first, rows1), from_row(high, first, rows1), S1, S1)
-    put_rows(up_out, 0, [s1_out[:, rows1 - S1 + r, :] for r in range(S1)])
-    put_rows(down_out, 0, [s1_out[:, r, :] for r in range(S1)])
+    at = 2 * S0 * rows
+    join(s1_out, s1, from_row(low, at, rows1), from_row(high, at, rows1), S1, S1)
+
+    def fill(after, before):
+        put_rows(after, 0, [s1_out[:, rows1 - S1 + r, :] for r in range(S1)])
+        put_rows(before, 0, [s1_out[:, r, :] for r in range(S1)])
+
+    send("gy", first, second, fill)
 
 
 def unpack(received, out, first, block_x, block_y, across, along):
@@ -715,7 +803,7 @@
 
 
 def fine_up_kernel(
-    region, k1, b1, s1_own, wl, ws, wz, total, b, s_own, low, high,
+    region, k1, b1, s1_own, wl, ws, wz, total, b, s_own, from_first, from_second,
     field_out, residual_out,
     wl1, ws1, wz1, total1, inverse1, inverse, first1, second1, grown, s, second, tall, thick, rest,
     out_sems,
@@ -724,6 +812,7 @@
     planes, rows, lanes = b.shape
     w1, w = (wl1, ws1, wz1), (wl, ws, wz)
     weigh(k1, wl1, ws1, wz1, total1, inverse1, False, True)
+    low, high = sides("gy", from_first, from_second)
     widen(first1, s1_own, from_row(low, 0, planes1), from_row(high, 0, planes1), S1)
     count_y, block_x = region.shape[0], region.shape[1] // 3
     expanded = widened(region[...], doubling(lanes1, 2 * lanes1, lanes1))
@@ -826,10 +915,10 @@
     pieces = (devices, qx * qy // 2, hz)
 
     slab = (K0 + B0, bx, nz)
-    up_rows, down_rows, right_side, coefficient = call(
+    first, second, right_side, coefficient = call(
         slab_kernel, [slab, slab, (bx, by, nz), (bx, by, nz)]
     )(right_side, coefficient)
-    low, high = rotate(up_rows, "gy", 1), rotate(down_rows, "gy", -1)
+    from_first, from_second = swap(first, second, "gy")
     group = 4
     message, k1 = call(
         conduct_kernel,
@@ -841,10 +930,10 @@
 
     plane = (bx, tall, nz)
     slab = (K0 + B0, tall, nz)
-    k_own, b_own, up_planes, down_planes = call(widen_kernel, [plane, plane, slab, slab], cost=1000000000000)(
-        right_side, coefficient, low, high
+    k_own, b_own, first, second = call(widen_kernel, [plane, plane, slab, slab], cost=LONG)(
+        right_side, coefficient, from_first, from_second
     )
-    low, high = rotate(up_planes, "gx", 1), rotate(down_planes, "gx", -1)
+    from_first, from_second = swap(first, second, "gx")
 
     k2 = lax.all_to_all(message, both, 0, 0, tiled=True)
 
@@ -855,22 +944,22 @@
     slab = (K1 + B1, hx, hz)
     edges = (2 * K0 + 2, tall, nz)
     field_slab = (2 * S0 * bx, hz)
-    *outer, s, b1, up_rows, down_rows, s_up, s_down = call(
+    *outer, s, b1, first, second, s_out_first, s_out_second = call(
         fine_outer_kernel,
         [edges] * 5 + [(bx, by, nz), (hx, hy, hz), slab, slab, field_slab, field_slab],
         [block] * 8 + [(hx, by, nz), block, (hx, by, hz)],
-    )(k_own, low, high, k1, *inner)
+    )(k_own, from_first, from_second, k1, *inner)
     planes = 5 * block[0] + VMEM_BYTES // (4 * tall * nz)
     (stash,) = call(stash_kernel, [(planes, tall, nz)], held=1, sems=(15,))(
         *inner[:4], inner[5], *outer
     )
-    low, high = rotate(up_rows, "gy", 1), rotate(down_rows, "gy", -1)
-    s_low, s_high = rotate(s_up, "gy", 1), rotate(s_down, "gy", -1)
+    from_first, from_second = swap(first, second, "gy")
+    s_first, s_second = swap(s_out_first, s_out_second, "gy")
     slab = (K1 + B1, tall1, hz)
-    k1_own, b1_own, up_planes, down_planes = call(
+    k1_own, b1_own, first, second = call(
         widen_middle_kernel, [(hx, tall1, hz), (hx, tall1, hz), slab, slab], kept=(4,)
-    )(k1, b1, low, high, stash)
-    low, high = rotate(up_planes, "gx", 1), rotate(down_planes, "gx", -1)
+    )(k1, b1, from_first, from_second, stash)
+    from_first, from_second = swap(first, second, "gx")
 
     block1 = (hx + 2 * K1, tall1, hz)
     message, k1, b1, s1 = call(
@@ -879,7 +968,7 @@
         [block1] * 7 + [(qx, hy, hz), (qx, hy, hz), (group, *pieces[1:])],
         held=1,
         sems=(devices // group,),
-    )(k1_own, b1_own, low, high, s_low, s_high)
+    )(k1_own, b1_own, from_first, from_second, s_first, s_second)
     received = lax.all_to_all(message, both, 0, 0, tiled=True)
 
     x2, y2 = across * qx, along * qy
@@ -893,15 +982,15 @@
         registers=48,
     )(k2)
     slab = (2 * S0 * tall + S1 * hy, hz)
-    s_rows, up_planes, down_planes = call(field_planes_kernel, [plane, slab, slab])(
-        s, s1, s_low, s_high
+    s_rows, first, second = call(field_planes_kernel, [plane, slab, slab])(
+        s, s1, s_first, s_second
     )
-    low, high = rotate(up_planes, "gx", 1), rotate(down_planes, "gx", -1)
+    from_first, from_second = swap(first, second, "gx")
     slab = (S1 * block1[0], hz)
-    s_own, s1_own, up_rows, down_rows = call(
+    s_own, s1_own, first, second = call(
         field_rows_kernel, [block, (block1[0], hy, hz), slab, slab]
-    )(s_rows, s1, low, high, coarse[-1])
-    low, high = rotate(up_rows, "gy", 1), rotate(down_rows, "gy", -1)
+    )(s_rows, s1, from_first, from_second, coarse[-1])
+    from_first, from_second = swap(first, second, "gy")
 
     region, *weights = call(
         partial(coarse_kernel, valid),
@@ -921,7 +1010,7 @@
         held=2,
         sems=(5,),
         registers=96,
-    )(region, k1, b1, s1_own, *weights, s_own, low, high)
+    )(region, k1, b1, s1_own, *weights, s_own, from_first, from_second)
     return field, rest
 
 

time: 61.1 us -> 56.4 us (0.923)
  starting transfers between devices: 32.1 us -> 25.2 us
  waiting for transfers between devices: 6.71 us -> 8.82 us
    ppermute x14, starting transfers between devices: 25.8 us -> 16.1 us  [the longest x7 9.34 us: swap(): lax.ppermute(first, axes, pairs(0))]
    all_to_all x1, waiting for transfers between devices: 0.01 us -> 3.18 us  [per_device(): received = lax.all_to_all(message, both, 0, 0, tiled=True)]
    all_to_all x1, starting transfers between devices: 3.42 us -> 6.52 us  [per_device(): k2 = lax.all_to_all(message, both, 0, 0, tiled=True)]
    ppermute x14, waiting for transfers between devices: 6.71 us -> 5.64 us  [the longest x7 5.62 us: swap(): lax.ppermute(second, axes, pairs(1))]
  transfers between devices with their start and end apart: 16 -> 16, of which waited for: 7 -> 4; matrix products, arithmetic and copies ran while one was open for 0% -> 0% of each run, Pallas kernels for 25% -> 27%
where the time goes in v7:
time: 56.4 us; the launch traced here: 56 us
  starting transfers between devices  25.2 us (45%)
  Pallas kernels  19.1 us (34%)
  waiting for transfers between devices  8.82 us (16%)
  local copies, waits for them, and re-layouts  2.08 us (4%)
  between operations  0.83 us (1%)
    pallas_call x13, Pallas kernels, run(): pl.pallas_call(body, out_shape=[jax.ShapeDtypeStruct(shape, F32) for shap...  19.1 us
    ppermute x7, starting transfers between devices, swap(): lax.ppermute(first, axes, pairs(0))  9.34 us
    ppermute x7, starting transfers between devices, swap(): lax.ppermute(second, axes, pairs(1))  6.77 us
    all_to_all x1, starting transfers between devices, per_device(): k2 = lax.all_to_all(message, both, 0, 0, tiled=True)  6.52 us
    ppermute x7, waiting for transfers between devices, swap(): lax.ppermute(second, axes, pairs(1))  5.62 us
    all_to_all x1, waiting for transfers between devices, per_device(): received = lax.all_to_all(message, both, 0, 0, tiled=True)  3.18 us
    all_to_all x1, starting transfers between devices, per_device(): received = lax.all_to_all(message, both, 0, 0, tiled=True)  2.6 us
    unnamed x4, local copies, waits for them, and re-layouts  2.08 us
  transfers between devices with their start and end apart: 16, of which 4 were waited for; matrix products, arithmetic and copies ran while one was open for 0% of the time, Pallas kernels for 27%

profile of v7, /device:TPU:0, one launch (start us, length us, event | category | flops | bytes accessed | tf_op | source)
XLA Modules:
  0.0 56.0 jit_solution(11393038396277235179)
XLA Ops:
  0.6 0.0 copy-start
  0.6 1.0 %copy-done = f32[32,16,256]{2,1,0:T(8,128)S(1)} copy-done((f32[32,16,256]{2,1,0:T(8,128)S(1)}, f32[32,16,256]{2,1,0:T(8,128)}, u32[]{:S(2)}) %copy-start) | copy-done | bytes 524312
  1.7 1.0 %copy-done.1 = f32[32,16,256]{2,1,0:T(8,128)S(1)} copy-done((f32[32,16,256]{2,1,0:T(8,128)S(1)}, f32[32,16,256]{2,1,0:T(8,128)}, u32[]{:S(2)}) %copy-start.1) | copy-done | bytes 524312
  2.7 0.2 shard_map.41
  2.9 3.0 %collective-permute-start = (f32[5,32,256]{2,1,0:T(8,128)S(1)}, f32[5,32,256]{2,1,0:T(8,128)S(1)}, u32[]{:S(2)}, u32[]{:S(2)}) collective-permute-start(f32[5,32,256]{2,1,0:T(8,128)S(1)} %get-tuple-element.62), channel_id=1, source_target_pairs={{0,1},{1,0},{2,3},{3,2},{4,5},{5,4},{6,7},{7,6},{8,9},{9,8},{10,11... | collective-permute-start | bytes 491528 | tf_op jit(solution)/shard_map/ppermute | solution.py:57
  5.9 0.0 collective-permute-start.1
  5.9 1.2 %shard_map.42 = (f32[32,16,128]{2,1,0:T(8,128)}, f32[16,8,128]{2,1,0:T(8,128)S(1)}) custom-call(f32[32,16,256]{2,1,0:T(8,128)S(1)} %get-tuple-element.59.refs_0_.refs_1_), custom_call_target="tpu_custom_call" | custom-call | tf_op jit(solution)/shard_map/pallas_call | solution.py:889
  7.1 6.5 %all-to-all-start.1 = ((f32[32,16,128]{2,1,0:T(8,128)}), f32[32,16,128]{2,1,0:T(8,128)}, u32[]{:S(2)}, u32[]{:S(2)}) async-start(f32[32,16,128]{2,1,0:T(8,128)} %get-tuple-element.92), calls=%async_computation.1 | async-start | bytes 524288 | tf_op jit(solution)/shard_map/all_to_all | solution.py:938
  13.6 0.0 collective-permute-done.refs_2_
  13.7 0.0 collective-permute-done.1.refs_3_
  13.7 0.2 shard_map.43
  13.9 0.2 collective-permute-start.2
  14.1 1.7 %collective-permute-start.3 = (f32[5,24,256]{2,1,0:T(8,128)S(1)}, f32[5,24,256]{2,1,0:T(8,128)S(1)}, u32[]{:S(2)}, u32[]{:S(2)}) collective-permute-start(f32[5,24,256]{2,1,0:T(8,128)S(1)} %get-tuple-element.66), channel_id=1, source_target_pairs={{8,16},{16,8},{9,17},{17,9},{10,18},{18,10},{11,19},{19,11},{12,20... | collective-permute-start | bytes 368648 | tf_op jit(solution)/shard_map/ppermute | solution.py:57
  15.8 2.5 %shard_map.44 = (f32[38,24,256]{2,1,0:T(8,128)S(1)}, f32[38,24,256]{2,1,0:T(8,128)S(1)}, f32[38,24,256]{2,1,0:T(8,128)S(1)}, f32[38,24,256]{2,1,0:T(8,128)S(1)},...) custom-call(f32[32,24,256]{2,1,0:T(8,128)S(1)} %get-tuple-element.64, ...), custom_call_target="tpu_custom_call" | custom-call | tf_op jit(solution)/shard_map/pallas_call | solution.py:889
  18.4 0.0 collective-permute-done.2.refs_1_
  18.4 1.9 %collective-permute-done.3.refs_2_ = f32[5,24,256]{2,1,0:T(8,128)S(1)} collective-permute-done((f32[5,24,256]{2,1,0:T(8,128)S(1)}, f32[5,24,256]{2,1,0:T(8,128)S(1)}, u32[]{:S(2)}, u32[]{:S(2)}) %collective-permute-start.3) | collective-permute-done | bytes 122912 | tf_op jit(solution)/shard_map/ppermute | solution.py:57
  20.3 0.8 %shard_map.45 = (f32[8,24,256]{2,1,0:T(8,128)S(1)}, f32[8,24,256]{2,1,0:T(8,128)S(1)}, f32[8,24,256]{2,1,0:T(8,128)S(1)}, f32[8,24,256]{2,1,0:T(8,128)S(1)}, f32...) custom-call(f32[32,24,256]{2,1,0:T(8,128)S(1)} %get-tuple-element.64, ...), custom_call_target="tpu_custom_call" | custom-call | tf_op jit(solution)/shard_map/pallas_call | solution.py:889
  21.2 1.1 %collective-permute-start.4 = (f32[7,16,128]{2,1,0:T(8,128)S(1)}, f32[7,16,128]{2,1,0:T(8,128)S(1)}, u32[]{:S(2)}, u32[]{:S(2)}) collective-permute-start(f32[7,16,128]{2,1,0:T(8,128)S(1)} %get-tuple-element.78), channel_id=1, source_target_pairs={{0,1},{1,0},{2,3},{3,2},{4,5},{5,4},{6,7},{7,6},{8,9},{9,8},{10,11... | collective-permute-start | bytes 172040 | tf_op jit(solution)/shard_map/ppermute | solution.py:57
  22.3 0.0 collective-permute-start.5
  22.3 2.8 %collective-permute-start.8 = (f32[192,128]{1,0:T(8,128)S(1)}, f32[192,128]{1,0:T(8,128)S(1)}, u32[]{:S(2)}, u32[]{:S(2)}) collective-permute-start(f32[192,128]{1,0:T(8,128)S(1)} %get-tuple-element.89), channel_id=1, source_target_pairs={{0,1},{1,0},{2,3},{3,2},{4,5},{5,4},{6,7},{7,6},{8,9},{9,8},{10,11... | collective-permute-start | bytes 294920 | tf_op jit(solution)/shard_map/ppermute | solution.py:57
  25.1 0.0 collective-permute-start.9
  25.1 2.3 %shard_map.46.refs_4_.refs_7_ = f32[2920,24,256]{2,1,0:T(8,128)} custom-call(f32[38,24,256]{2,1,0:T(8,128)S(1)} %get-tuple-element.68.refs_4_.refs_0_, f32[38,24,256]{2,1,0:T(8,128)S(1)} %get-tuple-element.69.refs_5_.refs_1_, f32[38,24,256]{2,1,0:T(8,128)S(1)} %get-tuple-element.70.refs_6_.refs_2_, f32[38,24,256]{2,1,0:T(8,128)S(1)} %get-tuple-element.71.refs_7_.refs_3_, ...), custom_call_target="tpu_custom_call" | custom-call | tf_op jit(solution)/shard_map/pallas_call | solution.py:889
  27.4 0.0 collective-permute-done.4.refs_2_
  27.4 0.0 collective-permute-done.5.refs_3_
  27.4 0.1 shard_map.47
  27.5 0.6 %collective-permute-start.6 = (f32[7,16,128]{2,1,0:T(8,128)S(1)}, f32[7,16,128]{2,1,0:T(8,128)S(1)}, u32[]{:S(2)}, u32[]{:S(2)}) collective-permute-start(f32[7,16,128]{2,1,0:T(8,128)S(1)} %get-tuple-element.87), channel_id=1, source_target_pairs={{0,8},{8,0},{16,24},{24,16},{1,9},{9,1},{17,25},{25,17},{2,10},{10... | collective-permute-start | bytes 172040 | tf_op jit(solution)/shard_map/ppermute | solution.py:57
  28.1 3.4 %collective-permute-start.7 = (f32[7,16,128]{2,1,0:T(8,128)S(1)}, f32[7,16,128]{2,1,0:T(8,128)S(1)}, u32[]{:S(2)}, u32[]{:S(2)}) collective-permute-start(f32[7,16,128]{2,1,0:T(8,128)S(1)} %get-tuple-element.88), channel_id=1, source_target_pairs={{8,16},{16,8},{9,17},{17,9},{10,18},{18,10},{11,19},{19,11},{12,20... | collective-permute-start | bytes 172040 | tf_op jit(solution)/shard_map/ppermute | solution.py:57
  31.4 0.0 collective-permute-done.8.refs_4_.refs_2_
  31.4 0.0 collective-permute-done.9.refs_5_.refs_3_
  31.4 0.0 collective-permute-done.6.refs_2_
  31.4 2.1 %collective-permute-done.7.refs_3_ = f32[7,16,128]{2,1,0:T(8,128)S(1)} collective-permute-done((f32[7,16,128]{2,1,0:T(8,128)S(1)}, f32[7,16,128]{2,1,0:T(8,128)S(1)}, u32[]{:S(2)}, u32[]{:S(2)}) %collective-permute-start.7) | collective-permute-done | bytes 57376 | tf_op jit(solution)/shard_map/ppermute | solution.py:57
  33.6 1.4 %shard_map.48 = (f32[32,16,128]{2,1,0:T(8,128)}, f32[24,16,128]{2,1,0:T(8,128)S(1)}, f32[24,16,128]{2,1,0:T(8,128)S(1)}, f32[16,8,128]{2,1,0:T(8,128)S(1)}) custom-call(f32[16,16,128]{2,1,0:T(8,128)S(1)} %get-tuple-element.85.refs_0_, f32[16,16,128]{2,1,0:T(8,128)S(1)} %get-tuple-element.86.refs_1_, f32[7,16,128]{2,1,0:T(8,128)S(1)} %collective-permute-done.6.refs_2_, ...), custom_call_target="tpu_custom_call" | custom-call | tf_op jit(solution)/shard_map/pallas_call | solution.py:889
  35.0 0.0 all-to-all-done.1.refs_0_
  35.0 2.6 %all-to-all-start = ((f32[32,16,128]{2,1,0:T(8,128)}), f32[32,16,128]{2,1,0:T(8,128)S(1)}, u32[]{:S(2)}, u32[]{:S(2)}) async-start(f32[32,16,128]{2,1,0:T(8,128)} %get-tuple-element.91), calls=%async_computation | async-start | bytes 524288 | tf_op jit(solution)/shard_map/all_to_all | solution.py:972
  37.6 0.1 shard_map.51
  37.8 0.2 collective-permute-start.10
  38.0 1.7 %collective-permute-start.11 = (f32[176,128]{1,0:T(8,128)S(1)}, f32[176,128]{1,0:T(8,128)S(1)}, u32[]{:S(2)}, u32[]{:S(2)}) collective-permute-start(f32[176,128]{1,0:T(8,128)S(1)} %get-tuple-element.106), channel_id=1, source_target_pairs={{8,16},{16,8},{9,17},{17,9},{10,18},{18,10},{11,19},{19,11},{12,20... | collective-permute-start | bytes 270344 | tf_op jit(solution)/shard_map/ppermute | solution.py:57
  39.7 2.3 %shard_map.49 = (f32[18,32,128]{2,1,0:T(8,128)S(1)}, f32[18,32,128]{2,1,0:T(8,128)S(1)}, f32[18,32,128]{2,1,0:T(8,128)S(1)}, f32[18,32,128]{2,1,0:T(8,128)S(1)},...) custom-call(f32[32,16,128]{2,1,0:T(8,128)} %all-to-all-done.1.refs_0_), custom_call_target="tpu_custom_call" | custom-call | tf_op jit(solution)/shard_map/pallas_call | solution.py:889
  42.0 0.0 collective-permute-done.10.refs_2_
  42.0 1.5 %collective-permute-done.11.refs_3_ = f32[176,128]{1,0:T(8,128)S(1)} collective-permute-done((f32[176,128]{1,0:T(8,128)S(1)}, f32[176,128]{1,0:T(8,128)S(1)}, u32[]{:S(2)}, u32[]{:S(2)}) %collective-permute-start.11) | collective-permute-done | bytes 90144 | tf_op jit(solution)/shard_map/ppermute | solution.py:57
  43.6 0.1 shard_map.52
  43.7 1.4 %collective-permute-start.12 = (f32[96,128]{1,0:T(8,128)S(1)}, f32[96,128]{1,0:T(8,128)S(1)}, u32[]{:S(2)}, u32[]{:S(2)}) collective-permute-start(f32[96,128]{1,0:T(8,128)S(1)} %get-tuple-element.114), channel_id=1, source_target_pairs={{0,1},{1,0},{2,3},{3,2},{4,5},{5,4},{6,7},{7,6},{8,9},{9,8},{10,11... | collective-permute-start | bytes 147464 | tf_op jit(solution)/shard_map/ppermute | solution.py:57
  45.1 0.0 collective-permute-start.13
  45.1 3.2 %all-to-all-done.refs_0_ = f32[32,16,128]{2,1,0:T(8,128)S(1)} async-done(((f32[32,16,128]{2,1,0:T(8,128)}), f32[32,16,128]{2,1,0:T(8,128)S(1)}, u32[]{:S(2)}, u32[]{:S(2)}) %all-to-all-start) | async-done | bytes 262176 | tf_op jit(solution)/shard_map/all_to_all | solution.py:972
  48.3 3.9 %shard_map.50 = (f32[4,24,128]{2,1,0:T(8,128)S(1)}, f32[38,24,256]{2,1,0:T(8,128)S(1)}, f32[38,24,256]{2,1,0:T(8,128)S(1)}, f32[38,24,256]{2,1,0:T(8,128)S(1)}, ...) custom-call(f32[32,16,128]{2,1,0:T(8,128)S(1)} %all-to-all-done.refs_0_, ...), custom_call_target="tpu_custom_call" | custom-call | tf_op jit(solution)/shard_map/pallas_call | solution.py:889
  52.2 0.0 collective-permute-done.12.refs_10_
  52.2 0.0 collective-permute-done.13.refs_11_
  52.2 3.8 %shard_map.53 = (f32[32,16,256]{2,1,0:T(8,128)}, f32[32,16,256]{2,1,0:T(8,128)}) custom-call(f32[4,24,128]{2,1,0:T(8,128)S(1)} %get-tuple-element.99.refs_0_, f32[24,16,128]{2,1,0:T(8,128)S(1)} %get-tuple-element.100.refs_1_, f32[24,16,128]{2,1,0:T(8,128)S(1)} %get-tuple-element.101.refs_2_, f32[24,8,128]{2,1,0:T(8,128)S(1)} %get-tuple-element.107.refs_3_, ...), custom_call_target="tpu_custom_call" | custom-call | tf_op jit(solution)/shard_map/pallas_call | solution.py:889
  (1 shorter events, 0.0 us)
Async XLA Ops:
  0.6 1.0 %copy-start = (f32[32,16,256]{2,1,0:T(8,128)S(1)}, f32[32,16,256]{2,1,0:T(8,128)}, u32[]{:S(2)}) copy-start(f32[32,16,256]{2,1,0:T(8,128)} %refs_0_.1) | copy-start | bytes 1572868
  1.7 1.0 %copy-start.1 = (f32[32,16,256]{2,1,0:T(8,128)S(1)}, f32[32,16,256]{2,1,0:T(8,128)}, u32[]{:S(2)}) copy-start(f32[32,16,256]{2,1,0:T(8,128)} %refs_1_.1) | copy-start | bytes 1572868
  2.9 10.7 %collective-permute-start = (f32[5,32,256]{2,1,0:T(8,128)S(1)}, f32[5,32,256]{2,1,0:T(8,128)S(1)}, u32[]{:S(2)}, u32[]{:S(2)}) collective-permute-start(f32[5,32,256]{2,1,0:T(8,128)S(1)} %get-tuple-element.62), channel_id=1, source_target_pairs={{0,1},{1,0},{2,3},{3,2},{4,5},{5,4},{6,7},{7,6},{8,9},{9,8},{10,11... | collective-permute-start | bytes 491528 | tf_op jit(solution)/shard_map/ppermute | solution.py:57
  5.9 7.8 %collective-permute-start.1 = (f32[5,32,256]{2,1,0:T(8,128)S(1)}, f32[5,32,256]{2,1,0:T(8,128)S(1)}, u32[]{:S(2)}, u32[]{:S(2)}) collective-permute-start(f32[5,32,256]{2,1,0:T(8,128)S(1)} %get-tuple-element.63), channel_id=1, source_target_pairs={{1,2},{2,1},{3,4},{4,3},{5,6},{6,5},{9,10},{10,9},{11,12},{12,11},... | collective-permute-start | bytes 491528 | tf_op jit(solution)/shard_map/ppermute | solution.py:57
  7.1 27.9 %all-to-all-start.1 = ((f32[32,16,128]{2,1,0:T(8,128)}), f32[32,16,128]{2,1,0:T(8,128)}, u32[]{:S(2)}, u32[]{:S(2)}) async-start(f32[32,16,128]{2,1,0:T(8,128)} %get-tuple-element.92), calls=%async_computation.1 | async-start | bytes 524288 | tf_op jit(solution)/shard_map/all_to_all | solution.py:938
  13.9 4.5 %collective-permute-start.2 = (f32[5,24,256]{2,1,0:T(8,128)S(1)}, f32[5,24,256]{2,1,0:T(8,128)S(1)}, u32[]{:S(2)}, u32[]{:S(2)}) collective-permute-start(f32[5,24,256]{2,1,0:T(8,128)S(1)} %get-tuple-element.65), channel_id=1, source_target_pairs={{0,8},{8,0},{16,24},{24,16},{1,9},{9,1},{17,25},{25,17},{2,10},{10... | collective-permute-start | bytes 368648 | tf_op jit(solution)/shard_map/ppermute | solution.py:57
  14.1 6.2 %collective-permute-start.3 = (f32[5,24,256]{2,1,0:T(8,128)S(1)}, f32[5,24,256]{2,1,0:T(8,128)S(1)}, u32[]{:S(2)}, u32[]{:S(2)}) collective-permute-start(f32[5,24,256]{2,1,0:T(8,128)S(1)} %get-tuple-element.66), channel_id=1, source_target_pairs={{8,16},{16,8},{9,17},{17,9},{10,18},{18,10},{11,19},{19,11},{12,20... | collective-permute-start | bytes 368648 | tf_op jit(solution)/shard_map/ppermute | solution.py:57
  21.2 6.2 %collective-permute-start.4 = (f32[7,16,128]{2,1,0:T(8,128)S(1)}, f32[7,16,128]{2,1,0:T(8,128)S(1)}, u32[]{:S(2)}, u32[]{:S(2)}) collective-permute-start(f32[7,16,128]{2,1,0:T(8,128)S(1)} %get-tuple-element.78), channel_id=1, source_target_pairs={{0,1},{1,0},{2,3},{3,2},{4,5},{5,4},{6,7},{7,6},{8,9},{9,8},{10,11... | collective-permute-start | bytes 172040 | tf_op jit(solution)/shard_map/ppermute | solution.py:57
  22.3 5.1 %collective-permute-start.5 = (f32[7,16,128]{2,1,0:T(8,128)S(1)}, f32[7,16,128]{2,1,0:T(8,128)S(1)}, u32[]{:S(2)}, u32[]{:S(2)}) collective-permute-start(f32[7,16,128]{2,1,0:T(8,128)S(1)} %get-tuple-element.79), channel_id=1, source_target_pairs={{1,2},{2,1},{3,4},{4,3},{5,6},{6,5},{9,10},{10,9},{11,12},{12,11},... | collective-permute-start | bytes 172040 | tf_op jit(solution)/shard_map/ppermute | solution.py:57
  22.3 9.1 %collective-permute-start.8 = (f32[192,128]{1,0:T(8,128)S(1)}, f32[192,128]{1,0:T(8,128)S(1)}, u32[]{:S(2)}, u32[]{:S(2)}) collective-permute-start(f32[192,128]{1,0:T(8,128)S(1)} %get-tuple-element.89), channel_id=1, source_target_pairs={{0,1},{1,0},{2,3},{3,2},{4,5},{5,4},{6,7},{7,6},{8,9},{9,8},{10,11... | collective-permute-start | bytes 294920 | tf_op jit(solution)/shard_map/ppermute | solution.py:57
  25.1 6.3 %collective-permute-start.9 = (f32[192,128]{1,0:T(8,128)S(1)}, f32[192,128]{1,0:T(8,128)S(1)}, u32[]{:S(2)}, u32[]{:S(2)}) collective-permute-start(f32[192,128]{1,0:T(8,128)S(1)} %get-tuple-element.90), channel_id=1, source_target_pairs={{1,2},{2,1},{3,4},{4,3},{5,6},{6,5},{9,10},{10,9},{11,12},{12,11},... | collective-permute-start | bytes 294920 | tf_op jit(solution)/shard_map/ppermute | solution.py:57
  27.5 3.9 %collective-permute-start.6 = (f32[7,16,128]{2,1,0:T(8,128)S(1)}, f32[7,16,128]{2,1,0:T(8,128)S(1)}, u32[]{:S(2)}, u32[]{:S(2)}) collective-permute-start(f32[7,16,128]{2,1,0:T(8,128)S(1)} %get-tuple-element.87), channel_id=1, source_target_pairs={{0,8},{8,0},{16,24},{24,16},{1,9},{9,1},{17,25},{25,17},{2,10},{10... | collective-permute-start | bytes 172040 | tf_op jit(solution)/shard_map/ppermute | solution.py:57
  28.1 5.5 %collective-permute-start.7 = (f32[7,16,128]{2,1,0:T(8,128)S(1)}, f32[7,16,128]{2,1,0:T(8,128)S(1)}, u32[]{:S(2)}, u32[]{:S(2)}) collective-permute-start(f32[7,16,128]{2,1,0:T(8,128)S(1)} %get-tuple-element.88), channel_id=1, source_target_pairs={{8,16},{16,8},{9,17},{17,9},{10,18},{18,10},{11,19},{19,11},{12,20... | collective-permute-start | bytes 172040 | tf_op jit(solution)/shard_map/ppermute | solution.py:57
  35.0 13.3 %all-to-all-start = ((f32[32,16,128]{2,1,0:T(8,128)}), f32[32,16,128]{2,1,0:T(8,128)S(1)}, u32[]{:S(2)}, u32[]{:S(2)}) async-start(f32[32,16,128]{2,1,0:T(8,128)} %get-tuple-element.91), calls=%async_computation | async-start | bytes 524288 | tf_op jit(solution)/shard_map/all_to_all | solution.py:972
  37.8 4.3 %collective-permute-start.10 = (f32[176,128]{1,0:T(8,128)S(1)}, f32[176,128]{1,0:T(8,128)S(1)}, u32[]{:S(2)}, u32[]{:S(2)}) collective-permute-start(f32[176,128]{1,0:T(8,128)S(1)} %get-tuple-element.105), channel_id=1, source_target_pairs={{0,8},{8,0},{16,24},{24,16},{1,9},{9,1},{17,25},{25,17},{2,10},{10... | collective-permute-start | bytes 270344 | tf_op jit(solution)/shard_map/ppermute | solution.py:57
  38.0 5.6 %collective-permute-start.11 = (f32[176,128]{1,0:T(8,128)S(1)}, f32[176,128]{1,0:T(8,128)S(1)}, u32[]{:S(2)}, u32[]{:S(2)}) collective-permute-start(f32[176,128]{1,0:T(8,128)S(1)} %get-tuple-element.106), channel_id=1, source_target_pairs={{8,16},{16,8},{9,17},{17,9},{10,18},{18,10},{11,19},{19,11},{12,20... | collective-permute-start | bytes 270344 | tf_op jit(solution)/shard_map/ppermute | solution.py:57
  43.7 8.5 %collective-permute-start.12 = (f32[96,128]{1,0:T(8,128)S(1)}, f32[96,128]{1,0:T(8,128)S(1)}, u32[]{:S(2)}, u32[]{:S(2)}) collective-permute-start(f32[96,128]{1,0:T(8,128)S(1)} %get-tuple-element.114), channel_id=1, source_target_pairs={{0,1},{1,0},{2,3},{3,2},{4,5},{5,4},{6,7},{7,6},{8,9},{9,8},{10,11... | collective-permute-start | bytes 147464 | tf_op jit(solution)/shard_map/ppermute | solution.py:57
  45.1 7.1 %collective-permute-start.13 = (f32[96,128]{1,0:T(8,128)S(1)}, f32[96,128]{1,0:T(8,128)S(1)}, u32[]{:S(2)}, u32[]{:S(2)}) collective-permute-start(f32[96,128]{1,0:T(8,128)S(1)} %get-tuple-element.115), channel_id=1, source_target_pairs={{1,2},{2,1},{3,4},{4,3},{5,6},{6,5},{9,10},{10,9},{11,12},{12,11},... | collective-permute-start | bytes 147464 | tf_op jit(solution)/shard_map/ppermute | solution.py:57

commit v8 on v7

--- a/solution.py
+++ b/solution.py
@@ -338,17 +338,54 @@
         out[:, rows + r, :] = masked(above, high(r))
 
 
+def diamond(count, own):
+    return count * own + sum(2 * (count - d) for d in range(1, count + 1))
+
+
+def put_planes(out, at, ref, planes, own):
+    count, size = len(planes), ref.shape[1]
+    for p in planes:
+        out[at : at + own] = ref[p, 0:own, :]
+        at += own
+    for d, p in enumerate(planes, 1):
+        n = count - d
+        if n:
+            out[at : at + n] = ref[p, own : own + n, :]
+            out[at + n : at + 2 * n] = ref[p, size - n : size, :]
+            at += 2 * n
+    return at
+
+
+def get_planes(out, planes, message, at, own, flag):
+    count, size = len(planes), out.shape[1]
+    halo = at + count * own
+    for d, p in enumerate(planes, 1):
+        out[p, 0:own, :] = masked(flag, message[at : at + own])
+        out[p, own:size, :] = jnp.zeros((size - own, out.shape[2]), F32)
+        at += own
+        n = count - d
+        if n:
+            out[p, own : own + n, :] = masked(flag, message[halo : halo + n])
+            out[p, size - n : size, :] = masked(flag, message[halo + n : halo + 2 * n])
+            halo += 2 * n
+
+
+def ends(planes, halo, count):
+    below = [halo - 1 - d for d in range(count)]
+    return below, [halo + planes + d for d in range(count)]
+
+
 def widen_kernel(b, k, from_first, from_second, k_out, b_out, first, second):
     low, high = sides("gy", from_first, from_second)
     widen(k_out, k, lambda r: low[r], lambda r: high[r], K0)
     widen(b_out, b, lambda r: low[K0 + r], lambda r: high[K0 + r], B0)
-    planes = k.shape[0]
+    planes, rows = k.shape[0], k.shape[1]
 
     def fill(after, before):
-        after[0:K0] = k_out[planes - K0 :]
-        after[K0:] = b_out[planes - B0 :]
-        before[0:K0] = k_out[0:K0]
-        before[K0:] = b_out[0:B0]
+        at = put_planes(after, 0, k_out, [planes - 1 - d for d in range(K0)], rows)
+        put_planes(after, at, b_out, [planes - 1 - d for d in range(B0)], rows)
+        at = put_planes(before, 0, k_out, list(range(K0)), rows)
+        put_planes(before, at, b_out, list(range(B0)), rows)
 
     send("gx", first, second, fill)
 
@@ -403,7 +440,7 @@
 def fine_outer_kernel(
     k_own, from_first, from_second, k1,
     wl_in, ws_in, wz_in, total_in, inverse_in, b_in, first_in, second_in, pairs_in,
-    wl_out, ws_out, wz_out, total_out, b_out, s_out, b1_out, first_out, second_out, s_first, s_second,
+    wl_out, ws_out, wz_out, total_out, b_out, s_out, b1_out, first_out, second_out,
     wl, ws, wz, total, inverse, b, first, second, pairs, k, halves,
 ):
     low, high = sides("gx", from_first, from_second)
@@ -416,12 +453,10 @@
         mine[K0 : K0 + 5] = inner[K0 : K0 + 5]
         mine[end - 5 : end] = inner[end - 5 : end]
     left, right = inside("gx", -1), inside("gx", 1)
-    for r in range(K0):
-        k[r] = masked(left, low[r])
-        k[end + r] = masked(right, high[r])
-    for r in range(B0):
-        b[K0 - B0 + r] = masked(left, low[K0 + r])
-        b[end + r] = masked(right, high[K0 + r])
+    for ref, count, at in ((k, K0, 0), (b, B0, diamond(K0, rows))):
+        below, above = ends(own, K0, count)
+        get_planes(ref, below, low, at, rows, left)
+        get_planes(ref, above, high, at, rows, right)
     for r in range(2):
         k[K0 + r] = k_own[r]
         k[end - 2 + r] = k_own[own - 2 + r]
@@ -451,12 +486,17 @@
             for r in range(B1):
                 out[K1 + r] = b1_out[:, b_from + r, :]
 
-    def fill_field(after, before):
-        put_rows(after, 0, [s_out[:, rows - S0 + r, :] for r in range(S0)])
-        put_rows(before, 0, [s_out[:, r, :] for r in range(S0)])
-
     send("gy", first_out, second_out, fill)
-    send("gy", s_first, s_second, fill_field)
+
+
+def field_slab_kernel(s, first, second):
+    rows = s.shape[1]
+
+    def fill(after, before):
+        put_rows(after, 0, [s[:, rows - S0 + r, :] for r in range(S0)])
+        put_rows(before, 0, [s[:, r, :] for r in range(S0)])
+
+    send("gy", first, second, fill)
 
 
 def stash_kernel(*refs):
@@ -482,7 +522,7 @@
 
 
 def widen_middle_kernel(
-    k1, b1, from_first, from_second, _stash, k_out, b_out, first, second
+    k1, b1, from_first, from_second, k_out, b_out, first, second
 ):
     low, high = sides("gy", from_first, from_second)
     widen(k_out, k1, lambda r: low[r], lambda r: high[r], K1)
@@ -499,7 +539,7 @@
 
 
 def middle_down_kernel(
-    k_own, b_own, from_first, from_second, _s_first, _s_second,
+    k_own, b_own, from_first, from_second, _s_first, _s_second, _stash,
     message, k, b, s_out,
     wl, ws, wz, inverse, total, first, second, pairs, halves, held, sems,
 ):
@@ -929,7 +969,7 @@
     )(coefficient)
 
     plane = (bx, tall, nz)
-    slab = (K0 + B0, tall, nz)
+    slab = (diamond(K0, by) + diamond(B0, by), nz)
     k_own, b_own, first, second = call(widen_kernel, [plane, plane, slab, slab], cost=LONG)(
         right_side, coefficient, from_first, from_second
     )
@@ -944,9 +984,9 @@
     slab = (K1 + B1, hx, hz)
     edges = (2 * K0 + 2, tall, nz)
     field_slab = (2 * S0 * bx, hz)
-    *outer, s, b1, first, second, s_out_first, s_out_second = call(
+    *outer, s, b1, first, second = call(
         fine_outer_kernel,
-        [edges] * 5 + [(bx, by, nz), (hx, hy, hz), slab, slab, field_slab, field_slab],
+        [edges] * 5 + [(bx, by, nz), (hx, hy, hz), slab, slab],
         [block] * 8 + [(hx, by, nz), block, (hx, by, hz)],
     )(k_own, from_first, from_second, k1, *inner)
     planes = 5 * block[0] + VMEM_BYTES // (4 * tall * nz)
@@ -954,11 +994,11 @@
         *inner[:4], inner[5], *outer
     )
     from_first, from_second = swap(first, second, "gy")
-    s_first, s_second = swap(s_out_first, s_out_second, "gy")
+    s_first, s_second = swap(*call(field_slab_kernel, [field_slab, field_slab])(s), "gy")
     slab = (K1 + B1, tall1, hz)
     k1_own, b1_own, first, second = call(
-        widen_middle_kernel, [(hx, tall1, hz), (hx, tall1, hz), slab, slab], kept=(4,)
-    )(k1, b1, from_first, from_second, stash)
+        widen_middle_kernel, [(hx, tall1, hz), (hx, tall1, hz), slab, slab]
+    )(k1, b1, from_first, from_second)
     from_first, from_second = swap(first, second, "gx")
 
     block1 = (hx + 2 * K1, tall1, hz)
@@ -967,8 +1007,9 @@
         [pieces] + [block1] * 2 + [(hx, hy, hz)],
         [block1] * 7 + [(qx, hy, hz), (qx, hy, hz), (group, *pieces[1:])],
         held=1,
+        kept=(6,),
         sems=(devices // group,),
-    )(k1_own, b1_own, from_first, from_second, s_first, s_second)
+    )(k1_own, b1_own, from_first, from_second, s_first, s_second, stash)
     received = lax.all_to_all(message, both, 0, 0, tiled=True)
 
     x2, y2 = across * qx, along * qy

time: 56.4 us -> 55.4 us (0.982)
  waiting for transfers between devices: 8.82 us -> 6.48 us
  starting transfers between devices: 25.2 us -> 26.5 us
    ppermute x7, waiting for transfers between devices: 5.62 us -> 3.13 us  [swap(): lax.ppermute(second, axes, pairs(1))]
    all_to_all x1, starting transfers between devices: 2.6 us -> 4.1 us  [per_device(): received = lax.all_to_all(message, both, 0, 0, tiled=True)]
    pallas_call x13 -> x14, Pallas kernels: 19.1 us -> 19.1 us  [run(): pl.pallas_call(body, out_shape=[jax.ShapeDtypeStruct(shape, F32) for shap...]
where the time goes in v8:
time: 55.4 us; the launch traced here: 55 us
  starting transfers between devices  26.5 us (48%)
  Pallas kernels  19.1 us (34%)
  waiting for transfers between devices  6.48 us (12%)
  local copies, waits for them, and re-layouts  2.08 us (4%)
  between operations  0.85 us (2%)
    pallas_call x14, Pallas kernels, run(): pl.pallas_call(body, out_shape=[jax.ShapeDtypeStruct(shape, F32) for shap...  19.1 us
    ppermute x7, starting transfers between devices, swap(): lax.ppermute(first, axes, pairs(0))  9.06 us
    ppermute x7, starting transfers between devices, swap(): lax.ppermute(second, axes, pairs(1))  6.82 us
    all_to_all x1, starting transfers between devices, per_device(): k2 = lax.all_to_all(message, both, 0, 0, tiled=True)  6.52 us
    all_to_all x1, starting transfers between devices, per_device(): received = lax.all_to_all(message, both, 0, 0, tiled=True)  4.1 us
    ppermute x7, waiting for transfers between devices, swap(): lax.ppermute(second, axes, pairs(1))  3.13 us
    all_to_all x1, waiting for transfers between devices, per_device(): received = lax.all_to_all(message, both, 0, 0, tiled=True)  3.05 us
    unnamed x4, local copies, waits for them, and re-layouts  2.08 us
  transfers between devices with their start and end apart: 16, of which 4 were waited for; matrix products, arithmetic and copies ran while one was open for 0% of the time, Pallas kernels for 27%

profile of v8, /device:TPU:0, one launch (start us, length us, event | category | flops | bytes accessed | tf_op | source)
XLA Modules:
  0.0 55.0 jit_solution(16906143114448902185)
XLA Ops:
  0.6 1.0 %copy-done = f32[32,16,256]{2,1,0:T(8,128)S(1)} copy-done((f32[32,16,256]{2,1,0:T(8,128)S(1)}, f32[32,16,256]{2,1,0:T(8,128)}, u32[]{:S(2)}) %copy-start) | copy-done | bytes 524312
  1.7 1.0 %copy-done.1 = f32[32,16,256]{2,1,0:T(8,128)S(1)} copy-done((f32[32,16,256]{2,1,0:T(8,128)S(1)}, f32[32,16,256]{2,1,0:T(8,128)}, u32[]{:S(2)}) %copy-start.1) | copy-done | bytes 524312
  2.7 0.2 shard_map.41
  2.9 3.0 %collective-permute-start = (f32[5,32,256]{2,1,0:T(8,128)S(1)}, f32[5,32,256]{2,1,0:T(8,128)S(1)}, u32[]{:S(2)}, u32[]{:S(2)}) collective-permute-start(f32[5,32,256]{2,1,0:T(8,128)S(1)} %get-tuple-element.62), channel_id=1, source_target_pairs={{0,1},{1,0},{2,3},{3,2},{4,5},{5,4},{6,7},{7,6},{8,9},{9,8},{10,11... | collective-permute-start | bytes 491528 | tf_op jit(solution)/shard_map/ppermute | solution.py:57
  5.9 0.0 collective-permute-start.1
  5.9 1.2 %shard_map.42 = (f32[32,16,128]{2,1,0:T(8,128)}, f32[16,8,128]{2,1,0:T(8,128)S(1)}) custom-call(f32[32,16,256]{2,1,0:T(8,128)S(1)} %get-tuple-element.59.refs_0_.refs_1_), custom_call_target="tpu_custom_call" | custom-call | tf_op jit(solution)/shard_map/pallas_call | solution.py:929
  7.1 6.5 %all-to-all-start.1 = ((f32[32,16,128]{2,1,0:T(8,128)}), f32[32,16,128]{2,1,0:T(8,128)}, u32[]{:S(2)}, u32[]{:S(2)}) async-start(f32[32,16,128]{2,1,0:T(8,128)} %get-tuple-element.93), calls=%async_computation.1 | async-start | bytes 524288 | tf_op jit(solution)/shard_map/all_to_all | solution.py:978
  13.6 0.0 collective-permute-done.refs_2_
  13.7 0.0 collective-permute-done.1.refs_3_
  13.7 0.2 shard_map.43
  13.9 0.2 collective-permute-start.2
  14.1 1.7 %collective-permute-start.3 = (f32[88,256]{1,0:T(8,128)S(1)}, f32[88,256]{1,0:T(8,128)S(1)}, u32[]{:S(2)}, u32[]{:S(2)}) collective-permute-start(f32[88,256]{1,0:T(8,128)S(1)} %get-tuple-element.66), channel_id=1, source_target_pairs={{8,16},{16,8},{9,17},{17,9},{10,18},{18,10},{11,19},{19,11},{12,20... | collective-permute-start | bytes 270344 | tf_op jit(solution)/shard_map/ppermute | solution.py:57
  15.8 2.5 %shard_map.44 = (f32[38,24,256]{2,1,0:T(8,128)S(1)}, f32[38,24,256]{2,1,0:T(8,128)S(1)}, f32[38,24,256]{2,1,0:T(8,128)S(1)}, f32[38,24,256]{2,1,0:T(8,128)S(1)},...) custom-call(f32[32,24,256]{2,1,0:T(8,128)S(1)} %get-tuple-element.64, ...), custom_call_target="tpu_custom_call" | custom-call | tf_op jit(solution)/shard_map/pallas_call | solution.py:929
  18.4 0.0 collective-permute-done.2.refs_1_
  18.4 1.4 %collective-permute-done.3.refs_2_ = f32[88,256]{1,0:T(8,128)S(1)} collective-permute-done((f32[88,256]{1,0:T(8,128)S(1)}, f32[88,256]{1,0:T(8,128)S(1)}, u32[]{:S(2)}, u32[]{:S(2)}) %collective-permute-start.3) | collective-permute-done | bytes 90144 | tf_op jit(solution)/shard_map/ppermute | solution.py:57
  19.8 0.8 %shard_map.45 = (f32[8,24,256]{2,1,0:T(8,128)S(1)}, f32[8,24,256]{2,1,0:T(8,128)S(1)}, f32[8,24,256]{2,1,0:T(8,128)S(1)}, f32[8,24,256]{2,1,0:T(8,128)S(1)}, f32...) custom-call(f32[32,24,256]{2,1,0:T(8,128)S(1)} %get-tuple-element.64, ...), custom_call_target="tpu_custom_call" | custom-call | tf_op jit(solution)/shard_map/pallas_call | solution.py:929
  20.6 1.2 %collective-permute-start.4 = (f32[7,16,128]{2,1,0:T(8,128)S(1)}, f32[7,16,128]{2,1,0:T(8,128)S(1)}, u32[]{:S(2)}, u32[]{:S(2)}) collective-permute-start(f32[7,16,128]{2,1,0:T(8,128)S(1)} %get-tuple-element.78), channel_id=1, source_target_pairs={{0,1},{1,0},{2,3},{3,2},{4,5},{5,4},{6,7},{7,6},{8,9},{9,8},{10,11... | collective-permute-start | bytes 172040 | tf_op jit(solution)/shard_map/ppermute | solution.py:57
  21.8 0.0 collective-permute-start.5
  21.8 0.1 shard_map.47
  21.9 2.7 %collective-permute-start.8 = (f32[192,128]{1,0:T(8,128)S(1)}, f32[192,128]{1,0:T(8,128)S(1)}, u32[]{:S(2)}, u32[]{:S(2)}) collective-permute-start(f32[192,128]{1,0:T(8,128)S(1)} %get-tuple-element.85), channel_id=1, source_target_pairs={{0,1},{1,0},{2,3},{3,2},{4,5},{5,4},{6,7},{7,6},{8,9},{9,8},{10,11... | collective-permute-start | bytes 294920 | tf_op jit(solution)/shard_map/ppermute | solution.py:57
  24.6 0.0 collective-permute-start.9
  24.6 0.3 collective-permute-done.4.refs_2_
  24.9 0.0 collective-permute-done.5.refs_3_
  24.9 0.1 shard_map.46
  25.0 0.3 collective-permute-start.6
  25.3 3.5 %collective-permute-start.7 = (f32[7,16,128]{2,1,0:T(8,128)S(1)}, f32[7,16,128]{2,1,0:T(8,128)S(1)}, u32[]{:S(2)}, u32[]{:S(2)}) collective-permute-start(f32[7,16,128]{2,1,0:T(8,128)S(1)} %get-tuple-element.83), channel_id=1, source_target_pairs={{8,16},{16,8},{9,17},{17,9},{10,18},{18,10},{11,19},{19,11},{12,20... | collective-permute-start | bytes 172040 | tf_op jit(solution)/shard_map/ppermute | solution.py:57
  28.7 2.3 %shard_map.48.refs_6_.refs_7_ = f32[2920,24,256]{2,1,0:T(8,128)} custom-call(f32[38,24,256]{2,1,0:T(8,128)S(1)} %get-tuple-element.68.refs_4_.refs_0_, f32[38,24,256]{2,1,0:T(8,128)S(1)} %get-tuple-element.69.refs_5_.refs_1_, f32[38,24,256]{2,1,0:T(8,128)S(1)} %get-tuple-element.70.refs_6_.refs_2_, f32[38,24,256]{2,1,0:T(8,128)S(1)} %get-tuple-element.71.refs_7_.refs_3_, ...), custom_call_target="tpu_custom_call" | custom-call | tf_op jit(solution)/shard_map/pallas_call | solution.py:929
  31.0 0.0 collective-permute-done.8.refs_4_.refs_2_
  31.0 0.0 collective-permute-done.9.refs_5_.refs_3_
  31.1 0.0 collective-permute-done.6.refs_2_
  31.1 0.0 collective-permute-done.7.refs_3_
  31.1 1.4 %shard_map.49 = (f32[32,16,128]{2,1,0:T(8,128)}, f32[24,16,128]{2,1,0:T(8,128)S(1)}, f32[24,16,128]{2,1,0:T(8,128)S(1)}, f32[16,8,128]{2,1,0:T(8,128)S(1)}) custom-call(f32[16,16,128]{2,1,0:T(8,128)S(1)} %get-tuple-element.80.refs_0_, f32[16,16,128]{2,1,0:T(8,128)S(1)} %get-tuple-element.81.refs_1_, f32[7,16,128]{2,1,0:T(8,128)S(1)} %collective-permute-done.6.refs_2_, ...), custom_call_target="tpu_custom_call" | custom-call | tf_op jit(solution)/shard_map/pallas_call | solution.py:929
  32.5 0.0 all-to-all-done.1.refs_0_
  32.5 4.1 %all-to-all-start = ((f32[32,16,128]{2,1,0:T(8,128)}), f32[32,16,128]{2,1,0:T(8,128)S(1)}, u32[]{:S(2)}, u32[]{:S(2)}) async-start(f32[32,16,128]{2,1,0:T(8,128)} %get-tuple-element.92), calls=%async_computation | async-start | bytes 524288 | tf_op jit(solution)/shard_map/all_to_all | solution.py:1013
  36.7 0.1 shard_map.52
  36.8 0.3 collective-permute-start.10
  37.1 1.7 %collective-permute-start.11 = (f32[176,128]{1,0:T(8,128)S(1)}, f32[176,128]{1,0:T(8,128)S(1)}, u32[]{:S(2)}, u32[]{:S(2)}) collective-permute-start(f32[176,128]{1,0:T(8,128)S(1)} %get-tuple-element.106), channel_id=1, source_target_pairs={{8,16},{16,8},{9,17},{17,9},{10,18},{18,10},{11,19},{19,11},{12,20... | collective-permute-start | bytes 270344 | tf_op jit(solution)/shard_map/ppermute | solution.py:57
  38.8 2.3 %shard_map.50 = (f32[18,32,128]{2,1,0:T(8,128)S(1)}, f32[18,32,128]{2,1,0:T(8,128)S(1)}, f32[18,32,128]{2,1,0:T(8,128)S(1)}, f32[18,32,128]{2,1,0:T(8,128)S(1)},...) custom-call(f32[32,16,128]{2,1,0:T(8,128)} %all-to-all-done.1.refs_0_), custom_call_target="tpu_custom_call" | custom-call | tf_op jit(solution)/shard_map/pallas_call | solution.py:929
  41.1 0.0 collective-permute-done.10.refs_2_
  41.1 1.7 %collective-permute-done.11.refs_3_ = f32[176,128]{1,0:T(8,128)S(1)} collective-permute-done((f32[176,128]{1,0:T(8,128)S(1)}, f32[176,128]{1,0:T(8,128)S(1)}, u32[]{:S(2)}, u32[]{:S(2)}) %collective-permute-start.11) | collective-permute-done | bytes 90144 | tf_op jit(solution)/shard_map/ppermute | solution.py:57
  42.8 0.1 shard_map.53
  42.9 1.3 %collective-permute-start.12 = (f32[96,128]{1,0:T(8,128)S(1)}, f32[96,128]{1,0:T(8,128)S(1)}, u32[]{:S(2)}, u32[]{:S(2)}) collective-permute-start(f32[96,128]{1,0:T(8,128)S(1)} %get-tuple-element.114), channel_id=1, source_target_pairs={{0,1},{1,0},{2,3},{3,2},{4,5},{5,4},{6,7},{7,6},{8,9},{9,8},{10,11... | collective-permute-start | bytes 147464 | tf_op jit(solution)/shard_map/ppermute | solution.py:57
  44.3 0.0 collective-permute-start.13
  44.3 3.0 %all-to-all-done.refs_0_ = f32[32,16,128]{2,1,0:T(8,128)S(1)} async-done(((f32[32,16,128]{2,1,0:T(8,128)}), f32[32,16,128]{2,1,0:T(8,128)S(1)}, u32[]{:S(2)}, u32[]{:S(2)}) %all-to-all-start) | async-done | bytes 262176 | tf_op jit(solution)/shard_map/all_to_all | solution.py:1013
  47.3 3.9 %shard_map.51 = (f32[4,24,128]{2,1,0:T(8,128)S(1)}, f32[38,24,256]{2,1,0:T(8,128)S(1)}, f32[38,24,256]{2,1,0:T(8,128)S(1)}, f32[38,24,256]{2,1,0:T(8,128)S(1)}, ...) custom-call(f32[32,16,128]{2,1,0:T(8,128)S(1)} %all-to-all-done.refs_0_, ...), custom_call_target="tpu_custom_call" | custom-call | tf_op jit(solution)/shard_map/pallas_call | solution.py:929
  51.2 0.0 collective-permute-done.12.refs_10_
  51.2 0.0 collective-permute-done.13.refs_11_
  51.2 3.8 %shard_map.54 = (f32[32,16,256]{2,1,0:T(8,128)}, f32[32,16,256]{2,1,0:T(8,128)}) custom-call(f32[4,24,128]{2,1,0:T(8,128)S(1)} %get-tuple-element.100.refs_0_, f32[24,16,128]{2,1,0:T(8,128)S(1)} %get-tuple-element.101.refs_1_, f32[24,16,128]{2,1,0:T(8,128)S(1)} %get-tuple-element.102.refs_2_, f32[24,8,128]{2,1,0:T(8,128)S(1)} %get-tuple-element.107.refs_3_, ...), custom_call_target="tpu_custom_call" | custom-call | tf_op jit(solution)/shard_map/pallas_call | solution.py:929
  (2 shorter events, 0.0 us)
Async XLA Ops:
  0.6 1.0 %copy-start = (f32[32,16,256]{2,1,0:T(8,128)S(1)}, f32[32,16,256]{2,1,0:T(8,128)}, u32[]{:S(2)}) copy-start(f32[32,16,256]{2,1,0:T(8,128)} %refs_0_.1) | copy-start | bytes 1572868
  1.7 1.0 %copy-start.1 = (f32[32,16,256]{2,1,0:T(8,128)S(1)}, f32[32,16,256]{2,1,0:T(8,128)}, u32[]{:S(2)}) copy-start(f32[32,16,256]{2,1,0:T(8,128)} %refs_1_.1) | copy-start | bytes 1572868
  2.9 10.7 %collective-permute-start = (f32[5,32,256]{2,1,0:T(8,128)S(1)}, f32[5,32,256]{2,1,0:T(8,128)S(1)}, u32[]{:S(2)}, u32[]{:S(2)}) collective-permute-start(f32[5,32,256]{2,1,0:T(8,128)S(1)} %get-tuple-element.62), channel_id=1, source_target_pairs={{0,1},{1,0},{2,3},{3,2},{4,5},{5,4},{6,7},{7,6},{8,9},{9,8},{10,11... | collective-permute-start | bytes 491528 | tf_op jit(solution)/shard_map/ppermute | solution.py:57
  5.9 7.8 %collective-permute-start.1 = (f32[5,32,256]{2,1,0:T(8,128)S(1)}, f32[5,32,256]{2,1,0:T(8,128)S(1)}, u32[]{:S(2)}, u32[]{:S(2)}) collective-permute-start(f32[5,32,256]{2,1,0:T(8,128)S(1)} %get-tuple-element.63), channel_id=1, source_target_pairs={{1,2},{2,1},{3,4},{4,3},{5,6},{6,5},{9,10},{10,9},{11,12},{12,11},... | collective-permute-start | bytes 491528 | tf_op jit(solution)/shard_map/ppermute | solution.py:57
  7.1 25.4 %all-to-all-start.1 = ((f32[32,16,128]{2,1,0:T(8,128)}), f32[32,16,128]{2,1,0:T(8,128)}, u32[]{:S(2)}, u32[]{:S(2)}) async-start(f32[32,16,128]{2,1,0:T(8,128)} %get-tuple-element.93), calls=%async_computation.1 | async-start | bytes 524288 | tf_op jit(solution)/shard_map/all_to_all | solution.py:978
  13.9 4.5 %collective-permute-start.2 = (f32[88,256]{1,0:T(8,128)S(1)}, f32[88,256]{1,0:T(8,128)S(1)}, u32[]{:S(2)}, u32[]{:S(2)}) collective-permute-start(f32[88,256]{1,0:T(8,128)S(1)} %get-tuple-element.65), channel_id=1, source_target_pairs={{0,8},{8,0},{16,24},{24,16},{1,9},{9,1},{17,25},{25,17},{2,10},{10... | collective-permute-start | bytes 270344 | tf_op jit(solution)/shard_map/ppermute | solution.py:57
  14.1 5.7 %collective-permute-start.3 = (f32[88,256]{1,0:T(8,128)S(1)}, f32[88,256]{1,0:T(8,128)S(1)}, u32[]{:S(2)}, u32[]{:S(2)}) collective-permute-start(f32[88,256]{1,0:T(8,128)S(1)} %get-tuple-element.66), channel_id=1, source_target_pairs={{8,16},{16,8},{9,17},{17,9},{10,18},{18,10},{11,19},{19,11},{12,20... | collective-permute-start | bytes 270344 | tf_op jit(solution)/shard_map/ppermute | solution.py:57
  20.6 4.2 %collective-permute-start.4 = (f32[7,16,128]{2,1,0:T(8,128)S(1)}, f32[7,16,128]{2,1,0:T(8,128)S(1)}, u32[]{:S(2)}, u32[]{:S(2)}) collective-permute-start(f32[7,16,128]{2,1,0:T(8,128)S(1)} %get-tuple-element.78), channel_id=1, source_target_pairs={{0,1},{1,0},{2,3},{3,2},{4,5},{5,4},{6,7},{7,6},{8,9},{9,8},{10,11... | collective-permute-start | bytes 172040 | tf_op jit(solution)/shard_map/ppermute | solution.py:57
  21.8 3.0 %collective-permute-start.5 = (f32[7,16,128]{2,1,0:T(8,128)S(1)}, f32[7,16,128]{2,1,0:T(8,128)S(1)}, u32[]{:S(2)}, u32[]{:S(2)}) collective-permute-start(f32[7,16,128]{2,1,0:T(8,128)S(1)} %get-tuple-element.79), channel_id=1, source_target_pairs={{1,2},{2,1},{3,4},{4,3},{5,6},{6,5},{9,10},{10,9},{11,12},{12,11},... | collective-permute-start | bytes 172040 | tf_op jit(solution)/shard_map/ppermute | solution.py:57
  21.9 9.1 %collective-permute-start.8 = (f32[192,128]{1,0:T(8,128)S(1)}, f32[192,128]{1,0:T(8,128)S(1)}, u32[]{:S(2)}, u32[]{:S(2)}) collective-permute-start(f32[192,128]{1,0:T(8,128)S(1)} %get-tuple-element.85), channel_id=1, source_target_pairs={{0,1},{1,0},{2,3},{3,2},{4,5},{5,4},{6,7},{7,6},{8,9},{9,8},{10,11... | collective-permute-start | bytes 294920 | tf_op jit(solution)/shard_map/ppermute | solution.py:57
  24.6 6.5 %collective-permute-start.9 = (f32[192,128]{1,0:T(8,128)S(1)}, f32[192,128]{1,0:T(8,128)S(1)}, u32[]{:S(2)}, u32[]{:S(2)}) collective-permute-start(f32[192,128]{1,0:T(8,128)S(1)} %get-tuple-element.86), channel_id=1, source_target_pairs={{1,2},{2,1},{3,4},{4,3},{5,6},{6,5},{9,10},{10,9},{11,12},{12,11},... | collective-permute-start | bytes 294920 | tf_op jit(solution)/shard_map/ppermute | solution.py:57
  25.0 6.1 %collective-permute-start.6 = (f32[7,16,128]{2,1,0:T(8,128)S(1)}, f32[7,16,128]{2,1,0:T(8,128)S(1)}, u32[]{:S(2)}, u32[]{:S(2)}) collective-permute-start(f32[7,16,128]{2,1,0:T(8,128)S(1)} %get-tuple-element.82), channel_id=1, source_target_pairs={{0,8},{8,0},{16,24},{24,16},{1,9},{9,1},{17,25},{25,17},{2,10},{10... | collective-permute-start | bytes 172040 | tf_op jit(solution)/shard_map/ppermute | solution.py:57
  25.3 5.8 %collective-permute-start.7 = (f32[7,16,128]{2,1,0:T(8,128)S(1)}, f32[7,16,128]{2,1,0:T(8,128)S(1)}, u32[]{:S(2)}, u32[]{:S(2)}) collective-permute-start(f32[7,16,128]{2,1,0:T(8,128)S(1)} %get-tuple-element.83), channel_id=1, source_target_pairs={{8,16},{16,8},{9,17},{17,9},{10,18},{18,10},{11,19},{19,11},{12,20... | collective-permute-start | bytes 172040 | tf_op jit(solution)/shard_map/ppermute | solution.py:57
  32.5 14.8 %all-to-all-start = ((f32[32,16,128]{2,1,0:T(8,128)}), f32[32,16,128]{2,1,0:T(8,128)S(1)}, u32[]{:S(2)}, u32[]{:S(2)}) async-start(f32[32,16,128]{2,1,0:T(8,128)} %get-tuple-element.92), calls=%async_computation | async-start | bytes 524288 | tf_op jit(solution)/shard_map/all_to_all | solution.py:1013
  36.8 4.3 %collective-permute-start.10 = (f32[176,128]{1,0:T(8,128)S(1)}, f32[176,128]{1,0:T(8,128)S(1)}, u32[]{:S(2)}, u32[]{:S(2)}) collective-permute-start(f32[176,128]{1,0:T(8,128)S(1)} %get-tuple-element.105), channel_id=1, source_target_pairs={{0,8},{8,0},{16,24},{24,16},{1,9},{9,1},{17,25},{25,17},{2,10},{10... | collective-permute-start | bytes 270344 | tf_op jit(solution)/shard_map/ppermute | solution.py:57
  37.1 5.7 %collective-permute-start.11 = (f32[176,128]{1,0:T(8,128)S(1)}, f32[176,128]{1,0:T(8,128)S(1)}, u32[]{:S(2)}, u32[]{:S(2)}) collective-permute-start(f32[176,128]{1,0:T(8,128)S(1)} %get-tuple-element.106), channel_id=1, source_target_pairs={{8,16},{16,8},{9,17},{17,9},{10,18},{18,10},{11,19},{19,11},{12,20... | collective-permute-start | bytes 270344 | tf_op jit(solution)/shard_map/ppermute | solution.py:57
  42.9 8.3 %collective-permute-start.12 = (f32[96,128]{1,0:T(8,128)S(1)}, f32[96,128]{1,0:T(8,128)S(1)}, u32[]{:S(2)}, u32[]{:S(2)}) collective-permute-start(f32[96,128]{1,0:T(8,128)S(1)} %get-tuple-element.114), channel_id=1, source_target_pairs={{0,1},{1,0},{2,3},{3,2},{4,5},{5,4},{6,7},{7,6},{8,9},{9,8},{10,11... | collective-permute-start | bytes 147464 | tf_op jit(solution)/shard_map/ppermute | solution.py:57
  44.3 6.9 %collective-permute-start.13 = (f32[96,128]{1,0:T(8,128)S(1)}, f32[96,128]{1,0:T(8,128)S(1)}, u32[]{:S(2)}, u32[]{:S(2)}) collective-permute-start(f32[96,128]{1,0:T(8,128)S(1)} %get-tuple-element.115), channel_id=1, source_target_pairs={{1,2},{2,1},{3,4},{4,3},{5,6},{6,5},{9,10},{10,9},{11,12},{12,11},... | collective-permute-start | bytes 147464 | tf_op jit(solution)/shard_map/ppermute | solution.py:57

commit v9 on v8

--- a/solution.py
+++ b/solution.py
@@ -241,10 +241,12 @@
         loop(*span, sweep, b.shape[1:])
 
 
-def post_smooth(b, first, second, w, inverse, scale, outer, inner):
+def post_smooth(b, first, second, w, inverse, scale, outer, inner, total=None):
     def sweep(i):
         x = first[i]
         near = beside(first, w, i)
+        if total is not None:
+            inverse[i] = invert(total[i])
         second[i] = x + ((b[i] * (1.0 / scale) + near) * inverse[i] - x) * (1.0 / THETA)
 
     loop(*outer, sweep, b.shape[1:])
@@ -890,11 +892,9 @@
 
     loop(1, count - 1, add, b.shape[1:])
 
-    def complete(i):
-        inverse[i] = invert(total[i])
-
-    loop(1, planes - 1, complete, b.shape[1:])
-    post_smooth(b, s, second, w, inverse, 1.0, (1, planes - 1), (2, planes - 2))
+    post_smooth(
+        b, s, second, w, inverse, 1.0, (1, planes - 1), (2, planes - 2), total
+    )
     own, own_rows = field_out.shape[0], field_out.shape[1]
     mine = s.at[K0 : K0 + own, 0:own_rows]
     copies = [pltpu.make_async_copy(mine, field_out, out_sems.at[0])]

time: 55.4 us -> 55.3 us (level)
  no operation moved by 1% of the time
where the time goes in v9:
time: 55.3 us; the launch traced here: 55 us
  starting transfers between devices  26.5 us (48%)
  Pallas kernels  19.1 us (35%)
  waiting for transfers between devices  6.48 us (12%)
  local copies, waits for them, and re-layouts  2.08 us (4%)
  between operations  0.85 us (2%)
    pallas_call x14, Pallas kernels, run(): pl.pallas_call(body, out_shape=[jax.ShapeDtypeStruct(shape, F32) for shap...  19.1 us
    ppermute x7, starting transfers between devices, swap(): lax.ppermute(first, axes, pairs(0))  9.06 us
    ppermute x7, starting transfers between devices, swap(): lax.ppermute(second, axes, pairs(1))  6.82 us
    all_to_all x1, starting transfers between devices, per_device(): k2 = lax.all_to_all(message, both, 0, 0, tiled=True)  6.52 us
    all_to_all x1, starting transfers between devices, per_device(): received = lax.all_to_all(message, both, 0, 0, tiled=True)  4.1 us
    ppermute x7, waiting for transfers between devices, swap(): lax.ppermute(second, axes, pairs(1))  3.13 us
    all_to_all x1, waiting for transfers between devices, per_device(): received = lax.all_to_all(message, both, 0, 0, tiled=True)  3.05 us
    unnamed x4, local copies, waits for them, and re-layouts  2.08 us
  transfers between devices with their start and end apart: 16, of which 4 were waited for; matrix products, arithmetic and copies ran while one was open for 0% of the time, Pallas kernels for 27%

profile of v9, /device:TPU:0, one launch (start us, length us, event | category | flops | bytes accessed | tf_op | source)
XLA Modules:
  0.0 55.0 jit_solution(14816685908922381814)
XLA Ops:
  0.6 1.0 %copy-done = f32[32,16,256]{2,1,0:T(8,128)S(1)} copy-done((f32[32,16,256]{2,1,0:T(8,128)S(1)}, f32[32,16,256]{2,1,0:T(8,128)}, u32[]{:S(2)}) %copy-start) | copy-done | bytes 524312
  1.7 1.0 %copy-done.1 = f32[32,16,256]{2,1,0:T(8,128)S(1)} copy-done((f32[32,16,256]{2,1,0:T(8,128)S(1)}, f32[32,16,256]{2,1,0:T(8,128)}, u32[]{:S(2)}) %copy-start.1) | copy-done | bytes 524312
  2.7 0.2 shard_map.41
  2.9 3.0 %collective-permute-start = (f32[5,32,256]{2,1,0:T(8,128)S(1)}, f32[5,32,256]{2,1,0:T(8,128)S(1)}, u32[]{:S(2)}, u32[]{:S(2)}) collective-permute-start(f32[5,32,256]{2,1,0:T(8,128)S(1)} %get-tuple-element.62), channel_id=1, source_target_pairs={{0,1},{1,0},{2,3},{3,2},{4,5},{5,4},{6,7},{7,6},{8,9},{9,8},{10,11... | collective-permute-start | bytes 491528 | tf_op jit(solution)/shard_map/ppermute | solution.py:57
  5.9 0.0 collective-permute-start.1
  5.9 1.2 %shard_map.42 = (f32[32,16,128]{2,1,0:T(8,128)}, f32[16,8,128]{2,1,0:T(8,128)S(1)}) custom-call(f32[32,16,256]{2,1,0:T(8,128)S(1)} %get-tuple-element.59.refs_0_.refs_1_), custom_call_target="tpu_custom_call" | custom-call | tf_op jit(solution)/shard_map/pallas_call | solution.py:929
  7.1 6.5 %all-to-all-start.1 = ((f32[32,16,128]{2,1,0:T(8,128)}), f32[32,16,128]{2,1,0:T(8,128)}, u32[]{:S(2)}, u32[]{:S(2)}) async-start(f32[32,16,128]{2,1,0:T(8,128)} %get-tuple-element.93), calls=%async_computation.1 | async-start | bytes 524288 | tf_op jit(solution)/shard_map/all_to_all | solution.py:978
  13.6 0.0 collective-permute-done.refs_2_
  13.7 0.0 collective-permute-done.1.refs_3_
  13.7 0.2 shard_map.43
  13.9 0.2 collective-permute-start.2
  14.1 1.7 %collective-permute-start.3 = (f32[88,256]{1,0:T(8,128)S(1)}, f32[88,256]{1,0:T(8,128)S(1)}, u32[]{:S(2)}, u32[]{:S(2)}) collective-permute-start(f32[88,256]{1,0:T(8,128)S(1)} %get-tuple-element.66), channel_id=1, source_target_pairs={{8,16},{16,8},{9,17},{17,9},{10,18},{18,10},{11,19},{19,11},{12,20... | collective-permute-start | bytes 270344 | tf_op jit(solution)/shard_map/ppermute | solution.py:57
  15.8 2.5 %shard_map.44 = (f32[38,24,256]{2,1,0:T(8,128)S(1)}, f32[38,24,256]{2,1,0:T(8,128)S(1)}, f32[38,24,256]{2,1,0:T(8,128)S(1)}, f32[38,24,256]{2,1,0:T(8,128)S(1)},...) custom-call(f32[32,24,256]{2,1,0:T(8,128)S(1)} %get-tuple-element.64, ...), custom_call_target="tpu_custom_call" | custom-call | tf_op jit(solution)/shard_map/pallas_call | solution.py:929
  18.4 0.0 collective-permute-done.2.refs_1_
  18.4 1.4 %collective-permute-done.3.refs_2_ = f32[88,256]{1,0:T(8,128)S(1)} collective-permute-done((f32[88,256]{1,0:T(8,128)S(1)}, f32[88,256]{1,0:T(8,128)S(1)}, u32[]{:S(2)}, u32[]{:S(2)}) %collective-permute-start.3) | collective-permute-done | bytes 90144 | tf_op jit(solution)/shard_map/ppermute | solution.py:57
  19.8 0.8 %shard_map.45 = (f32[8,24,256]{2,1,0:T(8,128)S(1)}, f32[8,24,256]{2,1,0:T(8,128)S(1)}, f32[8,24,256]{2,1,0:T(8,128)S(1)}, f32[8,24,256]{2,1,0:T(8,128)S(1)}, f32...) custom-call(f32[32,24,256]{2,1,0:T(8,128)S(1)} %get-tuple-element.64, ...), custom_call_target="tpu_custom_call" | custom-call | tf_op jit(solution)/shard_map/pallas_call | solution.py:929
  20.6 1.2 %collective-permute-start.4 = (f32[7,16,128]{2,1,0:T(8,128)S(1)}, f32[7,16,128]{2,1,0:T(8,128)S(1)}, u32[]{:S(2)}, u32[]{:S(2)}) collective-permute-start(f32[7,16,128]{2,1,0:T(8,128)S(1)} %get-tuple-element.78), channel_id=1, source_target_pairs={{0,1},{1,0},{2,3},{3,2},{4,5},{5,4},{6,7},{7,6},{8,9},{9,8},{10,11... | collective-permute-start | bytes 172040 | tf_op jit(solution)/shard_map/ppermute | solution.py:57
  21.8 0.0 collective-permute-start.5
  21.8 0.1 shard_map.47
  21.9 2.7 %collective-permute-start.8 = (f32[192,128]{1,0:T(8,128)S(1)}, f32[192,128]{1,0:T(8,128)S(1)}, u32[]{:S(2)}, u32[]{:S(2)}) collective-permute-start(f32[192,128]{1,0:T(8,128)S(1)} %get-tuple-element.85), channel_id=1, source_target_pairs={{0,1},{1,0},{2,3},{3,2},{4,5},{5,4},{6,7},{7,6},{8,9},{9,8},{10,11... | collective-permute-start | bytes 294920 | tf_op jit(solution)/shard_map/ppermute | solution.py:57
  24.6 0.0 collective-permute-start.9
  24.6 0.3 collective-permute-done.4.refs_2_
  24.9 0.0 collective-permute-done.5.refs_3_
  24.9 0.1 shard_map.46
  25.0 0.3 collective-permute-start.6
  25.3 3.5 %collective-permute-start.7 = (f32[7,16,128]{2,1,0:T(8,128)S(1)}, f32[7,16,128]{2,1,0:T(8,128)S(1)}, u32[]{:S(2)}, u32[]{:S(2)}) collective-permute-start(f32[7,16,128]{2,1,0:T(8,128)S(1)} %get-tuple-element.83), channel_id=1, source_target_pairs={{8,16},{16,8},{9,17},{17,9},{10,18},{18,10},{11,19},{19,11},{12,20... | collective-permute-start | bytes 172040 | tf_op jit(solution)/shard_map/ppermute | solution.py:57
  28.7 2.3 %shard_map.48.refs_6_.refs_7_ = f32[2920,24,256]{2,1,0:T(8,128)} custom-call(f32[38,24,256]{2,1,0:T(8,128)S(1)} %get-tuple-element.68.refs_4_.refs_0_, f32[38,24,256]{2,1,0:T(8,128)S(1)} %get-tuple-element.69.refs_5_.refs_1_, f32[38,24,256]{2,1,0:T(8,128)S(1)} %get-tuple-element.70.refs_6_.refs_2_, f32[38,24,256]{2,1,0:T(8,128)S(1)} %get-tuple-element.71.refs_7_.refs_3_, ...), custom_call_target="tpu_custom_call" | custom-call | tf_op jit(solution)/shard_map/pallas_call | solution.py:929
  31.0 0.0 collective-permute-done.8.refs_4_.refs_2_
  31.0 0.0 collective-permute-done.9.refs_5_.refs_3_
  31.1 0.0 collective-permute-done.6.refs_2_
  31.1 0.0 collective-permute-done.7.refs_3_
  31.1 1.4 %shard_map.49 = (f32[32,16,128]{2,1,0:T(8,128)}, f32[24,16,128]{2,1,0:T(8,128)S(1)}, f32[24,16,128]{2,1,0:T(8,128)S(1)}, f32[16,8,128]{2,1,0:T(8,128)S(1)}) custom-call(f32[16,16,128]{2,1,0:T(8,128)S(1)} %get-tuple-element.80.refs_0_, f32[16,16,128]{2,1,0:T(8,128)S(1)} %get-tuple-element.81.refs_1_, f32[7,16,128]{2,1,0:T(8,128)S(1)} %collective-permute-done.6.refs_2_, ...), custom_call_target="tpu_custom_call" | custom-call | tf_op jit(solution)/shard_map/pallas_call | solution.py:929
  32.5 0.0 all-to-all-done.1.refs_0_
  32.5 4.1 %all-to-all-start = ((f32[32,16,128]{2,1,0:T(8,128)}), f32[32,16,128]{2,1,0:T(8,128)S(1)}, u32[]{:S(2)}, u32[]{:S(2)}) async-start(f32[32,16,128]{2,1,0:T(8,128)} %get-tuple-element.92), calls=%async_computation | async-start | bytes 524288 | tf_op jit(solution)/shard_map/all_to_all | solution.py:1013
  36.7 0.1 shard_map.52
  36.8 0.3 collective-permute-start.10
  37.1 1.7 %collective-permute-start.11 = (f32[176,128]{1,0:T(8,128)S(1)}, f32[176,128]{1,0:T(8,128)S(1)}, u32[]{:S(2)}, u32[]{:S(2)}) collective-permute-start(f32[176,128]{1,0:T(8,128)S(1)} %get-tuple-element.106), channel_id=1, source_target_pairs={{8,16},{16,8},{9,17},{17,9},{10,18},{18,10},{11,19},{19,11},{12,20... | collective-permute-start | bytes 270344 | tf_op jit(solution)/shard_map/ppermute | solution.py:57
  38.8 2.3 %shard_map.50 = (f32[18,32,128]{2,1,0:T(8,128)S(1)}, f32[18,32,128]{2,1,0:T(8,128)S(1)}, f32[18,32,128]{2,1,0:T(8,128)S(1)}, f32[18,32,128]{2,1,0:T(8,128)S(1)},...) custom-call(f32[32,16,128]{2,1,0:T(8,128)} %all-to-all-done.1.refs_0_), custom_call_target="tpu_custom_call" | custom-call | tf_op jit(solution)/shard_map/pallas_call | solution.py:929
  41.1 0.0 collective-permute-done.10.refs_2_
  41.1 1.7 %collective-permute-done.11.refs_3_ = f32[176,128]{1,0:T(8,128)S(1)} collective-permute-done((f32[176,128]{1,0:T(8,128)S(1)}, f32[176,128]{1,0:T(8,128)S(1)}, u32[]{:S(2)}, u32[]{:S(2)}) %collective-permute-start.11) | collective-permute-done | bytes 90144 | tf_op jit(solution)/shard_map/ppermute | solution.py:57
  42.8 0.1 shard_map.53
  42.9 1.3 %collective-permute-start.12 = (f32[96,128]{1,0:T(8,128)S(1)}, f32[96,128]{1,0:T(8,128)S(1)}, u32[]{:S(2)}, u32[]{:S(2)}) collective-permute-start(f32[96,128]{1,0:T(8,128)S(1)} %get-tuple-element.114), channel_id=1, source_target_pairs={{0,1},{1,0},{2,3},{3,2},{4,5},{5,4},{6,7},{7,6},{8,9},{9,8},{10,11... | collective-permute-start | bytes 147464 | tf_op jit(solution)/shard_map/ppermute | solution.py:57
  44.3 0.0 collective-permute-start.13
  44.3 3.0 %all-to-all-done.refs_0_ = f32[32,16,128]{2,1,0:T(8,128)S(1)} async-done(((f32[32,16,128]{2,1,0:T(8,128)}), f32[32,16,128]{2,1,0:T(8,128)S(1)}, u32[]{:S(2)}, u32[]{:S(2)}) %all-to-all-start) | async-done | bytes 262176 | tf_op jit(solution)/shard_map/all_to_all | solution.py:1013
  47.3 3.9 %shard_map.51 = (f32[4,24,128]{2,1,0:T(8,128)S(1)}, f32[38,24,256]{2,1,0:T(8,128)S(1)}, f32[38,24,256]{2,1,0:T(8,128)S(1)}, f32[38,24,256]{2,1,0:T(8,128)S(1)}, ...) custom-call(f32[32,16,128]{2,1,0:T(8,128)S(1)} %all-to-all-done.refs_0_, ...), custom_call_target="tpu_custom_call" | custom-call | tf_op jit(solution)/shard_map/pallas_call | solution.py:929
  51.2 0.0 collective-permute-done.12.refs_10_
  51.2 0.0 collective-permute-done.13.refs_11_
  51.2 3.8 %shard_map.54 = (f32[32,16,256]{2,1,0:T(8,128)}, f32[32,16,256]{2,1,0:T(8,128)}) custom-call(f32[4,24,128]{2,1,0:T(8,128)S(1)} %get-tuple-element.100.refs_0_, f32[24,16,128]{2,1,0:T(8,128)S(1)} %get-tuple-element.101.refs_1_, f32[24,16,128]{2,1,0:T(8,128)S(1)} %get-tuple-element.102.refs_2_, f32[24,8,128]{2,1,0:T(8,128)S(1)} %get-tuple-element.107.refs_3_, ...), custom_call_target="tpu_custom_call" | custom-call | tf_op jit(solution)/shard_map/pallas_call | solution.py:929
  (2 shorter events, 0.0 us)
Async XLA Ops:
  0.6 1.0 %copy-start = (f32[32,16,256]{2,1,0:T(8,128)S(1)}, f32[32,16,256]{2,1,0:T(8,128)}, u32[]{:S(2)}) copy-start(f32[32,16,256]{2,1,0:T(8,128)} %refs_0_.1) | copy-start | bytes 1572868
  1.7 1.0 %copy-start.1 = (f32[32,16,256]{2,1,0:T(8,128)S(1)}, f32[32,16,256]{2,1,0:T(8,128)}, u32[]{:S(2)}) copy-start(f32[32,16,256]{2,1,0:T(8,128)} %refs_1_.1) | copy-start | bytes 1572868
  2.9 10.7 %collective-permute-start = (f32[5,32,256]{2,1,0:T(8,128)S(1)}, f32[5,32,256]{2,1,0:T(8,128)S(1)}, u32[]{:S(2)}, u32[]{:S(2)}) collective-permute-start(f32[5,32,256]{2,1,0:T(8,128)S(1)} %get-tuple-element.62), channel_id=1, source_target_pairs={{0,1},{1,0},{2,3},{3,2},{4,5},{5,4},{6,7},{7,6},{8,9},{9,8},{10,11... | collective-permute-start | bytes 491528 | tf_op jit(solution)/shard_map/ppermute | solution.py:57
  5.9 7.8 %collective-permute-start.1 = (f32[5,32,256]{2,1,0:T(8,128)S(1)}, f32[5,32,256]{2,1,0:T(8,128)S(1)}, u32[]{:S(2)}, u32[]{:S(2)}) collective-permute-start(f32[5,32,256]{2,1,0:T(8,128)S(1)} %get-tuple-element.63), channel_id=1, source_target_pairs={{1,2},{2,1},{3,4},{4,3},{5,6},{6,5},{9,10},{10,9},{11,12},{12,11},... | collective-permute-start | bytes 491528 | tf_op jit(solution)/shard_map/ppermute | solution.py:57
  7.1 25.4 %all-to-all-start.1 = ((f32[32,16,128]{2,1,0:T(8,128)}), f32[32,16,128]{2,1,0:T(8,128)}, u32[]{:S(2)}, u32[]{:S(2)}) async-start(f32[32,16,128]{2,1,0:T(8,128)} %get-tuple-element.93), calls=%async_computation.1 | async-start | bytes 524288 | tf_op jit(solution)/shard_map/all_to_all | solution.py:978
  13.9 4.5 %collective-permute-start.2 = (f32[88,256]{1,0:T(8,128)S(1)}, f32[88,256]{1,0:T(8,128)S(1)}, u32[]{:S(2)}, u32[]{:S(2)}) collective-permute-start(f32[88,256]{1,0:T(8,128)S(1)} %get-tuple-element.65), channel_id=1, source_target_pairs={{0,8},{8,0},{16,24},{24,16},{1,9},{9,1},{17,25},{25,17},{2,10},{10... | collective-permute-start | bytes 270344 | tf_op jit(solution)/shard_map/ppermute | solution.py:57
  14.1 5.7 %collective-permute-start.3 = (f32[88,256]{1,0:T(8,128)S(1)}, f32[88,256]{1,0:T(8,128)S(1)}, u32[]{:S(2)}, u32[]{:S(2)}) collective-permute-start(f32[88,256]{1,0:T(8,128)S(1)} %get-tuple-element.66), channel_id=1, source_target_pairs={{8,16},{16,8},{9,17},{17,9},{10,18},{18,10},{11,19},{19,11},{12,20... | collective-permute-start | bytes 270344 | tf_op jit(solution)/shard_map/ppermute | solution.py:57
  20.6 4.2 %collective-permute-start.4 = (f32[7,16,128]{2,1,0:T(8,128)S(1)}, f32[7,16,128]{2,1,0:T(8,128)S(1)}, u32[]{:S(2)}, u32[]{:S(2)}) collective-permute-start(f32[7,16,128]{2,1,0:T(8,128)S(1)} %get-tuple-element.78), channel_id=1, source_target_pairs={{0,1},{1,0},{2,3},{3,2},{4,5},{5,4},{6,7},{7,6},{8,9},{9,8},{10,11... | collective-permute-start | bytes 172040 | tf_op jit(solution)/shard_map/ppermute | solution.py:57
  21.8 3.0 %collective-permute-start.5 = (f32[7,16,128]{2,1,0:T(8,128)S(1)}, f32[7,16,128]{2,1,0:T(8,128)S(1)}, u32[]{:S(2)}, u32[]{:S(2)}) collective-permute-start(f32[7,16,128]{2,1,0:T(8,128)S(1)} %get-tuple-element.79), channel_id=1, source_target_pairs={{1,2},{2,1},{3,4},{4,3},{5,6},{6,5},{9,10},{10,9},{11,12},{12,11},... | collective-permute-start | bytes 172040 | tf_op jit(solution)/shard_map/ppermute | solution.py:57
  21.9 9.1 %collective-permute-start.8 = (f32[192,128]{1,0:T(8,128)S(1)}, f32[192,128]{1,0:T(8,128)S(1)}, u32[]{:S(2)}, u32[]{:S(2)}) collective-permute-start(f32[192,128]{1,0:T(8,128)S(1)} %get-tuple-element.85), channel_id=1, source_target_pairs={{0,1},{1,0},{2,3},{3,2},{4,5},{5,4},{6,7},{7,6},{8,9},{9,8},{10,11... | collective-permute-start | bytes 294920 | tf_op jit(solution)/shard_map/ppermute | solution.py:57
  24.6 6.5 %collective-permute-start.9 = (f32[192,128]{1,0:T(8,128)S(1)}, f32[192,128]{1,0:T(8,128)S(1)}, u32[]{:S(2)}, u32[]{:S(2)}) collective-permute-start(f32[192,128]{1,0:T(8,128)S(1)} %get-tuple-element.86), channel_id=1, source_target_pairs={{1,2},{2,1},{3,4},{4,3},{5,6},{6,5},{9,10},{10,9},{11,12},{12,11},... | collective-permute-start | bytes 294920 | tf_op jit(solution)/shard_map/ppermute | solution.py:57
  25.0 6.1 %collective-permute-start.6 = (f32[7,16,128]{2,1,0:T(8,128)S(1)}, f32[7,16,128]{2,1,0:T(8,128)S(1)}, u32[]{:S(2)}, u32[]{:S(2)}) collective-permute-start(f32[7,16,128]{2,1,0:T(8,128)S(1)} %get-tuple-element.82), channel_id=1, source_target_pairs={{0,8},{8,0},{16,24},{24,16},{1,9},{9,1},{17,25},{25,17},{2,10},{10... | collective-permute-start | bytes 172040 | tf_op jit(solution)/shard_map/ppermute | solution.py:57
  25.3 5.8 %collective-permute-start.7 = (f32[7,16,128]{2,1,0:T(8,128)S(1)}, f32[7,16,128]{2,1,0:T(8,128)S(1)}, u32[]{:S(2)}, u32[]{:S(2)}) collective-permute-start(f32[7,16,128]{2,1,0:T(8,128)S(1)} %get-tuple-element.83), channel_id=1, source_target_pairs={{8,16},{16,8},{9,17},{17,9},{10,18},{18,10},{11,19},{19,11},{12,20... | collective-permute-start | bytes 172040 | tf_op jit(solution)/shard_map/ppermute | solution.py:57
  32.5 14.8 %all-to-all-start = ((f32[32,16,128]{2,1,0:T(8,128)}), f32[32,16,128]{2,1,0:T(8,128)S(1)}, u32[]{:S(2)}, u32[]{:S(2)}) async-start(f32[32,16,128]{2,1,0:T(8,128)} %get-tuple-element.92), calls=%async_computation | async-start | bytes 524288 | tf_op jit(solution)/shard_map/all_to_all | solution.py:1013
  36.8 4.3 %collective-permute-start.10 = (f32[176,128]{1,0:T(8,128)S(1)}, f32[176,128]{1,0:T(8,128)S(1)}, u32[]{:S(2)}, u32[]{:S(2)}) collective-permute-start(f32[176,128]{1,0:T(8,128)S(1)} %get-tuple-element.105), channel_id=1, source_target_pairs={{0,8},{8,0},{16,24},{24,16},{1,9},{9,1},{17,25},{25,17},{2,10},{10... | collective-permute-start | bytes 270344 | tf_op jit(solution)/shard_map/ppermute | solution.py:57
  37.1 5.7 %collective-permute-start.11 = (f32[176,128]{1,0:T(8,128)S(1)}, f32[176,128]{1,0:T(8,128)S(1)}, u32[]{:S(2)}, u32[]{:S(2)}) collective-permute-start(f32[176,128]{1,0:T(8,128)S(1)} %get-tuple-element.106), channel_id=1, source_target_pairs={{8,16},{16,8},{9,17},{17,9},{10,18},{18,10},{11,19},{19,11},{12,20... | collective-permute-start | bytes 270344 | tf_op jit(solution)/shard_map/ppermute | solution.py:57
  42.9 8.3 %collective-permute-start.12 = (f32[96,128]{1,0:T(8,128)S(1)}, f32[96,128]{1,0:T(8,128)S(1)}, u32[]{:S(2)}, u32[]{:S(2)}) collective-permute-start(f32[96,128]{1,0:T(8,128)S(1)} %get-tuple-element.114), channel_id=1, source_target_pairs={{0,1},{1,0},{2,3},{3,2},{4,5},{5,4},{6,7},{7,6},{8,9},{9,8},{10,11... | collective-permute-start | bytes 147464 | tf_op jit(solution)/shard_map/ppermute | solution.py:57
  44.3 6.9 %collective-permute-start.13 = (f32[96,128]{1,0:T(8,128)S(1)}, f32[96,128]{1,0:T(8,128)S(1)}, u32[]{:S(2)}, u32[]{:S(2)}) collective-permute-start(f32[96,128]{1,0:T(8,128)S(1)} %get-tuple-element.115), channel_id=1, source_target_pairs={{1,2},{2,1},{3,4},{4,3},{5,6},{6,5},{9,10},{10,9},{11,12},{12,11},... | collective-permute-start | bytes 147464 | tf_op jit(solution)/shard_map/ppermute | solution.py:57

commit v10 on v9

--- a/solution.py
+++ b/solution.py
@@ -226,8 +226,10 @@
     return out + (lanes * up(here, 1) + down(lanes * here, 1))
 
 
-def pre_smooth(b, first, second, w, inverse, scale, outer, inner):
+def pre_smooth(b, first, second, w, inverse, scale, outer, inner, total=None):
     def start(i):
+        if total is not None:
+            inverse[i] = invert(total[i])
         first[i] = b[i] * inverse[i] * (1.0 / (scale * THETA))
 
     for span in outer:
@@ -669,11 +671,11 @@
     return out + (lanes * up(here, 1) + down(lanes * here, 1))
 
 
-def coarse_pre(b, w, inverse, first, second, scale):
+def coarse_pre(b, w, inverse, first, second, scale, total):
     ends = [(1, b.shape[0] - 1)]
     clear_ends(first)
     clear_ends(second)
-    pre_smooth(b, first, second, w, inverse, scale, ends, ends)
+    pre_smooth(b, first, second, w, inverse, scale, ends, ends, total)
 
 
 def widened(x, matrix):
@@ -781,7 +783,6 @@
 
     def complete(i):
         low2[i] = across_down(wl2[i], wl2[i - 1])
-        inverse2[i] = invert(total2[i])
 
     def unpack3(i):
         lane = iota(level3.shape[1:], 1)
@@ -790,13 +791,12 @@
             if f:
                 part = pltpu.roll(part, lanes - f * half, 1)
             ref[i] = jnp.where(lane < half, part, 0.0)
-        inverse3[i] = invert(total3[i])
 
     loop(1, own3 + 1, complete, b2.shape[1:])
     loop(0, own3 + 1, unpack3, level3.shape[1:])
     w2, w3 = (wl2, low2, ws2, wz2), (wl3, ws3, wz3)
     scale2, scale3 = 0.25**2, 0.25**3
-    coarse_pre(b2, w2, inverse2, first2, second2, scale2)
+    coarse_pre(b2, w2, inverse2, first2, second2, scale2, total2)
 
     def rest2(j):
         pairs2[j] = residual(b2, second2, w2, total2, scale2, j + 1)
@@ -804,7 +804,7 @@
     loop(0, own3, rest2, pairs2.shape[1:])
     clear_ends(b3)
     b3[1 : own3 + 1] = coarser(pairs2[...], halves2, matrix2)
-    coarse_pre(b3, w3, inverse3, first3, second3, scale3)
+    coarse_pre(b3, w3, inverse3, first3, second3, scale3, total3)
 
     def rest3(j):
         i = 2 * j + 1

time: 55.3 us -> 55.4 us (level)
  transfers between devices with their start and end apart: 16 -> 16, of which waited for: 4 -> 4; matrix products, arithmetic and copies ran while one was open for 0% -> 0% of each run, Pallas kernels for 27% -> 28%
where the time goes in v10:
time: 55.4 us; the launch traced here: 55 us
  starting transfers between devices  26.5 us (48%)
  Pallas kernels  19.1 us (34%)
  waiting for transfers between devices  6.48 us (12%)
  local copies, waits for them, and re-layouts  2.08 us (4%)
  between operations  0.85 us (2%)
    pallas_call x14, Pallas kernels, run(): pl.pallas_call(body, out_shape=[jax.ShapeDtypeStruct(shape, F32) for shap...  19.1 us
    ppermute x7, starting transfers between devices, swap(): lax.ppermute(first, axes, pairs(0))  9.06 us
    ppermute x7, starting transfers between devices, swap(): lax.ppermute(second, axes, pairs(1))  6.82 us
    all_to_all x1, starting transfers between devices, per_device(): k2 = lax.all_to_all(message, both, 0, 0, tiled=True)  6.52 us
    all_to_all x1, starting transfers between devices, per_device(): received = lax.all_to_all(message, both, 0, 0, tiled=True)  4.1 us
    ppermute x7, waiting for transfers between devices, swap(): lax.ppermute(second, axes, pairs(1))  3.13 us
    all_to_all x1, waiting for transfers between devices, per_device(): received = lax.all_to_all(message, both, 0, 0, tiled=True)  3.05 us
    unnamed x4, local copies, waits for them, and re-layouts  2.08 us
  transfers between devices with their start and end apart: 16, of which 4 were waited for; matrix products, arithmetic and copies ran while one was open for 0% of the time, Pallas kernels for 28%

profile of v10, /device:TPU:0, one launch (start us, length us, event | category | flops | bytes accessed | tf_op | source)
XLA Modules:
  0.0 55.0 jit_solution(15024973759742680886)
XLA Ops:
  0.6 1.0 %copy-done = f32[32,16,256]{2,1,0:T(8,128)S(1)} copy-done((f32[32,16,256]{2,1,0:T(8,128)S(1)}, f32[32,16,256]{2,1,0:T(8,128)}, u32[]{:S(2)}) %copy-start) | copy-done | bytes 524312
  1.7 1.0 %copy-done.1 = f32[32,16,256]{2,1,0:T(8,128)S(1)} copy-done((f32[32,16,256]{2,1,0:T(8,128)S(1)}, f32[32,16,256]{2,1,0:T(8,128)}, u32[]{:S(2)}) %copy-start.1) | copy-done | bytes 524312
  2.7 0.2 shard_map.41
  2.9 3.0 %collective-permute-start = (f32[5,32,256]{2,1,0:T(8,128)S(1)}, f32[5,32,256]{2,1,0:T(8,128)S(1)}, u32[]{:S(2)}, u32[]{:S(2)}) collective-permute-start(f32[5,32,256]{2,1,0:T(8,128)S(1)} %get-tuple-element.62), channel_id=1, source_target_pairs={{0,1},{1,0},{2,3},{3,2},{4,5},{5,4},{6,7},{7,6},{8,9},{9,8},{10,11... | collective-permute-start | bytes 491528 | tf_op jit(solution)/shard_map/ppermute | solution.py:57
  5.9 0.0 collective-permute-start.1
  5.9 1.2 %shard_map.42 = (f32[32,16,128]{2,1,0:T(8,128)}, f32[16,8,128]{2,1,0:T(8,128)S(1)}) custom-call(f32[32,16,256]{2,1,0:T(8,128)S(1)} %get-tuple-element.59.refs_0_.refs_1_), custom_call_target="tpu_custom_call" | custom-call | tf_op jit(solution)/shard_map/pallas_call | solution.py:929
  7.1 6.5 %all-to-all-start.1 = ((f32[32,16,128]{2,1,0:T(8,128)}), f32[32,16,128]{2,1,0:T(8,128)}, u32[]{:S(2)}, u32[]{:S(2)}) async-start(f32[32,16,128]{2,1,0:T(8,128)} %get-tuple-element.93), calls=%async_computation.1 | async-start | bytes 524288 | tf_op jit(solution)/shard_map/all_to_all | solution.py:978
  13.6 0.0 collective-permute-done.refs_2_
  13.7 0.0 collective-permute-done.1.refs_3_
  13.7 0.2 shard_map.43
  13.9 0.2 collective-permute-start.2
  14.1 1.7 %collective-permute-start.3 = (f32[88,256]{1,0:T(8,128)S(1)}, f32[88,256]{1,0:T(8,128)S(1)}, u32[]{:S(2)}, u32[]{:S(2)}) collective-permute-start(f32[88,256]{1,0:T(8,128)S(1)} %get-tuple-element.66), channel_id=1, source_target_pairs={{8,16},{16,8},{9,17},{17,9},{10,18},{18,10},{11,19},{19,11},{12,20... | collective-permute-start | bytes 270344 | tf_op jit(solution)/shard_map/ppermute | solution.py:57
  15.8 2.5 %shard_map.44 = (f32[38,24,256]{2,1,0:T(8,128)S(1)}, f32[38,24,256]{2,1,0:T(8,128)S(1)}, f32[38,24,256]{2,1,0:T(8,128)S(1)}, f32[38,24,256]{2,1,0:T(8,128)S(1)},...) custom-call(f32[32,24,256]{2,1,0:T(8,128)S(1)} %get-tuple-element.64, ...), custom_call_target="tpu_custom_call" | custom-call | tf_op jit(solution)/shard_map/pallas_call | solution.py:929
  18.4 0.0 collective-permute-done.2.refs_1_
  18.4 1.4 %collective-permute-done.3.refs_2_ = f32[88,256]{1,0:T(8,128)S(1)} collective-permute-done((f32[88,256]{1,0:T(8,128)S(1)}, f32[88,256]{1,0:T(8,128)S(1)}, u32[]{:S(2)}, u32[]{:S(2)}) %collective-permute-start.3) | collective-permute-done | bytes 90144 | tf_op jit(solution)/shard_map/ppermute | solution.py:57
  19.8 0.8 %shard_map.45 = (f32[8,24,256]{2,1,0:T(8,128)S(1)}, f32[8,24,256]{2,1,0:T(8,128)S(1)}, f32[8,24,256]{2,1,0:T(8,128)S(1)}, f32[8,24,256]{2,1,0:T(8,128)S(1)}, f32...) custom-call(f32[32,24,256]{2,1,0:T(8,128)S(1)} %get-tuple-element.64, ...), custom_call_target="tpu_custom_call" | custom-call | tf_op jit(solution)/shard_map/pallas_call | solution.py:929
  20.6 1.2 %collective-permute-start.4 = (f32[7,16,128]{2,1,0:T(8,128)S(1)}, f32[7,16,128]{2,1,0:T(8,128)S(1)}, u32[]{:S(2)}, u32[]{:S(2)}) collective-permute-start(f32[7,16,128]{2,1,0:T(8,128)S(1)} %get-tuple-element.78), channel_id=1, source_target_pairs={{0,1},{1,0},{2,3},{3,2},{4,5},{5,4},{6,7},{7,6},{8,9},{9,8},{10,11... | collective-permute-start | bytes 172040 | tf_op jit(solution)/shard_map/ppermute | solution.py:57
  21.8 0.0 collective-permute-start.5
  21.8 0.1 shard_map.47
  21.9 2.7 %collective-permute-start.8 = (f32[192,128]{1,0:T(8,128)S(1)}, f32[192,128]{1,0:T(8,128)S(1)}, u32[]{:S(2)}, u32[]{:S(2)}) collective-permute-start(f32[192,128]{1,0:T(8,128)S(1)} %get-tuple-element.85), channel_id=1, source_target_pairs={{0,1},{1,0},{2,3},{3,2},{4,5},{5,4},{6,7},{7,6},{8,9},{9,8},{10,11... | collective-permute-start | bytes 294920 | tf_op jit(solution)/shard_map/ppermute | solution.py:57
  24.6 0.0 collective-permute-start.9
  24.6 0.3 collective-permute-done.4.refs_2_
  24.9 0.0 collective-permute-done.5.refs_3_
  24.9 0.1 shard_map.46
  25.0 0.3 collective-permute-start.6
  25.3 3.5 %collective-permute-start.7 = (f32[7,16,128]{2,1,0:T(8,128)S(1)}, f32[7,16,128]{2,1,0:T(8,128)S(1)}, u32[]{:S(2)}, u32[]{:S(2)}) collective-permute-start(f32[7,16,128]{2,1,0:T(8,128)S(1)} %get-tuple-element.83), channel_id=1, source_target_pairs={{8,16},{16,8},{9,17},{17,9},{10,18},{18,10},{11,19},{19,11},{12,20... | collective-permute-start | bytes 172040 | tf_op jit(solution)/shard_map/ppermute | solution.py:57
  28.7 2.3 %shard_map.48.refs_6_.refs_7_ = f32[2920,24,256]{2,1,0:T(8,128)} custom-call(f32[38,24,256]{2,1,0:T(8,128)S(1)} %get-tuple-element.68.refs_4_.refs_0_, f32[38,24,256]{2,1,0:T(8,128)S(1)} %get-tuple-element.69.refs_5_.refs_1_, f32[38,24,256]{2,1,0:T(8,128)S(1)} %get-tuple-element.70.refs_6_.refs_2_, f32[38,24,256]{2,1,0:T(8,128)S(1)} %get-tuple-element.71.refs_7_.refs_3_, ...), custom_call_target="tpu_custom_call" | custom-call | tf_op jit(solution)/shard_map/pallas_call | solution.py:929
  31.0 0.0 collective-permute-done.8.refs_4_.refs_2_
  31.0 0.0 collective-permute-done.9.refs_5_.refs_3_
  31.1 0.0 collective-permute-done.6.refs_2_
  31.1 0.0 collective-permute-done.7.refs_3_
  31.1 1.4 %shard_map.49 = (f32[32,16,128]{2,1,0:T(8,128)}, f32[24,16,128]{2,1,0:T(8,128)S(1)}, f32[24,16,128]{2,1,0:T(8,128)S(1)}, f32[16,8,128]{2,1,0:T(8,128)S(1)}) custom-call(f32[16,16,128]{2,1,0:T(8,128)S(1)} %get-tuple-element.80.refs_0_, f32[16,16,128]{2,1,0:T(8,128)S(1)} %get-tuple-element.81.refs_1_, f32[7,16,128]{2,1,0:T(8,128)S(1)} %collective-permute-done.6.refs_2_, ...), custom_call_target="tpu_custom_call" | custom-call | tf_op jit(solution)/shard_map/pallas_call | solution.py:929
  32.5 0.0 all-to-all-done.1.refs_0_
  32.5 4.1 %all-to-all-start = ((f32[32,16,128]{2,1,0:T(8,128)}), f32[32,16,128]{2,1,0:T(8,128)S(1)}, u32[]{:S(2)}, u32[]{:S(2)}) async-start(f32[32,16,128]{2,1,0:T(8,128)} %get-tuple-element.92), calls=%async_computation | async-start | bytes 524288 | tf_op jit(solution)/shard_map/all_to_all | solution.py:1013
  36.7 0.1 shard_map.52
  36.8 0.3 collective-permute-start.10
  37.1 1.7 %collective-permute-start.11 = (f32[176,128]{1,0:T(8,128)S(1)}, f32[176,128]{1,0:T(8,128)S(1)}, u32[]{:S(2)}, u32[]{:S(2)}) collective-permute-start(f32[176,128]{1,0:T(8,128)S(1)} %get-tuple-element.106), channel_id=1, source_target_pairs={{8,16},{16,8},{9,17},{17,9},{10,18},{18,10},{11,19},{19,11},{12,20... | collective-permute-start | bytes 270344 | tf_op jit(solution)/shard_map/ppermute | solution.py:57
  38.8 2.3 %shard_map.50 = (f32[18,32,128]{2,1,0:T(8,128)S(1)}, f32[18,32,128]{2,1,0:T(8,128)S(1)}, f32[18,32,128]{2,1,0:T(8,128)S(1)}, f32[18,32,128]{2,1,0:T(8,128)S(1)},...) custom-call(f32[32,16,128]{2,1,0:T(8,128)} %all-to-all-done.1.refs_0_), custom_call_target="tpu_custom_call" | custom-call | tf_op jit(solution)/shard_map/pallas_call | solution.py:929
  41.1 0.0 collective-permute-done.10.refs_2_
  41.1 1.7 %collective-permute-done.11.refs_3_ = f32[176,128]{1,0:T(8,128)S(1)} collective-permute-done((f32[176,128]{1,0:T(8,128)S(1)}, f32[176,128]{1,0:T(8,128)S(1)}, u32[]{:S(2)}, u32[]{:S(2)}) %collective-permute-start.11) | collective-permute-done | bytes 90144 | tf_op jit(solution)/shard_map/ppermute | solution.py:57
  42.8 0.1 shard_map.53
  42.9 1.3 %collective-permute-start.12 = (f32[96,128]{1,0:T(8,128)S(1)}, f32[96,128]{1,0:T(8,128)S(1)}, u32[]{:S(2)}, u32[]{:S(2)}) collective-permute-start(f32[96,128]{1,0:T(8,128)S(1)} %get-tuple-element.114), channel_id=1, source_target_pairs={{0,1},{1,0},{2,3},{3,2},{4,5},{5,4},{6,7},{7,6},{8,9},{9,8},{10,11... | collective-permute-start | bytes 147464 | tf_op jit(solution)/shard_map/ppermute | solution.py:57
  44.3 0.0 collective-permute-start.13
  44.3 3.0 %all-to-all-done.refs_0_ = f32[32,16,128]{2,1,0:T(8,128)S(1)} async-done(((f32[32,16,128]{2,1,0:T(8,128)}), f32[32,16,128]{2,1,0:T(8,128)S(1)}, u32[]{:S(2)}, u32[]{:S(2)}) %all-to-all-start) | async-done | bytes 262176 | tf_op jit(solution)/shard_map/all_to_all | solution.py:1013
  47.3 3.9 %shard_map.51 = (f32[4,24,128]{2,1,0:T(8,128)S(1)}, f32[38,24,256]{2,1,0:T(8,128)S(1)}, f32[38,24,256]{2,1,0:T(8,128)S(1)}, f32[38,24,256]{2,1,0:T(8,128)S(1)}, ...) custom-call(f32[32,16,128]{2,1,0:T(8,128)S(1)} %all-to-all-done.refs_0_, ...), custom_call_target="tpu_custom_call" | custom-call | tf_op jit(solution)/shard_map/pallas_call | solution.py:929
  51.2 0.0 collective-permute-done.12.refs_10_
  51.2 0.0 collective-permute-done.13.refs_11_
  51.2 3.8 %shard_map.54 = (f32[32,16,256]{2,1,0:T(8,128)}, f32[32,16,256]{2,1,0:T(8,128)}) custom-call(f32[4,24,128]{2,1,0:T(8,128)S(1)} %get-tuple-element.100.refs_0_, f32[24,16,128]{2,1,0:T(8,128)S(1)} %get-tuple-element.101.refs_1_, f32[24,16,128]{2,1,0:T(8,128)S(1)} %get-tuple-element.102.refs_2_, f32[24,8,128]{2,1,0:T(8,128)S(1)} %get-tuple-element.107.refs_3_, ...), custom_call_target="tpu_custom_call" | custom-call | tf_op jit(solution)/shard_map/pallas_call | solution.py:929
  (2 shorter events, 0.0 us)
Async XLA Ops:
  0.6 1.0 %copy-start = (f32[32,16,256]{2,1,0:T(8,128)S(1)}, f32[32,16,256]{2,1,0:T(8,128)}, u32[]{:S(2)}) copy-start(f32[32,16,256]{2,1,0:T(8,128)} %refs_0_.1) | copy-start | bytes 1572868
  1.7 1.0 %copy-start.1 = (f32[32,16,256]{2,1,0:T(8,128)S(1)}, f32[32,16,256]{2,1,0:T(8,128)}, u32[]{:S(2)}) copy-start(f32[32,16,256]{2,1,0:T(8,128)} %refs_1_.1) | copy-start | bytes 1572868
  2.9 10.7 %collective-permute-start = (f32[5,32,256]{2,1,0:T(8,128)S(1)}, f32[5,32,256]{2,1,0:T(8,128)S(1)}, u32[]{:S(2)}, u32[]{:S(2)}) collective-permute-start(f32[5,32,256]{2,1,0:T(8,128)S(1)} %get-tuple-element.62), channel_id=1, source_target_pairs={{0,1},{1,0},{2,3},{3,2},{4,5},{5,4},{6,7},{7,6},{8,9},{9,8},{10,11... | collective-permute-start | bytes 491528 | tf_op jit(solution)/shard_map/ppermute | solution.py:57
  5.9 7.8 %collective-permute-start.1 = (f32[5,32,256]{2,1,0:T(8,128)S(1)}, f32[5,32,256]{2,1,0:T(8,128)S(1)}, u32[]{:S(2)}, u32[]{:S(2)}) collective-permute-start(f32[5,32,256]{2,1,0:T(8,128)S(1)} %get-tuple-element.63), channel_id=1, source_target_pairs={{1,2},{2,1},{3,4},{4,3},{5,6},{6,5},{9,10},{10,9},{11,12},{12,11},... | collective-permute-start | bytes 491528 | tf_op jit(solution)/shard_map/ppermute | solution.py:57
  7.1 25.4 %all-to-all-start.1 = ((f32[32,16,128]{2,1,0:T(8,128)}), f32[32,16,128]{2,1,0:T(8,128)}, u32[]{:S(2)}, u32[]{:S(2)}) async-start(f32[32,16,128]{2,1,0:T(8,128)} %get-tuple-element.93), calls=%async_computation.1 | async-start | bytes 524288 | tf_op jit(solution)/shard_map/all_to_all | solution.py:978
  13.9 4.5 %collective-permute-start.2 = (f32[88,256]{1,0:T(8,128)S(1)}, f32[88,256]{1,0:T(8,128)S(1)}, u32[]{:S(2)}, u32[]{:S(2)}) collective-permute-start(f32[88,256]{1,0:T(8,128)S(1)} %get-tuple-element.65), channel_id=1, source_target_pairs={{0,8},{8,0},{16,24},{24,16},{1,9},{9,1},{17,25},{25,17},{2,10},{10... | collective-permute-start | bytes 270344 | tf_op jit(solution)/shard_map/ppermute | solution.py:57
  14.1 5.7 %collective-permute-start.3 = (f32[88,256]{1,0:T(8,128)S(1)}, f32[88,256]{1,0:T(8,128)S(1)}, u32[]{:S(2)}, u32[]{:S(2)}) collective-permute-start(f32[88,256]{1,0:T(8,128)S(1)} %get-tuple-element.66), channel_id=1, source_target_pairs={{8,16},{16,8},{9,17},{17,9},{10,18},{18,10},{11,19},{19,11},{12,20... | collective-permute-start | bytes 270344 | tf_op jit(solution)/shard_map/ppermute | solution.py:57
  20.6 4.2 %collective-permute-start.4 = (f32[7,16,128]{2,1,0:T(8,128)S(1)}, f32[7,16,128]{2,1,0:T(8,128)S(1)}, u32[]{:S(2)}, u32[]{:S(2)}) collective-permute-start(f32[7,16,128]{2,1,0:T(8,128)S(1)} %get-tuple-element.78), channel_id=1, source_target_pairs={{0,1},{1,0},{2,3},{3,2},{4,5},{5,4},{6,7},{7,6},{8,9},{9,8},{10,11... | collective-permute-start | bytes 172040 | tf_op jit(solution)/shard_map/ppermute | solution.py:57
  21.8 3.0 %collective-permute-start.5 = (f32[7,16,128]{2,1,0:T(8,128)S(1)}, f32[7,16,128]{2,1,0:T(8,128)S(1)}, u32[]{:S(2)}, u32[]{:S(2)}) collective-permute-start(f32[7,16,128]{2,1,0:T(8,128)S(1)} %get-tuple-element.79), channel_id=1, source_target_pairs={{1,2},{2,1},{3,4},{4,3},{5,6},{6,5},{9,10},{10,9},{11,12},{12,11},... | collective-permute-start | bytes 172040 | tf_op jit(solution)/shard_map/ppermute | solution.py:57
  21.9 9.1 %collective-permute-start.8 = (f32[192,128]{1,0:T(8,128)S(1)}, f32[192,128]{1,0:T(8,128)S(1)}, u32[]{:S(2)}, u32[]{:S(2)}) collective-permute-start(f32[192,128]{1,0:T(8,128)S(1)} %get-tuple-element.85), channel_id=1, source_target_pairs={{0,1},{1,0},{2,3},{3,2},{4,5},{5,4},{6,7},{7,6},{8,9},{9,8},{10,11... | collective-permute-start | bytes 294920 | tf_op jit(solution)/shard_map/ppermute | solution.py:57
  24.6 6.5 %collective-permute-start.9 = (f32[192,128]{1,0:T(8,128)S(1)}, f32[192,128]{1,0:T(8,128)S(1)}, u32[]{:S(2)}, u32[]{:S(2)}) collective-permute-start(f32[192,128]{1,0:T(8,128)S(1)} %get-tuple-element.86), channel_id=1, source_target_pairs={{1,2},{2,1},{3,4},{4,3},{5,6},{6,5},{9,10},{10,9},{11,12},{12,11},... | collective-permute-start | bytes 294920 | tf_op jit(solution)/shard_map/ppermute | solution.py:57
  25.0 6.1 %collective-permute-start.6 = (f32[7,16,128]{2,1,0:T(8,128)S(1)}, f32[7,16,128]{2,1,0:T(8,128)S(1)}, u32[]{:S(2)}, u32[]{:S(2)}) collective-permute-start(f32[7,16,128]{2,1,0:T(8,128)S(1)} %get-tuple-element.82), channel_id=1, source_target_pairs={{0,8},{8,0},{16,24},{24,16},{1,9},{9,1},{17,25},{25,17},{2,10},{10... | collective-permute-start | bytes 172040 | tf_op jit(solution)/shard_map/ppermute | solution.py:57
  25.3 5.8 %collective-permute-start.7 = (f32[7,16,128]{2,1,0:T(8,128)S(1)}, f32[7,16,128]{2,1,0:T(8,128)S(1)}, u32[]{:S(2)}, u32[]{:S(2)}) collective-permute-start(f32[7,16,128]{2,1,0:T(8,128)S(1)} %get-tuple-element.83), channel_id=1, source_target_pairs={{8,16},{16,8},{9,17},{17,9},{10,18},{18,10},{11,19},{19,11},{12,20... | collective-permute-start | bytes 172040 | tf_op jit(solution)/shard_map/ppermute | solution.py:57
  32.5 14.8 %all-to-all-start = ((f32[32,16,128]{2,1,0:T(8,128)}), f32[32,16,128]{2,1,0:T(8,128)S(1)}, u32[]{:S(2)}, u32[]{:S(2)}) async-start(f32[32,16,128]{2,1,0:T(8,128)} %get-tuple-element.92), calls=%async_computation | async-start | bytes 524288 | tf_op jit(solution)/shard_map/all_to_all | solution.py:1013
  36.8 4.3 %collective-permute-start.10 = (f32[176,128]{1,0:T(8,128)S(1)}, f32[176,128]{1,0:T(8,128)S(1)}, u32[]{:S(2)}, u32[]{:S(2)}) collective-permute-start(f32[176,128]{1,0:T(8,128)S(1)} %get-tuple-element.105), channel_id=1, source_target_pairs={{0,8},{8,0},{16,24},{24,16},{1,9},{9,1},{17,25},{25,17},{2,10},{10... | collective-permute-start | bytes 270344 | tf_op jit(solution)/shard_map/ppermute | solution.py:57
  37.1 5.7 %collective-permute-start.11 = (f32[176,128]{1,0:T(8,128)S(1)}, f32[176,128]{1,0:T(8,128)S(1)}, u32[]{:S(2)}, u32[]{:S(2)}) collective-permute-start(f32[176,128]{1,0:T(8,128)S(1)} %get-tuple-element.106), channel_id=1, source_target_pairs={{8,16},{16,8},{9,17},{17,9},{10,18},{18,10},{11,19},{19,11},{12,20... | collective-permute-start | bytes 270344 | tf_op jit(solution)/shard_map/ppermute | solution.py:57
  42.9 8.3 %collective-permute-start.12 = (f32[96,128]{1,0:T(8,128)S(1)}, f32[96,128]{1,0:T(8,128)S(1)}, u32[]{:S(2)}, u32[]{:S(2)}) collective-permute-start(f32[96,128]{1,0:T(8,128)S(1)} %get-tuple-element.114), channel_id=1, source_target_pairs={{0,1},{1,0},{2,3},{3,2},{4,5},{5,4},{6,7},{7,6},{8,9},{9,8},{10,11... | collective-permute-start | bytes 147464 | tf_op jit(solution)/shard_map/ppermute | solution.py:57
  44.3 7.0 %collective-permute-start.13 = (f32[96,128]{1,0:T(8,128)S(1)}, f32[96,128]{1,0:T(8,128)S(1)}, u32[]{:S(2)}, u32[]{:S(2)}) collective-permute-start(f32[96,128]{1,0:T(8,128)S(1)} %get-tuple-element.115), channel_id=1, source_target_pairs={{1,2},{2,1},{3,4},{4,3},{5,6},{6,5},{9,10},{10,9},{11,12},{12,11},... | collective-permute-start | bytes 147464 | tf_op jit(solution)/shard_map/ppermute | solution.py:57
